TPU v7x, 32 devices: a whole 2x2x4 slice. The times are simulated.
32 devices in a mesh: section: 2 (over core), tensor: 4 (over y, x), dp: 4 (over z).
Axes of the slice: x: 2, y: 2, z: 4, core: 2. Of those that a mesh axis runs over, the one named last changes fastest.
Arguments:
- inputs: bfloat16 [2, 2048, 1152], P(None, 'dp'), may hold values from -6 to 6
- cotangent: bfloat16 [2, 2048, 1152], P(None, 'dp'), may hold values from -6 to 6
- conditioning: bfloat16 [2, 4, 4, 1152], P(None, 'dp'), may hold values from -6 to 6
- lengths: int32 [2, 4, 4], P(None, 'dp'), may hold values from 1 to 256, 512 in all within a row
- positions: int32 [2, 2, 2048], P(None, None, 'dp'), may hold values from 0 to 63
- modulator: bfloat16 [2, 1152, 6912], P('section', None, 'tensor'), may hold values from -0.1875 to 0.1875
- projections: bfloat16 [2, 3, 1152, 1152], P('section', None, None, 'tensor'), may hold values from -0.1875 to 0.1875
- norm_gains: float32 [2, 2, 72], P('section'), may hold values from 0.1 to 1.9
- out_weight: bfloat16 [2, 1152, 1152], P('section', 'tensor'), may hold values from -1 to 1
- gate_up: bfloat16 [2, 2, 1152, 3072], P('section', None, None, 'tensor'), may hold values from -0.1875 to 0.1875
- down_weight: bfloat16 [2, 3072, 1152], P('section', 'tensor'), may hold values from -0.109375 to 0.109375
Outputs:
- grad_modulator: float32 [2, 1152, 6912], P('section', 'dp', 'tensor')
- grad_projections: float32 [2, 3, 1152, 1152], P('section', None, 'dp', 'tensor')
- grad_norm_gains: float32 [2, 2, 72], P('section')
- grad_out_weight: float32 [2, 1152, 1152], P('section', 'tensor', 'dp')
- grad_gate_up: float32 [2, 2, 1152, 3072], P('section', None, 'dp', 'tensor')
- grad_down_weight: float32 [2, 3072, 1152], P('section', 'tensor', 'dp')
- grad_conditioning: float32 [2, 4, 4, 1152], P(None, 'dp')
- section_results: float32 [2, 2, 2048, 1152], P('section', None, ('dp', 'tensor'))
Inputs may be any that keep to these rules, and one draw needn't show every extreme that they name: Each pack's lengths add up to 512; in every pack the largest is exactly 256.
All inputs are finite; a program needn't handle non-finite values.
Results may differ from a plain program's by a relative error of at most 0.019.
Values may be sent and summed in bfloat16 or wider, within the bound.
No kernel may reach another device: no remote copies, remote signals or barrier semaphores. Data moves between devices by JAX's collectives and lax.ppermute only.
A program may use at most 256 MiB of HBM per device.

v0:
```python
import jax
import jax.numpy as jnp
from jax import lax
from jax.sharding import PartitionSpec as P

HEAD = 72


HIGHEST = lax.Precision.HIGHEST
epsilon = 1e-06


def shifted(value, axis, steps):
    count = lax.axis_size(axis)
    leading, last = (max(0, -steps), min(count, count - steps))
    return lax.ppermute(value, axis, [(source, source + steps) for source in range(leading, last)])


def inverse_rms(value):
    return lax.rsqrt(jnp.mean(value * value, axis=-1, keepdims=True) + epsilon)


def norm_back(grad, normed, inverse):
    return inverse * (grad - normed * jnp.mean(grad * normed, axis=-1, keepdims=True))


def rotate(value, cosine, sine):
    half = value.shape[-1] // 2
    first = value[..., :half]
    second = value[..., half:]
    return jnp.concatenate(
        [first * cosine - second * sine, first * sine + second * cosine], axis=-1
    )


def unrotate(grad, cosine, sine):
    half = grad.shape[-1] // 2
    first = grad[..., :half]
    second = grad[..., half:]
    return jnp.concatenate(
        [first * cosine + second * sine, second * cosine - first * sine], axis=-1
    )


def angles(rows, cols):
    quarter = HEAD // 4
    rates = 10000.0 ** (-jnp.arange(quarter).astype(jnp.float32) / quarter)
    phase = jnp.concatenate(
        [rows.astype(jnp.float32)[..., None] * rates, cols.astype(jnp.float32)[..., None] * rates],
        axis=-1,
    )
    return (jnp.cos(phase)[..., None, :], jnp.sin(phase)[..., None, :])


def branch_sum(partial_sum):
    shares = lax.psum_scatter(partial_sum, "tensor", scatter_dimension=0, tiled=True)
    return lax.all_gather(shares, "tensor", axis=0, tiled=True)


def input_sum(partial_sum):
    shares = lax.psum_scatter(partial_sum, "tensor", scatter_dimension=0, tiled=True)
    return lax.all_gather(shares, "tensor", axis=0, tiled=True)


def forward_pieces(layer_input, modulation, weights, shape_info):
    projections, out_weight, gains, gate_up, down_weight = weights
    same, cosine, sine = shape_info
    heads = projections.shape[2] // HEAD
    shift1, scale1, gate1, shift2, scale2, gate2 = jnp.split(modulation, 6, axis=1)
    inverse1 = inverse_rms(layer_input)
    normed1 = layer_input * inverse1
    attention_in = (normed1 * (1.0 + scale1) + shift1).astype(jnp.bfloat16)
    rows = attention_in.shape[0]
    projected_all = jnp.einsum(
        "td,kde->kte", attention_in, projections, preferred_element_type=jnp.float32
    )
    query_raw = projected_all[0].reshape(rows, heads, HEAD)
    key_raw = projected_all[1].reshape(rows, heads, HEAD)
    values = projected_all[2].reshape(rows, heads, HEAD).astype(jnp.bfloat16)
    query_inv = inverse_rms(query_raw)
    query_norm = query_raw * query_inv
    key_inv = inverse_rms(key_raw)
    key_norm = key_raw * key_inv
    query_rot = rotate(query_norm * gains[0], cosine, sine).astype(jnp.bfloat16)
    key_rot = rotate(key_norm * gains[1], cosine, sine).astype(jnp.bfloat16)
    scores = jnp.einsum(
        "thd,shd->hts", query_rot, key_rot, preferred_element_type=jnp.float32
    ) * HEAD ** (-0.5)
    attention = jax.nn.softmax(jnp.where(same[None], scores, -1e30), axis=-1)
    attention_low = attention.astype(jnp.bfloat16)
    mixed = jnp.einsum("hts,shd->thd", attention_low, values, preferred_element_type=jnp.float32)
    mixed = mixed.reshape(rows, heads * HEAD).astype(jnp.bfloat16)
    attended = branch_sum(jnp.dot(mixed, out_weight, preferred_element_type=jnp.float32))
    after = layer_input + gate1 * attended
    inverse2 = inverse_rms(after)
    normed2 = after * inverse2
    mlp_in = (normed2 * (1.0 + scale2) + shift2).astype(jnp.bfloat16)
    gate_pair = jnp.einsum("td,kdf->ktf", mlp_in, gate_up, preferred_element_type=jnp.float32)
    hidden = (jax.nn.silu(gate_pair[0]) * gate_pair[1]).astype(jnp.bfloat16)
    projected = branch_sum(jnp.dot(hidden, down_weight, preferred_element_type=jnp.float32))
    output = after + gate2 * projected
    cache = (
        normed1,
        inverse1,
        attention_in,
        query_norm,
        query_inv,
        key_norm,
        key_inv,
        query_rot,
        key_rot,
        values,
        attention,
        attention_low,
        mixed,
        attended,
        normed2,
        inverse2,
        mlp_in,
        gate_pair,
        hidden,
        projected,
    )
    return (output, attended, projected, cache)


def backward_pieces(grad_out, modulation, weights, shape_info, cache):
    projections, out_weight, gains, gate_up, down_weight = weights
    same, cosine, sine = shape_info
    (
        normed1,
        inverse1,
        attention_in,
        query_norm,
        query_inv,
        key_norm,
        key_inv,
        query_rot,
        key_rot,
        values,
        attention,
        attention_low,
        mixed,
        attended,
        normed2,
        inverse2,
        mlp_in,
        gate_pair,
        hidden,
        projected,
    ) = cache
    rows = attention_in.shape[0]
    heads = values.shape[1]
    shift1, scale1, gate1, shift2, scale2, gate2 = jnp.split(modulation, 6, axis=1)
    grad_gate2 = grad_out * projected
    grad_projected = (grad_out * gate2).astype(jnp.bfloat16)
    grad_down = jnp.einsum("tf,td->fd", hidden, grad_projected, preferred_element_type=jnp.float32)
    grad_hidden = jnp.einsum(
        "td,fd->tf", grad_projected, down_weight, preferred_element_type=jnp.float32
    )
    gate = gate_pair[0]
    upward = gate_pair[1]
    sigma = jax.nn.sigmoid(gate)
    grad_gate = (grad_hidden * upward * sigma * (1.0 + gate * (1.0 - sigma))).astype(jnp.bfloat16)
    grad_up = (grad_hidden * gate * sigma).astype(jnp.bfloat16)
    grad_pair = jnp.stack([grad_gate, grad_up])
    grad_gate_up = jnp.einsum("td,ktf->kdf", mlp_in, grad_pair, preferred_element_type=jnp.float32)
    grad_mlp_in = input_sum(
        jnp.einsum("ktf,kdf->td", grad_pair, gate_up, preferred_element_type=jnp.float32)
    )
    grad_after = grad_out + norm_back(grad_mlp_in * (1.0 + scale2), normed2, inverse2)
    grad_gate1 = grad_after * attended
    grad_attended = (grad_after * gate1).astype(jnp.bfloat16)
    grad_out_weight = jnp.einsum(
        "te,td->ed", mixed, grad_attended, preferred_element_type=jnp.float32
    )
    grad_mixed = jnp.einsum(
        "td,ed->te", grad_attended, out_weight, preferred_element_type=jnp.float32
    )
    grad_mixed = grad_mixed.astype(jnp.bfloat16).reshape(rows, heads, HEAD)
    grad_values = jnp.einsum(
        "hts,thd->shd", attention_low, grad_mixed, preferred_element_type=jnp.float32
    ).astype(jnp.bfloat16)
    grad_weights = jnp.einsum(
        "thd,shd->hts", grad_mixed, values, preferred_element_type=jnp.float32
    )
    delta = jnp.sum(attention * grad_weights, axis=-1, keepdims=True)
    grad_scores = (attention * (grad_weights - delta)).astype(jnp.bfloat16)
    grad_query_rot = jnp.einsum(
        "hts,shd->thd", grad_scores, key_rot, preferred_element_type=jnp.float32
    ) * HEAD ** (-0.5)
    grad_key_rot = jnp.einsum(
        "hts,thd->shd", grad_scores, query_rot, preferred_element_type=jnp.float32
    ) * HEAD ** (-0.5)
    grad_turned_q = unrotate(grad_query_rot, cosine, sine)
    grad_turned_k = unrotate(grad_key_rot, cosine, sine)
    grad_gains = jnp.stack(
        [
            jnp.sum(grad_turned_q * query_norm, axis=(0, 1)),
            jnp.sum(grad_turned_k * key_norm, axis=(0, 1)),
        ]
    )
    grad_query = norm_back(grad_turned_q * gains[0], query_norm, query_inv).astype(jnp.bfloat16)
    grad_key = norm_back(grad_turned_k * gains[1], key_norm, key_inv).astype(jnp.bfloat16)
    grad_three = jnp.stack(
        [
            grad_query.reshape(rows, heads * HEAD),
            grad_key.reshape(rows, heads * HEAD),
            grad_values.reshape(rows, heads * HEAD),
        ]
    )
    grad_projections = jnp.einsum(
        "td,kte->kde", attention_in, grad_three, preferred_element_type=jnp.float32
    )
    grad_attention_in = input_sum(
        jnp.einsum("kte,kde->td", grad_three, projections, preferred_element_type=jnp.float32)
    )
    grad_input = grad_after + norm_back(grad_attention_in * (1.0 + scale1), normed1, inverse1)
    grad_modulation = jnp.concatenate(
        [
            grad_attention_in,
            grad_attention_in * normed1,
            grad_gate1,
            grad_mlp_in,
            grad_mlp_in * normed2,
            grad_gate2,
        ],
        axis=1,
    )
    return (
        grad_input,
        grad_modulation,
        (grad_projections, grad_out_weight, grad_gate_up, grad_down),
        grad_gains,
    )


def shards(
    inputs,
    cotangent,
    conditioning,
    lengths,
    positions,
    modulator,
    projections,
    norm_gains,
    out_weight,
    gate_up,
    down_weight,
):
    section = lax.axis_index("section")
    tensor_index = lax.axis_index("tensor")
    micro = inputs.shape[0]
    rows = inputs.shape[1]
    width = inputs.shape[2]
    share = rows // lax.axis_size("tensor")
    weights = (projections[0], out_weight[0], norm_gains[0], gate_up[0], down_weight[0])
    cond_value = conditioning[:, 0].astype(jnp.float32)
    scaled = jax.nn.silu(cond_value).astype(jnp.bfloat16)
    modulation_part = jnp.einsum(
        "mid,dc->mic", scaled, modulator[0], preferred_element_type=jnp.float32
    ).astype(jnp.bfloat16)
    modulations = lax.all_gather(modulation_part, "tensor", axis=2, tiled=True)
    ends = jnp.cumsum(lengths[:, 0], axis=1)
    place = jnp.arange(rows)
    segment = jnp.sum((place[None, :, None] >= ends[:, None, :]).astype(jnp.int32), axis=2)
    labels = jnp.arange(lengths.shape[2])
    picks = (segment[:, :, None] == labels[None, None, :]).astype(jnp.bfloat16)
    sames = segment[:, :, None] == segment[:, None, :]
    cosines, sines = angles(positions[:, 0], positions[:, 1])

    def pick_micro(index):
        shape_info = (sames[index], cosines[index], sines[index])
        local_picks = picks[index]
        modulation = jnp.dot(local_picks, modulations[index], preferred_element_type=jnp.float32)
        return (shape_info, modulation, local_picks)

    steps = jnp.arange(micro + 1)

    def forward_step(received, step):
        index = jnp.clip(step - section, 0, micro - 1)
        shape_info, modulation, local_picks = pick_micro(index)
        own_input = inputs[jnp.minimum(step, micro - 1)].astype(jnp.float32)
        layer_input = jnp.where(section == 0, own_input, received.astype(jnp.float32))
        output, attended, projected, cache = forward_pieces(
            layer_input, modulation, weights, shape_info
        )
        sent = shifted(output.astype(jnp.bfloat16), "section", 1)
        return (sent, (layer_input, attended, projected, output))

    start = jnp.zeros((rows, width), jnp.bfloat16)
    unused, (kept_inputs, kept_attended, kept_projected, outputs) = lax.scan(
        forward_step, start, steps
    )
    grad_shapes = (
        projections.shape[1:],
        out_weight.shape[1:],
        gate_up.shape[1:],
        down_weight.shape[1:],
    )
    totals_start = tuple((jnp.zeros(shape, jnp.float32) for shape in grad_shapes))

    def backward_step(carry, step):
        returned, totals, total_gains, grad_mods = carry
        index_raw = step - 1 + section
        valid = ((index_raw >= 0) & (index_raw < micro)).astype(jnp.float32)
        index = jnp.clip(index_raw, 0, micro - 1)
        shape_info, modulation, local_picks = pick_micro(index)
        later = jnp.minimum(step + 1, micro)
        earlier = jnp.maximum(step - 1, 0)
        chosen = jnp.where(section == 1, later, earlier)
        layer_input = kept_inputs[chosen]
        output, attended, projected, cache = forward_pieces(
            layer_input, modulation, weights, shape_info
        )
        own_grad = cotangent[jnp.minimum(step, micro - 1)].astype(jnp.float32)
        grad_out = jnp.where(section == 1, own_grad, returned.astype(jnp.float32))
        grad_input, grad_modulation, grads, grad_gains = backward_pieces(
            grad_out, modulation, weights, shape_info, cache
        )
        grads = tuple((value * valid for value in grads))
        total_gains = total_gains + valid * grad_gains
        item_grad = jnp.einsum(
            "ti,tc->ic",
            local_picks.astype(jnp.float32),
            grad_modulation,
            precision=HIGHEST,
            preferred_element_type=jnp.float32,
        )
        selector = (jnp.arange(micro) == index).astype(jnp.float32) * valid
        grad_mods = grad_mods + selector[:, None, None] * item_grad[None]
        totals = tuple((left + right for left, right in zip(totals, grads)))
        sent = shifted(grad_input.astype(jnp.bfloat16), "section", -1)
        return ((sent, totals, total_gains, grad_mods), grad_input)

    carry_start = (
        start,
        totals_start,
        jnp.zeros(norm_gains.shape[1:], jnp.float32),
        jnp.zeros(modulations.shape, jnp.float32),
    )
    (unused_back, totals, total_gains, grad_mods), grad_inputs = lax.scan(
        backward_step, carry_start, steps
    )
    columns = modulator.shape[2]
    mods_low = grad_mods.astype(jnp.bfloat16)
    modulation_columns = lax.dynamic_slice_in_dim(mods_low, tensor_index * columns, columns, 2)
    grad_ada = jnp.einsum(
        "mid,mic->dc", scaled, modulation_columns, preferred_element_type=jnp.float32
    )
    sigma = jax.nn.sigmoid(cond_value)
    cond_part = jnp.einsum(
        "mic,dc->mid", modulation_columns, modulator[0], preferred_element_type=jnp.float32
    )
    cond_part = cond_part * sigma * (1.0 + cond_value * (1.0 - sigma))
    grad_cond = lax.psum(cond_part, ("section", "tensor"))
    gains_total = lax.psum(total_gains, ("tensor", "dp"))
    grad_qkv, grad_out_w, grad_pair, grad_down, grad_ada_share = (
        lax.psum_scatter(totals[0], "dp", scatter_dimension=1, tiled=True),
        lax.psum_scatter(totals[1], "dp", scatter_dimension=1, tiled=True),
        lax.psum_scatter(totals[2], "dp", scatter_dimension=1, tiled=True),
        lax.psum_scatter(totals[3], "dp", scatter_dimension=1, tiled=True),
        lax.psum_scatter(grad_ada, "dp", scatter_dimension=0, tiled=True),
    )
    results = jnp.where(section == 0, grad_inputs[1:], outputs[1:])
    results = lax.dynamic_slice_in_dim(results, tensor_index * share, share, 1)
    return (
        grad_ada_share[None],
        grad_qkv[None],
        gains_total[None],
        grad_out_w[None],
        grad_pair[None],
        grad_down[None],
        grad_cond[:, None],
        results[None],
    )


def solution(mesh):
    return jax.shard_map(
        shards,
        mesh=mesh,
        in_specs=(
            P(None, "dp", None),
            P(None, "dp", None),
            P(None, "dp", None, None),
            P(None, "dp", None),
            P(None, None, "dp"),
            P("section", None, "tensor"),
            P("section", None, None, "tensor"),
            P("section", None, None),
            P("section", "tensor", None),
            P("section", None, None, "tensor"),
            P("section", "tensor", None),
        ),
        out_specs=(
            P("section", "dp", "tensor"),
            P("section", None, "dp", "tensor"),
            P("section", None, None),
            P("section", "tensor", "dp"),
            P("section", None, "dp", "tensor"),
            P("section", "tensor", "dp"),
            P(None, "dp", None, None),
            P("section", None, ("dp", "tensor"), None),
        ),
        check_vma=False,
    )
```

profile of v0, /device:TPU:1, one launch (start us, length us, event | category | flops | bytes accessed | tf_op | source)
XLA Modules:
  0.0 2381.7 jit_solution(11065792657871187950)
XLA Ops:
  64.8 597.3 %while.42 = (s32[]{:T(128)}, bf16[512,1152]{1,0:T(8,128)(2,1)S(1)}, f32[3,512,1152]{2,1,0:T(8,128)}, f32[3,512,1152]{2,1,0:T(8,128)}, pred[]{:T(512)}, /*index=5...) while((s32[]{:T(128)}, bf16[512,1152]{1,0:T(8,128)(2,1)S(1)}, ...), condition=%wide.region_11.12_spmd, body=%wide.region_2.11_spmd.sunk | while | flops 4438971904 | bytes 252589984 | solution.py:292
  85.9 39.0 %reduce-scatter.24.cloned.1.call-done = f32[128,1152]{1,0:T(8,128)} async-done(((f32[512,1152]{1,0:T(8,128)}), f32[128,1152]{1,0:T(8,128)}) %reduce-scatter.24.cloned.1.call-update) | async-done | bytes 589840 | tf_op jit(solution)/shard_map/while/body/eval_jaxpr/reduce_scatter | solution.py:56
  124.9 39.4 %all-gather.7.cloned.1.call-done = f32[512,1152]{1,0:T(8,128)} async-done(((f32[128,1152]{1,0:T(8,128)}), f32[512,1152]{1,0:T(8,128)}) %all-gather.7.cloned.1.call-update) | async-done | bytes 2359312 | tf_op jit(solution)/shard_map/while/body/eval_jaxpr/all_gather | solution.py:57
  175.8 37.5 %reduce-scatter.26.cloned.1.call-done = f32[128,1152]{1,0:T(8,128)} async-done(((f32[512,1152]{1,0:T(8,128)}), f32[128,1152]{1,0:T(8,128)}) %reduce-scatter.26.cloned.1.call-update) | async-done | bytes 589840 | tf_op jit(solution)/shard_map/while/body/eval_jaxpr/reduce_scatter | solution.py:56
  213.3 39.3 %all-gather.9.cloned.1.call-done = f32[512,1152]{1,0:T(8,128)} async-done(((f32[128,1152]{1,0:T(8,128)}), f32[512,1152]{1,0:T(8,128)}) %all-gather.9.cloned.1.call-update) | async-done | bytes 2359312 | tf_op jit(solution)/shard_map/while/body/eval_jaxpr/all_gather | solution.py:57
  285.5 38.0 %reduce-scatter.24.cloned.1.call-done = f32[128,1152]{1,0:T(8,128)} async-done(((f32[512,1152]{1,0:T(8,128)}), f32[128,1152]{1,0:T(8,128)}) %reduce-scatter.24.cloned.1.call-update) | async-done | bytes 589840 | tf_op jit(solution)/shard_map/while/body/eval_jaxpr/reduce_scatter | solution.py:56
  323.6 39.3 %all-gather.7.cloned.1.call-done = f32[512,1152]{1,0:T(8,128)} async-done(((f32[128,1152]{1,0:T(8,128)}), f32[512,1152]{1,0:T(8,128)}) %all-gather.7.cloned.1.call-update) | async-done | bytes 2359312 | tf_op jit(solution)/shard_map/while/body/eval_jaxpr/all_gather | solution.py:57
  374.3 37.5 %reduce-scatter.26.cloned.1.call-done = f32[128,1152]{1,0:T(8,128)} async-done(((f32[512,1152]{1,0:T(8,128)}), f32[128,1152]{1,0:T(8,128)}) %reduce-scatter.26.cloned.1.call-update) | async-done | bytes 589840 | tf_op jit(solution)/shard_map/while/body/eval_jaxpr/reduce_scatter | solution.py:56
  411.9 39.4 %all-gather.9.cloned.1.call-done = f32[512,1152]{1,0:T(8,128)} async-done(((f32[128,1152]{1,0:T(8,128)}), f32[512,1152]{1,0:T(8,128)}) %all-gather.9.cloned.1.call-update) | async-done | bytes 2359312 | tf_op jit(solution)/shard_map/while/body/eval_jaxpr/all_gather | solution.py:57
  484.3 38.0 %reduce-scatter.24.cloned.1.call-done = f32[128,1152]{1,0:T(8,128)} async-done(((f32[512,1152]{1,0:T(8,128)}), f32[128,1152]{1,0:T(8,128)}) %reduce-scatter.24.cloned.1.call-update) | async-done | bytes 589840 | tf_op jit(solution)/shard_map/while/body/eval_jaxpr/reduce_scatter | solution.py:56
  522.4 39.2 %all-gather.7.cloned.1.call-done = f32[512,1152]{1,0:T(8,128)} async-done(((f32[128,1152]{1,0:T(8,128)}), f32[512,1152]{1,0:T(8,128)}) %all-gather.7.cloned.1.call-update) | async-done | bytes 2359312 | tf_op jit(solution)/shard_map/while/body/eval_jaxpr/all_gather | solution.py:57
  573.2 37.5 %reduce-scatter.26.cloned.1.call-done = f32[128,1152]{1,0:T(8,128)} async-done(((f32[512,1152]{1,0:T(8,128)}), f32[128,1152]{1,0:T(8,128)}) %reduce-scatter.26.cloned.1.call-update) | async-done | bytes 589840 | tf_op jit(solution)/shard_map/while/body/eval_jaxpr/reduce_scatter | solution.py:56
  610.7 39.3 %all-gather.9.cloned.1.call-done = f32[512,1152]{1,0:T(8,128)} async-done(((f32[128,1152]{1,0:T(8,128)}), f32[512,1152]{1,0:T(8,128)}) %all-gather.9.cloned.1.call-update) | async-done | bytes 2359312 | tf_op jit(solution)/shard_map/while/body/eval_jaxpr/all_gather | solution.py:57
  666.1 1227.2 %while.43 = (s32[]{:T(128)}, bf16[512,1152]{1,0:T(8,128)(2,1)S(1)}, f32[3,1152,288]{1,2,0:T(8,128)}, f32[288,1152]{1,0:T(8,128)}, f32[2,1152,768]{1,2,0:T(8,128)...) while((s32[]{:T(128)}, bf16[512,1152]{1,0:T(8,128)(2,1)S(1)}, ...), condition=%wide.region_32.33_spmd.clone, body=%wide.region_12.32_spmd.clone.sunk | while | flops 13417192448 | bytes 646542592 | solution.py:342
  716.6 38.0 %reduce-scatter.28.cloned.1.call-done = f32[128,1152]{1,0:T(8,128)} async-done(((f32[512,1152]{1,0:T(8,128)}), f32[128,1152]{1,0:T(8,128)}) %reduce-scatter.28.cloned.1.call-update) | async-done | bytes 589840 | tf_op jit(solution)/shard_map/while/body/eval_jaxpr/reduce_scatter | solution.py:56
  755.3 38.6 %all-gather.11.cloned.1.call-done = f32[512,1152]{1,0:T(8,128)} async-done(((f32[128,1152]{1,0:T(8,128)}), f32[512,1152]{1,0:T(8,128)}) %all-gather.11.cloned.1.call-update) | async-done | bytes 2359312 | tf_op jit(solution)/shard_map/while/body/eval_jaxpr/all_gather | solution.py:57
  811.6 37.5 %reduce-scatter.30.cloned.1.call-done = f32[128,1152]{1,0:T(8,128)} async-done(((f32[512,1152]{1,0:T(8,128)}), f32[128,1152]{1,0:T(8,128)}) %reduce-scatter.30.cloned.1.call-update) | async-done | bytes 589840 | tf_op jit(solution)/shard_map/while/body/eval_jaxpr/reduce_scatter | solution.py:61
  1157.2 38.8 %all-gather.11.cloned.1.call-done = f32[512,1152]{1,0:T(8,128)} async-done(((f32[128,1152]{1,0:T(8,128)}), f32[512,1152]{1,0:T(8,128)}) %all-gather.11.cloned.1.call-update) | async-done | bytes 2359312 | tf_op jit(solution)/shard_map/while/body/eval_jaxpr/all_gather | solution.py:57
  1213.6 37.5 %reduce-scatter.30.cloned.1.call-done = f32[128,1152]{1,0:T(8,128)} async-done(((f32[512,1152]{1,0:T(8,128)}), f32[128,1152]{1,0:T(8,128)}) %reduce-scatter.30.cloned.1.call-update) | async-done | bytes 589840 | tf_op jit(solution)/shard_map/while/body/eval_jaxpr/reduce_scatter | solution.py:61
  1559.1 38.6 %all-gather.11.cloned.1.call-done = f32[512,1152]{1,0:T(8,128)} async-done(((f32[128,1152]{1,0:T(8,128)}), f32[512,1152]{1,0:T(8,128)}) %all-gather.11.cloned.1.call-update) | async-done | bytes 2359312 | tf_op jit(solution)/shard_map/while/body/eval_jaxpr/all_gather | solution.py:57
  1615.4 37.5 %reduce-scatter.30.cloned.1.call-done = f32[128,1152]{1,0:T(8,128)} async-done(((f32[512,1152]{1,0:T(8,128)}), f32[128,1152]{1,0:T(8,128)}) %reduce-scatter.30.cloned.1.call-update) | async-done | bytes 589840 | tf_op jit(solution)/shard_map/while/body/eval_jaxpr/reduce_scatter | solution.py:61
  2005.5 96.1 %reduce-scatter.16.cloned.1.call-done = f32[3,288,288]{2,1,0:T(8,128)} async-done(((f32[3,1152,288]{2,1,0:T(8,128)}), f32[3,288,288]{2,1,0:T(8,128)}) %reduce-scatter.16.cloned.1.call-update) | async-done | bytes 995344 | tf_op jit(solution)/shard_map/reduce_scatter | solution.py:359
  2101.5 126.8 %reduce-scatter.18.cloned.1.call-done = f32[2,288,768]{2,1,0:T(8,128)} async-done(((f32[2,1152,768]{2,1,0:T(8,128)}), f32[2,288,768]{2,1,0:T(8,128)}) %reduce-scatter.18.cloned.1.call-update) | async-done | bytes 1769488 | tf_op jit(solution)/shard_map/reduce_scatter | solution.py:361
  2228.4 145.6 %reduce-scatter.14.cloned.1.call-done = f32[288,1728]{1,0:T(8,128)} async-done(((f32[1152,1728]{1,0:T(8,128)}), f32[288,1728]{1,0:T(8,128)}) %reduce-scatter.14.cloned.1.call-update) | async-done | bytes 1990672 | tf_op jit(solution)/shard_map/reduce_scatter | solution.py:363
  (922 shorter events, 1233.4 us)
Async XLA Ops:
  85.8 78.5 %all-gather.7.cloned.1.call-start = ((), (), s32[]{:S(2)}) async-start(), calls=%async_computation.17 | async-start | bytes 2949120 | tf_op jit(solution)/shard_map/while/body/eval_jaxpr/all_gather | solution.py:57
  124.9 88.4 %reduce-scatter.26.cloned.1.call-start = ((), (), s32[]{:S(2)}) async-start(), calls=%async_computation.18 | async-start | bytes 2949120 | tf_op jit(solution)/shard_map/while/body/eval_jaxpr/reduce_scatter | solution.py:56
  323.5 88.3 %reduce-scatter.26.cloned.1.call-start = ((), (), s32[]{:S(2)}) async-start(), calls=%async_computation.18 | async-start | bytes 2949120 | tf_op jit(solution)/shard_map/while/body/eval_jaxpr/reduce_scatter | solution.py:56
  522.4 88.3 %reduce-scatter.26.cloned.1.call-start = ((), (), s32[]{:S(2)}) async-start(), calls=%async_computation.18 | async-start | bytes 2949120 | tf_op jit(solution)/shard_map/while/body/eval_jaxpr/reduce_scatter | solution.py:56
  754.6 94.5 %reduce-scatter.30.cloned.1.call-start = ((), (), s32[]{:S(2)}) async-start(), calls=%async_computation.22 | async-start | bytes 2949120 | tf_op jit(solution)/shard_map/while/body/eval_jaxpr/reduce_scatter | solution.py:61
  849.1 99.0 %reduce-scatter.32.cloned.1.call-start = ((), (), s32[]{:S(2)}) async-start(), calls=%async_computation.24 | async-start | bytes 2949120 | tf_op jit(solution)/shard_map/while/body/eval_jaxpr/reduce_scatter | solution.py:61
  910.6 78.1 %reduce-scatter.34.cloned.1.call-start = ((), (), s32[]{:S(2)}) async-start(), calls=%async_computation.26 | async-start | bytes 2949120 | tf_op jit(solution)/shard_map/while/body/eval_jaxpr/reduce_scatter | solution.py:56
  915.0 113.2 %all-gather.15.cloned.1.call-start = ((), (), s32[]{:S(2)}) async-start(), calls=%async_computation.25 | async-start | bytes 2949120 | tf_op jit(solution)/shard_map/while/body/eval_jaxpr/all_gather | solution.py:62
  948.2 119.4 %all-gather.17.cloned.1.call-start = ((), (), s32[]{:S(2)}) async-start(), calls=%async_computation.27 | async-start | bytes 2949120 | tf_op jit(solution)/shard_map/while/body/eval_jaxpr/all_gather | solution.py:57
  1156.5 94.7 %reduce-scatter.30.cloned.1.call-start = ((), (), s32[]{:S(2)}) async-start(), calls=%async_computation.22 | async-start | bytes 2949120 | tf_op jit(solution)/shard_map/while/body/eval_jaxpr/reduce_scatter | solution.py:61
  1251.1 99.0 %reduce-scatter.32.cloned.1.call-start = ((), (), s32[]{:S(2)}) async-start(), calls=%async_computation.24 | async-start | bytes 2949120 | tf_op jit(solution)/shard_map/while/body/eval_jaxpr/reduce_scatter | solution.py:61
  1312.6 78.1 %reduce-scatter.34.cloned.1.call-start = ((), (), s32[]{:S(2)}) async-start(), calls=%async_computation.26 | async-start | bytes 2949120 | tf_op jit(solution)/shard_map/while/body/eval_jaxpr/reduce_scatter | solution.py:56
  1317.0 113.1 %all-gather.15.cloned.1.call-start = ((), (), s32[]{:S(2)}) async-start(), calls=%async_computation.25 | async-start | bytes 2949120 | tf_op jit(solution)/shard_map/while/body/eval_jaxpr/all_gather | solution.py:62
  1350.2 119.4 %all-gather.17.cloned.1.call-start = ((), (), s32[]{:S(2)}) async-start(), calls=%async_computation.27 | async-start | bytes 2949120 | tf_op jit(solution)/shard_map/while/body/eval_jaxpr/all_gather | solution.py:57
  1558.4 94.5 %reduce-scatter.30.cloned.1.call-start = ((), (), s32[]{:S(2)}) async-start(), calls=%async_computation.22 | async-start | bytes 2949120 | tf_op jit(solution)/shard_map/while/body/eval_jaxpr/reduce_scatter | solution.py:61
  1652.9 99.2 %reduce-scatter.32.cloned.1.call-start = ((), (), s32[]{:S(2)}) async-start(), calls=%async_computation.24 | async-start | bytes 2949120 | tf_op jit(solution)/shard_map/while/body/eval_jaxpr/reduce_scatter | solution.py:61
  1714.5 78.3 %reduce-scatter.34.cloned.1.call-start = ((), (), s32[]{:S(2)}) async-start(), calls=%async_computation.26 | async-start | bytes 2949120 | tf_op jit(solution)/shard_map/while/body/eval_jaxpr/reduce_scatter | solution.py:56
  1718.9 113.4 %all-gather.15.cloned.1.call-start = ((), (), s32[]{:S(2)}) async-start(), calls=%async_computation.25 | async-start | bytes 2949120 | tf_op jit(solution)/shard_map/while/body/eval_jaxpr/all_gather | solution.py:62
  1752.1 119.5 %all-gather.17.cloned.1.call-start = ((), (), s32[]{:S(2)}) async-start(), calls=%async_computation.27 | async-start | bytes 2949120 | tf_op jit(solution)/shard_map/while/body/eval_jaxpr/all_gather | solution.py:57
  1893.4 110.1 %reduce-scatter.22.cloned.1.call-start = ((), (), s32[]{:S(2)}) async-start(), calls=%async_computation.15 | async-start | bytes 2211840
  1896.7 108.8 %reduce-scatter.20.cloned.1.call-start = ((), (), s32[]{:S(2)}) async-start(), calls=%async_computation.14 | async-start | bytes 4423680 | tf_op jit(solution)/shard_map/reduce_scatter | solution.py:362
  1899.7 201.8 %reduce-scatter.16.cloned.1.call-start = ((), (), s32[]{:S(2)}) async-start(), calls=%async_computation.12 | async-start | bytes 6635520 | tf_op jit(solution)/shard_map/reduce_scatter | solution.py:359
  1905.8 322.6 %reduce-scatter.18.cloned.1.call-start = ((), (), s32[]{:S(2)}) async-start(), calls=%async_computation.13 | async-start | bytes 8847360 | tf_op jit(solution)/shard_map/reduce_scatter | solution.py:361
  1913.9 460.0 %reduce-scatter.14.cloned.1.call-start = ((), (), s32[]{:S(2)}) async-start(), calls=%async_computation.11 | async-start | bytes 10321920 | tf_op jit(solution)/shard_map/reduce_scatter | solution.py:363
  (264 other events, 2228.5 us)
Sparse Core Ops, SparseCore 0:
  86.0 38.8 reduce-scatter.23
  126.8 37.4 all-gather.6
  215.1 37.4 all-gather.8
  285.6 37.8 reduce-scatter.23
  325.3 37.4 all-gather.6
  413.8 37.4 all-gather.8
  484.4 37.9 reduce-scatter.23
  524.2 37.4 all-gather.6
  612.5 37.4 all-gather.8
  716.7 37.8 reduce-scatter.27
  756.4 37.4 all-gather.10
  851.0 37.4 all-gather.12
  990.7 37.4 all-gather.14
  1030.1 37.4 all-gather.16
  1158.4 37.4 all-gather.10
  1213.7 37.3 reduce-scatter.29
  1253.0 37.4 all-gather.12
  1312.7 37.3 reduce-scatter.31
  1392.6 37.4 all-gather.14
  1432.0 37.4 all-gather.16
  1560.2 37.4 all-gather.10
  1654.9 37.4 all-gather.12
  1794.8 37.4 all-gather.14
  1834.1 37.4 all-gather.16
  (12 shorter events, 447.3 us)
Sparse Core Ops, SparseCore 1:
  1896.8 37.7 reduce-scatter.21
  1937.4 66.0 reduce-scatter.19
  2006.3 95.2 reduce-scatter.15
  2104.4 123.9 reduce-scatter.17
  2231.3 142.6 reduce-scatter.13
where the time goes:
time: 2390 us; the launch traced here: 2380 us
  waiting for transfers between devices  1630 us (68%)
  matrix products  268 us (11%)
  other arithmetic  180 us (8%)
  local copies, waits for them, and re-layouts  139 us (6%)
  blocking collectives  103 us (4%)
  loops' own time  33.9 us (1%)
    all_gather x12, waiting for transfers between devices, branch_sum(): return lax.all_gather(shares, 'tensor', axis=0, tiled=True)  428 us
    reduce_scatter x12, waiting for transfers between devices, branch_sum(): lax.psum_scatter(partial_sum, 'tensor', scatter_dimension=0, tiled=True)  422 us
    reduce_scatter x6, waiting for transfers between devices, input_sum(): lax.psum_scatter(partial_sum, 'tensor', scatter_dimension=0, tiled=True)  212 us
    all_gather x6, waiting for transfers between devices, input_sum(): return lax.all_gather(shares, 'tensor', axis=0, tiled=True)  192 us
    reduce_scatter x1, waiting for transfers between devices, shards(): lax.psum_scatter(grad_ada, 'dp', scatter_dimension=0, tiled=True)  146 us
    reduce_scatter x1, waiting for transfers between devices, shards(): lax.psum_scatter(totals[2], 'dp', scatter_dimension=1, tiled=True)  127 us
    reduce_scatter x1, waiting for transfers between devices, shards(): lax.psum_scatter(totals[0], 'dp', scatter_dimension=1, tiled=True)  96.1 us
  transfers between devices with their start and end apart: 47, of which 42 were waited for; matrix products, arithmetic and copies ran while one was open for 8% of the time, Pallas kernels for 0%

commit v1 on v0

v1 whole, which is shorter than its diff:
```python
import functools

import jax
import jax.numpy as jnp
from jax import lax
from jax.experimental import pallas as pl
from jax.experimental.pallas import tpu as pltpu
from jax.sharding import PartitionSpec as P
import numpy as np

HEAD = 72
HALF = HEAD // 2
LANE = 128
epsilon = 1e-06
BF = jnp.bfloat16
F32 = jnp.float32
HIGHEST = lax.Precision.HIGHEST
VM = pl.BlockSpec(memory_space=pltpu.VMEM)
SM = pl.BlockSpec(memory_space=pltpu.SMEM)
ANY = pl.BlockSpec(memory_space=pl.ANY)


def nn(a, b):
    return lax.dot_general(a, b, (((1,), (0,)), ((), ())), preferred_element_type=F32)


def nt(a, b):
    return lax.dot_general(a, b, (((1,), (1,)), ((), ())), preferred_element_type=F32)


def tn(a, b):
    return lax.dot_general(a, b, (((0,), (0,)), ((), ())), preferred_element_type=F32)


def call(body, outs, in_specs, scratch=(), flops=0, size=0, name=None):
    return pl.pallas_call(
        body,
        out_shape=outs,
        in_specs=in_specs,
        out_specs=jax.tree.map(lambda _: VM, outs),
        scratch_shapes=list(scratch),
        compiler_params=pltpu.CompilerParams(vmem_limit_bytes=50 * 2**20),
        cost_estimate=pl.CostEstimate(flops=flops, bytes_accessed=size, transcendentals=0),
        name=name,
    )


def shape(dims, dtype):
    return jax.ShapeDtypeStruct(dims, dtype)


def fetch(is_own, own, other, where, sem):
    @pl.when(is_own)
    def _():
        pltpu.make_async_copy(own, where, sem).start()

    @pl.when(jnp.logical_not(is_own))
    def _():
        pltpu.make_async_copy(other, where, sem).start()


def arrived(own, where, sem):
    pltpu.make_async_copy(own, where, sem).wait()


def inverse_rms(value):
    return lax.rsqrt(jnp.mean(value * value, axis=-1, keepdims=True) + epsilon)


def norm_back(grad, normed, inverse):
    return inverse * (grad - normed * jnp.mean(grad * normed, axis=-1, keepdims=True))


def token_mod(picks, mods_ref, part):
    width = mods_ref.shape[1] // 6
    return nn(picks, mods_ref[:, part * width : (part + 1) * width])


def image_sums(picks, value):
    return lax.dot_general(
        picks.astype(F32),
        value,
        (((0,), (0,)), ((), ())),
        precision=HIGHEST,
        preferred_element_type=F32,
    )


def swap_halves(value):
    return pltpu.roll(value, LANE // 2, 1)


def rotate(value, cosine, sine):
    return value * cosine + swap_halves(value) * sine


def unrotate(grad, cosine, sine):
    return grad * cosine - swap_halves(grad) * sine


def head_inverse(raw):
    return lax.rsqrt(jnp.sum(raw * raw, axis=-1, keepdims=True) * (1.0 / HEAD) + epsilon)


def split_store(value, rows, block_refs):
    own = block_refs[0]
    share = own.shape[0]
    for k, ref in enumerate(block_refs):
        ref[:, rows] = value[k * share : (k + 1) * share].astype(ref.dtype)


def attention_forward(layer, blocks, weights, tables, mods, picks, section):
    (wq_own, wq_got, wo_own, wo_got) = weights
    cosine, sine, gains, seg_col, seg_row = tables
    width = wo_own.shape[1]
    padded = wo_own.shape[0]
    heads = padded // LANE
    raw_input = len(blocks) == 1
    rows = sum(b.shape[0] for b in blocks)
    share = rows // 4
    scale = HEAD**-0.5

    def body(sec_ref, *refs):
        refs = list(refs)
        in_refs = [refs.pop(0) for _ in blocks]
        wq_a, wq_b, wo_a, wo_b, cos_ref, sin_ref, gain_ref, segc_ref, segr_ref, mods_ref, picks_ref = refs[:11]
        refs = refs[11:]
        p_refs = refs[:4]
        qraw_ref, kraw_ref, qrot_ref, krot_ref, v_ref, mixed_ref, a_ref = refs[4:11]
        wq_ref, wo_ref, sems = refs[11:]
        own = sec_ref[0] == layer
        for i in range(3):
            fetch(own, wq_a.at[i], wq_b.at[i], wq_ref.at[i], sems.at[i])
        fetch(own, wo_a, wo_b, wo_ref, sems.at[3])
        for k, ref in enumerate(in_refs):
            if raw_input:
                x = ref[...].astype(F32)
                picked = picks_ref[...]
                shift1 = token_mod(picked, mods_ref, 0)
                scale1 = token_mod(picked, mods_ref, 1)
                a_ref[...] = (x * inverse_rms(x) * (1.0 + scale1) + shift1).astype(BF)
            else:
                a_ref[k * share : (k + 1) * share] = ref[...]
        cos = cos_ref[...]
        sin = sin_ref[...]
        for i, (raw_out, rot_out) in enumerate(((qraw_ref, qrot_ref), (kraw_ref, krot_ref))):
            arrived(wq_a.at[i], wq_ref.at[i], sems.at[i])
            gain = gain_ref[i : i + 1]
            for h in range(heads):
                at = slice(h * LANE, (h + 1) * LANE)
                raw = nn(a_ref[...], wq_ref[i, :, at])
                raw_out[:, at] = raw
                turned = rotate(raw * head_inverse(raw) * gain, cos, sin)
                rot_out[:, at] = turned.astype(BF)
        arrived(wq_a.at[2], wq_ref.at[2], sems.at[2])
        v_ref[...] = nn(a_ref[...], wq_ref[2]).astype(BF)

        def query_block(j, carry):
            at_rows = pl.ds(pl.multiple_of(j * LANE, LANE), LANE)
            same = segc_ref[at_rows] == segr_ref[...]
            for h in range(heads):
                at = slice(h * LANE, (h + 1) * LANE)
                scores = nt(qrot_ref[at_rows, at], krot_ref[:, at]) * scale
                grown = jnp.where(same, jnp.exp(scores), 0.0)
                total = jnp.sum(grown, axis=-1, keepdims=True)
                weights_low = (grown * (1.0 / total)).astype(BF)
                mixed_ref[at_rows, at] = nn(weights_low, v_ref[:, at]).astype(BF)
            return carry

        lax.fori_loop(0, rows // LANE, query_block, 0)
        arrived(wo_a, wo_ref, sems.at[3])
        step = 3 * LANE

        def out_block(j, carry):
            at = pl.ds(pl.multiple_of(j * step, LANE), step)
            split_store(nn(mixed_ref[...], wo_ref[:, at]), at, p_refs)
            return carry

        lax.fori_loop(0, width // step, out_block, 0)

    outs = [shape((share, width), F32)] + [shape((share, width), BF)] * 3
    outs += [shape((rows, padded), F32)] * 2 + [shape((rows, padded), BF)] * 4
    outs += [shape((rows, width), BF)]
    result = call(
        body,
        outs,
        [SM] + [VM] * len(blocks) + [ANY] * 4 + [VM] * 7,
        [
            pltpu.VMEM((3, width, padded), BF),
            pltpu.VMEM((padded, width), BF),
            pltpu.SemaphoreType.DMA((4,)),
        ],
        flops=2 * rows * width * padded * 4 + 4 * rows * rows * padded,
        size=12 * 2**20,
        name=f"attention_forward_{layer}",
    )(section, *blocks, wq_own, wq_got, wo_own, wo_got, cosine, sine, gains, seg_col, seg_row, mods, picks)
    partial, saved = result[:4], result[4:]
    return partial, saved


def after_attention(parts, state, mods, picks):
    def body(p0, p1, p2, p3, state_ref, mods_ref, picks_ref, attended_ref, after_ref, mlp_ref):
        picked = picks_ref[...]
        attended = p0[...] + p1[...].astype(F32) + p2[...].astype(F32) + p3[...].astype(F32)
        attended_ref[...] = attended
        after = state_ref[...].astype(F32) + token_mod(picked, mods_ref, 2) * attended
        after_ref[...] = after
        normed = after * inverse_rms(after)
        mlp_ref[...] = (normed * (1.0 + token_mod(picked, mods_ref, 4)) + token_mod(picked, mods_ref, 3)).astype(BF)

    dims = state.shape
    return call(
        body,
        [shape(dims, F32), shape(dims, F32), shape(dims, BF)],
        [VM] * 7,
        flops=20 * dims[0] * dims[1],
        size=12 * dims[0] * dims[1],
        name="after_attention",
    )(*parts, state, mods, picks)


def after_mlp(parts, after, mods, picks, mods_next):
    last = mods_next is None

    def body(p0, p1, p2, p3, after_ref, mods_ref, picks_ref, *refs):
        picked = picks_ref[...]
        projected = p0[...] + p1[...].astype(F32) + p2[...].astype(F32) + p3[...].astype(F32)
        output = after_ref[...] + token_mod(picked, mods_ref, 5) * projected
        if last:
            projected_ref, output_ref = refs
            output_ref[...] = output
        else:
            next_ref, projected_ref, state_ref, in_ref = refs
            low = output.astype(BF)
            state_ref[...] = low
            state = low.astype(F32)
            normed = state * inverse_rms(state)
            in_ref[...] = (normed * (1.0 + token_mod(picked, next_ref, 1)) + token_mod(picked, next_ref, 0)).astype(BF)
        projected_ref[...] = projected

    dims = after.shape
    outs = [shape(dims, F32)] + ([shape(dims, F32)] if last else [shape(dims, BF)] * 2)
    extra = () if last else (mods_next,)
    return call(
        body,
        outs,
        [VM] * (7 + len(extra)),
        flops=20 * dims[0] * dims[1],
        size=12 * dims[0] * dims[1],
        name="after_mlp",
    )(*parts, after, mods, picks, *extra)


def mlp_forward(layer, blocks, weights, section):
    gu_own, gu_got, wd_own, wd_got = weights
    hidden_size, width = wd_own.shape
    share = blocks[0].shape[0]
    rows = share * 4
    chunk = 2 * LANE

    def body(sec_ref, b0, b1, b2, b3, gu_a, gu_b, wd_a, wd_b, p0, p1, p2, p3, hid_ref, c1_ref, c2_ref, a_ref, gu_ref, wd_ref, sems):
        own = sec_ref[0] == layer
        fetch(own, gu_a.at[0], gu_b.at[0], gu_ref.at[0], sems.at[0])
        fetch(own, gu_a.at[1], gu_b.at[1], gu_ref.at[1], sems.at[1])
        fetch(own, wd_a, wd_b, wd_ref, sems.at[2])
        for k, ref in enumerate((b0, b1, b2, b3)):
            a_ref[k * share : (k + 1) * share] = ref[...]
        arrived(gu_a.at[0], gu_ref.at[0], sems.at[0])
        arrived(gu_a.at[1], gu_ref.at[1], sems.at[1])

        def hidden_block(j, carry):
            at = pl.ds(pl.multiple_of(j * chunk, LANE), chunk)
            gate = nn(a_ref[...], gu_ref[0, :, at])
            up = nn(a_ref[...], gu_ref[1, :, at])
            sigma = jax.nn.sigmoid(gate)
            silu = gate * sigma
            hid_ref[:, at] = (silu * up).astype(BF)
            c1_ref[:, at] = (up * (sigma + silu * (1.0 - sigma))).astype(BF)
            c2_ref[:, at] = silu.astype(BF)
            return carry

        lax.fori_loop(0, hidden_size // chunk, hidden_block, 0)
        arrived(wd_a, wd_ref, sems.at[2])
        step = 3 * LANE

        def out_block(j, carry):
            at = pl.ds(pl.multiple_of(j * step, LANE), step)
            split_store(nn(hid_ref[...], wd_ref[:, at]), at, (p0, p1, p2, p3))
            return carry

        lax.fori_loop(0, width // step, out_block, 0)

    outs = [shape((share, width), F32)] + [shape((share, width), BF)] * 3 + [shape((rows, hidden_size), BF)] * 3
    result = call(
        body,
        outs,
        [SM] + [VM] * 4 + [ANY] * 4,
        [
            pltpu.VMEM((rows, width), BF),
            pltpu.VMEM(gu_own.shape, BF),
            pltpu.VMEM(wd_own.shape, BF),
            pltpu.SemaphoreType.DMA((3,)),
        ],
        flops=6 * rows * width * hidden_size,
        size=10 * 2**20,
        name=f"mlp_forward_{layer}",
    )(section, *blocks, gu_own, gu_got, wd_own, wd_got)
    return result[:4], result[4:]


def mlp_backward(layer, blocks, weights, saved, mods, picks, section):
    gu_own, gu_got, wd_own, wd_got = weights
    hidden, c1, c2 = saved
    hidden_size, width = wd_own.shape
    rows = hidden.shape[0]
    share = rows // 4
    raw_input = len(blocks) == 1
    chunk = 2 * LANE

    def body(sec_ref, *refs):
        refs = list(refs)
        in_refs = [refs.pop(0) for _ in blocks]
        gu_a, gu_b, wd_a, wd_b, c1_ref, c2_ref, mods_ref, picks_ref = refs[:8]
        p_refs = refs[8:12]
        gg_ref, gup_ref, gp_ref = refs[12:15]
        gu_ref, wd_ref, sems = refs[15:]
        own = sec_ref[0] == layer
        fetch(own, wd_a, wd_b, wd_ref, sems.at[2])
        fetch(own, gu_a.at[0], gu_b.at[0], gu_ref.at[0], sems.at[0])
        fetch(own, gu_a.at[1], gu_b.at[1], gu_ref.at[1], sems.at[1])
        for k, ref in enumerate(in_refs):
            if raw_input:
                gp_ref[...] = (ref[...].astype(F32) * token_mod(picks_ref[...], mods_ref, 5)).astype(BF)
            else:
                gp_ref[k * share : (k + 1) * share] = ref[...]
        arrived(wd_a, wd_ref, sems.at[2])

        def hidden_block(j, carry):
            at = pl.ds(pl.multiple_of(j * chunk, LANE), chunk)
            grad_hidden = nt(gp_ref[...], wd_ref[at])
            gg_ref[:, at] = (grad_hidden * c1_ref[:, at].astype(F32)).astype(BF)
            gup_ref[:, at] = (grad_hidden * c2_ref[:, at].astype(F32)).astype(BF)
            return carry

        lax.fori_loop(0, hidden_size // chunk, hidden_block, 0)
        arrived(gu_a.at[0], gu_ref.at[0], sems.at[0])
        arrived(gu_a.at[1], gu_ref.at[1], sems.at[1])
        step = 3 * LANE

        def out_block(j, carry):
            at = pl.ds(pl.multiple_of(j * step, LANE), step)
            split_store(nt(gg_ref[...], gu_ref[0, at]) + nt(gup_ref[...], gu_ref[1, at]), at, p_refs)
            return carry

        lax.fori_loop(0, width // step, out_block, 0)

    outs = [shape((share, width), F32)] + [shape((share, width), BF)] * 3 + [shape((rows, hidden_size), BF)] * 2
    outs += [shape((rows, width), BF)]
    result = call(
        body,
        outs,
        [SM] + [VM] * len(blocks) + [ANY] * 4 + [VM] * 4,
        [
            pltpu.VMEM(gu_own.shape, BF),
            pltpu.VMEM(wd_own.shape, BF),
            pltpu.SemaphoreType.DMA((3,)),
        ],
        flops=6 * rows * width * hidden_size,
        size=10 * 2**20,
        name=f"mlp_backward_{layer}",
    )(section, *blocks, gu_own, gu_got, wd_own, wd_got, c1, c2, mods, picks)
    return result[:4], result[4:]


def mlp_weight_grads(mlp_blocks, grads, hidden, section):
    grad_gate, grad_up, grad_projected = grads
    rows, width = grad_projected.shape
    size = hidden.shape[1]
    share = rows // 4
    half = 3 * size // 2
    step = 3 * LANE

    def body(sec_ref, b0, b1, b2, b3, gg_ref, gu_ref, gp_ref, hid_ref, keep_ref, send_ref, a_ref):
        for k, ref in enumerate((b0, b1, b2, b3)):
            a_ref[k * share : (k + 1) * share] = ref[...]

        def row_block(j, carry):
            at = pl.ds(pl.multiple_of(j * step, LANE), step)
            left = a_ref[:, at]
            first = tn(left, gg_ref[...]).astype(BF)
            middle = tn(left, gu_ref[...]).astype(BF)
            last = tn(gp_ref[:, at], hid_ref[...]).astype(BF)

            def put(low_ref, high_ref):
                low_ref[at, :size] = first
                low_ref[at, size:] = middle[:, : half - size]
                high_ref[at, : half - size] = middle[:, half - size :]
                high_ref[at, half - size :] = last

            @pl.when(sec_ref[0] == 0)
            def _():
                put(keep_ref, send_ref)

            @pl.when(sec_ref[0] != 0)
            def _():
                put(send_ref, keep_ref)

            return carry

        lax.fori_loop(0, width // step, row_block, 0)

    return call(
        body,
        [shape((width, half), BF)] * 2,
        [SM] + [VM] * 8,
        [pltpu.VMEM((rows, width), BF)],
        flops=6 * rows * width * size,
        size=10 * 2**20,
        name="mlp_weight_grads",
    )(section, *mlp_blocks, grad_gate, grad_up, grad_projected, hidden)


def attention_backward(layer, blocks, weights, saved, tables, selects, section):
    wq_own, wq_got, wo_own, wo_got = weights
    q_raw, k_raw, q_rot, k_rot, values, mixed = saved
    cosine, sine, gains, seg_col, seg_row = tables
    pick_qk, pick_v = selects
    rows, padded = q_raw.shape
    width = wo_own.shape[1]
    heads = padded // LANE
    share = rows // 4
    narrow = pick_v.shape[1]
    scale = HEAD**-0.5

    def body(sec_ref, b0, b1, b2, b3, wq_a, wq_b, wo_a, wo_b, qraw_ref, kraw_ref, qrot_ref, krot_ref, v_ref, mixed_ref,
             cos_ref, sin_ref, gain_ref, segc_ref, segr_ref, selqk_ref, selv_ref,
             p0, p1, p2, p3, gqk_out, gv_out, mixed_out, ga_out, ggain_ref,
             wq_ref, wo_ref, gmix_ref, gq_ref, gk_ref, g_ref, gv_ref, sems):
        own = sec_ref[0] == layer
        fetch(own, wo_a, wo_b, wo_ref, sems.at[3])
        for i in range(3):
            fetch(own, wq_a.at[i], wq_b.at[i], wq_ref.at[i], sems.at[i])
        for k, ref in enumerate((b0, b1, b2, b3)):
            ga_out[k * share : (k + 1) * share] = ref[...]
        arrived(wo_a, wo_ref, sems.at[3])
        gmix_ref[...] = nt(ga_out[...], wo_ref[...]).astype(BF)
        gk_ref[...] = jnp.zeros_like(gk_ref)
        gv_ref[...] = jnp.zeros_like(gv_ref)

        def query_block(j, carry):
            at_rows = pl.ds(pl.multiple_of(j * LANE, LANE), LANE)
            same = segc_ref[...] == segr_ref[:, at_rows]
            for h in range(heads):
                at = slice(h * LANE, (h + 1) * LANE)
                query = qrot_ref[at_rows, at]
                grad_mixed = gmix_ref[at_rows, at]
                scores = nt(krot_ref[:, at], query) * scale
                grown = jnp.where(same, jnp.exp(scores), 0.0)
                weights_t = grown * (1.0 / jnp.sum(grown, axis=0, keepdims=True))
                grad_weights = nt(v_ref[:, at], grad_mixed)
                gv_ref[:, at] += nn(weights_t.astype(BF), grad_mixed)
                product = weights_t * grad_weights
                delta = jnp.sum(product, axis=0, keepdims=True)
                grad_scores = (product - weights_t * delta).astype(BF)
                gq_ref[at_rows, at] = tn(grad_scores, krot_ref[:, at])
                gk_ref[:, at] += nn(grad_scores, query)
            return carry

        lax.fori_loop(0, rows // LANE, query_block, 0)
        cos = cos_ref[...]
        sin = sin_ref[...]
        ggain_ref[...] = jnp.zeros_like(ggain_ref)
        for i, (raw_ref, grad_ref) in enumerate(((qraw_ref, gq_ref), (kraw_ref, gk_ref))):
            gain = gain_ref[i : i + 1]
            gain_sum = jnp.zeros((1, LANE), F32)
            for h in range(heads):
                at = slice(h * LANE, (h + 1) * LANE)
                raw = raw_ref[:, at]
                inverse = head_inverse(raw)
                normed = raw * inverse
                turned = unrotate(grad_ref[:, at], cos, sin) * scale
                gain_sum += jnp.sum(turned * normed, axis=0, keepdims=True)
                d = turned * gain
                back = inverse * (d - normed * (jnp.sum(d * normed, axis=-1, keepdims=True) * (1.0 / HEAD)))
                g_ref[:, i * padded + h * LANE : i * padded + (h + 1) * LANE] = back.astype(BF)
            ggain_ref[i : i + 1] = gain_sum
        g_ref[:, 2 * padded :] = gv_ref[...].astype(BF)
        for i in range(3):
            arrived(wq_a.at[i], wq_ref.at[i], sems.at[i])
        step = 3 * LANE

        def out_block(j, carry):
            at = pl.ds(pl.multiple_of(j * step, LANE), step)
            total = nt(g_ref[:, :padded], wq_ref[0, at])
            total += nt(g_ref[:, padded : 2 * padded], wq_ref[1, at])
            total += nt(g_ref[:, 2 * padded :], wq_ref[2, at])
            split_store(total, at, (p0, p1, p2, p3))
            return carry

        lax.fori_loop(0, width // step, out_block, 0)
        gqk_out[...] = nn(g_ref[:, : 2 * padded], selqk_ref[...]).astype(BF)
        gv_out[...] = nn(g_ref[:, 2 * padded :], selv_ref[...]).astype(BF)
        mixed_out[...] = nn(mixed_ref[...], selv_ref[...]).astype(BF)

    outs = [shape((share, width), F32)] + [shape((share, width), BF)] * 3
    outs += [shape((rows, 2 * narrow), BF), shape((rows, narrow), BF), shape((rows, narrow), BF)]
    outs += [shape((rows, width), BF), shape((8, LANE), F32)]
    result = call(
        body,
        outs,
        [SM] + [VM] * 4 + [ANY] * 4 + [VM] * 13,
        [
            pltpu.VMEM((3, width, padded), BF),
            pltpu.VMEM((padded, width), BF),
            pltpu.VMEM((rows, padded), BF),
            pltpu.VMEM((rows, padded), F32),
            pltpu.VMEM((rows, padded), F32),
            pltpu.VMEM((rows, 3 * padded), BF),
            pltpu.VMEM((rows, padded), F32),
            pltpu.SemaphoreType.DMA((4,)),
        ],
        flops=2 * rows * width * padded * 4 + 10 * rows * rows * padded,
        size=14 * 2**20,
        name=f"attention_backward_{layer}",
    )(section, *blocks, wq_own, wq_got, wo_own, wo_got, q_raw, k_raw, q_rot, k_rot, values, mixed,
      cosine, sine, gains, seg_col, seg_row, pick_qk, pick_v)
    return result[:4], result[4:]


def attention_weight_grads(attention_in, grads, section):
    gqk, gv, mixed, grad_attended = grads
    rows, width = attention_in.shape
    narrow = gv.shape[1]
    step = 3 * LANE

    def body(sec_ref, a_ref, gqk_ref, gv_ref, mixed_ref, ga_ref, keep_ref, send_ref):
        def row_block(j, carry):
            at = pl.ds(pl.multiple_of(j * step, LANE), step)
            left = a_ref[:, at]
            first = tn(left, gqk_ref[...]).astype(BF)
            second = tn(left, gv_ref[...]).astype(BF)
            third = tn(ga_ref[:, at], mixed_ref[...]).astype(BF)

            def put(low_ref, high_ref):
                low_ref[at] = first
                high_ref[at] = jnp.concatenate([second, third], axis=1)

            @pl.when(sec_ref[0] == 0)
            def _():
                put(keep_ref, send_ref)

            @pl.when(sec_ref[0] != 0)
            def _():
                put(send_ref, keep_ref)

            return carry

        lax.fori_loop(0, width // step, row_block, 0)

    return call(
        body,
        [shape((width, 2 * narrow), BF)] * 2,
        [SM] + [VM] * 5,
        flops=8 * rows * width * narrow,
        size=6 * 2**20,
        name="attention_weight_grads",
    )(section, attention_in, gqk, gv, mixed, grad_attended)


def back_of_mlp(parts, grad_out, after, attended, projected, mods, picks):
    def body(p0, p1, p2, p3, g_ref, after_ref, attended_ref, projected_ref, mods_ref, picks_ref, ga_ref, grad_ref, sums_ref):
        picked = picks_ref[...]
        g = g_ref[...].astype(F32)
        grad_in = p0[...] + p1[...].astype(F32) + p2[...].astype(F32) + p3[...].astype(F32)
        after = after_ref[...]
        inverse = inverse_rms(after)
        normed = after * inverse
        grad_after = g + norm_back(grad_in * (1.0 + token_mod(picked, mods_ref, 4)), normed, inverse)
        grad_ref[...] = grad_after
        ga_ref[...] = (grad_after * token_mod(picked, mods_ref, 2)).astype(BF)
        sums_ref[0] = image_sums(picked, grad_after * attended_ref[...])
        sums_ref[1] = image_sums(picked, grad_in)
        sums_ref[2] = image_sums(picked, grad_in * normed)
        sums_ref[3] = image_sums(picked, g * projected_ref[...])

    dims = after.shape
    return call(
        body,
        [shape(dims, BF), shape(dims, F32), shape((4, picks.shape[1], dims[1]), F32)],
        [VM] * 10,
        flops=40 * dims[0] * dims[1],
        size=24 * dims[0] * dims[1],
        name="back_of_mlp",
    )(*parts, grad_out, after, attended, projected, mods, picks)


def back_of_attention(parts, grad_after, state, mods, picks, mods_below):
    first = mods_below is None

    def body(p0, p1, p2, p3, grad_ref, state_ref, mods_ref, picks_ref, *refs):
        picked = picks_ref[...]
        grad_in = p0[...] + p1[...].astype(F32) + p2[...].astype(F32) + p3[...].astype(F32)
        state = state_ref[...].astype(F32)
        inverse = inverse_rms(state)
        normed = state * inverse
        grad_state = grad_ref[...] + norm_back(grad_in * (1.0 + token_mod(picked, mods_ref, 1)), normed, inverse)
        if first:
            sums_ref, out_ref = refs
            out_ref[...] = grad_state
        else:
            below_ref, sums_ref, low_ref, gp_ref = refs
            low = grad_state.astype(BF)
            low_ref[...] = low
            gp_ref[...] = (low.astype(F32) * token_mod(picked, below_ref, 5)).astype(BF)
        sums_ref[0] = image_sums(picked, grad_in)
        sums_ref[1] = image_sums(picked, grad_in * normed)

    dims = grad_after.shape
    outs = [shape((2, picks.shape[1], dims[1]), F32)] + ([shape(dims, F32)] if first else [shape(dims, BF)] * 2)
    extra = () if first else (mods_below,)
    return call(
        body,
        outs,
        [VM] * (8 + len(extra)),
        flops=40 * dims[0] * dims[1],
        size=16 * dims[0] * dims[1],
        name="back_of_attention",
    )(*parts, grad_after, state, mods, picks, *extra)


def exchange(value, axis, k):
    return lax.ppermute(value, axis, [(i, i ^ k) for i in range(lax.axis_size(axis))])


def send_parts(parts):
    got = {k: exchange(parts[k], "tensor", k) for k in (3, 1, 2)}
    return [parts[0], got[1], got[2], got[3]]


def gather_blocks(own):
    got = {k: exchange(own, "tensor", k) for k in (3, 1, 2)}
    return [own, got[1], got[2], got[3]]


def group_sum(value, axis):
    k = 1
    while k < lax.axis_size(axis):
        value = value + exchange(value, axis, k)
        k *= 2
    return value


def gather_dp(value):
    count = lax.axis_size("dp")
    if count > 4:
        return lax.all_gather(value, "dp", axis=0)
    me = lax.axis_index("dp")
    got = [value] + [exchange(value, "dp", k) for k in range(1, count)]
    stacked = jnp.stack(got)
    return jnp.stack([lax.dynamic_index_in_dim(stacked, me ^ j, 0, keepdims=False) for j in range(count)])


def head_places(heads):
    place = np.zeros((heads * HEAD, heads * LANE), np.float32)
    for h in range(heads):
        for j in range(HEAD):
            place[h * HEAD + j, h * LANE + (j // HALF) * (LANE // 2) + j % HALF] = 1.0
    return place


def shards(
    inputs,
    cotangent,
    conditioning,
    lengths,
    positions,
    modulator,
    projections,
    norm_gains,
    out_weight,
    gate_up,
    down_weight,
):
    section = lax.axis_index("section")
    other = 1 - section
    tensor = lax.axis_index("tensor")
    data = lax.axis_index("dp")
    micro, rows, width = inputs.shape
    group = lax.axis_size("tensor")
    share = rows // group
    items = lengths.shape[2]
    narrow = projections.shape[3]
    heads = narrow // HEAD
    padded = heads * LANE
    columns = modulator.shape[2]
    sec = section.reshape(1).astype(jnp.int32)

    cond_value = conditioning[:, 0].astype(F32)
    scaled = jax.nn.silu(cond_value).astype(BF)
    part = jnp.einsum("mid,dc->mic", scaled, modulator[0], preferred_element_type=F32).astype(BF)
    mine = lax.dynamic_index_in_dim(part, section, 0, keepdims=False)
    theirs = exchange(lax.dynamic_index_in_dim(part, other, 0, keepdims=False), "section", 1)
    is_first = section == 0
    both = jnp.stack([jnp.where(is_first, mine, theirs), jnp.where(is_first, theirs, mine)])
    pieces = jnp.stack(gather_blocks(both))
    ordered = [lax.dynamic_index_in_dim(pieces, tensor ^ j, 0, keepdims=False) for j in range(group)]
    mods_all = jnp.concatenate(ordered, axis=2)
    mods_all = jnp.pad(mods_all, ((0, 0), (0, 8 - items), (0, 0)))
    mods = [mods_all[0], mods_all[1]]

    place = jnp.asarray(head_places(heads), BF)
    wq_own = jnp.einsum("kde,ec->kdc", projections[0], place, preferred_element_type=F32).astype(BF)
    wo_own = jnp.einsum("ec,ed->cd", place, out_weight[0], preferred_element_type=F32).astype(BF)
    wq_got = exchange(wq_own, "section", 1)
    wo_got = exchange(wo_own, "section", 1)
    gu_got = exchange(gate_up[0], "section", 1)
    wd_got = exchange(down_weight[0], "section", 1)
    attention_weights = (wq_own, wq_got, wo_own, wo_got)
    mlp_weights = (gate_up[0], gu_got, down_weight[0], wd_got)
    select_v = place.T
    zero = jnp.zeros_like(select_v)
    select_qk = jnp.concatenate(
        [jnp.concatenate([select_v, zero], axis=1), jnp.concatenate([zero, select_v], axis=1)], axis=0
    )
    selects = (select_qk, select_v)

    def local(value):
        return jnp.concatenate(
            [
                lax.dynamic_slice_in_dim(value, (tensor ^ k) * share, share, 0)
                for k in range(group)
            ],
            axis=0,
        )

    def of_micro(value):
        return lax.dynamic_index_in_dim(value, section, 0, keepdims=False)

    ends = jnp.cumsum(of_micro(lengths)[0])
    index = jnp.arange(rows)
    index = (tensor ^ (index // share)) * share + index % share
    segment = jnp.sum((index[:, None] >= ends[None, :]).astype(jnp.int32), axis=1)
    picks = (segment[:, None] == jnp.arange(8)[None, :]).astype(BF)
    picks_own = picks[:share]
    lane = np.arange(LANE) % (LANE // 2)
    valid = jnp.asarray(lane < HALF)
    quarter = HEAD // 4
    rates = 10000.0 ** (-jnp.arange(quarter).astype(F32) / quarter)
    rate = jnp.concatenate([rates, rates, jnp.zeros(LANE // 2 - HALF, F32)] * 2)
    place_now = local(of_micro(positions).T).astype(F32)
    phase = jnp.where(jnp.asarray(lane < quarter), place_now[:, :1], place_now[:, 1:]) * rate
    cosine = jnp.where(valid, jnp.cos(phase), 0.0)
    sine = jnp.where(valid, jnp.sin(phase), 0.0) * jnp.where(jnp.asarray(np.arange(LANE) < LANE // 2), -1.0, 1.0)
    own_gains = jnp.dot(
        jnp.pad(norm_gains[0], ((0, 6), (0, 0))), jnp.asarray(head_places(1), F32), precision=HIGHEST
    )
    got_gains = exchange(own_gains, "section", 1)
    gains = [jnp.where(is_first, own_gains, got_gains), jnp.where(is_first, got_gains, own_gains)]
    tables = [(cosine, sine, gains[l], segment[:, None], segment[None, :]) for l in range(2)]
    x = local(of_micro(inputs))
    cotangent_now = local(of_micro(cotangent))

    states = [x[:share]]
    cache = []
    attention_blocks = [x]
    for l in range(2):
        partial, saved = attention_forward(l, attention_blocks, attention_weights, tables[l], mods[l], picks, sec)
        attended, after, mlp_in = after_attention(send_parts(partial), states[l], mods[l], picks_own)
        mlp_blocks = gather_blocks(mlp_in)
        partial, mlp_saved = mlp_forward(l, mlp_blocks, mlp_weights, sec)
        parts = send_parts(partial)
        if l == 0:
            projected, state, attention_in = after_mlp(parts, after, mods[0], picks_own, mods[1])
            states.append(state)
            attention_blocks = gather_blocks(attention_in)
        else:
            projected, output = after_mlp(parts, after, mods[1], picks_own, None)
        cache.append((saved, attended, after, mlp_blocks, mlp_saved, projected))

    grad_blocks = [cotangent_now]
    grad_out = cotangent_now[:share]
    item_sums = [None, None]
    gain_sums = [None, None]
    shares = [None, None]
    for l in (1, 0):
        saved, attended, after, mlp_blocks, mlp_saved, projected = cache[l]
        attention_in = saved[6]
        partial, grads = mlp_backward(l, grad_blocks, mlp_weights, mlp_saved, mods[l], picks, sec)
        parts = send_parts(partial)
        keep, send = mlp_weight_grads(mlp_blocks, grads, mlp_saved[0], sec)
        mlp_half = (keep.astype(F32) + exchange(send, "section", 1).astype(F32)).astype(BF)
        mlp_share = lax.psum_scatter(mlp_half, "dp", scatter_dimension=0, tiled=True)
        grad_attended, grad_after, sums2 = back_of_mlp(
            parts, grad_out, after, attended, projected, mods[l], picks_own
        )
        partial, results = attention_backward(
            l, gather_blocks(grad_attended), attention_weights, saved[:6], tables[l], selects, sec
        )
        gain_sums[l] = results[4]
        parts = send_parts(partial)
        keep, send = attention_weight_grads(attention_in, results[:4], sec)
        attention_half = (keep.astype(F32) + exchange(send, "section", 1).astype(F32)).astype(BF)
        attention_share = lax.psum_scatter(attention_half, "dp", scatter_dimension=0, tiled=True)
        if l == 1:
            sums1, grad_out, grad_projected = back_of_attention(
                parts, grad_after, states[1], mods[1], picks_own, mods[0]
            )
            grad_blocks = gather_blocks(grad_projected)
        else:
            sums1, grad_state = back_of_attention(parts, grad_after, states[0], mods[0], picks_own, None)
        item_sums[l] = jnp.concatenate([sums1, sums2], axis=0)
        shares[l] = (mlp_share, attention_share)

    mine = jnp.where(is_first, grad_state, output)
    theirs = exchange(jnp.where(is_first, output, grad_state), "section", 1)
    results = jnp.stack([jnp.where(is_first, mine, theirs), jnp.where(is_first, theirs, mine)])

    def joined(which):
        mine = jnp.where(is_first, shares[0][which], shares[1][which])
        theirs = exchange(jnp.where(is_first, shares[1][which], shares[0][which]), "section", 1)
        low = jnp.where(is_first, mine, theirs)
        high = jnp.where(is_first, theirs, mine)
        return jnp.concatenate([low, high], axis=1).astype(F32)

    size = down_weight.shape[1]
    mlp_grads = joined(0)
    grad_pair = jnp.stack([mlp_grads[:, :size], mlp_grads[:, size : 2 * size]])
    grad_down = mlp_grads[:, 2 * size :].T
    attention_grads = joined(1)
    grad_qkv = jnp.stack([attention_grads[:, i * narrow : (i + 1) * narrow] for i in range(3)])
    grad_out_w = attention_grads[:, 3 * narrow :].T

    sums = jnp.stack(item_sums)[:, :, :items].transpose(0, 2, 1, 3).reshape(2, items, 6 * width)
    pieces = [
        lax.dynamic_slice_in_dim(sums, (tensor ^ k) * columns, columns, 2) for k in range(group)
    ]
    got = send_parts(pieces)
    mods_grad = (got[0] + got[1] + got[2] + got[3]).astype(BF)
    mine = lax.dynamic_index_in_dim(mods_grad, section, 0, keepdims=False)
    theirs = exchange(lax.dynamic_index_in_dim(mods_grad, other, 0, keepdims=False), "section", 1)
    mods_low = jnp.stack([jnp.where(is_first, mine, theirs), jnp.where(is_first, theirs, mine)])
    all_scaled = gather_dp(scaled)
    all_mods = gather_dp(mods_low)
    deep = width // lax.axis_size("dp")
    scaled_share = lax.dynamic_slice_in_dim(all_scaled, data * deep, deep, 3)
    grad_ada = jnp.einsum("nmid,nmic->dc", scaled_share, all_mods, preferred_element_type=F32)
    sigma = jax.nn.sigmoid(cond_value)
    cond_part = jnp.einsum("mic,dc->mid", mods_low, modulator[0], preferred_element_type=F32)
    cond_part = cond_part * sigma * (1.0 + cond_value * (1.0 - sigma))
    grad_cond = group_sum(group_sum(cond_part, "section"), "tensor")
    gain_parts = jnp.stack(gain_sums)
    gain_own = lax.dynamic_index_in_dim(gain_parts, section, 0, keepdims=False)
    gain_other = lax.dynamic_index_in_dim(gain_parts, other, 0, keepdims=False)
    gain_total = gain_own + exchange(gain_other, "section", 1)
    gain_total = group_sum(group_sum(gain_total, "tensor"), "dp")
    half = LANE // 2
    grad_gains = jnp.concatenate([gain_total[:2, :HALF], gain_total[:2, half : half + HALF]], axis=1)
    return (
        grad_ada[None],
        grad_qkv[None],
        grad_gains[None],
        grad_out_w[None],
        grad_pair[None],
        grad_down[None],
        grad_cond[:, None],
        results[None],
    )


def solution(mesh):
    return jax.shard_map(
        shards,
        mesh=mesh,
        in_specs=(
            P(None, "dp", None),
            P(None, "dp", None),
            P(None, "dp", None, None),
            P(None, "dp", None),
            P(None, None, "dp"),
            P("section", None, "tensor"),
            P("section", None, None, "tensor"),
            P("section", None, None),
            P("section", "tensor", None),
            P("section", None, None, "tensor"),
            P("section", "tensor", None),
        ),
        out_specs=(
            P("section", "dp", "tensor"),
            P("section", None, "dp", "tensor"),
            P("section", None, None),
            P("section", "tensor", "dp"),
            P("section", None, "dp", "tensor"),
            P("section", "tensor", "dp"),
            P(None, "dp", None, None),
            P("section", None, ("dp", "tensor"), None),
        ),
        check_vma=False,
    )
```

time: 2390 us -> 535 us (0.22)
  waiting for transfers between devices: 1630 us -> 196 us
  matrix products: 268 us -> 14.1 us
  other arithmetic: 180 us -> 30.6 us
  Pallas kernels: 0 us -> 139 us
  blocking collectives: 103 us -> 0 us
  local copies, waits for them, and re-layouts: 139 us -> 44.7 us
  starting transfers between devices: 13.4 us -> 86.5 us
  loops' own time: 33.9 us -> 0 us
    reduce_scatter x22 -> x4, waiting for transfers between devices: 1000 us -> 63.5 us  [the longest x2 63.5 us: shards(): lax.psum_scatter(mlp_half, 'dp', scatter_dimension=0, tiled=True)]
    all_gather x18 -> x0, waiting for transfers between devices: 619 us -> none  [the longest x12 428 us: branch_sum(): return lax.all_gather(shares, 'tensor', axis=0, tiled=True)]
    dot_general x78 -> x6, matrix products: 242 us -> 14.1 us  [the longest x1 3.89 us: shards(): jnp.einsum('kde,ec->kdc', projections[0], place, preferred_element_type=F32)]
    pallas_call x0 -> x20, Pallas kernels: none -> 139 us  [the longest x2 40.5 us: attention_backward(): call(body, outs, [SM] + [VM] * 4 + [ANY] * 4 + [VM] * 13, [pltpu.VMEM((3,...]
    ppermute x6 -> x76, waiting for transfers between devices: 6.66 us -> 132 us  [exchange(): lax.ppermute(value, axis, [(i, i ^ k) for i in range(lax.axis_size(axis))])]
    ppermute x6 -> x76, starting transfers between devices: 11.8 us -> 86.4 us  [exchange(): lax.ppermute(value, axis, [(i, i ^ k) for i in range(lax.axis_size(axis))])]
    psum x2 -> x0, blocking collectives: 69 us -> none  [the longest x1 34.9 us: shards(): gains_total = lax.psum(total_gains, ('tensor', 'dp'))]
    while x481 -> x0, local copies, waits for them, and re-layouts: 67.9 us -> none
  transfers between devices with their start and end apart: 47 -> 80, of which waited for: 42 -> 49; matrix products, arithmetic and copies ran while one was open for 8% -> 9% of each run, Pallas kernels for 0% -> 15%
where the time goes in v1:
time: 535 us; the launch traced here: 525 us
  waiting for transfers between devices  196 us (37%)
  Pallas kernels  139 us (26%)
  starting transfers between devices  86.5 us (16%)
  local copies, waits for them, and re-layouts  44.7 us (8%)
  other arithmetic  30.6 us (6%)
  between operations  15 us (3%)
  matrix products  14.1 us (3%)
    ppermute x76, waiting for transfers between devices, exchange(): lax.ppermute(value, axis, [(i, i ^ k) for i in range(lax.axis_size(axis))])  132 us
    ppermute x76, starting transfers between devices, exchange(): lax.ppermute(value, axis, [(i, i ^ k) for i in range(lax.axis_size(axis))])  86.4 us
    reduce_scatter x2, waiting for transfers between devices, shards(): lax.psum_scatter(mlp_half, 'dp', scatter_dimension=0, tiled=True)  63.5 us
    pallas_call x2, Pallas kernels, attention_backward(): call(body, outs, [SM] + [VM] * 4 + [ANY] * 4 + [VM] * 13, [pltpu.VMEM((3,...  40.5 us
    pallas_call x2, Pallas kernels, attention_forward(): call(body, outs, [SM] + [VM] * len(blocks) + [ANY] * 4 + [VM] * 7, [pltpu...  33.1 us
    unnamed x165, local copies, waits for them, and re-layouts  29.4 us
    pallas_call x2, Pallas kernels, mlp_backward(): call(body, outs, [SM] + [VM] * len(blocks) + [ANY] * 4 + [VM] * 4, [pltpu...  15.7 us
    pallas_call x2, Pallas kernels, mlp_weight_grads(): call(body, [shape((width, half), BF)] * 2, [SM] + [VM] * 8, [pltpu.VMEM((...  15.7 us
  transfers between devices with their start and end apart: 80, of which 49 were waited for; matrix products, arithmetic and copies ran while one was open for 9% of the time, Pallas kernels for 15%

profile of v1, /device:TPU:1, one launch (start us, length us, event | category | flops | bytes accessed | tf_op | source)
XLA Modules:
  0.0 525.5 jit_solution(9295352351077232067)
XLA Ops:
  30.4 17.3 %attention_forward_0.1 = (f32[128,1152]{1,0:T(8,128)}, bf16[128,1152]{1,0:T(8,128)(2,1)S(1)}, bf16[128,1152]{1,0:T(8,128)(2,1)S(1)}, bf16[128,1152]{1,0:T(8,128)...) custom-call(s32[1]{0:T(128)} %bitcast.6.sec_ref, ...), custom_call_target="tpu_custom_call" | custom-call | flops 2952790016 | bytes 12582912 | tf_op jit(solution)/shard_map/attention_forward_0/pallas_call | solution.py:184
  61.0 5.0 collective-permute-done.14.p3
  77.1 5.7 %collective-permute-done.17.b3 = bf16[128,1152]{1,0:T(8,128)(2,1)S(1)} collective-permute-done((bf16[128,1152]{1,0:T(8,128)(2,1)S(1)}, bf16[128,1152]{1,0:T(8,128)(2,1)S(1)}, u32[]{:S(2)}, u32[]{:S(2)}) %collective-permute-start.17) | collective-permute-done | bytes 294944 | tf_op jit(solution)/shard_map/ppermute | solution.py:632
  82.8 7.2 %mlp_forward_0.1 = (f32[128,1152]{1,0:T(8,128)S(1)}, bf16[128,1152]{1,0:T(8,128)(2,1)S(1)}, bf16[128,1152]{1,0:T(8,128)(2,1)S(1)}, bf16[128,1152]{1,0:T(8,128)(2...) custom-call(s32[1]{0:T(128)} %bitcast.6.sec_ref, ...), custom_call_target="tpu_custom_call" | custom-call | flops 2717908992 | bytes 10485760 | tf_op jit(solution)/shard_map/mlp_forward_0/pallas_call | solution.py:294
  97.4 5.9 %collective-permute-done.20.p3 = bf16[128,1152]{1,0:T(8,128)(2,1)S(1)} collective-permute-done((bf16[128,1152]{1,0:T(8,128)(2,1)S(1)}, bf16[128,1152]{1,0:T(8,128)(2,1)S(1)}, u32[]{:S(2)}, u32[]{:S(2)}) %collective-permute-start.20) | collective-permute-done | bytes 294944 | tf_op jit(solution)/shard_map/ppermute | solution.py:632
  110.2 5.9 %collective-permute-done.22.refs_2_ = bf16[128,1152]{1,0:T(8,128)(2,1)S(1)} collective-permute-done((bf16[128,1152]{1,0:T(8,128)(2,1)S(1)}, bf16[128,1152]{1,0:T(8,128)(2,1)S(1)}, u32[]{:S(2)}, u32[]{:S(2)}) %collective-permute-start.22) | collective-permute-done | bytes 294944 | tf_op jit(solution)/shard_map/ppermute | solution.py:632
  116.1 15.8 %attention_forward_1.1 = (f32[128,1152]{1,0:T(8,128)}, bf16[128,1152]{1,0:T(8,128)(2,1)S(1)}, bf16[128,1152]{1,0:T(8,128)(2,1)S(1)}, bf16[128,1152]{1,0:T(8,128)...) custom-call(s32[1]{0:T(128)} %bitcast.6.sec_ref, ...), custom_call_target="tpu_custom_call" | custom-call | flops 2952790016 | bytes 12582912 | tf_op jit(solution)/shard_map/attention_forward_1/pallas_call | solution.py:184
  154.4 7.4 %mlp_forward_1.1 = (f32[128,1152]{1,0:T(8,128)S(1)}, bf16[128,1152]{1,0:T(8,128)(2,1)S(1)}, bf16[128,1152]{1,0:T(8,128)(2,1)S(1)}, bf16[128,1152]{1,0:T(8,128)(2...) custom-call(s32[1]{0:T(128)} %bitcast.6.sec_ref, ...), custom_call_target="tpu_custom_call" | custom-call | flops 2717908992 | bytes 10485760 | tf_op jit(solution)/shard_map/mlp_forward_1/pallas_call | solution.py:294
  166.7 7.8 %mlp_backward_1.1 = (f32[128,1152]{1,0:T(8,128)S(1)}, bf16[128,1152]{1,0:T(8,128)(2,1)S(1)}, bf16[128,1152]{1,0:T(8,128)(2,1)S(1)}, bf16[128,1152]{1,0:T(8,128)(...) custom-call(s32[1]{0:T(128)} %bitcast.6.sec_ref, ...), custom_call_target="tpu_custom_call" | custom-call | flops 2717908992 | bytes 10485760 | tf_op jit(solution)/shard_map/mlp_backward_1/pallas_call | solution.py:359
  183.6 4.9 collective-permute-done.31.p2
  198.4 4.8 collective-permute-done.37.b2
  203.3 20.0 %attention_backward_1.1 = (f32[128,1152]{1,0:T(8,128)}, bf16[128,1152]{1,0:T(8,128)(2,1)S(1)}, bf16[128,1152]{1,0:T(8,128)(2,1)S(1)}, bf16[128,1152]{1,0:T(8,128...) custom-call(s32[1]{0:T(128)} %bitcast.6.sec_ref, ...), custom_call_target="tpu_custom_call" | custom-call | flops 3758096384 | bytes 14680064 | tf_op jit(solution)/shard_map/attention_backward_1/pallas_call | solution.py:508
  234.0 7.9 %collective-permute-start.62 = (bf16[1152,576]{0,1:T(8,128)(2,1)}, bf16[1152,576]{0,1:T(8,128)(2,1)}, u32[]{:S(2)}, u32[]{:S(2)}) collective-permute-start(bf16[1152,576]{0,1:T(8,128)(2,1)} %copy.187), channel_id=1, source_target_pairs={{0,16},{16,0},{1,17},{17,1},{2,18},{18,2},{3,19},{19,3},{4,20},{20... | collective-permute-start | bytes 3981320 | tf_op jit(solution)/shard_map/ppermute | solution.py:632
  244.5 6.2 %collective-permute-done.39.p1 = bf16[128,1152]{1,0:T(8,128)(2,1)S(1)} collective-permute-done((bf16[128,1152]{1,0:T(8,128)(2,1)}, bf16[128,1152]{1,0:T(8,128)(2,1)S(1)}, u32[]{:S(2)}, u32[]{:S(2)}) %collective-permute-start.39) | collective-permute-done | bytes 294944 | tf_op jit(solution)/shard_map/ppermute | solution.py:632
  250.7 5.7 %collective-permute-done.41.p3 = bf16[128,1152]{1,0:T(8,128)(2,1)S(1)} collective-permute-done((bf16[128,1152]{1,0:T(8,128)(2,1)}, bf16[128,1152]{1,0:T(8,128)(2,1)S(1)}, u32[]{:S(2)}, u32[]{:S(2)}) %collective-permute-start.41) | collective-permute-done | bytes 294944 | tf_op jit(solution)/shard_map/ppermute | solution.py:632
  268.6 6.8 %collective-permute-done.44.refs_3_ = bf16[128,1152]{1,0:T(8,128)(2,1)S(1)} collective-permute-done((bf16[128,1152]{1,0:T(8,128)(2,1)S(1)}, bf16[128,1152]{1,0:T(8,128)(2,1)S(1)}, u32[]{:S(2)}, u32[]{:S(2)}) %collective-permute-start.44) | collective-permute-done | bytes 294944 | tf_op jit(solution)/shard_map/ppermute | solution.py:632
  275.3 7.9 %mlp_backward_0.1 = (f32[128,1152]{1,0:T(8,128)S(1)}, bf16[128,1152]{1,0:T(8,128)(2,1)S(1)}, bf16[128,1152]{1,0:T(8,128)(2,1)S(1)}, bf16[128,1152]{1,0:T(8,128)(...) custom-call(s32[1]{0:T(128)} %bitcast.6.sec_ref, ...), custom_call_target="tpu_custom_call" | custom-call | flops 2717908992 | bytes 10485760 | tf_op jit(solution)/shard_map/mlp_backward_0/pallas_call | solution.py:359
  313.4 20.5 %attention_backward_0.1 = (f32[128,1152]{1,0:T(8,128)}, bf16[128,1152]{1,0:T(8,128)(2,1)S(1)}, bf16[128,1152]{1,0:T(8,128)(2,1)S(1)}, bf16[128,1152]{1,0:T(8,128...) custom-call(s32[1]{0:T(128)} %bitcast.6.sec_ref, ...), custom_call_target="tpu_custom_call" | custom-call | flops 3758096384 | bytes 14680064 | tf_op jit(solution)/shard_map/attention_backward_0/pallas_call | solution.py:508
  337.0 4.9 attention_weight_grads.2
  351.5 7.7 %mlp_weight_grads.3 = (bf16[1152,1152]{1,0:T(8,128)(2,1)}, bf16[1152,1152]{1,0:T(8,128)(2,1)}) custom-call(s32[1]{0:T(128)} %bitcast.6.sec_ref, bf16[128,1152]{1,0:T(8,128)(2,1)S(1)} %copy-done.30, bf16[128,1152]{1,0:T(8,128)(2,1)S(1)} %copy-done.32, bf16[128,1152]{1,0:T(8,128)(2,1)S(1)} %copy-done.34, bf16[128,1152]{1,0:T(8,128)(2,1)S(1)} %copy-done.36, ...), custom_call_target="tpu_custom_call" | custom-call | flops 2717908992 | bytes 10485760 | tf_op jit(solution)/shard_map/mlp_weight_grads/pallas_call | solution.py:412
  373.8 8.0 %mlp_weight_grads.2 = (bf16[1152,1152]{1,0:T(8,128)(2,1)}, bf16[1152,1152]{1,0:T(8,128)(2,1)}) custom-call(s32[1]{0:T(128)} %bitcast.6.sec_ref, bf16[128,1152]{1,0:T(8,128)(2,1)S(1)} %copy-done.22, bf16[128,1152]{1,0:T(8,128)(2,1)S(1)} %copy-done.24, bf16[128,1152]{1,0:T(8,128)(2,1)S(1)} %copy-done.26, bf16[128,1152]{1,0:T(8,128)(2,1)S(1)} %copy-done.28, ...), custom_call_target="tpu_custom_call" | custom-call | flops 2717908992 | bytes 10485760 | tf_op jit(solution)/shard_map/mlp_weight_grads/pallas_call | solution.py:412
  400.9 6.1 %collective-permute-done.53.p3 = bf16[128,1152]{1,0:T(8,128)(2,1)S(1)} collective-permute-done((bf16[128,1152]{1,0:T(8,128)(2,1)}, bf16[128,1152]{1,0:T(8,128)(2,1)S(1)}, u32[]{:S(2)}, u32[]{:S(2)}) %collective-permute-start.53) | collective-permute-done | bytes 294944 | tf_op jit(solution)/shard_map/ppermute | solution.py:632
  445.7 9.0 %reduce-scatter.11.cloned.1.call-done = bf16[288,1152]{1,0:T(8,128)(2,1)} async-done(((bf16[1152,1152]{1,0:T(8,128)(2,1)}), bf16[288,1152]{1,0:T(8,128)(2,1)}) %reduce-scatter.11.cloned.1.call-update) | async-done | bytes 663568 | tf_op jit(solution)/shard_map/reduce_scatter | solution.py:792
  454.7 54.5 %reduce-scatter.9.cloned.1.call-done = bf16[288,1152]{1,0:T(8,128)(2,1)} async-done(((bf16[1152,1152]{1,0:T(8,128)(2,1)}), bf16[288,1152]{1,0:T(8,128)(2,1)}) %reduce-scatter.9.cloned.1.call-update) | async-done | bytes 663568 | tf_op jit(solution)/shard_map/reduce_scatter | solution.py:792
  (408 shorter events, 257.6 us)
Async XLA Ops:
  7.2 433.0 %reduce-scatter.7.cloned.1.call-start = ((), (), s32[]{:S(2)}) async-start(), calls=%async_computation.5 | async-start | bytes 1843200 | tf_op jit(solution)/shard_map/reduce_scatter | solution.py:803
  10.8 11.8 %collective-permute-start.8 = (bf16[4,1728]{1,0:T(4,128)(2,1)S(1)}, bf16[4,1728]{1,0:T(4,128)(2,1)S(1)}, u32[]{:S(2)}, u32[]{:S(2)}) collective-permute-start(bf16[4,1728]{1,0:T(4,128)(2,1)S(1)} %dynamic-slice_bitcast_fusion.13), channel_id=1, source_target_pairs={{0,16},{16,0},{1,17},{17,1},{2,18},{18,2},{3,19},{19,3},{4,20},{20... | collective-permute-start | bytes 41480 | tf_op jit(solution)/shard_map/ppermute | solution.py:632
  11.1 15.1 %collective-permute-start.7 = (f32[8,128]{1,0:T(8,128)S(1)}, f32[8,128]{1,0:T(8,128)S(1)}, u32[]{:S(2)}, u32[]{:S(2)}) collective-permute-start(f32[8,128]{1,0:T(8,128)S(1)} %fusion.57), channel_id=1, source_target_pairs={{0,16},{16,0},{1,17},{17,1},{2,18},{18,2},{3,19},{19,3},{4,20},{20... | collective-permute-start | bytes 12296 | tf_op jit(solution)/shard_map/ppermute | solution.py:632
  15.5 14.9 %collective-permute-start.5 = (bf16[3,1152,512]{2,1,0:T(8,128)(2,1)}, bf16[3,1152,512]{2,1,0:T(8,128)(2,1)}, u32[]{:S(2)}, u32[]{:S(2)}) collective-permute-start(bf16[3,1152,512]{2,1,0:T(8,128)(2,1)} %fusion.4.refs_1_.refs_4_.wq_a), channel_id=1, source_target_pairs={{0,16},{16,0},{1,17},{17,1},{2,18},{18,2},{3,19},{19,3},{4,20},{20... | collective-permute-start | bytes 10616840 | tf_op jit(solution)/shard_map/ppermute | solution.py:632
  15.6 55.5 %collective-permute-start.3 = (bf16[2,1152,768]{2,1,0:T(8,128)(2,1)}, bf16[2,1152,768]{2,1,0:T(8,128)(2,1)}, u32[]{:S(2)}, u32[]{:S(2)}) collective-permute-start(bf16[2,1152,768]{2,1,0:T(8,128)(2,1)} %bitcast.11.gu_a.refs_1_.refs_4_), channel_id=1, source_target_pairs={{0,16},{16,0},{1,17},{17,1},{2,18},{18,2},{3,19},{19,3},{4,20},{20... | collective-permute-start | bytes 10616840 | tf_op jit(solution)/shard_map/ppermute | solution.py:632
  27.7 43.4 %collective-permute-start.4 = (bf16[768,1152]{1,0:T(8,128)(2,1)}, bf16[768,1152]{1,0:T(8,128)(2,1)}, u32[]{:S(2)}, u32[]{:S(2)}) collective-permute-start(bf16[768,1152]{1,0:T(8,128)(2,1)} %bitcast.236), channel_id=1, source_target_pairs={{0,16},{16,0},{1,17},{17,1},{2,18},{18,2},{3,19},{19,3},{4,20},{20... | collective-permute-start | bytes 5308424 | tf_op jit(solution)/shard_map/ppermute | solution.py:632
  53.1 12.9 %collective-permute-start.14 = (bf16[128,1152]{1,0:T(8,128)(2,1)S(1)}, bf16[128,1152]{1,0:T(8,128)(2,1)S(1)}, u32[]{:S(2)}, u32[]{:S(2)}) collective-permute-start(bf16[128,1152]{1,0:T(8,128)(2,1)S(1)} %get-tuple-element.109), channel_id=1, source_target_pairs={{0,12},{4,8},{8,4},{12,0},{1,13},{5,9},{9,5},{13,1},{2,14},{6,10},... | collective-permute-start | bytes 884744 | tf_op jit(solution)/shard_map/ppermute | solution.py:632
  69.8 13.0 %collective-permute-start.17 = (bf16[128,1152]{1,0:T(8,128)(2,1)S(1)}, bf16[128,1152]{1,0:T(8,128)(2,1)S(1)}, u32[]{:S(2)}, u32[]{:S(2)}) collective-permute-start(bf16[128,1152]{1,0:T(8,128)(2,1)S(1)} %get-tuple-element.110.b0), channel_id=1, source_target_pairs={{0,12},{4,8},{8,4},{12,0},{1,13},{5,9},{9,5},{13,1},{2,14},{6,10},... | collective-permute-start | bytes 884744 | tf_op jit(solution)/shard_map/ppermute | solution.py:632
  162.7 14.2 %collective-permute-start.33 = (bf16[128,1152]{1,0:T(8,128)(2,1)S(1)}, bf16[128,1152]{1,0:T(8,128)(2,1)S(1)}, u32[]{:S(2)}, u32[]{:S(2)}) collective-permute-start(bf16[128,1152]{1,0:T(8,128)(2,1)S(1)} %get-tuple-element.132), channel_id=1, source_target_pairs={{0,4},{4,0},{8,12},{12,8},{1,5},{5,1},{9,13},{13,9},{2,6},{6,2},{1... | collective-permute-start | bytes 884744 | tf_op jit(solution)/shard_map/ppermute | solution.py:632
  165.5 12.6 %collective-permute-start.34 = (bf16[128,1152]{1,0:T(8,128)(2,1)S(1)}, bf16[128,1152]{1,0:T(8,128)(2,1)S(1)}, u32[]{:S(2)}, u32[]{:S(2)}) collective-permute-start(bf16[128,1152]{1,0:T(8,128)(2,1)S(1)} %get-tuple-element.133), channel_id=1, source_target_pairs={{0,8},{4,12},{8,0},{12,4},{1,9},{5,13},{9,1},{13,5},{2,10},{6,14},... | collective-permute-start | bytes 884744 | tf_op jit(solution)/shard_map/ppermute | solution.py:632
  165.5 12.6 %collective-permute-start.35 = (bf16[128,1152]{1,0:T(8,128)(2,1)S(1)}, bf16[128,1152]{1,0:T(8,128)(2,1)S(1)}, u32[]{:S(2)}, u32[]{:S(2)}) collective-permute-start(bf16[128,1152]{1,0:T(8,128)(2,1)S(1)} %get-tuple-element.134), channel_id=1, source_target_pairs={{0,12},{4,8},{8,4},{12,0},{1,13},{5,9},{9,5},{13,1},{2,14},{6,10},... | collective-permute-start | bytes 884744 | tf_op jit(solution)/shard_map/ppermute | solution.py:632
  176.9 11.5 %collective-permute-start.31 = (bf16[128,1152]{1,0:T(8,128)(2,1)S(1)}, bf16[128,1152]{1,0:T(8,128)(2,1)S(1)}, u32[]{:S(2)}, u32[]{:S(2)}) collective-permute-start(bf16[128,1152]{1,0:T(8,128)(2,1)S(1)} %get-tuple-element.127), channel_id=1, source_target_pairs={{0,8},{4,12},{8,0},{12,4},{1,9},{5,13},{9,1},{13,5},{2,10},{6,14},... | collective-permute-start | bytes 884744 | tf_op jit(solution)/shard_map/ppermute | solution.py:632
  177.0 11.5 %collective-permute-start.32 = (bf16[128,1152]{1,0:T(8,128)(2,1)S(1)}, bf16[128,1152]{1,0:T(8,128)(2,1)S(1)}, u32[]{:S(2)}, u32[]{:S(2)}) collective-permute-start(bf16[128,1152]{1,0:T(8,128)(2,1)S(1)} %get-tuple-element.128), channel_id=1, source_target_pairs={{0,12},{4,8},{8,4},{12,0},{1,13},{5,9},{9,5},{13,1},{2,14},{6,10},... | collective-permute-start | bytes 884744 | tf_op jit(solution)/shard_map/ppermute | solution.py:632
  234.0 69.1 %collective-permute-start.62 = (bf16[1152,576]{0,1:T(8,128)(2,1)}, bf16[1152,576]{0,1:T(8,128)(2,1)}, u32[]{:S(2)}, u32[]{:S(2)}) collective-permute-start(bf16[1152,576]{0,1:T(8,128)(2,1)} %copy.187), channel_id=1, source_target_pairs={{0,16},{16,0},{1,17},{17,1},{2,18},{18,2},{3,19},{19,3},{4,20},{20... | collective-permute-start | bytes 3981320 | tf_op jit(solution)/shard_map/ppermute | solution.py:632
  242.7 13.8 %collective-permute-start.41 = (bf16[128,1152]{1,0:T(8,128)(2,1)}, bf16[128,1152]{1,0:T(8,128)(2,1)S(1)}, u32[]{:S(2)}, u32[]{:S(2)}) collective-permute-start(bf16[128,1152]{1,0:T(8,128)(2,1)} %copy-done.60), channel_id=1, source_target_pairs={{0,12},{4,8},{8,4},{12,0},{1,13},{5,9},{9,5},{13,1},{2,14},{6,10},... | collective-permute-start | bytes 884744 | tf_op jit(solution)/shard_map/ppermute | solution.py:632
  261.6 13.7 %collective-permute-start.44 = (bf16[128,1152]{1,0:T(8,128)(2,1)S(1)}, bf16[128,1152]{1,0:T(8,128)(2,1)S(1)}, u32[]{:S(2)}, u32[]{:S(2)}) collective-permute-start(bf16[128,1152]{1,0:T(8,128)(2,1)S(1)} %get-tuple-element.148.refs_0_), channel_id=1, source_target_pairs={{0,12},{4,8},{8,4},{12,0},{1,13},{5,9},{9,5},{13,1},{2,14},{6,10},... | collective-permute-start | bytes 884744 | tf_op jit(solution)/shard_map/ppermute | solution.py:632
  301.9 11.5 %collective-permute-start.50 = (bf16[128,1152]{1,0:T(8,128)(2,1)S(1)}, bf16[128,1152]{1,0:T(8,128)(2,1)}, u32[]{:S(2)}, u32[]{:S(2)}) collective-permute-start(bf16[128,1152]{1,0:T(8,128)(2,1)S(1)} %get-tuple-element.158.b0), channel_id=1, source_target_pairs={{0,12},{4,8},{8,4},{12,0},{1,13},{5,9},{9,5},{13,1},{2,14},{6,10},... | collective-permute-start | bytes 884744 | tf_op jit(solution)/shard_map/ppermute | solution.py:632
  309.0 131.2 %reduce-scatter.5.cloned.1.call-start = ((), (), s32[]{:S(2)}) async-start(), calls=%async_computation.4 | async-start | bytes 1843200 | tf_op jit(solution)/shard_map/reduce_scatter | solution.py:803
  344.6 14.6 %collective-permute-start.61 = (bf16[1152,576]{0,1:T(8,128)(2,1)}, bf16[1152,576]{0,1:T(8,128)(2,1)}, u32[]{:S(2)}, u32[]{:S(2)}) collective-permute-start(bf16[1152,576]{0,1:T(8,128)(2,1)} %copy.185), channel_id=1, source_target_pairs={{0,16},{16,0},{1,17},{17,1},{2,18},{18,2},{3,19},{19,3},{4,20},{20... | collective-permute-start | bytes 3981320 | tf_op jit(solution)/shard_map/ppermute | solution.py:632
  364.2 90.4 %reduce-scatter.11.cloned.1.call-start = ((), (), s32[]{:S(2)}) async-start(), calls=%async_computation.7 | async-start | bytes 3317760 | tf_op jit(solution)/shard_map/reduce_scatter | solution.py:792
  369.2 140.0 %reduce-scatter.9.cloned.1.call-start = ((), (), s32[]{:S(2)}) async-start(), calls=%async_computation.6 | async-start | bytes 3317760 | tf_op jit(solution)/shard_map/reduce_scatter | solution.py:792
  381.8 26.3 %collective-permute-start.69 = (bf16[1152,1152]{1,0:T(8,128)(2,1)}, bf16[1152,1152]{1,0:T(8,128)(2,1)}, u32[]{:S(2)}, u32[]{:S(2)}) collective-permute-start(bf16[1152,1152]{1,0:T(8,128)(2,1)} %get-tuple-element.195), channel_id=1, source_target_pairs={{0,16},{16,0},{1,17},{17,1},{2,18},{18,2},{3,19},{19,3},{4,20},{20... | collective-permute-start | bytes 7962632 | tf_op jit(solution)/shard_map/ppermute | solution.py:632
  395.4 11.6 %collective-permute-start.53 = (bf16[128,1152]{1,0:T(8,128)(2,1)}, bf16[128,1152]{1,0:T(8,128)(2,1)S(1)}, u32[]{:S(2)}, u32[]{:S(2)}) collective-permute-start(bf16[128,1152]{1,0:T(8,128)(2,1)} %copy-done.57), channel_id=1, source_target_pairs={{0,12},{4,8},{8,4},{12,0},{1,13},{5,9},{9,5},{13,1},{2,14},{6,10},... | collective-permute-start | bytes 884744 | tf_op jit(solution)/shard_map/ppermute | solution.py:632
  422.9 21.4 %collective-permute-start.75 = (f32[128,1152]{1,0:T(8,128)S(1)}, f32[128,1152]{1,0:T(8,128)S(1)}, u32[]{:S(2)}, u32[]{:S(2)}) collective-permute-start(f32[128,1152]{1,0:T(8,128)S(1)} %broadcast_select_fusion.8), channel_id=1, source_target_pairs={{0,16},{16,0},{1,17},{17,1},{2,18},{18,2},{3,19},{19,3},{4,20},{20... | collective-permute-start | bytes 1769480 | tf_op jit(solution)/shard_map/ppermute | solution.py:632
  (138 other events, 940.4 us)
Sparse Core Ops, SparseCore 0:
  309.1 37.4 reduce-scatter.6
  364.4 34.6 reduce-scatter.4
  401.3 53.3 reduce-scatter.10
  456.9 52.3 reduce-scatter.8

commit v2 on v1

v2 whole, which is shorter than its diff:
```python
import functools

import jax
import jax.numpy as jnp
from jax import lax
from jax.experimental import pallas as pl
from jax.experimental.pallas import tpu as pltpu
from jax.sharding import PartitionSpec as P
import numpy as np

HEAD = 72
HALF = HEAD // 2
LANE = 128
epsilon = 1e-06
BF = jnp.bfloat16
F32 = jnp.float32
HIGHEST = lax.Precision.HIGHEST
VM = pl.BlockSpec(memory_space=pltpu.VMEM)
SM = pl.BlockSpec(memory_space=pltpu.SMEM)
HB = pl.BlockSpec(memory_space=pltpu.HBM)


def nn(a, b):
    return lax.dot_general(a, b, (((1,), (0,)), ((), ())), preferred_element_type=F32)


def nt(a, b):
    return lax.dot_general(a, b, (((1,), (1,)), ((), ())), preferred_element_type=F32)


def tn(a, b):
    return lax.dot_general(a, b, (((0,), (0,)), ((), ())), preferred_element_type=F32)


def call(body, outs, in_specs, scratch=(), name=None, kept=0, limit=24, aliases={}):
    small = len(outs) - kept
    kernel = pl.pallas_call(
        body,
        out_shape=list(outs[:small]) + [pltpu.HBM(o.shape, o.dtype) for o in outs[small:]],
        in_specs=in_specs,
        out_specs=[VM] * small + [HB] * kept,
        scratch_shapes=list(scratch),
        input_output_aliases=aliases,
        compiler_params=pltpu.CompilerParams(vmem_limit_bytes=limit * 2**20),
        cost_estimate=pl.CostEstimate(flops=1000, bytes_accessed=1000, transcendentals=0),
        name=name,
    )

    def run(*args):
        placed = [
            pltpu.with_memory_space_constraint(arg, pltpu.HBM) if spec is HB else arg
            for arg, spec in zip(args, in_specs)
        ]
        return kernel(*placed)

    return run


def shape(dims, dtype):
    return jax.ShapeDtypeStruct(dims, dtype)


def fetch(is_own, own, other, where, sem):
    @pl.when(is_own)
    def _():
        pltpu.make_async_copy(own, where, sem).start()

    @pl.when(jnp.logical_not(is_own))
    def _():
        pltpu.make_async_copy(other, where, sem).start()


def arrived(own, where, sem):
    pltpu.make_async_copy(own, where, sem).wait()


def load(pairs, sems):
    made = [pltpu.make_async_copy(there, here, sems.at[i]) for i, (there, here) in enumerate(pairs)]
    for one in made:
        one.start()
    return made


def finish(copies):
    for one in copies:
        one.wait()


def inverse_rms(value):
    return lax.rsqrt(jnp.mean(value * value, axis=-1, keepdims=True) + epsilon)


def norm_back(grad, normed, inverse):
    return inverse * (grad - normed * jnp.mean(grad * normed, axis=-1, keepdims=True))


def token_mod(picks, mods_ref, part):
    width = mods_ref.shape[1] // 6
    return nn(picks, mods_ref[:, part * width : (part + 1) * width])


def image_sums(picks, value):
    return lax.dot_general(
        picks.astype(F32),
        value,
        (((0,), (0,)), ((), ())),
        precision=HIGHEST,
        preferred_element_type=F32,
    )


def swap_halves(value):
    return pltpu.roll(value, LANE // 2, 1)


def rotate(value, cosine, sine):
    return value * cosine + swap_halves(value) * sine


def unrotate(grad, cosine, sine):
    return grad * cosine - swap_halves(grad) * sine


def head_mean(value):
    return nn(value.astype(BF), jnp.full((LANE, LANE), 1.0, BF)) * (1.0 / HEAD)


def head_inverse(raw):
    return lax.rsqrt(head_mean(raw * raw) + epsilon)


def split_store(value, rows, block_refs):
    own = block_refs[0]
    share = own.shape[0]
    for k, ref in enumerate(block_refs):
        ref[:, rows] = value[k * share : (k + 1) * share].astype(ref.dtype)


def modulation_part(conditioning, modulator_t):
    micro, items = conditioning.shape[0], conditioning.shape[2]
    columns, width = modulator_t.shape
    step = 5 * LANE
    spans = [(j, min(step, columns - j)) for j in range(0, columns, step)]

    def body(cond_ref, mod_in, scaled_ref, part_ref, mod_ref, sems):
        copies = load([(mod_in.at[pl.ds(j, size)], mod_ref.at[pl.ds(j, size)]) for j, size in spans], sems)
        cond = jnp.concatenate([cond_ref[m, 0].astype(F32) for m in range(micro)], axis=0)
        scaled = (cond * jax.nn.sigmoid(cond)).astype(BF)
        scaled_ref[...] = scaled
        for copy, (j, size) in zip(copies, spans):
            copy.wait()
            part_ref[:, j : j + size] = nt(scaled, mod_ref[j : j + size]).astype(BF)

    return call(
        body,
        [shape((micro * items, width), BF), shape((micro * items, columns), BF)],
        [VM, HB],
        [pltpu.VMEM((columns, width), BF), pltpu.SemaphoreType.DMA((len(spans),))],
        name="modulation_part",
        limit=12,
    )(conditioning, modulator_t)


def modulation_rows(pieces, where):
    rows, columns = pieces[0].shape
    count = len(pieces)
    items = rows // 2

    def body(where_ref, *refs):
        piece_refs, (own_ref, send_ref) = refs[:count], refs[count:]
        section, tensor = where_ref[0], where_ref[1]
        values = [ref[...].astype(F32) for ref in piece_refs]
        ordered = []
        for j in range(count):
            picked = jnp.zeros_like(values[0])
            for k in range(count):
                picked = jnp.where((tensor ^ k) == j, values[k], picked)
            ordered.append(picked)
        whole = jnp.concatenate(ordered, axis=1)
        blank = jnp.zeros((8 - items, whole.shape[1]), F32)
        first = jnp.concatenate([whole[:items], blank], axis=0)
        second = jnp.concatenate([whole[items:], blank], axis=0)
        own_ref[...] = jnp.where(section == 0, first, second).astype(BF)
        send_ref[...] = jnp.where(section == 0, second, first).astype(BF)

    return call(
        body,
        [shape((8, count * columns), BF)] * 2,
        [SM] + [VM] * count,
        name="modulation_rows",
        limit=8,
    )(where, *pieces)


def prepare_tables(where, lengths, positions, rates, inputs, cotangent):
    micro, rows, width = inputs.shape
    share = rows // 4
    items = lengths.shape[2]

    def body(where_ref, len_ref, pos_ref, rate_ref, x_in, cot_in,
             cos_ref, sin_ref, segc_ref, segr_ref, picks_ref, x_out, cot_out, xown_out, cown_out, x_ref, cot_ref, sems):
        section, tensor = where_ref[0], where_ref[1]
        pairs = []
        for k in range(4):
            there = pl.ds(pl.multiple_of((tensor ^ k) * share, LANE), share)
            pairs.append((x_in.at[section, there], x_ref.at[pl.ds(k * share, share)]))
            pairs.append((cot_in.at[section, there], cot_ref.at[pl.ds(k * share, share)]))
        copies = load(pairs, sems)

        def segments(index):
            place = (tensor ^ (index // share)) * share + index % share
            segment = jnp.zeros_like(index)
            end = 0
            for i in range(items):
                end = end + len_ref[section, 0, i]
                segment += (place >= end).astype(jnp.int32)
            return segment

        column = segments(lax.broadcasted_iota(jnp.int32, (rows, 1), 0))
        segc_ref[...] = column
        segr_ref[...] = segments(lax.broadcasted_iota(jnp.int32, (1, rows), 1))
        picks_ref[...] = jnp.where(column == lax.broadcasted_iota(jnp.int32, (rows, 8), 1), 1.0, 0.0).astype(BF)
        finish(copies)
        own = pl.ds(0, share)
        pairs = [(x_ref, x_out), (cot_ref, cot_out), (x_ref.at[own], xown_out), (cot_ref.at[own], cown_out)]
        copies = load(pairs, sems)
        blocks = [
            pos_ref[section, :, pl.ds(pl.multiple_of((tensor ^ k) * share, LANE), share)] for k in range(4)
        ]
        place = jnp.concatenate(blocks, axis=1).astype(F32)
        lane = lax.broadcasted_iota(jnp.int32, (LANE // 2, rows), 0)
        phase = jnp.where(lane < HEAD // 4, place[0:1], place[1:2]) * rate_ref[...]
        cosine = jnp.where(lane < HALF, jnp.cos(phase), 0.0)
        sine = jnp.where(lane < HALF, jnp.sin(phase), 0.0)
        cos_ref[...] = jnp.concatenate([cosine, cosine], axis=0).T
        sin_ref[...] = jnp.concatenate([-sine, sine], axis=0).T
        finish(copies)

    own = shape((share, width), BF)
    return call(
        body,
        [
            shape((rows, LANE), F32),
            shape((rows, LANE), F32),
            shape((rows, 1), jnp.int32),
            shape((1, rows), jnp.int32),
            shape((rows, 8), BF),
            shape((rows, width), BF),
            shape((rows, width), BF),
            own,
            own,
        ],
        [SM, SM, VM, VM, HB, HB],
        [pltpu.VMEM((rows, width), BF), pltpu.VMEM((rows, width), BF), pltpu.SemaphoreType.DMA((8,))],
        name="prepare_tables",
        limit=16,
        kept=4,
    )(where, lengths, positions, rates, inputs, cotangent)


def prepare_weights(where, own, got, place, place_one, begun=None):
    wq_own, wo_own, gains_own = own
    wq_got, wo_got, gains_got = got
    narrow, width = wq_own.shape[1:]
    padded = place.shape[1]
    again = begun is not None

    def body(where_ref, *refs):
        refs = list(refs)
        sources = []
        if not again:
            wqa, woa, ga = refs.pop(0), refs.pop(0), refs.pop(0)
            sources.append((wqa, woa))
        wqb, wob, gb = refs.pop(0), refs.pop(0), refs.pop(0)
        place_ref, one_ref = refs.pop(0), refs.pop(0)
        if again:
            refs = refs[2:]
        else:
            gains_ref = refs.pop(0)
        wq_out, wo_out, wq_ref, wo_ref, wide_ref, tall_ref, sems, out_sems = refs
        section = where_ref[0]
        if not again:
            a, b = ga[...], gb[...]
            first = jnp.where(section == 0, a, b)
            second = jnp.where(section == 0, b, a)
            both = jnp.concatenate([first, second, jnp.zeros((4, first.shape[1]), F32)], axis=0)
            gains_ref[...] = lax.dot_general(
                both, one_ref[...], (((1,), (0,)), ((), ())), precision=HIGHEST, preferred_element_type=F32
            )

        def make(wq, wo, layer):
            copies = load([(wq.at[i], wq_ref.at[i]) for i in range(3)] + [(wo, wo_ref)], sems)
            outs = []
            for i in range(3):
                copies[i].wait()
                wide_ref[i] = tn(wq_ref[i], place_ref[...]).astype(BF)
                outs.append(pltpu.make_async_copy(wide_ref.at[i], wq_out.at[layer, i], out_sems.at[i]))
                outs[-1].start()
            copies[3].wait()
            tall_ref[...] = tn(place_ref[...], wo_ref[...]).astype(BF)
            outs.append(pltpu.make_async_copy(tall_ref, wo_out.at[layer], out_sems.at[3]))
            outs[-1].start()
            finish(outs)

        if not again:
            make(wqa, woa, section)

            @pl.when(section == 1)
            def _():
                make(wqb, wob, 0)
        else:

            @pl.when(section == 0)
            def _():
                make(wqb, wob, 1)

    outs = [shape((2, 3, width, padded), BF), shape((2, padded, width), BF)]
    args = [where] + ([] if again else list(own)) + list(got) + [place, place_one] + (list(begun) if again else [])
    return call(
        body,
        ([] if again else [shape((8, LANE), F32)]) + outs,
        [SM] + ([HB] * 2 + [VM]) * (1 if again else 2) + [VM] * 2 + ([HB] * 2 if again else []),
        [
            pltpu.VMEM((3, narrow, width), BF),
            pltpu.VMEM((narrow, width), BF),
            pltpu.VMEM((3, width, padded), BF),
            pltpu.VMEM((padded, width), BF),
            pltpu.SemaphoreType.DMA((4,)),
            pltpu.SemaphoreType.DMA((4,)),
        ],
        name="prepare_weights",
        limit=24,
        kept=2,
        aliases={6: 0, 7: 1} if again else {},
    )(*args)


def attention_forward(layer, blocks, weights, tables, mods, picks):
    wq, wo = weights
    cosine, sine, gains, seg_col, seg_row = tables
    padded, width = wo.shape[1:]
    heads = padded // LANE
    raw_input = len(blocks) == 1
    rows = sum(b.shape[0] for b in blocks)
    share = rows // 4
    scale = HEAD**-0.5
    QB = 512

    def body(*refs):
        refs = list(refs)
        in_refs = [refs.pop(0) for _ in blocks]
        wq_in, wo_in, cos_ref, sin_ref, gain_ref, segc_ref, segr_ref, mods_ref, picks_ref = refs[:9]
        refs = refs[9:]
        p_refs = refs[:4]
        kept = refs[4:11]
        wq_ref, wo_ref, mask_ref = refs[11:14]
        here = refs[14:21]
        sems, out_sems = refs[21:]
        qraw_ref, kraw_ref, qrot_ref, krot_ref, v_ref, mixed_ref, a_ref = here
        weights_in = [(wq_in.at[layer, i], wq_ref.at[i]) for i in range(3)] + [(wo_in.at[layer], wo_ref)]
        weights_in = load(weights_in, sems)

        def keep(i):
            pltpu.make_async_copy(here[i], kept[i], out_sems.at[i]).start()

        for k, ref in enumerate(in_refs):
            if raw_input:
                x = ref[...].astype(F32)
                picked = picks_ref[...]
                shift1 = token_mod(picked, mods_ref, 0)
                scale1 = token_mod(picked, mods_ref, 1)
                a_ref[...] = (x * inverse_rms(x) * (1.0 + scale1) + shift1).astype(BF)
            else:
                a_ref[k * share : (k + 1) * share] = ref[...]
        keep(6)
        mask_ref[...] = jnp.where(segc_ref[...] == segr_ref[...], 1.0, 0.0).astype(BF)
        cos = cos_ref[...]
        sin = sin_ref[...]
        for i, (raw_out, rot_out) in enumerate(((qraw_ref, qrot_ref), (kraw_ref, krot_ref))):
            weights_in[i].wait()
            gain = gain_ref[2 * layer + i : 2 * layer + i + 1]
            for h2 in range(0, heads, 2):
                both = nn(a_ref[...], wq_ref[i, :, h2 * LANE : (h2 + 2) * LANE])
                for h in (h2, h2 + 1):
                    at = slice(h * LANE, (h + 1) * LANE)
                    raw = both[:, (h - h2) * LANE : (h - h2 + 1) * LANE]
                    raw_out[:, at] = raw.astype(BF)
                    turned = rotate(raw * head_inverse(raw) * gain, cos, sin)
                    rot_out[:, at] = turned.astype(BF)
            keep(i)
            keep(2 + i)
        weights_in[2].wait()
        one = jnp.where(lax.broadcasted_iota(jnp.int32, (1, padded), 1) % LANE == LANE - 1, 1.0, 0.0)
        v_ref[...] = (nn(a_ref[...], wq_ref[2]) + one).astype(BF)
        keep(4)

        for j in range(rows // QB):
            at_rows = slice(j * QB, (j + 1) * QB)
            for h in range(heads):
                at = slice(h * LANE, (h + 1) * LANE)
                scores = nt(qrot_ref[at_rows, at], krot_ref[:, at]) * scale
                grown = jnp.exp(scores).astype(BF) * mask_ref[at_rows]
                mixed = nn(grown, v_ref[:, at])
                mixed_ref[at_rows, at] = (mixed * (1.0 / mixed[:, LANE - 1 :])).astype(BF)
        keep(5)
        weights_in[3].wait()
        step = 3 * LANE
        for j in range(width // step):
            at = slice(j * step, (j + 1) * step)
            split_store(nn(mixed_ref[...], wo_ref[:, at]), at, p_refs)
        for i in range(7):
            pltpu.make_async_copy(here[i], kept[i], out_sems.at[i]).wait()

    outs = [shape((share, width), BF)] * 4
    saved_shapes = [shape((rows, padded), BF)] * 6 + [shape((rows, width), BF)]
    result = call(
        body,
        outs + saved_shapes,
        [VM] * len(blocks) + [HB] * 2 + [VM] * 7,
        [
            pltpu.VMEM((3, width, padded), BF),
            pltpu.VMEM((padded, width), BF),
            pltpu.VMEM((rows, rows), BF),
        ] + [pltpu.VMEM(s.shape, BF) for s in saved_shapes] + [
            pltpu.SemaphoreType.DMA((4,)),
            pltpu.SemaphoreType.DMA((7,)),
        ],
        name=f"attention_forward_{layer}",
        limit=28,
        kept=7,
    )(*blocks, wq, wo, cosine, sine, gains, seg_col, seg_row, mods, picks)
    return list(result[:4]), list(result[4:])


def add_parts(refs):
    total = refs[0][...].astype(F32)
    for ref in refs[1:]:
        total += ref[...].astype(F32)
    return total


def after_attention(parts, state, mods, picks):
    dims = state.shape

    def body(p0_in, p1, p2, p3, state_in, mods_ref, picks_ref, mlp_ref, attended_out, after_out,
             p0, state_ref, attended_ref, after_ref, sems, out_sems):
        copies = load([(p0_in, p0), (state_in, state_ref)], sems)
        picked = picks_ref[...]
        finish(copies)
        attended = add_parts((p0, p1, p2, p3))
        attended_ref[...] = attended.astype(BF)
        after = state_ref[...].astype(F32) + token_mod(picked, mods_ref, 2) * attended
        after_ref[...] = after
        kept = load([(attended_ref, attended_out), (after_ref, after_out)], out_sems)
        normed = after * inverse_rms(after)
        mlp_ref[...] = (normed * (1.0 + token_mod(picked, mods_ref, 4)) + token_mod(picked, mods_ref, 3)).astype(BF)
        finish(kept)

    return call(
        body,
        [shape(dims, BF), shape(dims, BF), shape(dims, F32)],
        [HB] + [VM] * 3 + [HB] + [VM] * 2,
        [pltpu.VMEM(dims, BF)] * 3
        + [pltpu.VMEM(dims, F32), pltpu.SemaphoreType.DMA((2,)), pltpu.SemaphoreType.DMA((2,))],
        name="after_attention",
        limit=8,
        kept=2,
    )(*parts, state, mods, picks)


def after_mlp(parts, after, mods, picks, mods_next):
    last = mods_next is None
    dims = after.shape

    def body(p0_in, p1, p2, p3, after_in, mods_ref, picks_ref, *refs):
        refs = list(refs)
        next_ref = None if last else refs.pop(0)
        in_ref = None if last else refs.pop(0)
        projected_out, result_out, p0, after_ref, projected_ref, result_ref, sems, out_sems = refs
        copies = load([(p0_in, p0), (after_in, after_ref)], sems)
        picked = picks_ref[...]
        finish(copies)
        projected = add_parts((p0, p1, p2, p3))
        projected_ref[...] = projected.astype(BF)
        output = after_ref[...] + token_mod(picked, mods_ref, 5) * projected
        result_ref[...] = output.astype(result_ref.dtype)
        kept = load([(projected_ref, projected_out), (result_ref, result_out)], out_sems)
        if not last:
            state = output.astype(BF).astype(F32)
            normed = state * inverse_rms(state)
            in_ref[...] = (normed * (1.0 + token_mod(picked, next_ref, 1)) + token_mod(picked, next_ref, 0)).astype(BF)
        finish(kept)

    result_type = F32 if last else BF
    outs = ([] if last else [shape(dims, BF)]) + [shape(dims, BF), shape(dims, result_type)]
    extra = () if last else (mods_next,)
    return call(
        body,
        outs,
        [HB] + [VM] * 3 + [HB] + [VM] * (2 + len(extra)),
        [
            pltpu.VMEM(dims, BF),
            pltpu.VMEM(dims, F32),
            pltpu.VMEM(dims, BF),
            pltpu.VMEM(dims, result_type),
            pltpu.SemaphoreType.DMA((2,)),
            pltpu.SemaphoreType.DMA((2,)),
        ],
        name="after_mlp",
        limit=8,
        kept=2,
    )(*parts, after, mods, picks, *extra)


def mlp_forward(layer, blocks, weights, section):
    gu_own, gu_got, wd_own, wd_got = weights
    hidden_size, width = wd_own.shape
    share = blocks[0].shape[0]
    rows = share * 4
    chunk = 2 * LANE

    def body(sec_ref, b0, b1, b2, b3, gu_a, gu_b, wd_a, wd_b, p0, p1, p2, p3, hid_out, c1_out, c2_out, a_out,
             a_ref, gu_ref, wd_ref, hid_ref, c1_ref, c2_ref, sems, out_sems):
        own = sec_ref[0] == layer
        fetch(own, gu_a.at[0], gu_b.at[0], gu_ref.at[0], sems.at[0])
        fetch(own, gu_a.at[1], gu_b.at[1], gu_ref.at[1], sems.at[1])
        fetch(own, wd_a, wd_b, wd_ref, sems.at[2])
        for k, ref in enumerate((b0, b1, b2, b3)):
            a_ref[k * share : (k + 1) * share] = ref[...]
        arrived(gu_a.at[0], gu_ref.at[0], sems.at[0])
        arrived(gu_a.at[1], gu_ref.at[1], sems.at[1])
        for j in range(hidden_size // chunk):
            at = slice(j * chunk, (j + 1) * chunk)
            gate = nn(a_ref[...], gu_ref[0, :, at])
            up = nn(a_ref[...], gu_ref[1, :, at])
            sigma = jax.nn.sigmoid(gate)
            silu = gate * sigma
            hid_ref[:, at] = (silu * up).astype(BF)
            c1_ref[:, at] = (up * (sigma + silu * (1.0 - sigma))).astype(BF)
            c2_ref[:, at] = silu.astype(BF)
        kept = load([(hid_ref, hid_out), (c1_ref, c1_out), (c2_ref, c2_out), (a_ref, a_out)], out_sems)
        arrived(wd_a, wd_ref, sems.at[2])
        step = 3 * LANE
        for j in range(width // step):
            at = slice(j * step, (j + 1) * step)
            split_store(nn(hid_ref[...], wd_ref[:, at]), at, (p0, p1, p2, p3))
        finish(kept)

    outs = [shape((share, width), BF)] * 4 + [shape((rows, hidden_size), BF)] * 3 + [shape((rows, width), BF)]
    result = call(
        body,
        outs,
        [SM] + [VM] * 4 + [HB] * 4,
        [
            pltpu.VMEM((rows, width), BF),
            pltpu.VMEM(gu_own.shape, BF),
            pltpu.VMEM(wd_own.shape, BF),
        ]
        + [pltpu.VMEM((rows, hidden_size), BF)] * 3
        + [pltpu.SemaphoreType.DMA((3,)), pltpu.SemaphoreType.DMA((4,))],
        name=f"mlp_forward_{layer}",
        kept=4,
    )(section, *blocks, gu_own, gu_got, wd_own, wd_got)
    return result[:4], result[4:]


def mlp_backward(layer, blocks, weights, saved, mods, picks, section):
    gu_own, gu_got, wd_own, wd_got = weights
    c1, c2 = saved
    hidden_size, width = wd_own.shape
    rows = c1.shape[0]
    share = rows // 4
    raw_input = len(blocks) == 1
    chunk = 2 * LANE

    def body(sec_ref, *refs):
        refs = list(refs)
        in_refs = [refs.pop(0) for _ in blocks]
        gu_a, gu_b, wd_a, wd_b, c1_in, c2_in, mods_ref, picks_ref = refs[:8]
        p_refs = refs[8:12]
        outs = refs[12:15]
        gu_ref, wd_ref, c1_ref, c2_ref, gg_ref, gup_ref, gp_ref, sems, out_sems = refs[15:]
        own = sec_ref[0] == layer
        fetch(own, wd_a, wd_b, wd_ref, sems.at[2])
        pltpu.make_async_copy(c1_in, c1_ref, sems.at[3]).start()
        pltpu.make_async_copy(c2_in, c2_ref, sems.at[4]).start()
        fetch(own, gu_a.at[0], gu_b.at[0], gu_ref.at[0], sems.at[0])
        fetch(own, gu_a.at[1], gu_b.at[1], gu_ref.at[1], sems.at[1])
        for k, ref in enumerate(in_refs):
            if raw_input:
                gp_ref[...] = (ref[...].astype(F32) * token_mod(picks_ref[...], mods_ref, 5)).astype(BF)
            else:
                gp_ref[k * share : (k + 1) * share] = ref[...]
        pltpu.make_async_copy(gp_ref, outs[2], out_sems.at[2]).start()
        arrived(wd_a, wd_ref, sems.at[2])
        pltpu.make_async_copy(c1_in, c1_ref, sems.at[3]).wait()
        pltpu.make_async_copy(c2_in, c2_ref, sems.at[4]).wait()
        for j in range(hidden_size // chunk):
            at = slice(j * chunk, (j + 1) * chunk)
            grad_hidden = nt(gp_ref[...], wd_ref[at])
            gg_ref[:, at] = (grad_hidden * c1_ref[:, at].astype(F32)).astype(BF)
            gup_ref[:, at] = (grad_hidden * c2_ref[:, at].astype(F32)).astype(BF)
        pltpu.make_async_copy(gg_ref, outs[0], out_sems.at[0]).start()
        pltpu.make_async_copy(gup_ref, outs[1], out_sems.at[1]).start()
        arrived(gu_a.at[0], gu_ref.at[0], sems.at[0])
        arrived(gu_a.at[1], gu_ref.at[1], sems.at[1])
        step = 3 * LANE
        for j in range(width // step):
            at = slice(j * step, (j + 1) * step)
            split_store(nt(gg_ref[...], gu_ref[0, at]) + nt(gup_ref[...], gu_ref[1, at]), at, p_refs)
        for i, here in enumerate((gg_ref, gup_ref, gp_ref)):
            pltpu.make_async_copy(here, outs[i], out_sems.at[i]).wait()

    outs = [shape((share, width), BF)] * 4 + [shape((rows, hidden_size), BF)] * 2
    outs += [shape((rows, width), BF)]
    result = call(
        body,
        outs,
        [SM] + [VM] * len(blocks) + [HB] * 6 + [VM] * 2,
        [
            pltpu.VMEM(gu_own.shape, BF),
            pltpu.VMEM(wd_own.shape, BF),
        ]
        + [pltpu.VMEM((rows, hidden_size), BF)] * 4
        + [
            pltpu.VMEM((rows, width), BF),
            pltpu.SemaphoreType.DMA((5,)),
            pltpu.SemaphoreType.DMA((3,)),
        ],
        name=f"mlp_backward_{layer}",
        kept=3,
    )(section, *blocks, gu_own, gu_got, wd_own, wd_got, c1, c2, mods, picks)
    return result[:4], result[4:]


def mlp_weight_grads(mlp_in, grads, hidden):
    grad_gate, grad_up, grad_projected = grads
    rows, width = grad_projected.shape
    size = hidden.shape[1]
    step = 3 * LANE

    def body(a_in, gg_in, gu_in, gp_in, hid_in, out, a_ref, gg_ref, gu_ref, gp_ref, hid_ref, full_ref, in_sems, sems):
        ins = load([(a_in, a_ref), (gg_in, gg_ref), (gu_in, gu_ref), (gp_in, gp_ref), (hid_in, hid_ref)], in_sems)
        finish(ins)
        kept = []
        for j in range(width // step):
            at = slice(j * step, (j + 1) * step)
            left = a_ref[:, at]
            full_ref[at, :size] = tn(left, gg_ref[...]).astype(BF)
            full_ref[at, size : 2 * size] = tn(left, gu_ref[...]).astype(BF)
            full_ref[at, 2 * size :] = tn(gp_ref[:, at], hid_ref[...]).astype(BF)
            here = pl.ds(j * step, step)
            kept.append(pltpu.make_async_copy(full_ref.at[here], out.at[here], sems.at[j]))
            kept[-1].start()
        finish(kept)

    (result,) = call(
        body,
        [shape((width, 3 * size), BF)],
        [HB] * 5,
        [pltpu.VMEM((rows, width), BF)]
        + [pltpu.VMEM((rows, size), BF)] * 2
        + [
            pltpu.VMEM((rows, width), BF),
            pltpu.VMEM((rows, size), BF),
            pltpu.VMEM((width, 3 * size), BF),
            pltpu.SemaphoreType.DMA((5,)),
            pltpu.SemaphoreType.DMA((width // step,)),
        ],
        name="mlp_weight_grads",
        kept=1,
    )(mlp_in, grad_gate, grad_up, grad_projected, hidden)
    return result


def attention_backward(layer, blocks, weights, saved, tables):
    wq, wo = weights
    cosine, sine, gains, seg_col, seg_row = tables
    rows, padded = saved[0].shape
    width = wo.shape[2]
    heads = padded // LANE
    share = rows // 4
    scale = HEAD**-0.5
    QB = 512

    def body(b0, b1, b2, b3, wq_in, wo_in, qraw_in, kraw_in, qrot_in, krot_in, v_in,
             cos_ref, sin_ref, gain_ref, segc_ref, segr_ref,
             p0, p1, p2, p3, ggain_ref, g_out, ga_out,
             wq_ref, wo_ref, qraw_ref, kraw_ref, qrot_ref, krot_ref, v_ref, mask_ref,
             ga_ref, gmix_ref, gq_ref, gk_ref, g_ref, sems, in_sems):
        ins = [(wo_in.at[layer], wo_ref)]
        ins += [(qrot_in, qrot_ref), (krot_in, krot_ref), (v_in, v_ref), (qraw_in, qraw_ref), (kraw_in, kraw_ref)]
        ins += [(wq_in.at[layer, i], wq_ref.at[i]) for i in range(3)]
        ins = load(ins, in_sems)
        for k, ref in enumerate((b0, b1, b2, b3)):
            ga_ref[k * share : (k + 1) * share] = ref[...]
        kept = [pltpu.make_async_copy(ga_ref, ga_out, sems.at[0]), pltpu.make_async_copy(g_ref, g_out, sems.at[1])]
        kept[0].start()
        mask_ref[...] = jnp.where(segc_ref[...] == segr_ref[...], 1.0, 0.0).astype(BF)
        ins[0].wait()
        gmix_ref[...] = nt(ga_ref[...], wo_ref[...]).astype(BF)
        finish(ins[1:4])
        for h in range(heads):
            at = slice(h * LANE, (h + 1) * LANE)
            for j in range(rows // QB):
                at_rows = slice(j * QB, (j + 1) * QB)
                query = qrot_ref[at_rows, at]
                grad_mixed = gmix_ref[at_rows, at]
                scores = nt(krot_ref[:, at], query) * scale
                grown = (jnp.exp(scores).astype(BF) * mask_ref[:, at_rows]).astype(F32)
                weights_t = grown * (1.0 / jnp.sum(grown, axis=0, keepdims=True))
                grad_weights = nt(v_ref[:, at], grad_mixed)
                add_v = nn(weights_t.astype(BF), grad_mixed)
                product = weights_t * grad_weights
                delta = jnp.sum(product, axis=0, keepdims=True)
                grad_scores = (product - weights_t * delta).astype(BF)
                gq_ref[at_rows, at] = tn(grad_scores, krot_ref[:, at])
                add_k = nn(grad_scores, query)
                total_v = add_v if j == 0 else total_v + add_v
                total_k = add_k if j == 0 else total_k + add_k
            gk_ref[:, at] = total_k
            g_ref[:, 2 * padded + h * LANE : 2 * padded + (h + 1) * LANE] = total_v.astype(BF)
        cos = cos_ref[...]
        sin = sin_ref[...]
        finish(ins[4:6])
        ggain_ref[...] = jnp.zeros_like(ggain_ref)
        for i, (raw_ref, grad_ref) in enumerate(((qraw_ref, gq_ref), (kraw_ref, gk_ref))):
            gain = gain_ref[2 * layer + i : 2 * layer + i + 1]
            gain_sum = jnp.zeros((1, LANE), F32)
            for h in range(heads):
                at = slice(h * LANE, (h + 1) * LANE)
                raw = raw_ref[:, at].astype(F32)
                inverse = head_inverse(raw)
                normed = raw * inverse
                turned = unrotate(grad_ref[:, at], cos, sin) * scale
                product = turned * normed
                gain_sum += jnp.sum(product, axis=0, keepdims=True)
                back = inverse * (turned * gain - normed * head_mean(product * gain))
                g_ref[:, i * padded + h * LANE : i * padded + (h + 1) * LANE] = back.astype(BF)
            ggain_ref[i : i + 1] = gain_sum
        kept[1].start()
        finish(ins[6:])
        step = 3 * LANE
        for j in range(width // step):
            at = slice(j * step, (j + 1) * step)
            total = nt(g_ref[:, :padded], wq_ref[0, at])
            total += nt(g_ref[:, padded : 2 * padded], wq_ref[1, at])
            total += nt(g_ref[:, 2 * padded :], wq_ref[2, at])
            split_store(total, at, (p0, p1, p2, p3))
        finish(kept)

    outs = [shape((share, width), BF)] * 4
    outs += [shape((8, LANE), F32), shape((rows, 3 * padded), BF), shape((rows, width), BF)]
    result = call(
        body,
        outs,
        [VM] * 4 + [HB] * 7 + [VM] * 5,
        [
            pltpu.VMEM((3, width, padded), BF),
            pltpu.VMEM((padded, width), BF),
        ]
        + [pltpu.VMEM((rows, padded), BF)] * 5
        + [
            pltpu.VMEM((rows, rows), BF),
            pltpu.VMEM((rows, width), BF),
            pltpu.VMEM((rows, padded), BF),
            pltpu.VMEM((rows, padded), F32),
            pltpu.VMEM((rows, padded), F32),
            pltpu.VMEM((rows, 3 * padded), BF),
            pltpu.SemaphoreType.DMA((2,)),
            pltpu.SemaphoreType.DMA((9,)),
        ],
        name=f"attention_backward_{layer}",
        limit=32,
        kept=2,
    )(*blocks, wq, wo, *saved[:5], cosine, sine, gains, seg_col, seg_row)
    return result[:4], result[4:]


def attention_weight_grads(attention_in, grads, mixed, grad_attended, place):
    rows, width = attention_in.shape
    padded, narrow = place.shape
    step = 3 * LANE

    def body(a_in, g_in, mixed_in, ga_in, place_ref, out, a_ref, g_ref, mixed_ref, ga_ref, right_ref, full_ref, in_sems, sems):
        ins = load([(g_in, g_ref), (mixed_in, mixed_ref), (a_in, a_ref), (ga_in, ga_ref)], in_sems)
        finish(ins[:2])
        for i in range(3):
            right_ref[i] = nn(g_ref[:, i * padded : (i + 1) * padded], place_ref[...]).astype(BF)
        right_ref[3] = nn(mixed_ref[...], place_ref[...]).astype(BF)
        finish(ins[2:])
        kept = []
        for j in range(width // step):
            at = slice(j * step, (j + 1) * step)
            left = a_ref[:, at]
            for i in range(3):
                full_ref[at, i * narrow : (i + 1) * narrow] = tn(left, right_ref[i]).astype(BF)
            full_ref[at, 3 * narrow :] = tn(ga_ref[:, at], right_ref[3]).astype(BF)
            here = pl.ds(j * step, step)
            kept.append(pltpu.make_async_copy(full_ref.at[here], out.at[here], sems.at[j]))
            kept[-1].start()
        finish(kept)

    (result,) = call(
        body,
        [shape((width, 4 * narrow), BF)],
        [HB] * 4 + [VM],
        [
            pltpu.VMEM((rows, width), BF),
            pltpu.VMEM((rows, 3 * padded), BF),
            pltpu.VMEM((rows, padded), BF),
            pltpu.VMEM((rows, width), BF),
            pltpu.VMEM((4, rows, narrow), BF),
            pltpu.VMEM((width, 4 * narrow), BF),
            pltpu.SemaphoreType.DMA((4,)),
            pltpu.SemaphoreType.DMA((width // step,)),
        ],
        name="attention_weight_grads",
        kept=1,
    )(attention_in, grads, mixed, grad_attended, place)
    return result


def back_of_mlp(parts, grad_out, after, attended, projected, mods, picks):
    dims = after.shape

    def body(p0_in, p1, p2, p3, g_in, after_in, attended_in, projected_in, mods_ref, picks_ref, ga_ref, sums_ref, grad_out_ref,
             p0, g_ref, after_ref, attended_ref, projected_ref, grad_ref, sems, out_sems):
        ins = [(p0_in, p0), (after_in, after_ref), (g_in, g_ref), (attended_in, attended_ref), (projected_in, projected_ref)]
        ins = load(ins, sems)
        picked = picks_ref[...]
        ins[0].wait()
        grad_in = add_parts((p0, p1, p2, p3))
        ins[1].wait()
        after = after_ref[...]
        inverse = inverse_rms(after)
        normed = after * inverse
        ins[2].wait()
        g = g_ref[...].astype(F32)
        grad_after = g + norm_back(grad_in * (1.0 + token_mod(picked, mods_ref, 4)), normed, inverse)
        grad_ref[...] = grad_after
        kept = load([(grad_ref, grad_out_ref)], out_sems)
        ga_ref[...] = (grad_after * token_mod(picked, mods_ref, 2)).astype(BF)
        finish(ins[3:])
        sums_ref[0] = image_sums(picked, grad_after * attended_ref[...].astype(F32))
        sums_ref[1] = image_sums(picked, grad_in)
        sums_ref[2] = image_sums(picked, grad_in * normed)
        sums_ref[3] = image_sums(picked, g * projected_ref[...].astype(F32))
        finish(kept)

    return call(
        body,
        [shape(dims, BF), shape((4, picks.shape[1], dims[1]), F32), shape(dims, F32)],
        [HB] + [VM] * 3 + [HB] * 4 + [VM] * 2,
        [
            pltpu.VMEM(dims, BF),
            pltpu.VMEM(dims, BF),
            pltpu.VMEM(dims, F32),
            pltpu.VMEM(dims, BF),
            pltpu.VMEM(dims, BF),
            pltpu.VMEM(dims, F32),
            pltpu.SemaphoreType.DMA((5,)),
            pltpu.SemaphoreType.DMA((1,)),
        ],
        name="back_of_mlp",
        limit=12,
        kept=1,
    )(*parts, grad_out, after, attended, projected, mods, picks)


def back_of_attention(parts, grad_after, state, mods, picks, mods_below):
    first = mods_below is None
    dims = grad_after.shape

    def body(p0_in, p1, p2, p3, grad_in_ref, state_in, mods_ref, picks_ref, *refs):
        refs = list(refs)
        below_ref = None if first else refs.pop(0)
        sums_ref = refs.pop(0)
        gp_ref = None if first else refs.pop(0)
        result_out, p0, grad_ref, state_ref, result_ref, sems, out_sems = refs
        ins = load([(p0_in, p0), (state_in, state_ref), (grad_in_ref, grad_ref)], sems)
        picked = picks_ref[...]
        ins[0].wait()
        grad_in = add_parts((p0, p1, p2, p3))
        ins[1].wait()
        state = state_ref[...].astype(F32)
        inverse = inverse_rms(state)
        normed = state * inverse
        ins[2].wait()
        grad_state = grad_ref[...] + norm_back(grad_in * (1.0 + token_mod(picked, mods_ref, 1)), normed, inverse)
        result_ref[...] = grad_state.astype(result_ref.dtype)
        kept = load([(result_ref, result_out)], out_sems)
        if not first:
            gp_ref[...] = (grad_state.astype(BF).astype(F32) * token_mod(picked, below_ref, 5)).astype(BF)
        sums_ref[0] = image_sums(picked, grad_in)
        sums_ref[1] = image_sums(picked, grad_in * normed)
        finish(kept)

    result_type = F32 if first else BF
    outs = [shape((2, picks.shape[1], dims[1]), F32)] + ([] if first else [shape(dims, BF)]) + [shape(dims, result_type)]
    extra = () if first else (mods_below,)
    return call(
        body,
        outs,
        [HB] + [VM] * 3 + [HB] * 2 + [VM] * (2 + len(extra)),
        [
            pltpu.VMEM(dims, BF),
            pltpu.VMEM(dims, F32),
            pltpu.VMEM(dims, BF),
            pltpu.VMEM(dims, result_type),
            pltpu.SemaphoreType.DMA((3,)),
            pltpu.SemaphoreType.DMA((1,)),
        ],
        name="back_of_attention",
        limit=12,
        kept=1,
    )(*parts, grad_after, state, mods, picks, *extra)


def exchange(value, axis, k):
    return lax.ppermute(value, axis, [(i, i ^ k) for i in range(lax.axis_size(axis))])


def send_parts(parts):
    got = {k: exchange(parts[k], "tensor", k) for k in (3, 1, 2)}
    return [parts[0], got[1], got[2], got[3]]


def gather_blocks(own):
    got = {k: exchange(own, "tensor", k) for k in (3, 1, 2)}
    return [own, got[1], got[2], got[3]]


def group_sum(value, axis):
    k = 1
    while k < lax.axis_size(axis):
        value = value + exchange(value, axis, k)
        k *= 2
    return value


def gather_dp(value):
    count = lax.axis_size("dp")
    if count > 4:
        return lax.all_gather(value, "dp", axis=0)
    me = lax.axis_index("dp")
    got = [value] + [exchange(value, "dp", k) for k in range(1, count)]
    stacked = jnp.stack(got)
    return jnp.stack([lax.dynamic_index_in_dim(stacked, me ^ j, 0, keepdims=False) for j in range(count)])


def head_places(heads):
    place = np.zeros((heads * HEAD, heads * LANE), np.float32)
    for h in range(heads):
        for j in range(HEAD):
            place[h * HEAD + j, h * LANE + (j // HALF) * (LANE // 2) + j % HALF] = 1.0
    return place


def shards(
    inputs,
    cotangent,
    conditioning,
    lengths,
    positions,
    modulator,
    projections,
    norm_gains,
    out_weight,
    gate_up,
    down_weight,
):
    section = lax.axis_index("section")
    other = 1 - section
    tensor = lax.axis_index("tensor")
    data = lax.axis_index("dp")
    micro, _, width = inputs.shape
    rows = inputs.shape[1]
    group = lax.axis_size("tensor")
    share = rows // group
    items = lengths.shape[2]
    narrow = projections.shape[3]
    heads = narrow // HEAD
    columns = modulator.shape[2]
    sec = section.reshape(1).astype(jnp.int32)

    where = jnp.stack([section, tensor]).astype(jnp.int32)
    is_first = section == 0

    own = (jnp.swapaxes(projections[0], 1, 2), out_weight[0], norm_gains[0])
    got = tuple(exchange(value, "section", 1) for value in own)
    scaled, part = modulation_part(conditioning, jnp.swapaxes(modulator[0], 0, 1))
    pieces = gather_blocks(part)
    quarter = HEAD // 4
    rates = 10000.0 ** (-jnp.arange(quarter).astype(F32) / quarter)
    rates = jnp.concatenate([rates, rates, jnp.zeros(LANE // 2 - HALF, F32)])[:, None]
    where_late, part = lax.optimization_barrier((where, part))
    cosine, sine, seg_col, seg_row, picks, x, cotangent_now, x_own, cotangent_own = prepare_tables(
        where_late, lengths, positions, rates, inputs, cotangent
    )
    pieces, cosine = lax.optimization_barrier((pieces, cosine))
    mods_own, mods_send = modulation_rows([part] + pieces[1:], where)
    mods_got = exchange(mods_send, "section", 1)
    place = jnp.asarray(head_places(heads), BF)
    place_one = jnp.asarray(head_places(1), F32)
    got, mods_own = lax.optimization_barrier((got, mods_own))
    gu_send, wd_send, mods_got = lax.optimization_barrier((gate_up[0], down_weight[0], mods_got))
    got, mods_got = lax.optimization_barrier((got, mods_got))
    gains, wq, wo = prepare_weights(where, own, got, place, place_one)
    mods = [jnp.where(is_first, mods_own, mods_got), jnp.where(is_first, mods_got, mods_own)]
    gu_got = exchange(gu_send, "section", 1)
    wd_got = exchange(wd_send, "section", 1)
    mlp_weights = (gate_up[0], gu_got, down_weight[0], wd_got)

    picks_own = picks[:share]
    tables = (cosine, sine, gains, seg_col, seg_row)

    states = [x_own]
    cache = []
    attention_blocks = [x]
    for l in range(2):
        partial, saved = attention_forward(l, attention_blocks, (wq, wo), tables, mods[l], picks)
        parts = send_parts(partial)
        if l == 0:
            wq, mixed = lax.optimization_barrier((wq, saved[5]))
            saved[5] = mixed
            wq, wo = prepare_weights(where, own, got, place, place_one, (wq, wo))
            parts, wq = lax.optimization_barrier((parts, wq))
            attention_weights = (wq, wo)
        mlp_in, attended, after = after_attention(parts, states[l], mods[l], picks_own)
        partial, mlp_saved = mlp_forward(l, gather_blocks(mlp_in), mlp_weights, sec)
        parts = send_parts(partial)
        if l == 0:
            attention_in, projected, state = after_mlp(parts, after, mods[0], picks_own, mods[1])
            states.append(state)
            attention_blocks = gather_blocks(attention_in)
        else:
            projected, output = after_mlp(parts, after, mods[1], picks_own, None)
        cache.append((saved, attended, after, mlp_saved, projected))

    grad_blocks = [cotangent_now]
    grad_out = cotangent_own
    item_sums = [None, None]
    gain_sums = [None, None]
    shares = [None, None]
    earlier = None

    def data_sum(value):
        return lax.psum_scatter(value, ("dp", "section"), scatter_dimension=0, tiled=True)

    for l in (1, 0):
        saved, attended, after, (hidden, c1, c2, mlp_in), projected = cache[l]
        mixed, attention_in = saved[5:]
        partial, grads = mlp_backward(l, grad_blocks, mlp_weights, (c1, c2), mods[l], picks, sec)
        parts = send_parts(partial)
        mlp_grads = mlp_weight_grads(mlp_in, grads, hidden)
        if earlier is not None:
            parts, earlier = lax.optimization_barrier((parts, earlier))
            shares[1] = (shares[1][0], earlier)
            mlp_grads, earlier = lax.optimization_barrier((mlp_grads, earlier))
        parts, mlp_grads = lax.optimization_barrier((parts, mlp_grads))
        mlp_share = data_sum(mlp_grads)
        grad_attended, sums2, grad_after = back_of_mlp(
            parts, grad_out, after, attended, projected, mods[l], picks_own
        )
        blocks = gather_blocks(grad_attended)
        partial, (gain_sums[l], grads, grad_attended) = attention_backward(l, blocks, (wq, wo), saved, tables)
        parts = send_parts(partial)
        attention_grads = attention_weight_grads(attention_in, grads, mixed, grad_attended, place.T)
        if l == 1:
            parts, mlp_share = lax.optimization_barrier((parts, mlp_share))
        attention_grads, mlp_share = lax.optimization_barrier((attention_grads, mlp_share))
        parts, attention_grads = lax.optimization_barrier((parts, attention_grads))
        attention_share = data_sum(attention_grads)
        if l == 1:
            sums1, grad_projected, grad_out = back_of_attention(
                parts, grad_after, states[1], mods[1], picks_own, mods[0]
            )
            grad_blocks = gather_blocks(grad_projected)
            earlier = attention_share
        else:
            sums1, grad_state = back_of_attention(parts, grad_after, states[0], mods[0], picks_own, None)
        item_sums[l] = jnp.concatenate([sums1, sums2], axis=0)
        shares[l] = (mlp_share, attention_share)
    shares[1] = (shares[1][0], earlier)

    mine = jnp.where(is_first, grad_state, output)
    theirs = exchange(jnp.where(is_first, output, grad_state), "section", 1)
    results = jnp.stack([jnp.where(is_first, mine, theirs), jnp.where(is_first, theirs, mine)])

    def joined(which):
        mine = jnp.where(is_first, shares[0][which], shares[1][which])
        theirs = exchange(jnp.where(is_first, shares[1][which], shares[0][which]), "section", 1)
        low = jnp.where(is_first, mine, theirs)
        high = jnp.where(is_first, theirs, mine)
        return jnp.concatenate([low, high], axis=0).astype(F32)

    size = down_weight.shape[1]
    mlp_grads = joined(0)
    grad_pair = jnp.stack([mlp_grads[:, :size], mlp_grads[:, size : 2 * size]])
    grad_down = mlp_grads[:, 2 * size :].T
    attention_grads = joined(1)
    grad_qkv = jnp.stack([attention_grads[:, i * narrow : (i + 1) * narrow] for i in range(3)])
    grad_out_w = attention_grads[:, 3 * narrow :].T

    sums = jnp.stack(item_sums)[:, :, :items].transpose(0, 2, 1, 3).reshape(2, items, 6 * width)
    pieces = [
        lax.dynamic_slice_in_dim(sums, (tensor ^ k) * columns, columns, 2) for k in range(group)
    ]
    got = send_parts(pieces)
    mods_grad = (got[0] + got[1] + got[2] + got[3]).astype(BF)
    mine = lax.dynamic_index_in_dim(mods_grad, section, 0, keepdims=False)
    theirs = exchange(lax.dynamic_index_in_dim(mods_grad, other, 0, keepdims=False), "section", 1)
    mods_low = jnp.stack([jnp.where(is_first, mine, theirs), jnp.where(is_first, theirs, mine)])
    all_scaled = gather_dp(scaled.reshape(micro, items, width))
    all_mods = gather_dp(mods_low)
    deep = width // lax.axis_size("dp")
    scaled_share = lax.dynamic_slice_in_dim(all_scaled, data * deep, deep, 3)
    grad_ada = jnp.einsum("nmid,nmic->dc", scaled_share, all_mods, preferred_element_type=F32)
    cond_value = conditioning[:, 0].astype(F32)
    sigma = jax.nn.sigmoid(cond_value)
    cond_part = jnp.einsum("mic,dc->mid", mods_low, modulator[0], preferred_element_type=F32)
    cond_part = cond_part * sigma * (1.0 + cond_value * (1.0 - sigma))
    grad_cond = group_sum(group_sum(cond_part, "section"), "tensor")
    gain_parts = jnp.stack(gain_sums)
    gain_own = lax.dynamic_index_in_dim(gain_parts, section, 0, keepdims=False)
    gain_other = lax.dynamic_index_in_dim(gain_parts, other, 0, keepdims=False)
    gain_total = gain_own + exchange(gain_other, "section", 1)
    gain_total = group_sum(group_sum(gain_total, "tensor"), "dp")
    half = LANE // 2
    grad_gains = jnp.concatenate([gain_total[:2, :HALF], gain_total[:2, half : half + HALF]], axis=1)
    return (
        grad_ada[None],
        grad_qkv[None],
        grad_gains[None],
        grad_out_w[None],
        grad_pair[None],
        grad_down[None],
        grad_cond[:, None],
        results[None],
    )


def solution(mesh):
    return jax.shard_map(
        shards,
        mesh=mesh,
        in_specs=(
            P(None, "dp", None),
            P(None, "dp", None),
            P(None, "dp", None, None),
            P(None, "dp", None),
            P(None, None, "dp"),
            P("section", None, "tensor"),
            P("section", None, None, "tensor"),
            P("section", None, None),
            P("section", "tensor", None),
            P("section", None, None, "tensor"),
            P("section", "tensor", None),
        ),
        out_specs=(
            P("section", "dp", "tensor"),
            P("section", None, "dp", "tensor"),
            P("section", None, None),
            P("section", "tensor", "dp"),
            P("section", None, "dp", "tensor"),
            P("section", "tensor", "dp"),
            P(None, "dp", None, None),
            P("section", None, ("dp", "tensor"), None),
        ),
        check_vma=False,
    )
```

time: 535 us -> 420 us (0.79)
  waiting for transfers between devices: 196 us -> 153 us
  local copies, waits for them, and re-layouts: 44.7 us -> 11.5 us
  other arithmetic: 30.6 us -> 9.19 us
  matrix products: 14.1 us -> 4.98 us
    reduce_scatter x4, waiting for transfers between devices: 63.5 us -> 23.6 us  [data_sum(): lax.psum_scatter(value, ('dp', 'section'), scatter_dimension=0, tiled=True)]
    unnamed x165 -> x67, local copies, waits for them, and re-layouts: 29.4 us -> 7.63 us
    convert_element_type x10 -> x2, other arithmetic: 15.5 us -> 0.26 us  [joined(): return jnp.concatenate([low, high], axis=0).astype(F32)]
    dot_general x4 -> x0, matrix products: 9.39 us -> none  [the longest x1 3.89 us: shards(): jnp.einsum('kde,ec->kdc', projections[0], place, preferred_element_type=F32)]
    ppermute x76 -> x72, starting transfers between devices: 86.4 us -> 80.8 us  [exchange(): lax.ppermute(value, axis, [(i, i ^ k) for i in range(lax.axis_size(axis))])]
    ppermute x76 -> x72, waiting for transfers between devices: 132 us -> 130 us  [exchange(): lax.ppermute(value, axis, [(i, i ^ k) for i in range(lax.axis_size(axis))])]
    pallas_call x20 -> x25, Pallas kernels: 139 us -> 139 us  [run(): return kernel(*placed)]
  transfers between devices with their start and end apart: 80 -> 76, of which waited for: 49 -> 43; matrix products, arithmetic and copies ran while one was open for 9% -> 3% of each run, Pallas kernels for 15% -> 25%
where the time goes in v2:
time: 420 us; the launch traced here: 414 us
  waiting for transfers between devices  153 us (36%)
  Pallas kernels  139 us (33%)
  starting transfers between devices  81.5 us (19%)
  between operations  14.8 us (4%)
  local copies, waits for them, and re-layouts  11.5 us (3%)
  other arithmetic  9.19 us (2%)
  matrix products  4.98 us (1%)
    pallas_call x25, Pallas kernels, run(): return kernel(*placed)  139 us
    ppermute x72, waiting for transfers between devices, exchange(): lax.ppermute(value, axis, [(i, i ^ k) for i in range(lax.axis_size(axis))])  130 us
    ppermute x72, starting transfers between devices, exchange(): lax.ppermute(value, axis, [(i, i ^ k) for i in range(lax.axis_size(axis))])  80.8 us
    reduce_scatter x4, waiting for transfers between devices, data_sum(): lax.psum_scatter(value, ('dp', 'section'), scatter_dimension=0, tiled=True)  23.6 us
  transfers between devices with their start and end apart: 76, of which 43 were waited for; matrix products, arithmetic and copies ran while one was open for 3% of the time, Pallas kernels for 25%

profile of v2, /device:TPU:1, one launch (start us, length us, event | category | flops | bytes accessed | tf_op | source)
XLA Modules:
  0.0 414.2 jit_solution(8786802876234452884)
XLA Ops:
  29.6 11.8 %prepare_weights.2 = (f32[8,128]{1,0:T(8,128)S(1)}, bf16[2,3,1152,512]{3,2,1,0:T(8,128)(2,1)}, bf16[2,512,1152]{2,1,0:T(8,128)(2,1)}) custom-call(s32[2]{0:T(128)S(1)} %pad_add_fusion.where_ref, bf16[3,288,1152]{2,1,0:T(8,128)(2,1)} %bitcast.115, bf16[288,1152]{1,0:T(8,128)(2,1)} %bitcast.12.refs_1_, f32[2,72]{1,0:T(2,128)S(1)} %bitcast.107, ...), custom_call_target="tpu_custom_call" | custom-call | flops 1000 | bytes 1000 | tf_op jit(solution)/shard_map/prepare_weights/pallas_call | solution.py:54
  41.5 9.8 %attention_forward_0.1 = (bf16[128,1152]{1,0:T(8,128)(2,1)S(1)}, bf16[128,1152]{1,0:T(8,128)(2,1)S(1)}, bf16[128,1152]{1,0:T(8,128)(2,1)S(1)}, bf16[128,1152]{1,...) custom-call(bf16[512,1152]{1,0:T(8,128)(2,1)S(1)} %copy-done.1, ...), custom_call_target="tpu_custom_call" | custom-call | flops 1000 | bytes 1000 | tf_op jit(solution)/shard_map/attention_forward_0/pallas_call | solution.py:54
  77.9 6.2 %mlp_forward_0.1 = (bf16[128,1152]{1,0:T(8,128)(2,1)S(1)}, bf16[128,1152]{1,0:T(8,128)(2,1)S(1)}, bf16[128,1152]{1,0:T(8,128)(2,1)S(1)}, bf16[128,1152]{1,0:T(8,...) custom-call(s32[1]{0:T(128)} %bitcast.5.sec_ref, ...), custom_call_target="tpu_custom_call" | custom-call | flops 1000 | bytes 1000 | tf_op jit(solution)/shard_map/mlp_forward_0/pallas_call | solution.py:54
  87.4 5.6 %collective-permute-done.18.p1 = bf16[128,1152]{1,0:T(8,128)(2,1)S(1)} collective-permute-done((bf16[128,1152]{1,0:T(8,128)(2,1)S(1)}, bf16[128,1152]{1,0:T(8,128)(2,1)S(1)}, u32[]{:S(2)}, u32[]{:S(2)}) %collective-permute-start.18) | collective-permute-done | bytes 294944 | tf_op jit(solution)/shard_map/ppermute | solution.py:921
  102.0 6.3 %collective-permute-done.21.refs_1_ = bf16[128,1152]{1,0:T(8,128)(2,1)S(1)} collective-permute-done((bf16[128,1152]{1,0:T(8,128)(2,1)S(1)}, bf16[128,1152]{1,0:T(8,128)(2,1)S(1)}, u32[]{:S(2)}, u32[]{:S(2)}) %collective-permute-start.21) | collective-permute-done | bytes 294944 | tf_op jit(solution)/shard_map/ppermute | solution.py:921
  108.3 5.5 %collective-permute-done.22.refs_2_ = bf16[128,1152]{1,0:T(8,128)(2,1)S(1)} collective-permute-done((bf16[128,1152]{1,0:T(8,128)(2,1)S(1)}, bf16[128,1152]{1,0:T(8,128)(2,1)S(1)}, u32[]{:S(2)}, u32[]{:S(2)}) %collective-permute-start.22) | collective-permute-done | bytes 294944 | tf_op jit(solution)/shard_map/ppermute | solution.py:921
  113.8 8.9 %attention_forward_1.1 = (bf16[128,1152]{1,0:T(8,128)(2,1)S(1)}, bf16[128,1152]{1,0:T(8,128)(2,1)S(1)}, bf16[128,1152]{1,0:T(8,128)(2,1)S(1)}, bf16[128,1152]{1,...) custom-call(bf16[128,1152]{1,0:T(8,128)(2,1)S(1)} %get-tuple-element, ...), custom_call_target="tpu_custom_call" | custom-call | flops 1000 | bytes 1000 | tf_op jit(solution)/shard_map/attention_forward_1/pallas_call | solution.py:54
  126.1 6.4 %collective-permute-done.24.p1 = bf16[128,1152]{1,0:T(8,128)(2,1)S(1)} collective-permute-done((bf16[128,1152]{1,0:T(8,128)(2,1)S(1)}, bf16[128,1152]{1,0:T(8,128)(2,1)S(1)}, u32[]{:S(2)}, u32[]{:S(2)}) %collective-permute-start.24) | collective-permute-done | bytes 294944 | tf_op jit(solution)/shard_map/ppermute | solution.py:921
  132.5 6.3 %collective-permute-done.25.p2 = bf16[128,1152]{1,0:T(8,128)(2,1)S(1)} collective-permute-done((bf16[128,1152]{1,0:T(8,128)(2,1)S(1)}, bf16[128,1152]{1,0:T(8,128)(2,1)S(1)}, u32[]{:S(2)}, u32[]{:S(2)}) %collective-permute-start.25) | collective-permute-done | bytes 294944 | tf_op jit(solution)/shard_map/ppermute | solution.py:921
  143.8 5.5 %collective-permute-done.27.b1 = bf16[128,1152]{1,0:T(8,128)(2,1)S(1)} collective-permute-done((bf16[128,1152]{1,0:T(8,128)(2,1)S(1)}, bf16[128,1152]{1,0:T(8,128)(2,1)S(1)}, u32[]{:S(2)}, u32[]{:S(2)}) %collective-permute-start.27) | collective-permute-done | bytes 294944 | tf_op jit(solution)/shard_map/ppermute | solution.py:921
  150.0 6.6 %collective-permute-done.29.b3 = bf16[128,1152]{1,0:T(8,128)(2,1)S(1)} collective-permute-done((bf16[128,1152]{1,0:T(8,128)(2,1)S(1)}, bf16[128,1152]{1,0:T(8,128)(2,1)S(1)}, u32[]{:S(2)}, u32[]{:S(2)}) %collective-permute-start.29) | collective-permute-done | bytes 294944 | tf_op jit(solution)/shard_map/ppermute | solution.py:921
  156.6 6.2 %mlp_forward_1.1 = (bf16[128,1152]{1,0:T(8,128)(2,1)S(1)}, bf16[128,1152]{1,0:T(8,128)(2,1)S(1)}, bf16[128,1152]{1,0:T(8,128)(2,1)S(1)}, bf16[128,1152]{1,0:T(8,...) custom-call(s32[1]{0:T(128)} %bitcast.5.sec_ref, ...), custom_call_target="tpu_custom_call" | custom-call | flops 1000 | bytes 1000 | tf_op jit(solution)/shard_map/mlp_forward_1/pallas_call | solution.py:54
  162.9 8.6 %mlp_backward_1.1 = (bf16[128,1152]{1,0:T(8,128)(2,1)S(1)}, bf16[128,1152]{1,0:T(8,128)(2,1)}, bf16[128,1152]{1,0:T(8,128)(2,1)}, bf16[128,1152]{1,0:T(8,128)(2,...) custom-call(s32[1]{0:T(128)} %bitcast.5.sec_ref, ...), custom_call_target="tpu_custom_call" | custom-call | flops 1000 | bytes 1000 | tf_op jit(solution)/shard_map/mlp_backward_1/pallas_call | solution.py:54
  174.9 6.6 %mlp_weight_grads.2 = bf16[1152,2304]{1,0:T(8,128)(2,1)} custom-call(bf16[512,1152]{1,0:T(8,128)(2,1)} %get-tuple-element.238.a_in, bf16[512,768]{1,0:T(8,128)(2,1)} %get-tuple-element.239.gg_in, bf16[512,768]{1,0:T(8,128)(2,1)} %get-tuple-element.240.gu_in, bf16[512,1152]{1,0:T(8,128)(2,1)} %get-tuple-element.241.gp_in, ...), custom_call_target="tpu_custom_call" | custom-call | flops 1000 | bytes 1000 | tf_op jit(solution)/shard_map/mlp_weight_grads/pallas_call | solution.py:54
  192.8 6.5 %collective-permute-done.35.p3 = bf16[128,1152]{1,0:T(8,128)(2,1)S(1)} collective-permute-done((bf16[128,1152]{1,0:T(8,128)(2,1)S(1)}, bf16[128,1152]{1,0:T(8,128)(2,1)S(1)}, u32[]{:S(2)}, u32[]{:S(2)}) %collective-permute-start.35) | collective-permute-done | bytes 294944 | tf_op jit(solution)/shard_map/ppermute | solution.py:921
  216.1 11.9 %attention_backward_1.1 = (bf16[128,1152]{1,0:T(8,128)(2,1)S(1)}, bf16[128,1152]{1,0:T(8,128)(2,1)}, bf16[128,1152]{1,0:T(8,128)(2,1)S(1)}, bf16[128,1152]{1,0:T...) custom-call(bf16[128,1152]{1,0:T(8,128)(2,1)S(1)} %get-tuple-element.255.b0, ...), custom_call_target="tpu_custom_call" | custom-call | flops 1000 | bytes 1000 | tf_op jit(solution)/shard_map/attention_backward_1/pallas_call | solution.py:54
  231.4 6.7 %attention_weight_grads.2 = bf16[1152,1152]{1,0:T(8,128)(2,1)} custom-call(bf16[512,1152]{1,0:T(8,128)(2,1)} %get-tuple-element.270.a_in, bf16[512,1536]{1,0:T(8,128)(2,1)} %get-tuple-element.271.g_in, bf16[512,512]{1,0:T(8,128)(2,1)} %get-tuple-element.272.mixed_in, bf16[512,1152]{1,0:T(8,128)(2,1)} %get-tuple-element.273.ga_in, bf16[512,288]{1,0:T(8,128)(2,1)S(1)} %copy-done), custom_call_target="tpu_custom_call" | custom-call | flops 1000 | bytes 1000 | tf_op jit(solution)/shard_map/attention_weight_grads/pallas_call | solution.py:54
  240.0 6.7 %reduce-scatter.5.cloned.1.call-done = bf16[144,2304]{1,0:T(8,128)(2,1)} async-done(((bf16[1152,2304]{1,0:T(8,128)(2,1)}), bf16[144,2304]{1,0:T(8,128)(2,1)}) %reduce-scatter.5.cloned.1.call-update) | async-done | bytes 663568 | tf_op jit(solution)/shard_map/reduce_scatter | solution.py:1049
  262.4 8.6 %mlp_backward_0.1 = (bf16[128,1152]{1,0:T(8,128)(2,1)S(1)}, bf16[128,1152]{1,0:T(8,128)(2,1)}, bf16[128,1152]{1,0:T(8,128)(2,1)S(1)}, bf16[128,1152]{1,0:T(8,128...) custom-call(s32[1]{0:T(128)} %bitcast.5.sec_ref, ...), custom_call_target="tpu_custom_call" | custom-call | flops 1000 | bytes 1000 | tf_op jit(solution)/shard_map/mlp_backward_0/pallas_call | solution.py:54
  274.4 6.7 %mlp_weight_grads.3 = bf16[1152,2304]{1,0:T(8,128)(2,1)} custom-call(bf16[512,1152]{1,0:T(8,128)(2,1)} %get-tuple-element.293.a_in, bf16[512,768]{1,0:T(8,128)(2,1)} %get-tuple-element.294.gg_in, bf16[512,768]{1,0:T(8,128)(2,1)} %get-tuple-element.295.gu_in, bf16[512,1152]{1,0:T(8,128)(2,1)} %get-tuple-element.296.gp_in, ...), custom_call_target="tpu_custom_call" | custom-call | flops 1000 | bytes 1000 | tf_op jit(solution)/shard_map/mlp_weight_grads/pallas_call | solution.py:54
  300.6 11.0 %attention_backward_0.1 = (bf16[128,1152]{1,0:T(8,128)(2,1)S(1)}, bf16[128,1152]{1,0:T(8,128)(2,1)S(1)}, bf16[128,1152]{1,0:T(8,128)(2,1)S(1)}, bf16[128,1152]{1...) custom-call(bf16[128,1152]{1,0:T(8,128)(2,1)S(1)} %get-tuple-element.307.b0, ...), custom_call_target="tpu_custom_call" | custom-call | flops 1000 | bytes 1000 | tf_op jit(solution)/shard_map/attention_backward_0/pallas_call | solution.py:54
  318.6 7.0 %collective-permute-start = (bf16[2,4,1152]{2,1,0:T(4,128)(2,1)S(1)}, bf16[2,4,1152]{2,1,0:T(4,128)(2,1)S(1)}, u32[]{:S(2)}, u32[]{:S(2)}) collective-permute-start(bf16[2,4,1152]{2,1,0:T(4,128)(2,1)S(1)} %reshape.27), channel_id=1, source_target_pairs={{0,1},{1,0},{2,3},{3,2},{4,5},{5,4},{6,7},{7,6},{8,9},{9,8},{10,11... | collective-permute-start | bytes 55304 | tf_op jit(solution)/shard_map/ppermute | solution.py:921
  341.3 6.7 %attention_weight_grads.3 = bf16[1152,1152]{1,0:T(8,128)(2,1)} custom-call(bf16[512,1152]{1,0:T(8,128)(2,1)} %get-tuple-element.317.a_in, bf16[512,1536]{1,0:T(8,128)(2,1)} %get-tuple-element.318.g_in, bf16[512,512]{1,0:T(8,128)(2,1)} %get-tuple-element.319.mixed_in, bf16[512,1152]{1,0:T(8,128)(2,1)} %get-tuple-element.320.ga_in, bf16[512,288]{1,0:T(8,128)(2,1)S(1)} %copy-done), custom_call_target="tpu_custom_call" | custom-call | flops 1000 | bytes 1000 | tf_op jit(solution)/shard_map/attention_weight_grads/pallas_call | solution.py:54
  386.2 13.0 %reduce-scatter.11.cloned.1.call-done = bf16[144,1152]{1,0:T(8,128)(2,1)} async-done(((bf16[1152,1152]{1,0:T(8,128)(2,1)}), bf16[144,1152]{1,0:T(8,128)(2,1)}) %reduce-scatter.11.cloned.1.call-update) | async-done | bytes 331792 | tf_op jit(solution)/shard_map/reduce_scatter | solution.py:1049
  (279 shorter events, 214.4 us)
Async XLA Ops:
  7.2 239.5 %reduce-scatter.5.cloned.1.call-start = ((), (), s32[]{:S(2)}) async-start(), calls=%async_computation.4 | async-start | bytes 5971968 | tf_op jit(solution)/shard_map/reduce_scatter | solution.py:1049
  7.2 22.4 %collective-permute-start.9 = (bf16[3,288,1152]{2,1,0:T(8,128)(2,1)}, bf16[3,288,1152]{2,1,0:T(8,128)(2,1)}, u32[]{:S(2)}, u32[]{:S(2)}) collective-permute-start(bf16[3,288,1152]{2,1,0:T(8,128)(2,1)} %bitcast.114), channel_id=1, source_target_pairs={{0,16},{16,0},{1,17},{17,1},{2,18},{18,2},{3,19},{19,3},{4,20},{20... | collective-permute-start | bytes 5971976 | tf_op jit(solution)/shard_map/ppermute | solution.py:921
  22.1 55.8 %collective-permute-start.7 = (bf16[2,1152,768]{2,1,0:T(8,128)(2,1)}, bf16[2,1152,768]{2,1,0:T(8,128)(2,1)}, u32[]{:S(2)}, u32[]{:S(2)}) collective-permute-start(bf16[2,1152,768]{2,1,0:T(8,128)(2,1)} %bitcast.8.gu_a.refs_1_.refs_4_), channel_id=1, source_target_pairs={{0,16},{16,0},{1,17},{17,1},{2,18},{18,2},{3,19},{19,3},{4,20},{20... | collective-permute-start | bytes 10616840 | tf_op jit(solution)/shard_map/ppermute | solution.py:921
  23.1 45.0 %collective-permute-start.8 = (bf16[768,1152]{1,0:T(8,128)(2,1)S(1)}, bf16[768,1152]{1,0:T(8,128)(2,1)S(1)}, u32[]{:S(2)}, u32[]{:S(2)}) collective-permute-start(bf16[768,1152]{1,0:T(8,128)(2,1)S(1)} %bitcast.112), channel_id=1, source_target_pairs={{0,16},{16,0},{1,17},{17,1},{2,18},{18,2},{3,19},{19,3},{4,20},{20... | collective-permute-start | bytes 5308424 | tf_op jit(solution)/shard_map/ppermute | solution.py:921
  66.2 11.7 %collective-permute-start.16 = (bf16[128,1152]{1,0:T(8,128)(2,1)S(1)}, bf16[128,1152]{1,0:T(8,128)(2,1)S(1)}, u32[]{:S(2)}, u32[]{:S(2)}) collective-permute-start(bf16[128,1152]{1,0:T(8,128)(2,1)S(1)} %get-tuple-element.217.b0), channel_id=1, source_target_pairs={{0,8},{4,12},{8,0},{12,4},{1,9},{5,13},{9,1},{13,5},{2,10},{6,14},... | collective-permute-start | bytes 884744 | tf_op jit(solution)/shard_map/ppermute | solution.py:921
  67.0 10.9 %collective-permute-start.17 = (bf16[128,1152]{1,0:T(8,128)(2,1)S(1)}, bf16[128,1152]{1,0:T(8,128)(2,1)S(1)}, u32[]{:S(2)}, u32[]{:S(2)}) collective-permute-start(bf16[128,1152]{1,0:T(8,128)(2,1)S(1)} %get-tuple-element.217.b0), channel_id=1, source_target_pairs={{0,12},{4,8},{8,4},{12,0},{1,13},{5,9},{9,5},{13,1},{2,14},{6,10},... | collective-permute-start | bytes 884744 | tf_op jit(solution)/shard_map/ppermute | solution.py:921
  85.1 11.7 %collective-permute-start.19 = (bf16[128,1152]{1,0:T(8,128)(2,1)S(1)}, bf16[128,1152]{1,0:T(8,128)(2,1)S(1)}, u32[]{:S(2)}, u32[]{:S(2)}) collective-permute-start(bf16[128,1152]{1,0:T(8,128)(2,1)S(1)} %get-tuple-element.220), channel_id=1, source_target_pairs={{0,8},{4,12},{8,0},{12,4},{1,9},{5,13},{9,1},{13,5},{2,10},{6,14},... | collective-permute-start | bytes 884744 | tf_op jit(solution)/shard_map/ppermute | solution.py:921
  100.5 13.4 %collective-permute-start.22 = (bf16[128,1152]{1,0:T(8,128)(2,1)S(1)}, bf16[128,1152]{1,0:T(8,128)(2,1)S(1)}, u32[]{:S(2)}, u32[]{:S(2)}) collective-permute-start(bf16[128,1152]{1,0:T(8,128)(2,1)S(1)} %get-tuple-element.223.refs_0_), channel_id=1, source_target_pairs={{0,8},{4,12},{8,0},{12,4},{1,9},{5,13},{9,1},{13,5},{2,10},{6,14},... | collective-permute-start | bytes 884744 | tf_op jit(solution)/shard_map/ppermute | solution.py:921
  100.9 12.9 %collective-permute-start.23 = (bf16[128,1152]{1,0:T(8,128)(2,1)S(1)}, bf16[128,1152]{1,0:T(8,128)(2,1)S(1)}, u32[]{:S(2)}, u32[]{:S(2)}) collective-permute-start(bf16[128,1152]{1,0:T(8,128)(2,1)S(1)} %get-tuple-element.223.refs_0_), channel_id=1, source_target_pairs={{0,12},{4,8},{8,4},{12,0},{1,13},{5,9},{9,5},{13,1},{2,14},{6,10},... | collective-permute-start | bytes 884744 | tf_op jit(solution)/shard_map/ppermute | solution.py:921
  123.5 15.3 %collective-permute-start.25 = (bf16[128,1152]{1,0:T(8,128)(2,1)S(1)}, bf16[128,1152]{1,0:T(8,128)(2,1)S(1)}, u32[]{:S(2)}, u32[]{:S(2)}) collective-permute-start(bf16[128,1152]{1,0:T(8,128)(2,1)S(1)} %get-tuple-element.228), channel_id=1, source_target_pairs={{0,8},{4,12},{8,0},{12,4},{1,9},{5,13},{9,1},{13,5},{2,10},{6,14},... | collective-permute-start | bytes 884744 | tf_op jit(solution)/shard_map/ppermute | solution.py:921
  124.4 14.4 %collective-permute-start.26 = (bf16[128,1152]{1,0:T(8,128)(2,1)S(1)}, bf16[128,1152]{1,0:T(8,128)(2,1)S(1)}, u32[]{:S(2)}, u32[]{:S(2)}) collective-permute-start(bf16[128,1152]{1,0:T(8,128)(2,1)S(1)} %get-tuple-element.229), channel_id=1, source_target_pairs={{0,12},{4,8},{8,4},{12,0},{1,13},{5,9},{9,5},{13,1},{2,14},{6,10},... | collective-permute-start | bytes 884744 | tf_op jit(solution)/shard_map/ppermute | solution.py:921
  142.6 14.0 %collective-permute-start.29 = (bf16[128,1152]{1,0:T(8,128)(2,1)S(1)}, bf16[128,1152]{1,0:T(8,128)(2,1)S(1)}, u32[]{:S(2)}, u32[]{:S(2)}) collective-permute-start(bf16[128,1152]{1,0:T(8,128)(2,1)S(1)} %get-tuple-element.231.b0), channel_id=1, source_target_pairs={{0,12},{4,8},{8,4},{12,0},{1,13},{5,9},{9,5},{13,1},{2,14},{6,10},... | collective-permute-start | bytes 884744 | tf_op jit(solution)/shard_map/ppermute | solution.py:921
  173.5 12.3 %collective-permute-start.32 = (bf16[128,1152]{1,0:T(8,128)(2,1)S(1)}, bf16[128,1152]{1,0:T(8,128)(2,1)S(1)}, u32[]{:S(2)}, u32[]{:S(2)}) collective-permute-start(bf16[128,1152]{1,0:T(8,128)(2,1)S(1)} %get-tuple-element.237), channel_id=1, source_target_pairs={{0,12},{4,8},{8,4},{12,0},{1,13},{5,9},{9,5},{13,1},{2,14},{6,10},... | collective-permute-start | bytes 884744 | tf_op jit(solution)/shard_map/ppermute | solution.py:921
  185.9 99.0 %reduce-scatter.7.cloned.1.call-start = ((), (), s32[]{:S(2)}) async-start(), calls=%async_computation.5 | async-start | bytes 2985984 | tf_op jit(solution)/shard_map/reduce_scatter | solution.py:1049
  187.6 11.7 %collective-permute-start.35 = (bf16[128,1152]{1,0:T(8,128)(2,1)S(1)}, bf16[128,1152]{1,0:T(8,128)(2,1)S(1)}, u32[]{:S(2)}, u32[]{:S(2)}) collective-permute-start(bf16[128,1152]{1,0:T(8,128)(2,1)S(1)} %get-tuple-element.253), channel_id=1, source_target_pairs={{0,12},{4,8},{8,4},{12,0},{1,13},{5,9},{9,5},{13,1},{2,14},{6,10},... | collective-permute-start | bytes 884744 | tf_op jit(solution)/shard_map/ppermute | solution.py:921
  205.3 10.9 %collective-permute-start.38 = (bf16[128,1152]{1,0:T(8,128)(2,1)S(1)}, bf16[128,1152]{1,0:T(8,128)(2,1)S(1)}, u32[]{:S(2)}, u32[]{:S(2)}) collective-permute-start(bf16[128,1152]{1,0:T(8,128)(2,1)S(1)} %get-tuple-element.255.b0), channel_id=1, source_target_pairs={{0,12},{4,8},{8,4},{12,0},{1,13},{5,9},{9,5},{13,1},{2,14},{6,10},... | collective-permute-start | bytes 884744 | tf_op jit(solution)/shard_map/ppermute | solution.py:921
  246.6 104.1 %reduce-scatter.9.cloned.1.call-start = ((), (), s32[]{:S(2)}) async-start(), calls=%async_computation.6 | async-start | bytes 5971968 | tf_op jit(solution)/shard_map/reduce_scatter | solution.py:1049
  284.9 114.3 %reduce-scatter.11.cloned.1.call-start = ((), (), s32[]{:S(2)}) async-start(), calls=%async_computation.7 | async-start | bytes 2985984 | tf_op jit(solution)/shard_map/reduce_scatter | solution.py:1049
  313.8 14.1 %collective-permute-start.62 = (f32[8,128]{1,0:T(8,128)S(1)}, f32[8,128]{1,0:T(8,128)S(1)}, u32[]{:S(2)}, u32[]{:S(2)}) collective-permute-start(f32[8,128]{1,0:T(8,128)S(1)} %fusion.27), channel_id=1, source_target_pairs={{0,16},{16,0},{1,17},{17,1},{2,18},{18,2},{3,19},{19,3},{4,20},{20... | collective-permute-start | bytes 12296 | tf_op jit(solution)/shard_map/ppermute | solution.py:921
  338.6 12.1 %collective-permute-start.51 = (bf16[128,1152]{1,0:T(8,128)(2,1)}, bf16[128,1152]{1,0:T(8,128)(2,1)S(1)}, u32[]{:S(2)}, u32[]{:S(2)}) collective-permute-start(bf16[128,1152]{1,0:T(8,128)(2,1)} %copy-done.19), channel_id=1, source_target_pairs={{0,4},{4,0},{8,12},{12,8},{1,5},{5,1},{9,13},{13,9},{2,6},{6,2},{1... | collective-permute-start | bytes 884744 | tf_op jit(solution)/shard_map/ppermute | solution.py:921
  339.8 11.0 %collective-permute-start.52 = (bf16[128,1152]{1,0:T(8,128)(2,1)}, bf16[128,1152]{1,0:T(8,128)(2,1)S(1)}, u32[]{:S(2)}, u32[]{:S(2)}) collective-permute-start(bf16[128,1152]{1,0:T(8,128)(2,1)} %copy-done.18), channel_id=1, source_target_pairs={{0,8},{4,12},{8,0},{12,4},{1,9},{5,13},{9,1},{13,5},{2,10},{6,14},... | collective-permute-start | bytes 884744 | tf_op jit(solution)/shard_map/ppermute | solution.py:921
  340.1 12.1 %collective-permute-start.53 = (bf16[128,1152]{1,0:T(8,128)(2,1)S(1)}, bf16[128,1152]{1,0:T(8,128)(2,1)S(1)}, u32[]{:S(2)}, u32[]{:S(2)}) collective-permute-start(bf16[128,1152]{1,0:T(8,128)(2,1)S(1)} %get-tuple-element.316), channel_id=1, source_target_pairs={{0,12},{4,8},{8,4},{12,0},{1,13},{5,9},{9,5},{13,1},{2,14},{6,10},... | collective-permute-start | bytes 884744 | tf_op jit(solution)/shard_map/ppermute | solution.py:921
  359.4 25.3 %collective-permute-start.71 = (f32[128,1152]{1,0:T(8,128)}, f32[128,1152]{1,0:T(8,128)S(1)}, u32[]{:S(2)}, u32[]{:S(2)}) collective-permute-start(f32[128,1152]{1,0:T(8,128)} %broadcast_select_fusion.8), channel_id=1, source_target_pairs={{0,16},{16,0},{1,17},{17,1},{2,18},{18,2},{3,19},{19,3},{4,20},{20... | collective-permute-start | bytes 1769480 | tf_op jit(solution)/shard_map/ppermute | solution.py:921
  367.9 17.9 %collective-permute-start.67 = (bf16[144,2304]{1,0:T(8,128)(2,1)S(1)}, bf16[144,2304]{1,0:T(8,128)(2,1)S(1)}, u32[]{:S(2)}, u32[]{:S(2)}) collective-permute-start(bf16[144,2304]{1,0:T(8,128)(2,1)S(1)} %broadcast_select_fusion.2), channel_id=1, source_target_pairs={{0,16},{16,0},{1,17},{17,1},{2,18},{18,2},{3,19},{19,3},{4,20},{20... | collective-permute-start | bytes 1990664 | tf_op jit(solution)/shard_map/ppermute | solution.py:921
  (85 other events, 602.2 us)
Sparse Core Ops, SparseCore 0:
  186.0 60.5 reduce-scatter.4
  248.9 35.8 reduce-scatter.6
  287.2 63.4 reduce-scatter.8
  364.1 35.0 reduce-scatter.10

commit v3 on v2

v3 whole, which is shorter than its diff:
```python
import functools

import jax
import jax.numpy as jnp
from jax import lax
from jax.experimental import pallas as pl
from jax.experimental.pallas import tpu as pltpu
from jax.sharding import PartitionSpec as P
import numpy as np

HEAD = 72
HALF = HEAD // 2
LANE = 128
epsilon = 1e-06
BF = jnp.bfloat16
F32 = jnp.float32
HIGHEST = lax.Precision.HIGHEST
VM = pl.BlockSpec(memory_space=pltpu.VMEM)
SM = pl.BlockSpec(memory_space=pltpu.SMEM)
HB = pl.BlockSpec(memory_space=pltpu.HBM)
FREE = pl.BlockSpec(memory_space=pltpu.VMEM)


def nn(a, b):
    return lax.dot_general(a, b, (((1,), (0,)), ((), ())), preferred_element_type=F32)


def nt(a, b):
    return lax.dot_general(a, b, (((1,), (1,)), ((), ())), preferred_element_type=F32)


def tn(a, b):
    return lax.dot_general(a, b, (((0,), (0,)), ((), ())), preferred_element_type=F32)


def call(body, outs, in_specs, scratch=(), name=None, kept=0, limit=24, aliases={}):
    small = len(outs) - kept
    kernel = pl.pallas_call(
        body,
        out_shape=[pltpu.VMEM(o.shape, o.dtype) for o in outs[:small]] + [pltpu.HBM(o.shape, o.dtype) for o in outs[small:]],
        in_specs=in_specs,
        out_specs=[VM] * small + [HB] * kept,
        scratch_shapes=list(scratch),
        input_output_aliases=aliases,
        compiler_params=pltpu.CompilerParams(vmem_limit_bytes=limit * 2**20),
        cost_estimate=pl.CostEstimate(flops=1000, bytes_accessed=1000, transcendentals=0),
        name=name,
    )

    def run(*args):
        spaces = {id(HB): pltpu.HBM, id(VM): pltpu.VMEM}
        placed = [
            pltpu.with_memory_space_constraint(arg, spaces[id(spec)]) if id(spec) in spaces else arg
            for arg, spec in zip(args, in_specs)
        ]
        return kernel(*placed)

    return run


def shape(dims, dtype):
    return jax.ShapeDtypeStruct(dims, dtype)


def fetch(is_own, own, other, where, sem):
    @pl.when(is_own)
    def _():
        pltpu.make_async_copy(own, where, sem).start()

    @pl.when(jnp.logical_not(is_own))
    def _():
        pltpu.make_async_copy(other, where, sem).start()


def arrived(own, where, sem):
    pltpu.make_async_copy(own, where, sem).wait()


def load(pairs, sems):
    made = [pltpu.make_async_copy(there, here, sems.at[i]) for i, (there, here) in enumerate(pairs)]
    for one in made:
        one.start()
    return made


def finish(copies):
    for one in copies:
        one.wait()


def rows_of(whole, where_ref, here):
    share = whole.shape[1] // 4
    pairs = []
    for k in range(here.shape[0] // share):
        there = pl.ds(pl.multiple_of((where_ref[1] ^ k) * share, LANE), share)
        pairs.append((whole.at[where_ref[0], there], here.at[pl.ds(k * share, share)]))
    return pairs


def inverse_rms(value):
    return lax.rsqrt(jnp.mean(value * value, axis=-1, keepdims=True) + epsilon)


def norm_back(grad, normed, inverse):
    return inverse * (grad - normed * jnp.mean(grad * normed, axis=-1, keepdims=True))


def token_mod(picks, mods_ref, part):
    width = mods_ref.shape[1] // 6
    return nn(picks, mods_ref[:, part * width : (part + 1) * width])


def image_sums(picks, value):
    return lax.dot_general(
        picks.astype(F32),
        value,
        (((0,), (0,)), ((), ())),
        precision=HIGHEST,
        preferred_element_type=F32,
    )


def swap_halves(value):
    return pltpu.roll(value, LANE // 2, 1)


def rotate(value, cosine, sine):
    return value * cosine + swap_halves(value) * sine


def unrotate(grad, cosine, sine):
    return grad * cosine - swap_halves(grad) * sine


def head_mean(value):
    return nn(value.astype(BF), jnp.full((LANE, LANE), 1.0, BF)) * (1.0 / HEAD)


def head_inverse(raw):
    return lax.rsqrt(head_mean(raw * raw) + epsilon)


def split_store(value, rows, block_refs):
    own = block_refs[0]
    share = own.shape[0]
    for k, ref in enumerate(block_refs):
        ref[:, rows] = value[k * share : (k + 1) * share].astype(ref.dtype)


def modulation_part(conditioning, modulator_t):
    micro, items = conditioning.shape[0], conditioning.shape[2]
    columns, width = modulator_t.shape
    step = 5 * LANE
    spans = [(j, min(step, columns - j)) for j in range(0, columns, step)]

    def body(cond_ref, mod_in, scaled_ref, part_ref, mod_ref, sems):
        copies = load([(mod_in.at[pl.ds(j, size)], mod_ref.at[pl.ds(j, size)]) for j, size in spans], sems)
        cond = jnp.concatenate([cond_ref[m, 0].astype(F32) for m in range(micro)], axis=0)
        scaled = (cond * jax.nn.sigmoid(cond)).astype(BF)
        scaled_ref[...] = scaled
        for copy, (j, size) in zip(copies, spans):
            copy.wait()
            part_ref[:, j : j + size] = nt(scaled, mod_ref[j : j + size]).astype(BF)

    return call(
        body,
        [shape((micro * items, width), BF), shape((micro * items, columns), BF)],
        [FREE, HB],
        [pltpu.VMEM((columns, width), BF), pltpu.SemaphoreType.DMA((len(spans),))],
        name="modulation_part",
        limit=12,
    )(conditioning, modulator_t)


def modulation_rows(pieces, gains, where, place_one):
    rows, columns = pieces[0].shape
    count = len(pieces)
    items = rows // 2

    def body(where_ref, *refs):
        piece_refs, (ga, gb, one_ref, own_ref, send_ref, gains_ref) = refs[:count], refs[count:]
        section, tensor = where_ref[0], where_ref[1]
        values = [ref[...].astype(F32) for ref in piece_refs]
        ordered = []
        for j in range(count):
            picked = jnp.zeros_like(values[0])
            for k in range(count):
                picked = jnp.where((tensor ^ k) == j, values[k], picked)
            ordered.append(picked)
        whole = jnp.concatenate(ordered, axis=1)
        blank = jnp.zeros((8 - items, whole.shape[1]), F32)
        first = jnp.concatenate([whole[:items], blank], axis=0)
        second = jnp.concatenate([whole[items:], blank], axis=0)
        own_ref[...] = jnp.where(section == 0, first, second).astype(BF)
        send_ref[...] = jnp.where(section == 0, second, first).astype(BF)
        a, b = ga[...], gb[...]
        first = jnp.where(section == 0, a, b)
        second = jnp.where(section == 0, b, a)
        both = jnp.concatenate([first, second, jnp.zeros((4, first.shape[1]), F32)], axis=0)
        gains_ref[...] = lax.dot_general(
            both, one_ref[...], (((1,), (0,)), ((), ())), precision=HIGHEST, preferred_element_type=F32
        )

    return call(
        body,
        [shape((8, count * columns), BF)] * 2 + [shape((8, LANE), F32)],
        [SM] + [VM] * count + [FREE] * 3,
        name="modulation_rows",
        limit=8,
    )(where, *pieces, *gains, place_one)


def prepare_tables(where, lengths, positions, rates):
    rows = positions.shape[2]
    share = rows // 4
    items = lengths.shape[2]

    def body(where_ref, len_ref, pos_ref, rate_ref, cos_ref, sin_ref, segc_ref, segr_ref, picks_ref, own_ref):
        section, tensor = where_ref[0], where_ref[1]

        def segments(index):
            place = (tensor ^ (index // share)) * share + index % share
            segment = jnp.zeros_like(index)
            end = 0
            for i in range(items):
                end = end + len_ref[section, 0, i]
                segment += (place >= end).astype(jnp.int32)
            return segment

        column = segments(lax.broadcasted_iota(jnp.int32, (rows, 1), 0))
        segc_ref[...] = column
        segr_ref[...] = segments(lax.broadcasted_iota(jnp.int32, (1, rows), 1))
        picks = jnp.where(column == lax.broadcasted_iota(jnp.int32, (rows, 8), 1), 1.0, 0.0).astype(BF)
        picks_ref[...] = picks
        own_ref[...] = picks[:share]
        blocks = [
            pos_ref[section, :, pl.ds(pl.multiple_of((tensor ^ k) * share, LANE), share)] for k in range(4)
        ]
        place = jnp.concatenate(blocks, axis=1).astype(F32)
        lane = lax.broadcasted_iota(jnp.int32, (LANE // 2, rows), 0)
        phase = jnp.where(lane < HEAD // 4, place[0:1], place[1:2]) * rate_ref[...]
        cosine = jnp.where(lane < HALF, jnp.cos(phase), 0.0)
        sine = jnp.where(lane < HALF, jnp.sin(phase), 0.0)
        cos_ref[...] = jnp.concatenate([cosine, cosine], axis=0).T
        sin_ref[...] = jnp.concatenate([-sine, sine], axis=0).T

    return call(
        body,
        [
            shape((rows, LANE), F32),
            shape((rows, LANE), F32),
            shape((rows, 1), jnp.int32),
            shape((1, rows), jnp.int32),
            shape((rows, 8), BF),
            shape((share, 8), BF),
        ],
        [SM, SM, FREE, FREE],
        name="prepare_tables",
        limit=16,
    )(where, lengths, positions, rates)


def prepare_weights(where, source, place, begun=None, only=None):
    wq, wo = source
    narrow, width = wq.shape[1:]
    padded = place.shape[1]

    def body(where_ref, wq_in, wo_in, place_ref, *refs):
        wq_out, wo_out, wq_ref, wo_ref, wide_ref, tall_ref, sems, out_sems = refs if begun is None else refs[2:]
        section = where_ref[0]

        def make(layer):
            copies = load([(wq_in.at[i], wq_ref.at[i]) for i in range(3)] + [(wo_in, wo_ref)], sems)
            outs = []
            for i in range(3):
                copies[i].wait()
                wide_ref[i] = tn(wq_ref[i], place_ref[...]).astype(BF)
                outs.append(pltpu.make_async_copy(wide_ref.at[i], wq_out.at[layer, i], out_sems.at[i]))
                outs[-1].start()
            copies[3].wait()
            tall_ref[...] = tn(place_ref[...], wo_ref[...]).astype(BF)
            outs.append(pltpu.make_async_copy(tall_ref, wo_out.at[layer], out_sems.at[3]))
            outs[-1].start()
            finish(outs)

        if only is None:
            make(section)
        else:

            @pl.when(section == only)
            def _():
                make(1 - only)

    args = [where, wq, wo, place] + ([] if begun is None else list(begun))
    return call(
        body,
        [shape((2, 3, width, padded), BF), shape((2, padded, width), BF)],
        [SM, HB, HB, FREE] + ([] if begun is None else [HB, HB]),
        [
            pltpu.VMEM((3, narrow, width), BF),
            pltpu.VMEM((narrow, width), BF),
            pltpu.VMEM((3, width, padded), BF),
            pltpu.VMEM((padded, width), BF),
            pltpu.SemaphoreType.DMA((4,)),
            pltpu.SemaphoreType.DMA((4,)),
        ],
        name="prepare_weights",
        limit=24,
        kept=2,
        aliases={} if begun is None else {4: 0, 5: 1},
    )(*args)


def attention_forward(layer, where, blocks, weights, tables, mods, picks, carried=()):
    wq, wo = weights
    cosine, sine, gains, seg_col, seg_row = tables
    padded, width = wo.shape[1:]
    heads = padded // LANE
    raw_input = len(blocks) == 1
    rows = cosine.shape[0]
    share = rows // 4
    scale = HEAD**-0.5
    QB = 512

    def body(where_ref, *refs):
        refs = list(refs)
        in_refs = [refs.pop(0) for _ in blocks]
        wq_in, wo_in, cos_ref, sin_ref, gain_ref, segc_ref, segr_ref, mods_ref, picks_ref = refs[:9]
        refs = refs[9:]
        carried_refs = [refs.pop(0) for _ in carried]
        p_refs = [refs.pop(0) for _ in range(4)]
        state_ref = refs.pop(0) if raw_input else None
        kept = [refs.pop(0) for _ in range(7)]
        carried_outs = [refs.pop(0) for _ in carried]
        wq_ref, wo_ref, mask_ref = refs[:3]
        here = refs[3:10]
        sems, out_sems, carried_sems, a_x_ref, x_sems = refs[10:]
        carried_copies = load(list(zip(carried_refs, carried_outs)), carried_sems)
        if raw_input:
            x_ref = a_x_ref
            x_copies = load(rows_of(in_refs[0], where_ref, x_ref), x_sems)
        qraw_ref, kraw_ref, qrot_ref, krot_ref, v_ref, mixed_ref, a_ref = here
        weights_in = [(wq_in.at[layer, i], wq_ref.at[i]) for i in range(3)] + [(wo_in.at[layer], wo_ref)]
        weights_in = load(weights_in, sems)

        def keep(i):
            pltpu.make_async_copy(here[i], kept[i], out_sems.at[i]).start()

        if raw_input:
            picked = picks_ref[...]
            shift1 = token_mod(picked, mods_ref, 0)
            scale1 = token_mod(picked, mods_ref, 1)
            finish(x_copies)
            state_ref[...] = x_ref[:share]
            x = x_ref[...].astype(F32)
            a_ref[...] = (x * inverse_rms(x) * (1.0 + scale1) + shift1).astype(BF)
        else:
            for k, ref in enumerate(in_refs):
                a_ref[k * share : (k + 1) * share] = ref[...]
        keep(6)
        mask_ref[...] = jnp.where(segc_ref[...] == segr_ref[...], 1.0, 0.0).astype(BF)
        cos = cos_ref[...]
        sin = sin_ref[...]
        for i, (raw_out, rot_out) in enumerate(((qraw_ref, qrot_ref), (kraw_ref, krot_ref))):
            weights_in[i].wait()
            gain = gain_ref[2 * layer + i : 2 * layer + i + 1]
            for h2 in range(0, heads, 2):
                both = nn(a_ref[...], wq_ref[i, :, h2 * LANE : (h2 + 2) * LANE])
                for h in (h2, h2 + 1):
                    at = slice(h * LANE, (h + 1) * LANE)
                    raw = both[:, (h - h2) * LANE : (h - h2 + 1) * LANE]
                    raw_out[:, at] = raw.astype(BF)
                    turned = rotate(raw * head_inverse(raw) * gain, cos, sin)
                    rot_out[:, at] = turned.astype(BF)
            keep(i)
            keep(2 + i)
        weights_in[2].wait()
        one = jnp.where(lax.broadcasted_iota(jnp.int32, (1, padded), 1) % LANE == LANE - 1, 1.0, 0.0)
        v_ref[...] = (nn(a_ref[...], wq_ref[2]) + one).astype(BF)
        keep(4)

        for j in range(rows // QB):
            at_rows = slice(j * QB, (j + 1) * QB)
            for h in range(heads):
                at = slice(h * LANE, (h + 1) * LANE)
                scores = nt(qrot_ref[at_rows, at], krot_ref[:, at]) * scale
                grown = jnp.exp(scores).astype(BF) * mask_ref[at_rows]
                mixed = nn(grown, v_ref[:, at])
                mixed_ref[at_rows, at] = (mixed * (1.0 / mixed[:, LANE - 1 :])).astype(BF)
        keep(5)
        weights_in[3].wait()
        step = 3 * LANE
        for j in range(width // step):
            at = slice(j * step, (j + 1) * step)
            split_store(nn(mixed_ref[...], wo_ref[:, at]), at, p_refs)
        for i in range(7):
            pltpu.make_async_copy(here[i], kept[i], out_sems.at[i]).wait()
        finish(carried_copies)

    outs = [shape((share, width), BF)] * (5 if raw_input else 4)
    saved_shapes = [shape((rows, padded), BF)] * 6 + [shape((rows, width), BF)]
    result = call(
        body,
        outs + saved_shapes + [shape(c.shape, c.dtype) for c in carried],
        [SM] + ([HB] if raw_input else [VM] * 4) + [HB] * 2 + [VM] * (7 + len(carried)),
        [
            pltpu.VMEM((3, width, padded), BF),
            pltpu.VMEM((padded, width), BF),
            pltpu.VMEM((rows, rows), BF),
        ] + [pltpu.VMEM(s.shape, BF) for s in saved_shapes] + [
            pltpu.SemaphoreType.DMA((4,)),
            pltpu.SemaphoreType.DMA((7,)),
            pltpu.SemaphoreType.DMA((max(1, len(carried)),)),
            pltpu.VMEM((rows if raw_input else 16, width), BF),
            pltpu.SemaphoreType.DMA((4,)),
        ],
        name=f"attention_forward_{layer}",
        limit=28,
        kept=7 + len(carried),
    )(where, *blocks, wq, wo, cosine, sine, gains, seg_col, seg_row, mods, picks, *carried)
    n = len(outs)
    return list(result[:4]), list(result[4:n]), list(result[n : n + 7]), list(result[n + 7 :])


def add_parts(refs):
    total = refs[0][...].astype(F32)
    for ref in refs[1:]:
        total += ref[...].astype(F32)
    return total


def after_attention(parts, state, mods, picks):
    dims = state.shape

    def body(p0, p1, p2, p3, state_ref, mods_ref, picks_ref, mlp_ref, attended_ref, after_ref):
        picked = picks_ref[...]
        attended = add_parts((p0, p1, p2, p3))
        attended_ref[...] = attended.astype(BF)
        after = state_ref[...].astype(F32) + token_mod(picked, mods_ref, 2) * attended
        after_ref[...] = after
        normed = after * inverse_rms(after)
        mlp_ref[...] = (normed * (1.0 + token_mod(picked, mods_ref, 4)) + token_mod(picked, mods_ref, 3)).astype(BF)

    return call(
        body,
        [shape(dims, BF), shape(dims, BF), shape(dims, F32)],
        [VM] * 7,
        name="after_attention",
        limit=8,
    )(*parts, state, mods, picks)


def after_mlp(parts, after, mods, picks, mods_next):
    dims = after.shape

    def body(p0, p1, p2, p3, after_ref, mods_ref, picks_ref, next_ref, in_ref, projected_ref, state_ref):
        picked = picks_ref[...]
        projected = add_parts((p0, p1, p2, p3))
        output = after_ref[...] + token_mod(picked, mods_ref, 5) * projected
        low = output.astype(BF)
        state_ref[...] = low
        state = low.astype(F32)
        normed = state * inverse_rms(state)
        in_ref[...] = (normed * (1.0 + token_mod(picked, next_ref, 1)) + token_mod(picked, next_ref, 0)).astype(BF)
        projected_ref[...] = projected.astype(BF)

    return call(
        body,
        [shape(dims, BF)] * 3,
        [VM] * 8,
        name="after_mlp",
        limit=8,
    )(*parts, after, mods, picks, mods_next)


def last_output(parts, after, mods, picks):
    dims = after.shape

    def body(p0_in, p1, p2, p3, after_in, mods_ref, picks_ref, output_ref, projected_out, p0, after_ref, projected_ref, sems, out_sems):
        copies = load([(p0_in, p0), (after_in, after_ref)], sems)
        gate2 = token_mod(picks_ref[...], mods_ref, 5)
        finish(copies)
        projected = add_parts((p0, p1, p2, p3))
        projected_ref[...] = projected.astype(BF)
        kept = load([(projected_ref, projected_out)], out_sems)
        output_ref[...] = after_ref[...] + gate2 * projected
        finish(kept)

    return call(
        body,
        [shape(dims, F32), shape(dims, BF)],
        [HB] + [VM] * 3 + [HB] + [VM] * 2,
        [
            pltpu.VMEM(dims, BF),
            pltpu.VMEM(dims, F32),
            pltpu.VMEM(dims, BF),
            pltpu.SemaphoreType.DMA((2,)),
            pltpu.SemaphoreType.DMA((1,)),
        ],
        name="last_output",
        limit=8,
        kept=1,
    )(*parts, after, mods, picks)


def mlp_forward(layer, blocks, weights, section, carried):
    gu_own, gu_got, wd_own, wd_got = weights
    hidden_size, width = wd_own.shape
    share = blocks[0].shape[0]
    rows = share * 4
    chunk = 2 * LANE
    chunks = hidden_size // chunk

    def body(sec_ref, b0, b1, b2, b3, gu_a, gu_b, wd_a, wd_b, attended_ref, after_ref,
             p0, p1, p2, p3, hid_out, c1_out, c2_out, a_out, attended_out, after_out, p0_out,
             a_ref, gu_ref, wd_ref, hid_ref, c1_ref, c2_ref, sems, out_sems, carried_sems):
        own = sec_ref[0] == layer
        for j in range(chunks):
            at = pl.ds(j * chunk, chunk)
            for i in range(2):
                fetch(own, gu_a.at[i, :, at], gu_b.at[i, :, at], gu_ref.at[i, :, at], sems.at[2 * j + i])
        fetch(own, wd_a, wd_b, wd_ref, sems.at[2 * chunks])
        carried_copies = load([(attended_ref, attended_out), (after_ref, after_out)], carried_sems)
        for k, ref in enumerate((b0, b1, b2, b3)):
            a_ref[k * share : (k + 1) * share] = ref[...]
        for j in range(chunks):
            at = slice(j * chunk, (j + 1) * chunk)
            for i in range(2):
                arrived(gu_a.at[i, :, pl.ds(j * chunk, chunk)], gu_ref.at[i, :, pl.ds(j * chunk, chunk)], sems.at[2 * j + i])
            gate = nn(a_ref[...], gu_ref[0, :, at])
            up = nn(a_ref[...], gu_ref[1, :, at])
            sigma = jax.nn.sigmoid(gate)
            silu = gate * sigma
            hid_ref[:, at] = (silu * up).astype(BF)
            c1_ref[:, at] = (up * (sigma + silu * (1.0 - sigma))).astype(BF)
            c2_ref[:, at] = silu.astype(BF)
        kept = load([(hid_ref, hid_out), (c1_ref, c1_out), (c2_ref, c2_out), (a_ref, a_out)], out_sems)
        arrived(wd_a, wd_ref, sems.at[2 * chunks])
        step = 3 * LANE
        for j in range(width // step):
            at = slice(j * step, (j + 1) * step)
            split_store(nn(hid_ref[...], wd_ref[:, at]), at, (p0, p1, p2, p3))
        kept.append(pltpu.make_async_copy(p0, p0_out, out_sems.at[4]))
        kept[-1].start()
        finish(kept + carried_copies)

    outs = [shape((share, width), BF)] * 4 + [shape((rows, hidden_size), BF)] * 3 + [shape((rows, width), BF)]
    outs += [shape(c.shape, c.dtype) for c in carried] + [shape((share, width), BF)]
    result = call(
        body,
        outs,
        [SM] + [VM] * 4 + [HB] * 4 + [VM] * 2,
        [
            pltpu.VMEM((rows, width), BF),
            pltpu.VMEM(gu_own.shape, BF),
            pltpu.VMEM(wd_own.shape, BF),
        ]
        + [pltpu.VMEM((rows, hidden_size), BF)] * 3
        + [
            pltpu.SemaphoreType.DMA((2 * chunks + 1,)),
            pltpu.SemaphoreType.DMA((5,)),
            pltpu.SemaphoreType.DMA((2,)),
        ],
        name=f"mlp_forward_{layer}",
        kept=7,
    )(section, *blocks, gu_own, gu_got, wd_own, wd_got, *carried)
    return list(result[:4]), list(result[4:8]), list(result[8:])


def mlp_backward(layer, where, blocks, weights, saved, carried):
    gu_own, gu_got, wd_own, wd_got = weights
    c1, c2 = saved
    hidden_size, width = wd_own.shape
    rows = c1.shape[0]
    share = rows // 4
    chunk = 2 * LANE
    chunks = hidden_size // chunk

    def body(where_ref, *refs):
        refs = list(refs)
        in_refs = [refs.pop(0) for _ in blocks]
        gu_a, gu_b, wd_a, wd_b, c1_in, c2_in = refs[:6]
        refs = refs[6:]
        carried_refs = [refs.pop(0) for _ in carried]
        p_refs = [refs.pop(0) for _ in range(3)]
        outs = [refs.pop(0) for _ in range(4)]
        carried_outs = [refs.pop(0) for _ in carried]
        gu_ref, wd_ref, c1_ref, c2_ref, gg_ref, gup_ref, gp_ref, p0, sems, in_sems, out_sems, carried_sems = refs
        own = where_ref[0] == layer
        for j in range(chunks):
            at = pl.ds(j * chunk, chunk)
            fetch(own, wd_a.at[at], wd_b.at[at], wd_ref.at[at], sems.at[j])
        saved_copies = load([(c1_in, c1_ref), (c2_in, c2_ref)], in_sems)
        for i in range(2):
            fetch(own, gu_a.at[i], gu_b.at[i], gu_ref.at[i], sems.at[chunks + i])
        kept = load(list(zip(carried_refs, carried_outs)), carried_sems)
        for k, ref in enumerate(in_refs):
            gp_ref[k * share : (k + 1) * share] = ref[...]

        def keep(i, here):
            kept.append(pltpu.make_async_copy(here, outs[i], out_sems.at[i]))
            kept[-1].start()

        keep(0, gp_ref)
        for j in range(chunks):
            at = slice(j * chunk, (j + 1) * chunk)
            arrived(wd_a.at[pl.ds(j * chunk, chunk)], wd_ref.at[pl.ds(j * chunk, chunk)], sems.at[j])
            grad_hidden = nt(gp_ref[...], wd_ref[at])
            if j == 0:
                finish(saved_copies)
            gg_ref[:, at] = (grad_hidden * c1_ref[:, at].astype(F32)).astype(BF)
            gup_ref[:, at] = (grad_hidden * c2_ref[:, at].astype(F32)).astype(BF)
        keep(1, gg_ref)
        keep(2, gup_ref)
        for i in range(2):
            arrived(gu_a.at[i], gu_ref.at[i], sems.at[chunks + i])
        step = 3 * LANE
        for j in range(width // step):
            at = slice(j * step, (j + 1) * step)
            split_store(nt(gg_ref[...], gu_ref[0, at]) + nt(gup_ref[...], gu_ref[1, at]), at, [p0] + p_refs)
        keep(3, p0)
        finish(kept)

    outs = [shape((share, width), BF)] * 3
    outs += [shape((rows, width), BF)] + [shape((rows, hidden_size), BF)] * 2 + [shape((share, width), BF)]
    outs += [shape(c.shape, c.dtype) for c in carried]
    result = call(
        body,
        outs,
        [SM] + [VM] * 4 + [HB] * 6 + [VM] * len(carried),
        [
            pltpu.VMEM(gu_own.shape, BF),
            pltpu.VMEM(wd_own.shape, BF),
        ]
        + [pltpu.VMEM((rows, hidden_size), BF)] * 4
        + [
            pltpu.VMEM((rows, width), BF),
            pltpu.VMEM((share, width), BF),
            pltpu.SemaphoreType.DMA((chunks + 2,)),
            pltpu.SemaphoreType.DMA((2,)),
            pltpu.SemaphoreType.DMA((4,)),
            pltpu.SemaphoreType.DMA((max(1, len(carried)),)),
        ],
        name=f"mlp_backward_{layer}",
        kept=4 + len(carried),
    )(where, *blocks, gu_own, gu_got, wd_own, wd_got, c1, c2, *carried)
    return list(result[:3]), list(result[3:6]), list(result[6:])


def mlp_backward_last(layer, where, cotangent, weights, saved, mods, picks):
    gu_own, gu_got, wd_own, wd_got = weights
    hidden, c1, c2, mlp_in = saved
    hidden_size, width = wd_own.shape
    rows = c1.shape[0]
    share = rows // 4
    chunk = 2 * LANE
    chunks = hidden_size // chunk
    step = 3 * LANE
    size = hidden_size

    def body(where_ref, cot_in, gu_a, gu_b, wd_a, wd_b, hid_in, c1_in, c2_in, a_in, mods_ref, picks_ref, *refs):
        refs = list(refs)
        p_refs = [refs.pop(0) for _ in range(3)]
        (out, p0_out, p0, gu_ref, wd_ref, c1_ref, c2_ref, gg_ref, gup_ref, hid_ref, gp_ref, a_ref, full_ref,
         sems, in_sems, cot_sems, out_sems) = refs
        own = where_ref[0] == layer
        cot_copies = load(rows_of(cot_in, where_ref, gp_ref), cot_sems)
        for j in range(chunks):
            at = pl.ds(j * chunk, chunk)
            fetch(own, wd_a.at[at], wd_b.at[at], wd_ref.at[at], sems.at[j])
        ins = load([(c1_in, c1_ref), (c2_in, c2_ref), (hid_in, hid_ref), (a_in, a_ref)], in_sems)
        for i in range(2):
            fetch(own, gu_a.at[i], gu_b.at[i], gu_ref.at[i], sems.at[chunks + i])
        kept = []
        finish(cot_copies)
        gp_ref[...] = (gp_ref[...].astype(F32) * token_mod(picks_ref[...], mods_ref, 5)).astype(BF)
        for j in range(chunks):
            at = slice(j * chunk, (j + 1) * chunk)
            arrived(wd_a.at[pl.ds(j * chunk, chunk)], wd_ref.at[pl.ds(j * chunk, chunk)], sems.at[j])
            grad_hidden = nt(gp_ref[...], wd_ref[at])
            if j == 0:
                finish(ins[:2])
            gg_ref[:, at] = (grad_hidden * c1_ref[:, at].astype(F32)).astype(BF)
            gup_ref[:, at] = (grad_hidden * c2_ref[:, at].astype(F32)).astype(BF)
        finish(ins[2:])
        for j in range(width // step):
            at = slice(j * step, (j + 1) * step)
            left = a_ref[:, at]
            full_ref[at, :size] = tn(left, gg_ref[...]).astype(BF)
            full_ref[at, size : 2 * size] = tn(left, gup_ref[...]).astype(BF)
            full_ref[at, 2 * size :] = tn(gp_ref[:, at], hid_ref[...]).astype(BF)
            here = pl.ds(j * step, step)
            kept.append(pltpu.make_async_copy(full_ref.at[here], out.at[here], out_sems.at[j]))
            kept[-1].start()
        for i in range(2):
            arrived(gu_a.at[i], gu_ref.at[i], sems.at[chunks + i])
        for j in range(width // step):
            at = slice(j * step, (j + 1) * step)
            split_store(nt(gg_ref[...], gu_ref[0, at]) + nt(gup_ref[...], gu_ref[1, at]), at, [p0] + p_refs)
        kept += load([(p0, p0_out)], cot_sems)
        finish(kept)

    outs = [shape((share, width), BF)] * 3 + [shape((width, 3 * size), BF), shape((share, width), BF)]
    result = call(
        body,
        outs,
        [SM] + [HB] * 9 + [VM] * 2,
        [
            pltpu.VMEM((share, width), BF),
            pltpu.VMEM(gu_own.shape, BF),
            pltpu.VMEM(wd_own.shape, BF),
        ]
        + [pltpu.VMEM((rows, hidden_size), BF)] * 5
        + [
            pltpu.VMEM((rows, width), BF),
            pltpu.VMEM((rows, width), BF),
            pltpu.VMEM((width, 3 * size), BF),
            pltpu.SemaphoreType.DMA((chunks + 2,)),
            pltpu.SemaphoreType.DMA((4,)),
            pltpu.SemaphoreType.DMA((4,)),
            pltpu.SemaphoreType.DMA((width // step,)),
        ],
        name=f"mlp_backward_{layer}",
        kept=2,
        limit=32,
    )(where, cotangent, gu_own, gu_got, wd_own, wd_got, hidden, c1, c2, mlp_in, mods, picks)
    return [result[4]] + list(result[:3]), result[3]


def mlp_weight_grads(mlp_in, grads, hidden):
    grad_projected, grad_gate, grad_up = grads
    rows, width = grad_projected.shape
    size = hidden.shape[1]
    step = 3 * LANE

    def body(a_in, gg_in, gu_in, gp_in, hid_in, *refs):
        out, a_ref, gg_ref, gu_ref, gp_ref, hid_ref, full_ref, in_sems, sems = refs
        ins = load([(a_in, a_ref), (gg_in, gg_ref), (gu_in, gu_ref), (gp_in, gp_ref), (hid_in, hid_ref)], in_sems)
        kept = []
        finish(ins[:2])
        for j in range(width // step):
            at = slice(j * step, (j + 1) * step)
            left = a_ref[:, at]
            full_ref[at, :size] = tn(left, gg_ref[...]).astype(BF)
            if j == 0:
                ins[2].wait()
            full_ref[at, size : 2 * size] = tn(left, gu_ref[...]).astype(BF)
            if j == 0:
                finish(ins[3:])
            full_ref[at, 2 * size :] = tn(gp_ref[:, at], hid_ref[...]).astype(BF)
            here = pl.ds(j * step, step)
            kept.append(pltpu.make_async_copy(full_ref.at[here], out.at[here], sems.at[j]))
            kept[-1].start()
        finish(kept)

    result = call(
        body,
        [shape((width, 3 * size), BF)],
        [HB] * 5,
        [pltpu.VMEM((rows, width), BF)]
        + [pltpu.VMEM((rows, size), BF)] * 2
        + [
            pltpu.VMEM((rows, width), BF),
            pltpu.VMEM((rows, size), BF),
            pltpu.VMEM((width, 3 * size), BF),
            pltpu.SemaphoreType.DMA((5,)),
            pltpu.SemaphoreType.DMA((width // step,)),
        ],
        name="mlp_weight_grads",
        kept=1,
    )(mlp_in, grad_gate, grad_up, grad_projected, hidden)
    return result[0]


def attention_backward(layer, blocks, weights, saved, tables, grad_after):
    wq, wo = weights
    cosine, sine, gains, seg_col, seg_row = tables
    rows, padded = saved[0].shape
    width = wo.shape[2]
    heads = padded // LANE
    share = rows // 4
    scale = HEAD**-0.5
    QB = 512

    def body(b0, b1, b2, b3, wq_in, wo_in, qraw_in, kraw_in, qrot_in, krot_in, v_in,
             cos_ref, sin_ref, gain_ref, segc_ref, segr_ref, grad_ref,
             p1, p2, p3, g_out, ga_out, p0_out, ggain_out, grad_out,
             wq_ref, wo_ref, qraw_ref, kraw_ref, qrot_ref, krot_ref, v_ref, mask_ref,
             ga_ref, gmix_ref, gq_ref, gk_ref, g_ref, p0, ggain_ref, sems, in_sems):
        ins = [(wo_in.at[layer], wo_ref)]
        ins += [(qrot_in, qrot_ref), (krot_in, krot_ref), (v_in, v_ref), (qraw_in, qraw_ref), (kraw_in, kraw_ref)]
        ins += [(wq_in.at[layer, i], wq_ref.at[i]) for i in range(3)]
        ins = load(ins, in_sems)
        for k, ref in enumerate((b0, b1, b2, b3)):
            ga_ref[k * share : (k + 1) * share] = ref[...]
        kept = []

        def keep(here, there):
            kept.append(pltpu.make_async_copy(here, there, sems.at[len(kept)]))
            kept[-1].start()

        keep(ga_ref, ga_out)
        keep(grad_ref, grad_out)
        mask_ref[...] = jnp.where(segc_ref[...] == segr_ref[...], 1.0, 0.0).astype(BF)
        ins[0].wait()
        gmix_ref[...] = nt(ga_ref[...], wo_ref[...]).astype(BF)
        finish(ins[1:4])
        for h in range(heads):
            at = slice(h * LANE, (h + 1) * LANE)
            for j in range(rows // QB):
                at_rows = slice(j * QB, (j + 1) * QB)
                query = qrot_ref[at_rows, at]
                grad_mixed = gmix_ref[at_rows, at]
                scores = nt(krot_ref[:, at], query) * scale
                grown = (jnp.exp(scores).astype(BF) * mask_ref[:, at_rows]).astype(F32)
                weights_t = grown * (1.0 / jnp.sum(grown, axis=0, keepdims=True))
                grad_weights = nt(v_ref[:, at], grad_mixed)
                add_v = nn(weights_t.astype(BF), grad_mixed)
                product = weights_t * grad_weights
                delta = jnp.sum(product, axis=0, keepdims=True)
                grad_scores = (product - weights_t * delta).astype(BF)
                gq_ref[at_rows, at] = tn(grad_scores, krot_ref[:, at])
                add_k = nn(grad_scores, query)
                total_v = add_v if j == 0 else total_v + add_v
                total_k = add_k if j == 0 else total_k + add_k
            gk_ref[:, at] = total_k
            g_ref[:, 2 * padded + h * LANE : 2 * padded + (h + 1) * LANE] = total_v.astype(BF)
        cos = cos_ref[...]
        sin = sin_ref[...]
        finish(ins[4:6])
        ggain_ref[...] = jnp.zeros_like(ggain_ref)
        for i, (raw_ref, grad_ref) in enumerate(((qraw_ref, gq_ref), (kraw_ref, gk_ref))):
            gain = gain_ref[2 * layer + i : 2 * layer + i + 1]
            gain_sum = jnp.zeros((1, LANE), F32)
            for h in range(heads):
                at = slice(h * LANE, (h + 1) * LANE)
                raw = raw_ref[:, at].astype(F32)
                inverse = head_inverse(raw)
                normed = raw * inverse
                turned = unrotate(grad_ref[:, at], cos, sin) * scale
                product = turned * normed
                gain_sum += jnp.sum(product, axis=0, keepdims=True)
                back = inverse * (turned * gain - normed * head_mean(product * gain))
                g_ref[:, i * padded + h * LANE : i * padded + (h + 1) * LANE] = back.astype(BF)
            ggain_ref[i : i + 1] = gain_sum
        keep(g_ref, g_out)
        keep(ggain_ref, ggain_out)
        finish(ins[6:])
        step = 3 * LANE
        for j in range(width // step):
            at = slice(j * step, (j + 1) * step)
            total = nt(g_ref[:, :padded], wq_ref[0, at])
            total += nt(g_ref[:, padded : 2 * padded], wq_ref[1, at])
            total += nt(g_ref[:, 2 * padded :], wq_ref[2, at])
            split_store(total, at, (p0, p1, p2, p3))
        keep(p0, p0_out)
        finish(kept)

    outs = [shape((share, width), BF)] * 3
    outs += [shape((rows, 3 * padded), BF), shape((rows, width), BF), shape((share, width), BF), shape((8, LANE), F32)]
    outs += [shape(grad_after.shape, F32)]
    result = call(
        body,
        outs,
        [VM] * 4 + [HB] * 7 + [VM] * 6,
        [
            pltpu.VMEM((3, width, padded), BF),
            pltpu.VMEM((padded, width), BF),
        ]
        + [pltpu.VMEM((rows, padded), BF)] * 5
        + [
            pltpu.VMEM((rows, rows), BF),
            pltpu.VMEM((rows, width), BF),
            pltpu.VMEM((rows, padded), BF),
            pltpu.VMEM((rows, padded), F32),
            pltpu.VMEM((rows, padded), F32),
            pltpu.VMEM((rows, 3 * padded), BF),
            pltpu.VMEM((share, width), BF),
            pltpu.VMEM((8, LANE), F32),
            pltpu.SemaphoreType.DMA((5,)),
            pltpu.SemaphoreType.DMA((9,)),
        ],
        name=f"attention_backward_{layer}",
        limit=32,
        kept=5,
    )(*blocks, wq, wo, *saved[:5], cosine, sine, gains, seg_col, seg_row, grad_after)
    return list(result[:3]), list(result[3:])


def attention_weight_grads(attention_in, grads, mixed, grad_attended, place):
    rows, width = attention_in.shape
    padded, narrow = place.shape
    step = 3 * LANE


    def body(a_in, g_in, mixed_in, ga_in, place_ref, out, a_ref, g_ref, mixed_ref, ga_ref, right_ref, full_ref, in_sems, sems):
        ins = load([(g_in, g_ref), (mixed_in, mixed_ref), (a_in, a_ref), (ga_in, ga_ref)], in_sems)
        finish(ins[:2])
        for i in range(3):
            right_ref[i] = nn(g_ref[:, i * padded : (i + 1) * padded], place_ref[...]).astype(BF)
        right_ref[3] = nn(mixed_ref[...], place_ref[...]).astype(BF)
        finish(ins[2:])
        kept = []
        for j in range(width // step):
            at = slice(j * step, (j + 1) * step)
            left = a_ref[:, at]
            for i in range(3):
                full_ref[at, i * narrow : (i + 1) * narrow] = tn(left, right_ref[i]).astype(BF)
            full_ref[at, 3 * narrow :] = tn(ga_ref[:, at], right_ref[3]).astype(BF)
            here = pl.ds(j * step, step)
            kept.append(pltpu.make_async_copy(full_ref.at[here], out.at[here], sems.at[j]))
            kept[-1].start()
        finish(kept)

    result = call(
        body,
        [shape((width, 4 * narrow), BF)],
        [HB] * 4 + [FREE],
        [
            pltpu.VMEM((rows, width), BF),
            pltpu.VMEM((rows, 3 * padded), BF),
            pltpu.VMEM((rows, padded), BF),
            pltpu.VMEM((rows, width), BF),
            pltpu.VMEM((4, rows, narrow), BF),
            pltpu.VMEM((width, 4 * narrow), BF),
            pltpu.SemaphoreType.DMA((4,)),
            pltpu.SemaphoreType.DMA((width // step,)),
        ],
        name="attention_weight_grads",
        kept=1,
    )(attention_in, grads, mixed, grad_attended, place)
    return result[0]


def own_rows(whole, where_ref, here):
    return rows_of(whole, where_ref, here) if len(whole.shape) == 3 else [(whole, here)]


def back_of_mlp(where, parts, grad_out, after, attended, projected, mods, picks):
    dims = after.shape

    def body(where_ref, p0_in, p1, p2, p3, g_in, after_in, attended_in, projected_in, mods_ref, picks_ref,
             ga_ref, grad_ref, sums_out,
             p0, g_ref, after_ref, attended_ref, projected_ref, sums_ref, sems, out_sems):
        pairs = [(p0_in, p0), (after_in, after_ref)] + own_rows(g_in, where_ref, g_ref)
        ins = load(pairs + [(attended_in, attended_ref), (projected_in, projected_ref)], sems)
        picked = picks_ref[...]
        scale2 = token_mod(picked, mods_ref, 4)
        gate1 = token_mod(picked, mods_ref, 2)
        finish(ins[:2])
        grad_in = add_parts((p0, p1, p2, p3))
        after = after_ref[...]
        inverse = inverse_rms(after)
        normed = after * inverse
        finish(ins[2:])
        g = g_ref[...].astype(F32)
        grad_after = g + norm_back(grad_in * (1.0 + scale2), normed, inverse)
        sums_ref[0] = image_sums(picked, grad_after * attended_ref[...].astype(F32))
        sums_ref[1] = image_sums(picked, grad_in)
        sums_ref[2] = image_sums(picked, grad_in * normed)
        sums_ref[3] = image_sums(picked, g * projected_ref[...].astype(F32))
        kept = load([(sums_ref, sums_out)], out_sems)
        grad_ref[...] = grad_after
        ga_ref[...] = (grad_after * gate1).astype(BF)
        finish(kept)

    return call(
        body,
        [shape(dims, BF), shape(dims, F32), shape((4, picks.shape[1], dims[1]), F32)],
        [SM, HB] + [VM] * 3 + [HB] * 4 + [VM] * 2,
        [
            pltpu.VMEM(dims, BF),
            pltpu.VMEM(dims, BF),
            pltpu.VMEM(dims, F32),
            pltpu.VMEM(dims, BF),
            pltpu.VMEM(dims, BF),
            pltpu.VMEM((4, picks.shape[1], dims[1]), F32),
            pltpu.SemaphoreType.DMA((5,)),
            pltpu.SemaphoreType.DMA((1,)),
        ],
        name="back_of_mlp",
        limit=10,
        kept=1,
    )(where, *parts, grad_out, after, attended, projected, mods, picks)


def back_of_attention(where, parts, grad_after, state, mods, picks, mods_below):
    first = mods_below is None
    dims = grad_after.shape

    def body(where_ref, p0_in, p1, p2, p3, grad_in_ref, state_in, mods_ref, picks_ref, *refs):
        refs = list(refs)
        below_ref = None if first else refs.pop(0)
        sums_ref = refs.pop(0)
        gp_ref = None if first else refs.pop(0)
        out_ref, p0, grad_ref, state_ref, sems = refs
        ins = load([(p0_in, p0), (grad_in_ref, grad_ref)] + own_rows(state_in, where_ref, state_ref), sems)
        picked = picks_ref[...]
        scale1 = token_mod(picked, mods_ref, 1)
        finish(ins)
        grad_in = add_parts((p0, p1, p2, p3))
        state = state_ref[...].astype(F32)
        inverse = inverse_rms(state)
        normed = state * inverse
        grad_state = grad_ref[...] + norm_back(grad_in * (1.0 + scale1), normed, inverse)
        out_ref[...] = grad_state.astype(out_ref.dtype)
        if not first:
            gp_ref[...] = (grad_state.astype(BF).astype(F32) * token_mod(picked, below_ref, 5)).astype(BF)
        sums_ref[0] = image_sums(picked, grad_in)
        sums_ref[1] = image_sums(picked, grad_in * normed)

    outs = [shape((2, picks.shape[1], dims[1]), F32)] + ([shape(dims, F32)] if first else [shape(dims, BF)] * 2)
    extra = () if first else (mods_below,)
    return call(
        body,
        outs,
        [SM, HB] + [VM] * 3 + [HB] * 2 + [VM] * (2 + len(extra)),
        [
            pltpu.VMEM(dims, BF),
            pltpu.VMEM(dims, F32),
            pltpu.VMEM(dims, BF),
            pltpu.SemaphoreType.DMA((3,)),
        ],
        name="back_of_attention",
        limit=10,
    )(where, *parts, grad_after, state, mods, picks, *extra)


def exchange(value, axis, k):
    return lax.ppermute(value, axis, [(i, i ^ k) for i in range(lax.axis_size(axis))])


def send_parts(parts):
    got = {k: exchange(parts[k], "tensor", k) for k in (3, 1, 2)}
    return [parts[0], got[1], got[2], got[3]]


def gather_blocks(own):
    got = {k: exchange(own, "tensor", k) for k in (3, 1, 2)}
    return [own, got[1], got[2], got[3]]


def group_sum(value, axis):
    k = 1
    while k < lax.axis_size(axis):
        value = value + exchange(value, axis, k)
        k *= 2
    return value


def gather_dp(value):
    count = lax.axis_size("dp")
    if count > 4:
        return lax.all_gather(value, "dp", axis=0)
    me = lax.axis_index("dp")
    got = [value] + [exchange(value, "dp", k) for k in range(1, count)]
    stacked = jnp.stack(got)
    return jnp.stack([lax.dynamic_index_in_dim(stacked, me ^ j, 0, keepdims=False) for j in range(count)])


def head_places(heads):
    place = np.zeros((heads * HEAD, heads * LANE), np.float32)
    for h in range(heads):
        for j in range(HEAD):
            place[h * HEAD + j, h * LANE + (j // HALF) * (LANE // 2) + j % HALF] = 1.0
    return place


def shards(
    inputs,
    cotangent,
    conditioning,
    lengths,
    positions,
    modulator,
    projections,
    norm_gains,
    out_weight,
    gate_up,
    down_weight,
):
    section = lax.axis_index("section")
    other = 1 - section
    tensor = lax.axis_index("tensor")
    data = lax.axis_index("dp")
    micro, _, width = inputs.shape
    rows = inputs.shape[1]
    group = lax.axis_size("tensor")
    share = rows // group
    items = lengths.shape[2]
    narrow = projections.shape[3]
    heads = narrow // HEAD
    columns = modulator.shape[2]
    sec = section.reshape(1).astype(jnp.int32)

    where = jnp.stack([section, tensor]).astype(jnp.int32)
    is_first = section == 0

    where = jnp.stack([section, tensor]).astype(jnp.int32)
    is_first = section == 0
    place = jnp.asarray(head_places(heads), BF)
    place_one = jnp.asarray(head_places(1), F32)

    own = (jnp.swapaxes(projections[0], 1, 2), out_weight[0])
    got = [exchange(value, "section", 1) for value in own]
    got_gains = exchange(norm_gains[0], "section", 1)
    scaled, part = modulation_part(conditioning, jnp.swapaxes(modulator[0], 0, 1))
    pieces = gather_blocks(part)
    quarter = HEAD // 4
    rates = 10000.0 ** (-jnp.arange(quarter).astype(F32) / quarter)
    rates = jnp.concatenate([rates, rates, jnp.zeros(LANE // 2 - HALF, F32)])[:, None]
    where_late, part = lax.optimization_barrier((where, part))
    cosine, sine, seg_col, seg_row, picks, picks_own = prepare_tables(where_late, lengths, positions, rates)
    wq, wo = prepare_weights(where_late, own, place)
    pieces, got, cosine, wq = lax.optimization_barrier((pieces, got, cosine, wq))
    mods_own, mods_send, gains = modulation_rows([part] + pieces[1:], (norm_gains[0], got_gains), where, place_one)
    mods_got = exchange(mods_send, "section", 1)
    gu_send, wd_send, mods_got = lax.optimization_barrier((gate_up[0], down_weight[0], mods_got))
    mods = [jnp.where(is_first, mods_own, mods_got), jnp.where(is_first, mods_got, mods_own)]
    gu_got = exchange(gu_send, "section", 1)
    wd_got = exchange(wd_send, "section", 1)
    mlp_weights = (gate_up[0], gu_got, down_weight[0], wd_got)
    wq, mods_first = lax.optimization_barrier((wq, mods[0]))
    mods[0] = mods_first
    wq, wo = prepare_weights(where, got, place, (wq, wo), 1)
    tables = (cosine, sine, gains, seg_col, seg_row)

    cache = []
    attention_blocks = [inputs]
    carried = ()
    for l in range(2):
        partial, state, saved, kept = attention_forward(
            l, where, attention_blocks, (wq, wo), tables, mods[l], picks, carried
        )
        parts = send_parts(partial)
        if l == 0:
            state = state[0]
            wq, mixed = lax.optimization_barrier((wq, saved[5]))
            saved[5] = mixed
            wq, wo = prepare_weights(where, got, place, (wq, wo), 0)
            parts, wq = lax.optimization_barrier((parts, wq))
        else:
            cache[0].append(kept[0])
            state = carried[1]
            state_kept = kept[1]
        mlp_in, attended, after = after_attention(parts, state, mods[l], picks_own)
        partial, mlp_saved, kept = mlp_forward(l, gather_blocks(mlp_in), mlp_weights, sec, (attended, after))
        parts = send_parts(partial)
        cache.append([saved, mlp_saved] + kept)
        if l == 0:
            attention_in, projected, state = after_mlp(parts, after, mods[0], picks_own, mods[1])
            carried = (projected, state)
            attention_blocks = gather_blocks(attention_in)

    item_sums = [None, None]
    gain_sums = [None, None]
    shares = [None, None]

    def data_sum(value):
        return lax.psum_scatter(value, ("dp", "section"), scatter_dimension=0, tiled=True)

    for l in (1, 0):
        saved, (hidden, c1, c2, mlp_in), attended, after, own_partial = cache[l][:5]
        mixed, attention_in = saved[5:]
        if l == 1:
            partial, mlp_grads = mlp_backward_last(l, where, cotangent, mlp_weights, cache[1][1], mods[1], picks)
            parts, partial[1:], mlp_grads = lax.optimization_barrier((parts, partial[1:], mlp_grads))
            output, projected = last_output([own_partial] + parts[1:], after, mods[1], picks_own)
            mlp_share = data_sum(mlp_grads)
            parts = send_parts(partial)
            grad_out = cotangent
        else:
            partial, grads, kept = mlp_backward(
                l, where, grad_blocks, mlp_weights, (c1, c2), [grad_out]
            )
            projected = cache[0][5]
            grad_out = kept[1]
            mlp_grads = mlp_weight_grads(mlp_in, grads, hidden)
            parts, mlp_grads, earlier = lax.optimization_barrier(
                (send_parts([kept[0]] + partial)[1:], mlp_grads, shares[1][1])
            )
            parts = [kept[0]] + parts
            shares[1] = (shares[1][0], earlier)
            mlp_share = data_sum(mlp_grads)
        grad_attended, grad_after, sums2 = back_of_mlp(
            where, parts, grad_out, after, attended, projected, mods[l], picks_own
        )
        blocks = gather_blocks(grad_attended)
        partial, kept = attention_backward(l, blocks, (wq, wo), saved, tables, grad_after)
        grads, grad_attended, own, gain_sums[l], grad_after = kept
        attention_grads = attention_weight_grads(attention_in, grads, mixed, grad_attended, place.T)
        parts, attention_grads, mlp_share = lax.optimization_barrier(
            (send_parts([own] + partial)[1:], attention_grads, mlp_share)
        )
        parts = [own] + parts
        attention_share = data_sum(attention_grads)
        if l == 1:
            sums1, grad_projected, grad_out = back_of_attention(
                where, parts, grad_after, state_kept, mods[1], picks_own, mods[0]
            )
            grad_blocks = gather_blocks(grad_projected)
        else:
            sums1, grad_state = back_of_attention(where, parts, grad_after, inputs, mods[0], picks_own, None)
        item_sums[l] = jnp.concatenate([sums1, sums2], axis=0)
        shares[l] = (mlp_share, attention_share)

    mine = jnp.where(is_first, grad_state, output)
    theirs = exchange(jnp.where(is_first, output, grad_state), "section", 1)
    results = jnp.stack([jnp.where(is_first, mine, theirs), jnp.where(is_first, theirs, mine)])

    def joined(which):
        mine = jnp.where(is_first, shares[0][which], shares[1][which])
        theirs = exchange(jnp.where(is_first, shares[1][which], shares[0][which]), "section", 1)
        low = jnp.where(is_first, mine, theirs)
        high = jnp.where(is_first, theirs, mine)
        return jnp.concatenate([low, high], axis=0).astype(F32)

    size = down_weight.shape[1]
    mlp_grads = joined(0)
    grad_pair = jnp.stack([mlp_grads[:, :size], mlp_grads[:, size : 2 * size]])
    grad_down = mlp_grads[:, 2 * size :].T
    attention_grads = joined(1)
    grad_qkv = jnp.stack([attention_grads[:, i * narrow : (i + 1) * narrow] for i in range(3)])
    grad_out_w = attention_grads[:, 3 * narrow :].T

    sums = jnp.stack(item_sums)[:, :, :items].transpose(0, 2, 1, 3).reshape(2 * items, 6 * width)
    gain_parts = jnp.concatenate([jnp.concatenate([g[0:1], g[1:2]], axis=1) for g in gain_sums])
    gain_parts = jnp.pad(gain_parts, ((0, 2 * items - 2), (0, 0)))
    pieces = [
        jnp.concatenate([lax.dynamic_slice_in_dim(sums, (tensor ^ k) * columns, columns, 1), gain_parts], axis=1)
        for k in range(group)
    ]
    got = send_parts(pieces)
    total = (got[0] + got[1]) + (got[2] + got[3])
    layers = total[:, :columns].reshape(2, items, columns).astype(BF).astype(F32)
    gain_rows = jnp.pad(total[:2, None, columns:], ((0, 0), (0, items - 1), (0, 0)))
    layers = jnp.concatenate([layers, gain_rows], axis=2)
    mine = jnp.where(is_first, layers[0], layers[1])
    theirs = exchange(jnp.where(is_first, layers[1], layers[0]), "section", 1)
    gain_total = mine[0:1, columns:] + theirs[0:1, columns:]
    mods_grad = jnp.concatenate(
        [jnp.where(is_first, mine, theirs)[:, :columns], jnp.where(is_first, theirs, mine)[:, :columns]]
    )
    packed = jnp.concatenate(
        [mods_grad, scaled.astype(F32), jnp.pad(gain_total, ((0, 2 * items - 1), (0, 0)))], axis=1
    )
    gathered = gather_dp(packed)
    all_mods = gathered[:, :, :columns].astype(BF)
    deep = width // lax.axis_size("dp")
    scaled_share = lax.dynamic_slice_in_dim(gathered, columns + data * deep, deep, 2).astype(BF)
    grad_ada = jnp.einsum("nid,nic->dc", scaled_share, all_mods, preferred_element_type=F32)
    gain_total = jnp.sum(gathered[:, 0, columns + width :], axis=0)
    cond_value = conditioning[:, 0].astype(F32)
    sigma = jax.nn.sigmoid(cond_value)
    cond_part = jnp.einsum("ic,dc->id", mods_grad.astype(BF), modulator[0], preferred_element_type=F32)
    cond_part = cond_part.reshape(micro, items, width) * sigma * (1.0 + cond_value * (1.0 - sigma))
    grad_cond = group_sum(group_sum(cond_part, "section"), "tensor")
    half = LANE // 2
    gain_total = gain_total.reshape(2, LANE)
    grad_gains = jnp.concatenate([gain_total[:, :HALF], gain_total[:, half : half + HALF]], axis=1)
    return (
        grad_ada[None],
        grad_qkv[None],
        grad_gains[None],
        grad_out_w[None],
        grad_pair[None],
        grad_down[None],
        grad_cond[:, None],
        results[None],
    )


def solution(mesh):
    return jax.shard_map(
        shards,
        mesh=mesh,
        in_specs=(
            P(None, "dp", None),
            P(None, "dp", None),
            P(None, "dp", None, None),
            P(None, "dp", None),
            P(None, None, "dp"),
            P("section", None, "tensor"),
            P("section", None, None, "tensor"),
            P("section", None, None),
            P("section", "tensor", None),
            P("section", None, None, "tensor"),
            P("section", "tensor", None),
        ),
        out_specs=(
            P("section", "dp", "tensor"),
            P("section", None, "dp", "tensor"),
            P("section", None, None),
            P("section", "tensor", "dp"),
            P("section", None, "dp", "tensor"),
            P("section", "tensor", "dp"),
            P(None, "dp", None, None),
            P("section", None, ("dp", "tensor"), None),
        ),
        check_vma=False,
    )
```

time: 420 us -> 395 us (0.940)
  starting transfers between devices: 81.5 us -> 60 us
    ppermute x72 -> x64, starting transfers between devices: 80.8 us -> 59.3 us  [exchange(): lax.ppermute(value, axis, [(i, i ^ k) for i in range(lax.axis_size(axis))])]
    ppermute x72 -> x64, waiting for transfers between devices: 130 us -> 124 us  [exchange(): lax.ppermute(value, axis, [(i, i ^ k) for i in range(lax.axis_size(axis))])]
    unnamed x67 -> x34, local copies, waits for them, and re-layouts: 7.63 us -> 3.01 us
  transfers between devices with their start and end apart: 76 -> 68, of which waited for: 43 -> 37; matrix products, arithmetic and copies ran while one was open for 3% -> 4% of each run, Pallas kernels for 25% -> 29%
where the time goes in v3:
time: 395 us; the launch traced here: 389 us
  waiting for transfers between devices  150 us (38%)
  Pallas kernels  142 us (36%)
  starting transfers between devices  60 us (15%)
  between operations  14.8 us (4%)
  other arithmetic  9.79 us (2%)
  local copies, waits for them, and re-layouts  8.34 us (2%)
  matrix products  4.76 us (1%)
    pallas_call x25, Pallas kernels, run(): return kernel(*placed)  142 us
    ppermute x64, waiting for transfers between devices, exchange(): lax.ppermute(value, axis, [(i, i ^ k) for i in range(lax.axis_size(axis))])  124 us
    ppermute x64, starting transfers between devices, exchange(): lax.ppermute(value, axis, [(i, i ^ k) for i in range(lax.axis_size(axis))])  59.3 us
    reduce_scatter x4, waiting for transfers between devices, data_sum(): lax.psum_scatter(value, ('dp', 'section'), scatter_dimension=0, tiled=True)  25.5 us
  transfers between devices with their start and end apart: 68, of which 37 were waited for; matrix products, arithmetic and copies ran while one was open for 4% of the time, Pallas kernels for 29%

profile of v3, /device:TPU:1, one launch (start us, length us, event | category | flops | bytes accessed | tf_op | source)
XLA Modules:
  0.0 389.4 jit_solution(5661554540750179830)
XLA Ops:
  15.4 6.2 %prepare_weights.3 = (bf16[2,3,1152,512]{3,2,1,0:T(8,128)(2,1)}, bf16[2,512,1152]{2,1,0:T(8,128)(2,1)}) custom-call(s32[2]{0:T(128)S(1)} %pad_add_fusion.where_ref, bf16[3,288,1152]{2,1,0:T(8,128)(2,1)} %bitcast.96, bf16[288,1152]{1,0:T(8,128)(2,1)} %bitcast.100, bf16[288,512]{1,0:T(8,128)(2,1)S(1)} %copy-done), custom_call_target="tpu_custom_call" | custom-call | flops 1000 | bytes 1000 | tf_op jit(solution)/shard_map/prepare_weights/pallas_call | solution.py:56
  26.7 6.6 %prepare_weights.4 = (bf16[2,3,1152,512]{3,2,1,0:T(8,128)(2,1)}, bf16[2,512,1152]{2,1,0:T(8,128)(2,1)}) custom-call(s32[2]{0:T(128)S(1)} %pad_add_fusion.where_ref, bf16[3,288,1152]{2,1,0:T(8,128)(2,1)} %collective-permute-done.3.wq_in, bf16[288,1152]{1,0:T(8,128)(2,1)} %collective-permute-done.4.wo_in, ...), custom_call_target="tpu_custom_call", output_to_operand_aliasing={{0}: (4, {}), {1}: (5, {})} | custom-call | flops 1000 | bytes 1000 | tf_op jit(solution)/shard_map/prepare_weights/pallas_call | solution.py:56
  33.3 11.7 %attention_forward_0.1 = (bf16[128,1152]{1,0:T(8,128)(2,1)S(1)}, bf16[128,1152]{1,0:T(8,128)(2,1)S(1)}, bf16[128,1152]{1,0:T(8,128)(2,1)S(1)}, bf16[128,1152]{1,...) custom-call(s32[2]{0:T(128)S(1)} %pad_add_fusion.where_ref, ...), custom_call_target="tpu_custom_call" | custom-call | flops 1000 | bytes 1000 | tf_op jit(solution)/shard_map/attention_forward_0/pallas_call | solution.py:56
  52.3 8.5 %collective-permute-done.10.p2 = bf16[128,1152]{1,0:T(8,128)(2,1)S(1)} collective-permute-done((bf16[128,1152]{1,0:T(8,128)(2,1)S(1)}, bf16[128,1152]{1,0:T(8,128)(2,1)S(1)}, u32[]{:S(2)}, u32[]{:S(2)}) %collective-permute-start.10) | collective-permute-done | bytes 294944 | tf_op jit(solution)/shard_map/ppermute | solution.py:1030
  72.3 6.4 %mlp_forward_0.1 = (bf16[128,1152]{1,0:T(8,128)(2,1)S(1)}, bf16[128,1152]{1,0:T(8,128)(2,1)S(1)}, bf16[128,1152]{1,0:T(8,128)(2,1)S(1)}, bf16[128,1152]{1,0:T(8,...) custom-call(s32[1]{0:T(128)} %bitcast.sec_ref, ...), custom_call_target="tpu_custom_call" | custom-call | flops 1000 | bytes 1000 | tf_op jit(solution)/shard_map/mlp_forward_0/pallas_call | solution.py:56
  84.4 7.5 %collective-permute-done.16.p2 = bf16[128,1152]{1,0:T(8,128)(2,1)S(1)} collective-permute-done((bf16[128,1152]{1,0:T(8,128)(2,1)S(1)}, bf16[128,1152]{1,0:T(8,128)(2,1)S(1)}, u32[]{:S(2)}, u32[]{:S(2)}) %collective-permute-start.16) | collective-permute-done | bytes 294944 | tf_op jit(solution)/shard_map/ppermute | solution.py:1030
  102.1 9.8 %attention_forward_1.1 = (bf16[128,1152]{1,0:T(8,128)(2,1)S(1)}, bf16[128,1152]{1,0:T(8,128)(2,1)S(1)}, bf16[128,1152]{1,0:T(8,128)(2,1)S(1)}, bf16[128,1152]{1,...) custom-call(s32[2]{0:T(128)S(1)} %pad_add_fusion.where_ref, ...), custom_call_target="tpu_custom_call" | custom-call | flops 1000 | bytes 1000 | tf_op jit(solution)/shard_map/attention_forward_1/pallas_call | solution.py:56
  117.8 8.2 %collective-permute-done.22.p2 = bf16[128,1152]{1,0:T(8,128)(2,1)S(1)} collective-permute-done((bf16[128,1152]{1,0:T(8,128)(2,1)S(1)}, bf16[128,1152]{1,0:T(8,128)(2,1)S(1)}, u32[]{:S(2)}, u32[]{:S(2)}) %collective-permute-start.22) | collective-permute-done | bytes 294944 | tf_op jit(solution)/shard_map/ppermute | solution.py:1030
  136.4 7.4 %mlp_forward_1.1 = (bf16[128,1152]{1,0:T(8,128)(2,1)}, bf16[128,1152]{1,0:T(8,128)(2,1)S(1)}, bf16[128,1152]{1,0:T(8,128)(2,1)S(1)}, bf16[128,1152]{1,0:T(8,128)...) custom-call(s32[1]{0:T(128)} %bitcast.sec_ref, ...), custom_call_target="tpu_custom_call" | custom-call | flops 1000 | bytes 1000 | tf_op jit(solution)/shard_map/mlp_forward_1/pallas_call | solution.py:56
  146.4 14.7 %mlp_backward_1.1 = (bf16[128,1152]{1,0:T(8,128)(2,1)}, bf16[128,1152]{1,0:T(8,128)(2,1)S(1)}, bf16[128,1152]{1,0:T(8,128)(2,1)S(1)}, bf16[1152,2304]{1,0:T(8,128)(2,1)}, bf16[128,1152]{1,0:T(8,128)(2,1)}) custom-call(s32[2]{0:T(128)S(1)} %pad_add_fusion.where_ref, bf16[2,512,1152]{2,1,0:T(8,128)(2,1)} %g_in.1, bf16[2,1152,768]{2,1,0:T(8,128)(2,1)} %bitcast.87, ...), custom_call_target="tpu_custom_call" | custom-call | flops 1000 | bytes 1000 | tf_op jit(solution)/shard_map/mlp_backward_1/pallas_call | solution.py:56
  178.8 5.6 %collective-permute-done.35.b3 = bf16[128,1152]{1,0:T(8,128)(2,1)S(1)} collective-permute-done((bf16[128,1152]{1,0:T(8,128)(2,1)S(1)}, bf16[128,1152]{1,0:T(8,128)(2,1)S(1)}, u32[]{:S(2)}, u32[]{:S(2)}) %collective-permute-start.35) | collective-permute-done | bytes 294944 | tf_op jit(solution)/shard_map/ppermute | solution.py:1030
  187.5 12.7 %attention_backward_1.1 = (bf16[128,1152]{1,0:T(8,128)(2,1)}, bf16[128,1152]{1,0:T(8,128)(2,1)}, bf16[128,1152]{1,0:T(8,128)(2,1)S(1)}, bf16[512,1536]{1,0:T(8,1...) custom-call(bf16[128,1152]{1,0:T(8,128)(2,1)S(1)} %get-tuple-element.2, ...), custom_call_target="tpu_custom_call" | custom-call | flops 1000 | bytes 1000 | tf_op jit(solution)/shard_map/attention_backward_1/pallas_call | solution.py:56
  202.9 6.7 %attention_weight_grads.2 = bf16[1152,1152]{1,0:T(8,128)(2,1)} custom-call(bf16[512,1152]{1,0:T(8,128)(2,1)} %get-tuple-element.256.a_in, bf16[512,1536]{1,0:T(8,128)(2,1)} %get-tuple-element.257.g_in, bf16[512,512]{1,0:T(8,128)(2,1)} %get-tuple-element.258.mixed_in, bf16[512,1152]{1,0:T(8,128)(2,1)} %get-tuple-element.259.ga_in, bf16[512,288]{1,0:T(8,128)(2,1)S(1)} %copy-done.1), custom_call_target="tpu_custom_call" | custom-call | flops 1000 | bytes 1000 | tf_op jit(solution)/shard_map/attention_weight_grads/pallas_call | solution.py:56
  209.6 5.8 %collective-permute-done.37.p2 = bf16[128,1152]{1,0:T(8,128)(2,1)S(1)} collective-permute-done((bf16[128,1152]{1,0:T(8,128)(2,1)}, bf16[128,1152]{1,0:T(8,128)(2,1)S(1)}, u32[]{:S(2)}, u32[]{:S(2)}) %collective-permute-start.37) | collective-permute-done | bytes 294944 | tf_op jit(solution)/shard_map/ppermute | solution.py:1030
  228.4 8.8 %collective-permute-done.40.refs_2_ = bf16[128,1152]{1,0:T(8,128)(2,1)S(1)} collective-permute-done((bf16[128,1152]{1,0:T(8,128)(2,1)S(1)}, bf16[128,1152]{1,0:T(8,128)(2,1)S(1)}, u32[]{:S(2)}, u32[]{:S(2)}) %collective-permute-start.40) | collective-permute-done | bytes 294944 | tf_op jit(solution)/shard_map/ppermute | solution.py:1030
  237.2 10.2 %mlp_backward_0.1 = (bf16[128,1152]{1,0:T(8,128)(2,1)}, bf16[128,1152]{1,0:T(8,128)(2,1)}, bf16[128,1152]{1,0:T(8,128)(2,1)S(1)}, bf16[512,1152]{1,0:T(8,128)(2,...) custom-call(s32[2]{0:T(128)S(1)} %pad_add_fusion.where_ref, ...), custom_call_target="tpu_custom_call" | custom-call | flops 1000 | bytes 1000 | tf_op jit(solution)/shard_map/mlp_backward_0/pallas_call | solution.py:56
  250.4 6.4 %mlp_weight_grads.1 = bf16[1152,2304]{1,0:T(8,128)(2,1)} custom-call(bf16[512,1152]{1,0:T(8,128)(2,1)} %get-tuple-element.274.a_in, bf16[512,768]{1,0:T(8,128)(2,1)} %get-tuple-element.275.gg_in, bf16[512,768]{1,0:T(8,128)(2,1)} %get-tuple-element.276.gu_in, bf16[512,1152]{1,0:T(8,128)(2,1)} %get-tuple-element.277.gp_in, ...), custom_call_target="tpu_custom_call" | custom-call | flops 1000 | bytes 1000 | tf_op jit(solution)/shard_map/mlp_weight_grads/pallas_call | solution.py:56
  256.8 5.8 %collective-permute-done.44.p3 = bf16[128,1152]{1,0:T(8,128)(2,1)S(1)} collective-permute-done((bf16[128,1152]{1,0:T(8,128)(2,1)S(1)}, bf16[128,1152]{1,0:T(8,128)(2,1)S(1)}, u32[]{:S(2)}, u32[]{:S(2)}) %collective-permute-start.44) | collective-permute-done | bytes 294944 | tf_op jit(solution)/shard_map/ppermute | solution.py:1030
  274.4 9.3 %collective-permute-done.46.b2 = bf16[128,1152]{1,0:T(8,128)(2,1)S(1)} collective-permute-done((bf16[128,1152]{1,0:T(8,128)(2,1)S(1)}, bf16[128,1152]{1,0:T(8,128)(2,1)S(1)}, u32[]{:S(2)}, u32[]{:S(2)}) %collective-permute-start.46) | collective-permute-done | bytes 294944 | tf_op jit(solution)/shard_map/ppermute | solution.py:1030
  283.7 12.6 %attention_backward_0.1 = (bf16[128,1152]{1,0:T(8,128)(2,1)}, bf16[128,1152]{1,0:T(8,128)(2,1)}, bf16[128,1152]{1,0:T(8,128)(2,1)S(1)}, bf16[512,1536]{1,0:T(8,1...) custom-call(bf16[128,1152]{1,0:T(8,128)(2,1)S(1)} %get-tuple-element.2, ...), custom_call_target="tpu_custom_call" | custom-call | flops 1000 | bytes 1000 | tf_op jit(solution)/shard_map/attention_backward_0/pallas_call | solution.py:56
  299.0 6.8 %attention_weight_grads.3 = bf16[1152,1152]{1,0:T(8,128)(2,1)} custom-call(bf16[512,1152]{1,0:T(8,128)(2,1)} %get-tuple-element.298.a_in, bf16[512,1536]{1,0:T(8,128)(2,1)} %get-tuple-element.299.g_in, bf16[512,512]{1,0:T(8,128)(2,1)} %get-tuple-element.300.mixed_in, bf16[512,1152]{1,0:T(8,128)(2,1)} %get-tuple-element.301.ga_in, bf16[512,288]{1,0:T(8,128)(2,1)S(1)} %copy-done.1), custom_call_target="tpu_custom_call" | custom-call | flops 1000 | bytes 1000 | tf_op jit(solution)/shard_map/attention_weight_grads/pallas_call | solution.py:56
  310.5 12.6 %reduce-scatter.9.cloned.1.call-done = bf16[144,2304]{1,0:T(8,128)(2,1)} async-done(((bf16[1152,2304]{1,0:T(8,128)(2,1)}), bf16[144,2304]{1,0:T(8,128)(2,1)}) %reduce-scatter.9.cloned.1.call-update) | async-done | bytes 663568 | tf_op jit(solution)/shard_map/reduce_scatter | solution.py:1160
  350.8 7.4 %collective-permute-done.56 = f32[8,3136]{1,0:T(8,128)S(1)} collective-permute-done((f32[8,3136]{1,0:T(8,128)S(1)}, f32[8,3136]{1,0:T(8,128)S(1)}, u32[]{:S(2)}, u32[]{:S(2)}) %collective-permute-start.56) | collective-permute-done | bytes 100384 | tf_op jit(solution)/shard_map/ppermute | solution.py:1030
  364.8 9.7 %reduce-scatter.11.cloned.1.call-done = bf16[144,1152]{1,0:T(8,128)(2,1)} async-done(((bf16[1152,1152]{1,0:T(8,128)(2,1)}), bf16[144,1152]{1,0:T(8,128)(2,1)}) %reduce-scatter.11.cloned.1.call-update) | async-done | bytes 331792 | tf_op jit(solution)/shard_map/reduce_scatter | solution.py:1160
  (228 shorter events, 167.3 us)
Async XLA Ops:
  7.2 211.6 %reduce-scatter.5.cloned.1.call-start = ((), (), s32[]{:S(2)}) async-start(), calls=%async_computation.4 | async-start | bytes 5971968 | tf_op jit(solution)/shard_map/reduce_scatter | solution.py:1160
  7.2 16.8 %collective-permute-start.3 = (bf16[3,288,1152]{2,1,0:T(8,128)(2,1)}, bf16[3,288,1152]{2,1,0:T(8,128)(2,1)}, u32[]{:S(2)}, u32[]{:S(2)}) collective-permute-start(bf16[3,288,1152]{2,1,0:T(8,128)(2,1)} %bitcast.95), channel_id=1, source_target_pairs={{0,16},{16,0},{1,17},{17,1},{2,18},{18,2},{3,19},{19,3},{4,20},{20... | collective-permute-start | bytes 5971976 | tf_op jit(solution)/shard_map/ppermute | solution.py:1030
  7.3 16.7 %collective-permute-start.4 = (bf16[288,1152]{1,0:T(8,128)(2,1)}, bf16[288,1152]{1,0:T(8,128)(2,1)}, u32[]{:S(2)}, u32[]{:S(2)}) collective-permute-start(bf16[288,1152]{1,0:T(8,128)(2,1)} %bitcast.99), channel_id=1, source_target_pairs={{0,16},{16,0},{1,17},{17,1},{2,18},{18,2},{3,19},{19,3},{4,20},{20... | collective-permute-start | bytes 1990664 | tf_op jit(solution)/shard_map/ppermute | solution.py:1030
  26.1 45.0 %collective-permute-start.7 = (bf16[2,1152,768]{2,1,0:T(8,128)(2,1)}, bf16[2,1152,768]{2,1,0:T(8,128)(2,1)}, u32[]{:S(2)}, u32[]{:S(2)}) collective-permute-start(bf16[2,1152,768]{2,1,0:T(8,128)(2,1)} %bitcast.84), channel_id=1, source_target_pairs={{0,16},{16,0},{1,17},{17,1},{2,18},{18,2},{3,19},{19,3},{4,20},{20... | collective-permute-start | bytes 10616840 | tf_op jit(solution)/shard_map/ppermute | solution.py:1030
  26.3 44.8 %collective-permute-start.8 = (bf16[768,1152]{1,0:T(8,128)(2,1)S(1)}, bf16[768,1152]{1,0:T(8,128)(2,1)S(1)}, u32[]{:S(2)}, u32[]{:S(2)}) collective-permute-start(bf16[768,1152]{1,0:T(8,128)(2,1)S(1)} %bitcast.93), channel_id=1, source_target_pairs={{0,16},{16,0},{1,17},{17,1},{2,18},{18,2},{3,19},{19,3},{4,20},{20... | collective-permute-start | bytes 5308424 | tf_op jit(solution)/shard_map/ppermute | solution.py:1030
  46.7 14.2 %collective-permute-start.10 = (bf16[128,1152]{1,0:T(8,128)(2,1)S(1)}, bf16[128,1152]{1,0:T(8,128)(2,1)S(1)}, u32[]{:S(2)}, u32[]{:S(2)}) collective-permute-start(bf16[128,1152]{1,0:T(8,128)(2,1)S(1)} %get-tuple-element.193), channel_id=1, source_target_pairs={{0,8},{4,12},{8,0},{12,4},{1,9},{5,13},{9,1},{13,5},{2,10},{6,14},... | collective-permute-start | bytes 884744 | tf_op jit(solution)/shard_map/ppermute | solution.py:1030
  47.9 12.9 %collective-permute-start.11 = (bf16[128,1152]{1,0:T(8,128)(2,1)S(1)}, bf16[128,1152]{1,0:T(8,128)(2,1)S(1)}, u32[]{:S(2)}, u32[]{:S(2)}) collective-permute-start(bf16[128,1152]{1,0:T(8,128)(2,1)S(1)} %get-tuple-element.194), channel_id=1, source_target_pairs={{0,12},{4,8},{8,4},{12,0},{1,13},{5,9},{9,5},{13,1},{2,14},{6,10},... | collective-permute-start | bytes 884744 | tf_op jit(solution)/shard_map/ppermute | solution.py:1030
  143.7 17.4 %collective-permute-start.27 = (bf16[128,1152]{1,0:T(8,128)(2,1)S(1)}, bf16[128,1152]{1,0:T(8,128)(2,1)S(1)}, u32[]{:S(2)}, u32[]{:S(2)}) collective-permute-start(bf16[128,1152]{1,0:T(8,128)(2,1)S(1)} %get-tuple-element.228), channel_id=1, source_target_pairs={{0,4},{4,0},{8,12},{12,8},{1,5},{5,1},{9,13},{13,9},{2,6},{6,2},{1... | collective-permute-start | bytes 884744 | tf_op jit(solution)/shard_map/ppermute | solution.py:1030
  143.8 17.4 %collective-permute-start.28 = (bf16[128,1152]{1,0:T(8,128)(2,1)S(1)}, bf16[128,1152]{1,0:T(8,128)(2,1)S(1)}, u32[]{:S(2)}, u32[]{:S(2)}) collective-permute-start(bf16[128,1152]{1,0:T(8,128)(2,1)S(1)} %get-tuple-element.229), channel_id=1, source_target_pairs={{0,8},{4,12},{8,0},{12,4},{1,9},{5,13},{9,1},{13,5},{2,10},{6,14},... | collective-permute-start | bytes 884744 | tf_op jit(solution)/shard_map/ppermute | solution.py:1030
  144.4 16.8 %collective-permute-start.29 = (bf16[128,1152]{1,0:T(8,128)(2,1)S(1)}, bf16[128,1152]{1,0:T(8,128)(2,1)S(1)}, u32[]{:S(2)}, u32[]{:S(2)}) collective-permute-start(bf16[128,1152]{1,0:T(8,128)(2,1)S(1)} %get-tuple-element.230), channel_id=1, source_target_pairs={{0,12},{4,8},{8,4},{12,0},{1,13},{5,9},{9,5},{13,1},{2,14},{6,10},... | collective-permute-start | bytes 884744 | tf_op jit(solution)/shard_map/ppermute | solution.py:1030
  161.2 101.4 %reduce-scatter.7.cloned.1.call-start = ((), (), s32[]{:S(2)}) async-start(), calls=%async_computation.5 | async-start | bytes 2985984 | tf_op jit(solution)/shard_map/reduce_scatter | solution.py:1160
  201.1 14.4 %collective-permute-start.37 = (bf16[128,1152]{1,0:T(8,128)(2,1)}, bf16[128,1152]{1,0:T(8,128)(2,1)S(1)}, u32[]{:S(2)}, u32[]{:S(2)}) collective-permute-start(bf16[128,1152]{1,0:T(8,128)(2,1)} %get-tuple-element.254), channel_id=1, source_target_pairs={{0,8},{4,12},{8,0},{12,4},{1,9},{5,13},{9,1},{13,5},{2,10},{6,14},... | collective-permute-start | bytes 884744 | tf_op jit(solution)/shard_map/ppermute | solution.py:1030
  202.2 13.3 %collective-permute-start.38 = (bf16[128,1152]{1,0:T(8,128)(2,1)S(1)}, bf16[128,1152]{1,0:T(8,128)(2,1)S(1)}, u32[]{:S(2)}, u32[]{:S(2)}) collective-permute-start(bf16[128,1152]{1,0:T(8,128)(2,1)S(1)} %get-tuple-element.255), channel_id=1, source_target_pairs={{0,12},{4,8},{8,4},{12,0},{1,13},{5,9},{9,5},{13,1},{2,14},{6,10},... | collective-permute-start | bytes 884744 | tf_op jit(solution)/shard_map/ppermute | solution.py:1030
  218.7 104.3 %reduce-scatter.9.cloned.1.call-start = ((), (), s32[]{:S(2)}) async-start(), calls=%async_computation.6 | async-start | bytes 5971968 | tf_op jit(solution)/shard_map/reduce_scatter | solution.py:1160
  223.9 13.3 %collective-permute-start.40 = (bf16[128,1152]{1,0:T(8,128)(2,1)S(1)}, bf16[128,1152]{1,0:T(8,128)(2,1)S(1)}, u32[]{:S(2)}, u32[]{:S(2)}) collective-permute-start(bf16[128,1152]{1,0:T(8,128)(2,1)S(1)} %get-tuple-element.266.refs_0_), channel_id=1, source_target_pairs={{0,8},{4,12},{8,0},{12,4},{1,9},{5,13},{9,1},{13,5},{2,10},{6,14},... | collective-permute-start | bytes 884744 | tf_op jit(solution)/shard_map/ppermute | solution.py:1030
  224.2 13.0 %collective-permute-start.39 = (bf16[128,1152]{1,0:T(8,128)(2,1)S(1)}, bf16[128,1152]{1,0:T(8,128)(2,1)S(1)}, u32[]{:S(2)}, u32[]{:S(2)}) collective-permute-start(bf16[128,1152]{1,0:T(8,128)(2,1)S(1)} %get-tuple-element.266.refs_0_), channel_id=1, source_target_pairs={{0,4},{4,0},{8,12},{12,8},{1,5},{5,1},{9,13},{13,9},{2,6},{6,2},{1... | collective-permute-start | bytes 884744 | tf_op jit(solution)/shard_map/ppermute | solution.py:1030
  249.4 13.2 %collective-permute-start.44 = (bf16[128,1152]{1,0:T(8,128)(2,1)S(1)}, bf16[128,1152]{1,0:T(8,128)(2,1)S(1)}, u32[]{:S(2)}, u32[]{:S(2)}) collective-permute-start(bf16[128,1152]{1,0:T(8,128)(2,1)S(1)} %get-tuple-element.273), channel_id=1, source_target_pairs={{0,12},{4,8},{8,4},{12,0},{1,13},{5,9},{9,5},{13,1},{2,14},{6,10},... | collective-permute-start | bytes 884744 | tf_op jit(solution)/shard_map/ppermute | solution.py:1030
  262.7 111.8 %reduce-scatter.11.cloned.1.call-start = ((), (), s32[]{:S(2)}) async-start(), calls=%async_computation.7 | async-start | bytes 2985984 | tf_op jit(solution)/shard_map/reduce_scatter | solution.py:1160
  268.6 15.0 %collective-permute-start.46 = (bf16[128,1152]{1,0:T(8,128)(2,1)S(1)}, bf16[128,1152]{1,0:T(8,128)(2,1)S(1)}, u32[]{:S(2)}, u32[]{:S(2)}) collective-permute-start(bf16[128,1152]{1,0:T(8,128)(2,1)S(1)} %get-tuple-element.287.b0), channel_id=1, source_target_pairs={{0,8},{4,12},{8,0},{12,4},{1,9},{5,13},{9,1},{13,5},{2,10},{6,14},... | collective-permute-start | bytes 884744 | tf_op jit(solution)/shard_map/ppermute | solution.py:1030
  268.6 15.0 %collective-permute-start.45 = (bf16[128,1152]{1,0:T(8,128)(2,1)S(1)}, bf16[128,1152]{1,0:T(8,128)(2,1)S(1)}, u32[]{:S(2)}, u32[]{:S(2)}) collective-permute-start(bf16[128,1152]{1,0:T(8,128)(2,1)S(1)} %get-tuple-element.287.b0), channel_id=1, source_target_pairs={{0,4},{4,0},{8,12},{12,8},{1,5},{5,1},{9,13},{13,9},{2,6},{6,2},{1... | collective-permute-start | bytes 884744 | tf_op jit(solution)/shard_map/ppermute | solution.py:1030
  337.6 24.1 %collective-permute-start.63 = (f32[128,1152]{1,0:T(8,128)}, f32[128,1152]{1,0:T(8,128)S(1)}, u32[]{:S(2)}, u32[]{:S(2)}) collective-permute-start(f32[128,1152]{1,0:T(8,128)} %broadcast_select_fusion.8), channel_id=1, source_target_pairs={{0,16},{16,0},{1,17},{17,1},{2,18},{18,2},{3,19},{19,3},{4,20},{20... | collective-permute-start | bytes 1769480 | tf_op jit(solution)/shard_map/ppermute | solution.py:1030
  342.1 16.1 %collective-permute-start.56 = (f32[8,3136]{1,0:T(8,128)S(1)}, f32[8,3136]{1,0:T(8,128)S(1)}, u32[]{:S(2)}, u32[]{:S(2)}) collective-permute-start(f32[8,3136]{1,0:T(8,128)S(1)} %concatenate.60), channel_id=1, source_target_pairs={{0,2},{1,3},{2,0},{3,1},{4,6},{5,7},{6,4},{7,5},{8,10},{9,11},{10,... | collective-permute-start | bytes 301064 | tf_op jit(solution)/shard_map/ppermute | solution.py:1030
  342.1 16.1 %collective-permute-start.55 = (f32[8,3136]{1,0:T(8,128)S(1)}, f32[8,3136]{1,0:T(8,128)S(1)}, u32[]{:S(2)}, u32[]{:S(2)}) collective-permute-start(f32[8,3136]{1,0:T(8,128)S(1)} %concatenate.60), channel_id=1, source_target_pairs={{0,1},{1,0},{2,3},{3,2},{4,5},{5,4},{6,7},{7,6},{8,9},{9,8},{10,11... | collective-permute-start | bytes 301064 | tf_op jit(solution)/shard_map/ppermute | solution.py:1030
  348.3 14.6 %collective-permute-start.59 = (bf16[144,2304]{1,0:T(8,128)(2,1)S(1)}, bf16[144,2304]{1,0:T(8,128)(2,1)S(1)}, u32[]{:S(2)}, u32[]{:S(2)}) collective-permute-start(bf16[144,2304]{1,0:T(8,128)(2,1)S(1)} %broadcast_select_fusion.2), channel_id=1, source_target_pairs={{0,16},{16,0},{1,17},{17,1},{2,18},{18,2},{3,19},{19,3},{4,20},{20... | collective-permute-start | bytes 1990664 | tf_op jit(solution)/shard_map/ppermute | solution.py:1030
  (60 other events, 471.7 us)
Sparse Core Ops, SparseCore 0:
  161.3 57.3 reduce-scatter.4
  221.0 35.8 reduce-scatter.6
  262.8 60.2 reduce-scatter.8
  329.2 45.2 reduce-scatter.10

commit v4 on v3

--- a/solution.py
+++ b/solution.py
@@ -95,6 +95,10 @@
         there = pl.ds(pl.multiple_of((where_ref[1] ^ k) * share, LANE), share)
         pairs.append((whole.at[where_ref[0], there], here.at[pl.ds(k * share, share)]))
     return pairs
+
+
+def own_rows(whole, where_ref, here):
+    return rows_of(whole, where_ref, here) if len(whole.shape) == 3 else [(whole, here)]
 
 
 def inverse_rms(value):
@@ -275,13 +279,10 @@
             for i in range(3):
                 copies[i].wait()
                 wide_ref[i] = tn(wq_ref[i], place_ref[...]).astype(BF)
-                outs.append(pltpu.make_async_copy(wide_ref.at[i], wq_out.at[layer, i], out_sems.at[i]))
-                outs[-1].start()
+                outs += load([(wide_ref.at[i], wq_out.at[layer, i])], out_sems.at[pl.ds(i, 1)])
             copies[3].wait()
             tall_ref[...] = tn(place_ref[...], wo_ref[...]).astype(BF)
-            outs.append(pltpu.make_async_copy(tall_ref, wo_out.at[layer], out_sems.at[3]))
-            outs[-1].start()
-            finish(outs)
+            finish(outs + load([(tall_ref, wo_out.at[layer])], out_sems.at[pl.ds(3, 1)]))
 
         if only is None:
             make(section)
@@ -309,6 +310,36 @@
         kept=2,
         aliases={} if begun is None else {4: 0, 5: 1},
     )(*args)
+
+
+def last_ahead(where, cotangent, down_own, down_got, mods, picks):
+    rows = picks.shape[0]
+    size, width = down_own.shape
+
+    def body(where_ref, cot_in, wd_a, wd_b, mods_ref, picks_ref, gp_out, gh_out, gp_ref, gh_ref, wd_ref, sems):
+        copies = load(rows_of(cot_in, where_ref, gp_ref), sems)
+        fetch(where_ref[0] == 1, wd_a, wd_b, wd_ref, sems.at[4])
+        finish(copies)
+        gp_ref[...] = (gp_ref[...].astype(F32) * token_mod(picks_ref[...], mods_ref, 5)).astype(BF)
+        outs = load([(gp_ref, gp_out)], sems)
+        arrived(wd_a, wd_ref, sems.at[4])
+        gh_ref[...] = nt(gp_ref[...], wd_ref[...]).astype(BF)
+        finish(outs + load([(gh_ref, gh_out)], sems.at[pl.ds(1, 1)]))
+
+    return call(
+        body,
+        [shape((rows, width), BF), shape((rows, size), BF)],
+        [SM] + [HB] * 3 + [VM] * 2,
+        [
+            pltpu.VMEM((rows, width), BF),
+            pltpu.VMEM((rows, size), BF),
+            pltpu.VMEM((size, width), BF),
+            pltpu.SemaphoreType.DMA((5,)),
+        ],
+        name="last_ahead",
+        limit=16,
+        kept=2,
+    )(where, cotangent, down_own, down_got, mods, picks)
 
 
 def attention_forward(layer, where, blocks, weights, tables, mods, picks, carried=()):
@@ -476,34 +507,55 @@
 def last_output(parts, after, mods, picks):
     dims = after.shape
 
-    def body(p0_in, p1, p2, p3, after_in, mods_ref, picks_ref, output_ref, projected_out, p0, after_ref, projected_ref, sems, out_sems):
+    def body(p0_in, p1, p2, p3, after_in, mods_ref, picks_ref, output_ref, p0, after_ref, sems):
         copies = load([(p0_in, p0), (after_in, after_ref)], sems)
         gate2 = token_mod(picks_ref[...], mods_ref, 5)
         finish(copies)
-        projected = add_parts((p0, p1, p2, p3))
-        projected_ref[...] = projected.astype(BF)
-        kept = load([(projected_ref, projected_out)], out_sems)
-        output_ref[...] = after_ref[...] + gate2 * projected
-        finish(kept)
+        output_ref[...] = after_ref[...] + gate2 * add_parts((p0, p1, p2, p3))
 
     return call(
         body,
-        [shape(dims, F32), shape(dims, BF)],
+        [shape(dims, F32)],
         [HB] + [VM] * 3 + [HB] + [VM] * 2,
+        [pltpu.VMEM(dims, BF), pltpu.VMEM(dims, F32), pltpu.SemaphoreType.DMA((2,))],
+        name="last_output",
+        limit=8,
+    )(*parts, after, mods, picks)[0]
+
+
+def last_gate_sums(where, parts, cotangent, picks):
+    share, width = parts[0].shape
+    rows = picks.shape[0]
+
+    def body(where_ref, *refs):
+        part_refs = refs[:4]
+        cot_in, picks_ref, sums_out, p_ref, g_ref, sums_ref, sems, cot_sems, out_sems = refs[4:]
+        copies = load([(ref, p_ref.at[pl.ds(k * share, share)]) for k, ref in enumerate(part_refs)], sems)
+        copies += load(rows_of(cot_in, where_ref, g_ref), cot_sems)
+        finish(copies)
+        sums_ref[0] = image_sums(picks_ref[...], g_ref[...].astype(F32) * p_ref[...].astype(F32))
+        finish(load([(sums_ref, sums_out)], out_sems))
+
+    sums = (1, picks.shape[1], width)
+    return call(
+        body,
+        [shape(sums, F32)],
+        [SM] + [HB] * 5 + [VM],
         [
-            pltpu.VMEM(dims, BF),
-            pltpu.VMEM(dims, F32),
-            pltpu.VMEM(dims, BF),
-            pltpu.SemaphoreType.DMA((2,)),
+            pltpu.VMEM((rows, width), BF),
+            pltpu.VMEM((rows, width), BF),
+            pltpu.VMEM(sums, F32),
+            pltpu.SemaphoreType.DMA((4,)),
+            pltpu.SemaphoreType.DMA((4,)),
             pltpu.SemaphoreType.DMA((1,)),
         ],
-        name="last_output",
-        limit=8,
+        name="last_gate_sums",
+        limit=16,
         kept=1,
-    )(*parts, after, mods, picks)
-
-
-def mlp_forward(layer, blocks, weights, section, carried):
+    )(where, *parts, cotangent, picks)[0]
+
+
+def mlp_forward(layer, blocks, weights, section, carried, late):
     gu_own, gu_got, wd_own, wd_got = weights
     hidden_size, width = wd_own.shape
     share = blocks[0].shape[0]
@@ -512,8 +564,15 @@
     chunks = hidden_size // chunk
 
     def body(sec_ref, b0, b1, b2, b3, gu_a, gu_b, wd_a, wd_b, attended_ref, after_ref,
-             p0, p1, p2, p3, hid_out, c1_out, c2_out, a_out, attended_out, after_out, p0_out,
-             a_ref, gu_ref, wd_ref, hid_ref, c1_ref, c2_ref, sems, out_sems, carried_sems):
+             *refs):
+        refs = list(refs)
+        p_refs = [] if late else [refs.pop(0) for _ in range(4)]
+        hid_out, c1_out, c2_out, a_out, attended_out, after_out = refs[:6]
+        refs = refs[6:]
+        p_outs = [refs.pop(0) for _ in range(4)] if late else []
+        a_ref, gu_ref, wd_ref, hid_ref, c1_ref, c2_ref, sems, out_sems, carried_sems = refs[:9]
+        if late:
+            p_refs, p_sems = refs[9:13], refs[13]
         own = sec_ref[0] == layer
         for j in range(chunks):
             at = pl.ds(j * chunk, chunk)
@@ -539,13 +598,14 @@
         step = 3 * LANE
         for j in range(width // step):
             at = slice(j * step, (j + 1) * step)
-            split_store(nn(hid_ref[...], wd_ref[:, at]), at, (p0, p1, p2, p3))
-        kept.append(pltpu.make_async_copy(p0, p0_out, out_sems.at[4]))
-        kept[-1].start()
+            split_store(nn(hid_ref[...], wd_ref[:, at]), at, p_refs)
+        if late:
+            kept += load(list(zip(p_refs, p_outs)), p_sems)
         finish(kept + carried_copies)
 
-    outs = [shape((share, width), BF)] * 4 + [shape((rows, hidden_size), BF)] * 3 + [shape((rows, width), BF)]
-    outs += [shape(c.shape, c.dtype) for c in carried] + [shape((share, width), BF)]
+    parts = [shape((share, width), BF)] * 4
+    outs = ([] if late else parts) + [shape((rows, hidden_size), BF)] * 3 + [shape((rows, width), BF)]
+    outs += [shape(c.shape, c.dtype) for c in carried] + (parts if late else [])
     result = call(
         body,
         outs,
@@ -558,13 +618,17 @@
         + [pltpu.VMEM((rows, hidden_size), BF)] * 3
         + [
             pltpu.SemaphoreType.DMA((2 * chunks + 1,)),
-            pltpu.SemaphoreType.DMA((5,)),
+            pltpu.SemaphoreType.DMA((4,)),
             pltpu.SemaphoreType.DMA((2,)),
-        ],
+        ]
+        + ([pltpu.VMEM((share, width), BF)] * 4 + [pltpu.SemaphoreType.DMA((4,))] if late else []),
         name=f"mlp_forward_{layer}",
-        kept=7,
+        kept=10 if late else 6,
     )(section, *blocks, gu_own, gu_got, wd_own, wd_got, *carried)
-    return list(result[:4]), list(result[4:8]), list(result[8:])
+    result = list(result)
+    partial = result[6:] if late else result[:4]
+    result = result[:6] if late else result[4:]
+    return partial, result[:4], result[4:]
 
 
 def mlp_backward(layer, where, blocks, weights, saved, carried):
@@ -647,42 +711,23 @@
     return list(result[:3]), list(result[3:6]), list(result[6:])
 
 
-def mlp_backward_last(layer, where, cotangent, weights, saved, mods, picks):
-    gu_own, gu_got, wd_own, wd_got = weights
+def mlp_backward_last(layer, ahead, saved):
+    grad_projected, grad_hidden = ahead
     hidden, c1, c2, mlp_in = saved
-    hidden_size, width = wd_own.shape
-    rows = c1.shape[0]
-    share = rows // 4
-    chunk = 2 * LANE
-    chunks = hidden_size // chunk
+    rows, width = grad_projected.shape
+    size = hidden.shape[1]
     step = 3 * LANE
-    size = hidden_size
-
-    def body(where_ref, cot_in, gu_a, gu_b, wd_a, wd_b, hid_in, c1_in, c2_in, a_in, mods_ref, picks_ref, *refs):
-        refs = list(refs)
-        p_refs = [refs.pop(0) for _ in range(3)]
-        (out, p0_out, p0, gu_ref, wd_ref, c1_ref, c2_ref, gg_ref, gup_ref, hid_ref, gp_ref, a_ref, full_ref,
-         sems, in_sems, cot_sems, out_sems) = refs
-        own = where_ref[0] == layer
-        cot_copies = load(rows_of(cot_in, where_ref, gp_ref), cot_sems)
-        for j in range(chunks):
-            at = pl.ds(j * chunk, chunk)
-            fetch(own, wd_a.at[at], wd_b.at[at], wd_ref.at[at], sems.at[j])
-        ins = load([(c1_in, c1_ref), (c2_in, c2_ref), (hid_in, hid_ref), (a_in, a_ref)], in_sems)
-        for i in range(2):
-            fetch(own, gu_a.at[i], gu_b.at[i], gu_ref.at[i], sems.at[chunks + i])
+
+    def body(gp_in, gh_in, hid_in, c1_in, c2_in, a_in, gg_ref, gup_ref, out,
+             gh_ref, c1_ref, c2_ref, hid_ref, gp_ref, a_ref, full_ref, in_sems, out_sems):
+        ins = [(gh_in, gh_ref), (c1_in, c1_ref), (c2_in, c2_ref), (a_in, a_ref), (gp_in, gp_ref), (hid_in, hid_ref)]
+        ins = load(ins, in_sems)
+        finish(ins[:2])
+        gg_ref[...] = gh_ref[...] * c1_ref[...]
+        ins[2].wait()
+        gup_ref[...] = gh_ref[...] * c2_ref[...]
+        finish(ins[3:])
         kept = []
-        finish(cot_copies)
-        gp_ref[...] = (gp_ref[...].astype(F32) * token_mod(picks_ref[...], mods_ref, 5)).astype(BF)
-        for j in range(chunks):
-            at = slice(j * chunk, (j + 1) * chunk)
-            arrived(wd_a.at[pl.ds(j * chunk, chunk)], wd_ref.at[pl.ds(j * chunk, chunk)], sems.at[j])
-            grad_hidden = nt(gp_ref[...], wd_ref[at])
-            if j == 0:
-                finish(ins[:2])
-            gg_ref[:, at] = (grad_hidden * c1_ref[:, at].astype(F32)).astype(BF)
-            gup_ref[:, at] = (grad_hidden * c2_ref[:, at].astype(F32)).astype(BF)
-        finish(ins[2:])
         for j in range(width // step):
             at = slice(j * step, (j + 1) * step)
             left = a_ref[:, at]
@@ -692,39 +737,63 @@
             here = pl.ds(j * step, step)
             kept.append(pltpu.make_async_copy(full_ref.at[here], out.at[here], out_sems.at[j]))
             kept[-1].start()
-        for i in range(2):
-            arrived(gu_a.at[i], gu_ref.at[i], sems.at[chunks + i])
-        for j in range(width // step):
-            at = slice(j * step, (j + 1) * step)
-            split_store(nt(gg_ref[...], gu_ref[0, at]) + nt(gup_ref[...], gu_ref[1, at]), at, [p0] + p_refs)
-        kept += load([(p0, p0_out)], cot_sems)
         finish(kept)
 
-    outs = [shape((share, width), BF)] * 3 + [shape((width, 3 * size), BF), shape((share, width), BF)]
-    result = call(
-        body,
-        outs,
-        [SM] + [HB] * 9 + [VM] * 2,
-        [
-            pltpu.VMEM((share, width), BF),
-            pltpu.VMEM(gu_own.shape, BF),
-            pltpu.VMEM(wd_own.shape, BF),
-        ]
-        + [pltpu.VMEM((rows, hidden_size), BF)] * 5
+    return call(
+        body,
+        [shape((rows, size), BF)] * 2 + [shape((width, 3 * size), BF)],
+        [HB] * 6,
+        [pltpu.VMEM((rows, size), BF)] * 4
         + [
             pltpu.VMEM((rows, width), BF),
             pltpu.VMEM((rows, width), BF),
             pltpu.VMEM((width, 3 * size), BF),
-            pltpu.SemaphoreType.DMA((chunks + 2,)),
-            pltpu.SemaphoreType.DMA((4,)),
-            pltpu.SemaphoreType.DMA((4,)),
+            pltpu.SemaphoreType.DMA((6,)),
             pltpu.SemaphoreType.DMA((width // step,)),
         ],
         name=f"mlp_backward_{layer}",
-        kept=2,
-        limit=32,
-    )(where, cotangent, gu_own, gu_got, wd_own, wd_got, hidden, c1, c2, mlp_in, mods, picks)
-    return [result[4]] + list(result[:3]), result[3]
+        kept=1,
+        limit=24,
+    )(grad_projected, grad_hidden, hidden, c1, c2, mlp_in)
+
+
+def mlp_input_grad(layer, section, grad_gate, grad_up, weights):
+    gu_own, gu_got = weights[:2]
+    rows = grad_gate.shape[0]
+    width = gu_own.shape[1]
+    share = rows // 4
+    step = 3 * LANE
+
+    def body(sec_ref, gg_ref, gup_ref, gu_a, gu_b, p1, p2, p3, p0_out, p0, gu_ref, sems, out_sems):
+        own = sec_ref[0] == layer
+        spans = [pl.ds(j * step, step) for j in range(width // step)]
+        for j, at in enumerate(spans):
+            for i in range(2):
+                fetch(own, gu_a.at[i, at], gu_b.at[i, at], gu_ref.at[i, at], sems.at[2 * j + i])
+        for j, at in enumerate(spans):
+            for i in range(2):
+                arrived(gu_a.at[i, at], gu_ref.at[i, at], sems.at[2 * j + i])
+            here = slice(j * step, (j + 1) * step)
+            split_store(
+                nt(gg_ref[...], gu_ref[0, here]) + nt(gup_ref[...], gu_ref[1, here]), here, (p0, p1, p2, p3)
+            )
+        finish(load([(p0, p0_out)], out_sems))
+
+    result = call(
+        body,
+        [shape((share, width), BF)] * 4,
+        [SM, VM, VM, HB, HB],
+        [
+            pltpu.VMEM((share, width), BF),
+            pltpu.VMEM(gu_own.shape, BF),
+            pltpu.SemaphoreType.DMA((2 * (width // step),)),
+            pltpu.SemaphoreType.DMA((1,)),
+        ],
+        name="mlp_input_grad",
+        kept=1,
+        limit=16,
+    )(section, grad_gate, grad_up, gu_own, gu_got)
+    return [result[3]] + list(result[:3])
 
 
 def mlp_weight_grads(mlp_in, grads, hidden):
@@ -932,18 +1001,18 @@
     return result[0]
 
 
-def own_rows(whole, where_ref, here):
-    return rows_of(whole, where_ref, here) if len(whole.shape) == 3 else [(whole, here)]
-
-
 def back_of_mlp(where, parts, grad_out, after, attended, projected, mods, picks):
     dims = after.shape
-
-    def body(where_ref, p0_in, p1, p2, p3, g_in, after_in, attended_in, projected_in, mods_ref, picks_ref,
-             ga_ref, grad_ref, sums_out,
-             p0, g_ref, after_ref, attended_ref, projected_ref, sums_ref, sems, out_sems):
+    extra = [] if projected is None else [projected]
+    sums = (3 + len(extra), picks.shape[1], dims[1])
+
+    def body(where_ref, p0_in, p1, p2, p3, g_in, after_in, attended_in, *refs):
+        refs = list(refs)
+        extra_refs = [refs.pop(0) for _ in extra]
+        (mods_ref, picks_ref, ga_ref, grad_ref, sums_out,
+         p0, g_ref, after_ref, attended_ref, projected_ref, sums_ref, sems, out_sems) = refs
         pairs = [(p0_in, p0), (after_in, after_ref)] + own_rows(g_in, where_ref, g_ref)
-        ins = load(pairs + [(attended_in, attended_ref), (projected_in, projected_ref)], sems)
+        ins = load(pairs + [(attended_in, attended_ref)] + [(ref, projected_ref) for ref in extra_refs], sems)
         picked = picks_ref[...]
         scale2 = token_mod(picked, mods_ref, 4)
         gate1 = token_mod(picked, mods_ref, 2)
@@ -958,7 +1027,8 @@
         sums_ref[0] = image_sums(picked, grad_after * attended_ref[...].astype(F32))
         sums_ref[1] = image_sums(picked, grad_in)
         sums_ref[2] = image_sums(picked, grad_in * normed)
-        sums_ref[3] = image_sums(picked, g * projected_ref[...].astype(F32))
+        if extra:
+            sums_ref[3] = image_sums(picked, g * projected_ref[...].astype(F32))
         kept = load([(sums_ref, sums_out)], out_sems)
         grad_ref[...] = grad_after
         ga_ref[...] = (grad_after * gate1).astype(BF)
@@ -966,22 +1036,22 @@
 
     return call(
         body,
-        [shape(dims, BF), shape(dims, F32), shape((4, picks.shape[1], dims[1]), F32)],
-        [SM, HB] + [VM] * 3 + [HB] * 4 + [VM] * 2,
+        [shape(dims, BF), shape(dims, F32), shape(sums, F32)],
+        [SM, HB] + [VM] * 3 + [HB] * (3 + len(extra)) + [VM] * 2,
         [
             pltpu.VMEM(dims, BF),
             pltpu.VMEM(dims, BF),
             pltpu.VMEM(dims, F32),
             pltpu.VMEM(dims, BF),
             pltpu.VMEM(dims, BF),
-            pltpu.VMEM((4, picks.shape[1], dims[1]), F32),
+            pltpu.VMEM(sums, F32),
             pltpu.SemaphoreType.DMA((5,)),
             pltpu.SemaphoreType.DMA((1,)),
         ],
         name="back_of_mlp",
         limit=10,
         kept=1,
-    )(where, *parts, grad_out, after, attended, projected, mods, picks)
+    )(where, *parts, grad_out, after, attended, *extra, mods, picks)
 
 
 def back_of_attention(where, parts, grad_after, state, mods, picks, mods_below):
@@ -1030,13 +1100,34 @@
     return lax.ppermute(value, axis, [(i, i ^ k) for i in range(lax.axis_size(axis))])
 
 
-def send_parts(parts):
+def handed_on(value):
+    def body(source, target):
+        target[...] = source[...]
+
+    return call(body, [shape(value.shape, value.dtype)], [VM], name="handed_on", limit=4)(value)[0]
+
+
+def in_order(got, order):
+    for place, k in enumerate(order):
+        for _ in range(len(order) - 1 - place):
+            got[k] = handed_on(got[k])
+
+
+def send_parts(parts, beside=None, whole=False):
     got = {k: exchange(parts[k], "tensor", k) for k in (3, 1, 2)}
-    return [parts[0], got[1], got[2], got[3]]
+    if beside is not None and not whole:
+        got[1], beside = lax.optimization_barrier((got[1], beside))
+    if whole:
+        got, beside = lax.optimization_barrier((got, beside))
+    else:
+        in_order(got, (1, 2, 3))
+    result = [parts[0], got[1], got[2], got[3]]
+    return result if beside is None else (result, beside)
 
 
 def gather_blocks(own):
     got = {k: exchange(own, "tensor", k) for k in (3, 1, 2)}
+    in_order(got, (3, 2, 1))
     return [own, got[1], got[2], got[3]]
 
 
@@ -1132,22 +1223,24 @@
         partial, state, saved, kept = attention_forward(
             l, where, attention_blocks, (wq, wo), tables, mods[l], picks, carried
         )
-        parts = send_parts(partial)
         if l == 0:
             state = state[0]
             wq, mixed = lax.optimization_barrier((wq, saved[5]))
             saved[5] = mixed
             wq, wo = prepare_weights(where, got, place, (wq, wo), 0)
-            parts, wq = lax.optimization_barrier((parts, wq))
+            parts, wq = send_parts(partial, wq)
         else:
+            parts = send_parts(partial)
             cache[0].append(kept[0])
             state = carried[1]
             state_kept = kept[1]
         mlp_in, attended, after = after_attention(parts, state, mods[l], picks_own)
-        partial, mlp_saved, kept = mlp_forward(l, gather_blocks(mlp_in), mlp_weights, sec, (attended, after))
-        parts = send_parts(partial)
+        partial, mlp_saved, kept = mlp_forward(l, gather_blocks(mlp_in), mlp_weights, sec, (attended, after), l == 1)
         cache.append([saved, mlp_saved] + kept)
         if l == 0:
+            where_late, partial[0] = lax.optimization_barrier((where, partial[0]))
+            ahead = last_ahead(where_late, cotangent, down_weight[0], wd_got, mods[1], picks)
+            parts, ahead = send_parts(partial, ahead)
             attention_in, projected, state = after_mlp(parts, after, mods[0], picks_own, mods[1])
             carried = (projected, state)
             attention_blocks = gather_blocks(attention_in)
@@ -1160,26 +1253,26 @@
         return lax.psum_scatter(value, ("dp", "section"), scatter_dimension=0, tiled=True)
 
     for l in (1, 0):
-        saved, (hidden, c1, c2, mlp_in), attended, after, own_partial = cache[l][:5]
+        saved, (hidden, c1, c2, mlp_in), attended, after = cache[l][:4]
         mixed, attention_in = saved[5:]
         if l == 1:
-            partial, mlp_grads = mlp_backward_last(l, where, cotangent, mlp_weights, cache[1][1], mods[1], picks)
-            parts, partial[1:], mlp_grads = lax.optimization_barrier((parts, partial[1:], mlp_grads))
-            output, projected = last_output([own_partial] + parts[1:], after, mods[1], picks_own)
+            last_partial = partial
+            grad_gate, grad_up, mlp_grads = mlp_backward_last(l, ahead, cache[1][1])
             mlp_share = data_sum(mlp_grads)
-            parts = send_parts(partial)
+            partial = mlp_input_grad(l, sec, grad_gate, grad_up, mlp_weights)
+            where_late, partial[0] = lax.optimization_barrier((where, partial[0]))
+            last_sums = last_gate_sums(where_late, last_partial, cotangent, picks)
+            parts, last_sums = send_parts(partial, last_sums, True)
             grad_out = cotangent
+            projected = None
         else:
             partial, grads, kept = mlp_backward(
                 l, where, grad_blocks, mlp_weights, (c1, c2), [grad_out]
             )
-            projected = cache[0][5]
+            projected = cache[0][4]
             grad_out = kept[1]
             mlp_grads = mlp_weight_grads(mlp_in, grads, hidden)
-            parts, mlp_grads, earlier = lax.optimization_barrier(
-                (send_parts([kept[0]] + partial)[1:], mlp_grads, shares[1][1])
-            )
-            parts = [kept[0]] + parts
+            parts, (mlp_grads, earlier) = send_parts([kept[0]] + partial, (mlp_grads, shares[1][1]), True)
             shares[1] = (shares[1][0], earlier)
             mlp_share = data_sum(mlp_grads)
         grad_attended, grad_after, sums2 = back_of_mlp(
@@ -1189,40 +1282,20 @@
         partial, kept = attention_backward(l, blocks, (wq, wo), saved, tables, grad_after)
         grads, grad_attended, own, gain_sums[l], grad_after = kept
         attention_grads = attention_weight_grads(attention_in, grads, mixed, grad_attended, place.T)
-        parts, attention_grads, mlp_share = lax.optimization_barrier(
-            (send_parts([own] + partial)[1:], attention_grads, mlp_share)
-        )
-        parts = [own] + parts
-        attention_share = data_sum(attention_grads)
         if l == 1:
+            parts, (attention_grads, mlp_share) = send_parts([own] + partial, (attention_grads, mlp_share), True)
+            attention_share = data_sum(attention_grads)
             sums1, grad_projected, grad_out = back_of_attention(
                 where, parts, grad_after, state_kept, mods[1], picks_own, mods[0]
             )
             grad_blocks = gather_blocks(grad_projected)
+            shares[1] = (mlp_share, attention_share)
         else:
+            parts, attention_grads = send_parts([own] + partial, attention_grads, True)
             sums1, grad_state = back_of_attention(where, parts, grad_after, inputs, mods[0], picks_own, None)
         item_sums[l] = jnp.concatenate([sums1, sums2], axis=0)
-        shares[l] = (mlp_share, attention_share)
-
-    mine = jnp.where(is_first, grad_state, output)
-    theirs = exchange(jnp.where(is_first, output, grad_state), "section", 1)
-    results = jnp.stack([jnp.where(is_first, mine, theirs), jnp.where(is_first, theirs, mine)])
-
-    def joined(which):
-        mine = jnp.where(is_first, shares[0][which], shares[1][which])
-        theirs = exchange(jnp.where(is_first, shares[1][which], shares[0][which]), "section", 1)
-        low = jnp.where(is_first, mine, theirs)
-        high = jnp.where(is_first, theirs, mine)
-        return jnp.concatenate([low, high], axis=0).astype(F32)
-
-    size = down_weight.shape[1]
-    mlp_grads = joined(0)
-    grad_pair = jnp.stack([mlp_grads[:, :size], mlp_grads[:, size : 2 * size]])
-    grad_down = mlp_grads[:, 2 * size :].T
-    attention_grads = joined(1)
-    grad_qkv = jnp.stack([attention_grads[:, i * narrow : (i + 1) * narrow] for i in range(3)])
-    grad_out_w = attention_grads[:, 3 * narrow :].T
-
+
+    item_sums[1] = jnp.concatenate([item_sums[1], last_sums], axis=0)
     sums = jnp.stack(item_sums)[:, :, :items].transpose(0, 2, 1, 3).reshape(2 * items, 6 * width)
     gain_parts = jnp.concatenate([jnp.concatenate([g[0:1], g[1:2]], axis=1) for g in gain_sums])
     gain_parts = jnp.pad(gain_parts, ((0, 2 * items - 2), (0, 0)))
@@ -1232,6 +1305,10 @@
     ]
     got = send_parts(pieces)
     total = (got[0] + got[1]) + (got[2] + got[3])
+    total, attention_grads, mlp_share = lax.optimization_barrier((total, attention_grads, mlp_share))
+    shares[0] = (mlp_share, data_sum(attention_grads))
+    last_partial[1:], total = lax.optimization_barrier((last_partial[1:], total))
+    output = last_output(send_parts(last_partial), cache[1][3], mods[1], picks_own)
     layers = total[:, :columns].reshape(2, items, columns).astype(BF).astype(F32)
     gain_rows = jnp.pad(total[:2, None, columns:], ((0, 0), (0, items - 1), (0, 0)))
     layers = jnp.concatenate([layers, gain_rows], axis=2)
@@ -1258,6 +1335,25 @@
     half = LANE // 2
     gain_total = gain_total.reshape(2, LANE)
     grad_gains = jnp.concatenate([gain_total[:, :HALF], gain_total[:, half : half + HALF]], axis=1)
+    mine = jnp.where(is_first, grad_state, output)
+    theirs = exchange(jnp.where(is_first, output, grad_state), "section", 1)
+    results = jnp.stack([jnp.where(is_first, mine, theirs), jnp.where(is_first, theirs, mine)])
+
+    def joined(which):
+        mine = jnp.where(is_first, shares[0][which], shares[1][which])
+        theirs = exchange(jnp.where(is_first, shares[1][which], shares[0][which]), "section", 1)
+        low = jnp.where(is_first, mine, theirs)
+        high = jnp.where(is_first, theirs, mine)
+        return jnp.concatenate([low, high], axis=0).astype(F32)
+
+    size = down_weight.shape[1]
+    mlp_grads = joined(0)
+    grad_pair = jnp.stack([mlp_grads[:, :size], mlp_grads[:, size : 2 * size]])
+    grad_down = mlp_grads[:, 2 * size :].T
+    attention_grads = joined(1)
+    grad_qkv = jnp.stack([attention_grads[:, i * narrow : (i + 1) * narrow] for i in range(3)])
+    grad_out_w = attention_grads[:, 3 * narrow :].T
+
     return (
         grad_ada[None],
         grad_qkv[None],

time: 395 us -> 375 us (0.949)
  waiting for transfers between devices: 150 us -> 122 us
  starting transfers between devices: 60 us -> 65.7 us
    ppermute x64, waiting for transfers between devices: 124 us -> 110 us  [exchange(): lax.ppermute(value, axis, [(i, i ^ k) for i in range(lax.axis_size(axis))])]
    reduce_scatter x4, waiting for transfers between devices: 25.5 us -> 12.1 us  [data_sum(): lax.psum_scatter(value, ('dp', 'section'), scatter_dimension=0, tiled=True)]
    ppermute x64, starting transfers between devices: 59.3 us -> 65.4 us  [exchange(): lax.ppermute(value, axis, [(i, i ^ k) for i in range(lax.axis_size(axis))])]
    pallas_call x25 -> x64, Pallas kernels: 142 us -> 145 us  [run(): return kernel(*placed)]
  transfers between devices with their start and end apart: 68 -> 68, of which waited for: 37 -> 32; matrix products, arithmetic and copies ran while one was open for 4% -> 4% of each run, Pallas kernels for 29% -> 31%
where the time goes in v4:
time: 375 us; the launch traced here: 369 us
  Pallas kernels  145 us (39%)
  waiting for transfers between devices  122 us (33%)
  starting transfers between devices  65.7 us (18%)
  between operations  14.9 us (4%)
  other arithmetic  9.39 us (3%)
  local copies, waits for them, and re-layouts  6.63 us (2%)
  matrix products  4.76 us (1%)
    pallas_call x64, Pallas kernels, run(): return kernel(*placed)  145 us
    ppermute x64, waiting for transfers between devices, exchange(): lax.ppermute(value, axis, [(i, i ^ k) for i in range(lax.axis_size(axis))])  110 us
    ppermute x64, starting transfers between devices, exchange(): lax.ppermute(value, axis, [(i, i ^ k) for i in range(lax.axis_size(axis))])  65.4 us
    reduce_scatter x4, waiting for transfers between devices, data_sum(): lax.psum_scatter(value, ('dp', 'section'), scatter_dimension=0, tiled=True)  12.1 us
  transfers between devices with their start and end apart: 68, of which 32 were waited for; matrix products, arithmetic and copies ran while one was open for 4% of the time, Pallas kernels for 31%

profile of v4, /device:TPU:1, one launch (start us, length us, event | category | flops | bytes accessed | tf_op | source)
XLA Modules:
  0.0 369.1 jit_solution(12694561941969623073)
XLA Ops:
  15.4 6.1 %prepare_weights.3 = (bf16[2,3,1152,512]{3,2,1,0:T(8,128)(2,1)}, bf16[2,512,1152]{2,1,0:T(8,128)(2,1)}) custom-call(s32[2]{0:T(128)S(1)} %pad_add_fusion.where_ref, bf16[3,288,1152]{2,1,0:T(8,128)(2,1)} %bitcast.98, bf16[288,1152]{1,0:T(8,128)(2,1)} %bitcast.102, bf16[288,512]{1,0:T(8,128)(2,1)S(1)} %copy-done), custom_call_target="tpu_custom_call" | custom-call | flops 1000 | bytes 1000 | tf_op jit(solution)/shard_map/prepare_weights/pallas_call | solution.py:56
  26.7 6.2 %prepare_weights.4 = (bf16[2,3,1152,512]{3,2,1,0:T(8,128)(2,1)}, bf16[2,512,1152]{2,1,0:T(8,128)(2,1)}) custom-call(s32[2]{0:T(128)S(1)} %pad_add_fusion.where_ref, bf16[3,288,1152]{2,1,0:T(8,128)(2,1)} %collective-permute-done.3.wq_in, bf16[288,1152]{1,0:T(8,128)(2,1)} %collective-permute-done.4.wo_in, ...), custom_call_target="tpu_custom_call", output_to_operand_aliasing={{0}: (4, {}), {1}: (5, {})} | custom-call | flops 1000 | bytes 1000 | tf_op jit(solution)/shard_map/prepare_weights/pallas_call | solution.py:56
  32.9 11.6 %attention_forward_0.1 = (bf16[128,1152]{1,0:T(8,128)(2,1)S(1)}, bf16[128,1152]{1,0:T(8,128)(2,1)S(1)}, bf16[128,1152]{1,0:T(8,128)(2,1)S(1)}, bf16[128,1152]{1,...) custom-call(s32[2]{0:T(128)S(1)} %pad_add_fusion.where_ref, ...), custom_call_target="tpu_custom_call" | custom-call | flops 1000 | bytes 1000 | tf_op jit(solution)/shard_map/attention_forward_0/pallas_call | solution.py:56
  52.0 8.4 %collective-permute-done.8.source = bf16[128,1152]{1,0:T(8,128)(2,1)S(1)} collective-permute-done((bf16[128,1152]{1,0:T(8,128)(2,1)S(1)}, bf16[128,1152]{1,0:T(8,128)(2,1)S(1)}, u32[]{:S(2)}, u32[]{:S(2)}) %collective-permute-start.8) | collective-permute-done | bytes 294944 | tf_op jit(solution)/shard_map/ppermute | solution.py:1100
  71.9 6.3 %mlp_forward_0.1 = (bf16[128,1152]{1,0:T(8,128)(2,1)S(1)}, bf16[128,1152]{1,0:T(8,128)(2,1)S(1)}, bf16[128,1152]{1,0:T(8,128)(2,1)S(1)}, bf16[128,1152]{1,0:T(8,...) custom-call(s32[1]{0:T(128)} %bitcast.sec_ref, ...), custom_call_target="tpu_custom_call" | custom-call | flops 1000 | bytes 1000 | tf_op jit(solution)/shard_map/mlp_forward_0/pallas_call | solution.py:56
  85.8 5.7 %collective-permute-done.16.source = bf16[128,1152]{1,0:T(8,128)(2,1)S(1)} collective-permute-done((bf16[128,1152]{1,0:T(8,128)(2,1)S(1)}, bf16[128,1152]{1,0:T(8,128)(2,1)S(1)}, u32[]{:S(2)}, u32[]{:S(2)}) %collective-permute-start.16) | collective-permute-done | bytes 294944 | tf_op jit(solution)/shard_map/ppermute | solution.py:1100
  101.7 9.8 %attention_forward_1.1 = (bf16[128,1152]{1,0:T(8,128)(2,1)S(1)}, bf16[128,1152]{1,0:T(8,128)(2,1)S(1)}, bf16[128,1152]{1,0:T(8,128)(2,1)S(1)}, bf16[128,1152]{1,...) custom-call(s32[2]{0:T(128)S(1)} %pad_add_fusion.where_ref, ...), custom_call_target="tpu_custom_call" | custom-call | flops 1000 | bytes 1000 | tf_op jit(solution)/shard_map/attention_forward_1/pallas_call | solution.py:56
  117.4 7.9 %collective-permute-done.22.source = bf16[128,1152]{1,0:T(8,128)(2,1)S(1)} collective-permute-done((bf16[128,1152]{1,0:T(8,128)(2,1)S(1)}, bf16[128,1152]{1,0:T(8,128)(2,1)S(1)}, u32[]{:S(2)}, u32[]{:S(2)}) %collective-permute-start.22) | collective-permute-done | bytes 294944 | tf_op jit(solution)/shard_map/ppermute | solution.py:1100
  136.1 6.7 %mlp_forward_1.1 = (bf16[512,768]{1,0:T(8,128)(2,1)}, bf16[512,768]{1,0:T(8,128)(2,1)}, bf16[512,768]{1,0:T(8,128)(2,1)}, bf16[512,1152]{1,0:T(8,128)(2,1)}, bf1...) custom-call(s32[1]{0:T(128)} %bitcast.sec_ref, ...), custom_call_target="tpu_custom_call" | custom-call | flops 1000 | bytes 1000 | tf_op jit(solution)/shard_map/mlp_forward_1/pallas_call | solution.py:56
  142.8 6.9 %mlp_backward_1.1 = (bf16[512,768]{1,0:T(8,128)(2,1)S(1)}, bf16[512,768]{1,0:T(8,128)(2,1)S(1)}, bf16[1152,2304]{1,0:T(8,128)(2,1)}) custom-call(bf16[512,1152]{1,0:T(8,128)(2,1)} %get-tuple-element.237.gp_in, bf16[512,768]{1,0:T(8,128)(2,1)} %get-tuple-element.238.gh_in, bf16[512,768]{1,0:T(8,128)(2,1)} %get-tuple-element.239.hid_in, ...), custom_call_target="tpu_custom_call" | custom-call | flops 1000 | bytes 1000 | tf_op jit(solution)/shard_map/mlp_backward_1/pallas_call | solution.py:56
  149.8 4.9 %mlp_input_grad.1 = (bf16[128,1152]{1,0:T(8,128)(2,1)S(1)}, bf16[128,1152]{1,0:T(8,128)(2,1)S(1)}, bf16[128,1152]{1,0:T(8,128)(2,1)S(1)}, bf16[128,1152]{1,0:T(8,128)(2,1)}) custom-call(s32[1]{0:T(128)} %bitcast.sec_ref, bf16[512,768]{1,0:T(8,128)(2,1)S(1)} %get-tuple-element.243.gg_ref, bf16[512,768]{1,0:T(8,128)(2,1)S(1)} %get-tuple-element.244.gup_ref, ...), custom_call_target="tpu_custom_call" | custom-call | flops 1000 | bytes 1000 | tf_op jit(solution)/shard_map/mlp_input_grad/pallas_call | solution.py:56
  171.1 5.1 %collective-permute-done.32.source = bf16[128,1152]{1,0:T(8,128)(2,1)S(1)} collective-permute-done((bf16[128,1152]{1,0:T(8,128)(2,1)S(1)}, bf16[128,1152]{1,0:T(8,128)(2,1)S(1)}, u32[]{:S(2)}, u32[]{:S(2)}) %collective-permute-start.32) | collective-permute-done | bytes 294944 | tf_op jit(solution)/shard_map/ppermute | solution.py:1100
  179.3 12.2 %attention_backward_1.1 = (bf16[128,1152]{1,0:T(8,128)(2,1)S(1)}, bf16[128,1152]{1,0:T(8,128)(2,1)S(1)}, bf16[128,1152]{1,0:T(8,128)(2,1)S(1)}, bf16[512,1536]{1...) custom-call(bf16[128,1152]{1,0:T(8,128)(2,1)S(1)} %get-tuple-element, ...), custom_call_target="tpu_custom_call" | custom-call | flops 1000 | bytes 1000 | tf_op jit(solution)/shard_map/attention_backward_1/pallas_call | solution.py:56
  194.2 6.5 %attention_weight_grads.2 = bf16[1152,1152]{1,0:T(8,128)(2,1)} custom-call(bf16[512,1152]{1,0:T(8,128)(2,1)} %get-tuple-element.268.a_in, bf16[512,1536]{1,0:T(8,128)(2,1)} %get-tuple-element.269.g_in, bf16[512,512]{1,0:T(8,128)(2,1)} %get-tuple-element.270.mixed_in, bf16[512,1152]{1,0:T(8,128)(2,1)} %get-tuple-element.271.ga_in, bf16[512,288]{1,0:T(8,128)(2,1)S(1)} %copy-done.1), custom_call_target="tpu_custom_call" | custom-call | flops 1000 | bytes 1000 | tf_op jit(solution)/shard_map/attention_weight_grads/pallas_call | solution.py:56
  200.8 5.4 %collective-permute-done.34.p2 = bf16[128,1152]{1,0:T(8,128)(2,1)S(1)} collective-permute-done((bf16[128,1152]{1,0:T(8,128)(2,1)S(1)}, bf16[128,1152]{1,0:T(8,128)(2,1)S(1)}, u32[]{:S(2)}, u32[]{:S(2)}) %collective-permute-start.34) | collective-permute-done | bytes 294944 | tf_op jit(solution)/shard_map/ppermute | solution.py:1100
  217.0 8.8 %collective-permute-done.37.source = bf16[128,1152]{1,0:T(8,128)(2,1)S(1)} collective-permute-done((bf16[128,1152]{1,0:T(8,128)(2,1)S(1)}, bf16[128,1152]{1,0:T(8,128)(2,1)S(1)}, u32[]{:S(2)}, u32[]{:S(2)}) %collective-permute-start.37) | collective-permute-done | bytes 294944 | tf_op jit(solution)/shard_map/ppermute | solution.py:1100
  225.8 9.4 %mlp_backward_0.1 = (bf16[128,1152]{1,0:T(8,128)(2,1)S(1)}, bf16[128,1152]{1,0:T(8,128)(2,1)S(1)}, bf16[128,1152]{1,0:T(8,128)(2,1)S(1)}, bf16[512,1152]{1,0:T(8...) custom-call(s32[2]{0:T(128)S(1)} %pad_add_fusion.where_ref, ...), custom_call_target="tpu_custom_call" | custom-call | flops 1000 | bytes 1000 | tf_op jit(solution)/shard_map/mlp_backward_0/pallas_call | solution.py:56
  238.2 6.3 %mlp_weight_grads.1 = bf16[1152,2304]{1,0:T(8,128)(2,1)} custom-call(bf16[512,1152]{1,0:T(8,128)(2,1)} %get-tuple-element.286.a_in, bf16[512,768]{1,0:T(8,128)(2,1)} %get-tuple-element.287.gg_in, bf16[512,768]{1,0:T(8,128)(2,1)} %get-tuple-element.288.gu_in, bf16[512,1152]{1,0:T(8,128)(2,1)} %get-tuple-element.289.gp_in, ...), custom_call_target="tpu_custom_call" | custom-call | flops 1000 | bytes 1000 | tf_op jit(solution)/shard_map/mlp_weight_grads/pallas_call | solution.py:56
  244.5 5.7 %collective-permute-done.41.p3 = bf16[128,1152]{1,0:T(8,128)(2,1)S(1)} collective-permute-done((bf16[128,1152]{1,0:T(8,128)(2,1)S(1)}, bf16[128,1152]{1,0:T(8,128)(2,1)S(1)}, u32[]{:S(2)}, u32[]{:S(2)}) %collective-permute-start.41) | collective-permute-done | bytes 294944 | tf_op jit(solution)/shard_map/ppermute | solution.py:1100
  262.1 9.1 %collective-permute-done.43.source = bf16[128,1152]{1,0:T(8,128)(2,1)S(1)} collective-permute-done((bf16[128,1152]{1,0:T(8,128)(2,1)S(1)}, bf16[128,1152]{1,0:T(8,128)(2,1)S(1)}, u32[]{:S(2)}, u32[]{:S(2)}) %collective-permute-start.43) | collective-permute-done | bytes 294944 | tf_op jit(solution)/shard_map/ppermute | solution.py:1100
  271.2 12.4 %attention_backward_0.1 = (bf16[128,1152]{1,0:T(8,128)(2,1)}, bf16[128,1152]{1,0:T(8,128)(2,1)S(1)}, bf16[128,1152]{1,0:T(8,128)(2,1)S(1)}, bf16[512,1536]{1,0:T...) custom-call(bf16[128,1152]{1,0:T(8,128)(2,1)S(1)} %get-tuple-element, ...), custom_call_target="tpu_custom_call" | custom-call | flops 1000 | bytes 1000 | tf_op jit(solution)/shard_map/attention_backward_0/pallas_call | solution.py:56
  286.4 6.7 %attention_weight_grads.3 = bf16[1152,1152]{1,0:T(8,128)(2,1)} custom-call(bf16[512,1152]{1,0:T(8,128)(2,1)} %get-tuple-element.310.a_in, bf16[512,1536]{1,0:T(8,128)(2,1)} %get-tuple-element.311.g_in, bf16[512,512]{1,0:T(8,128)(2,1)} %get-tuple-element.312.mixed_in, bf16[512,1152]{1,0:T(8,128)(2,1)} %get-tuple-element.313.ga_in, bf16[512,288]{1,0:T(8,128)(2,1)S(1)} %copy-done.1), custom_call_target="tpu_custom_call" | custom-call | flops 1000 | bytes 1000 | tf_op jit(solution)/shard_map/attention_weight_grads/pallas_call | solution.py:56
  327.6 5.5 %collective-permute-start.56 = (bf16[144,2304]{1,0:T(8,128)(2,1)S(1)}, bf16[144,2304]{1,0:T(8,128)(2,1)S(1)}, u32[]{:S(2)}, u32[]{:S(2)}) collective-permute-start(bf16[144,2304]{1,0:T(8,128)(2,1)S(1)} %broadcast_select_fusion.2), channel_id=1, source_target_pairs={{0,16},{16,0},{1,17},{17,1},{2,18},{18,2},{3,19},{19,3},{4,20},{20... | collective-permute-start | bytes 1990664 | tf_op jit(solution)/shard_map/ppermute | solution.py:1100
  347.8 8.4 %reduce-scatter.11.cloned.1.call-done = bf16[144,1152]{1,0:T(8,128)(2,1)} async-done(((bf16[1152,1152]{1,0:T(8,128)(2,1)}), bf16[144,1152]{1,0:T(8,128)(2,1)}) %reduce-scatter.11.cloned.1.call-update) | async-done | bytes 331792 | tf_op jit(solution)/shard_map/reduce_scatter | solution.py:1253
  (273 shorter events, 172.1 us)
Async XLA Ops:
  7.2 200.1 %reduce-scatter.5.cloned.1.call-start = ((), (), s32[]{:S(2)}) async-start(), calls=%async_computation.4 | async-start | bytes 5971968 | tf_op jit(solution)/shard_map/reduce_scatter | solution.py:1253
  7.2 16.8 %collective-permute-start.3 = (bf16[3,288,1152]{2,1,0:T(8,128)(2,1)}, bf16[3,288,1152]{2,1,0:T(8,128)(2,1)}, u32[]{:S(2)}, u32[]{:S(2)}) collective-permute-start(bf16[3,288,1152]{2,1,0:T(8,128)(2,1)} %bitcast.97), channel_id=1, source_target_pairs={{0,16},{16,0},{1,17},{17,1},{2,18},{18,2},{3,19},{19,3},{4,20},{20... | collective-permute-start | bytes 5971976 | tf_op jit(solution)/shard_map/ppermute | solution.py:1100
  7.3 16.7 %collective-permute-start.4 = (bf16[288,1152]{1,0:T(8,128)(2,1)}, bf16[288,1152]{1,0:T(8,128)(2,1)}, u32[]{:S(2)}, u32[]{:S(2)}) collective-permute-start(bf16[288,1152]{1,0:T(8,128)(2,1)} %bitcast.101), channel_id=1, source_target_pairs={{0,16},{16,0},{1,17},{17,1},{2,18},{18,2},{3,19},{19,3},{4,20},{20... | collective-permute-start | bytes 1990664 | tf_op jit(solution)/shard_map/ppermute | solution.py:1100
  26.1 44.6 %collective-permute-start.13 = (bf16[2,1152,768]{2,1,0:T(8,128)(2,1)}, bf16[2,1152,768]{2,1,0:T(8,128)(2,1)}, u32[]{:S(2)}, u32[]{:S(2)}) collective-permute-start(bf16[2,1152,768]{2,1,0:T(8,128)(2,1)} %bitcast.86), channel_id=1, source_target_pairs={{0,16},{16,0},{1,17},{17,1},{2,18},{18,2},{3,19},{19,3},{4,20},{20... | collective-permute-start | bytes 10616840 | tf_op jit(solution)/shard_map/ppermute | solution.py:1100
  26.3 44.4 %collective-permute-start.14 = (bf16[768,1152]{1,0:T(8,128)(2,1)S(1)}, bf16[768,1152]{1,0:T(8,128)(2,1)S(1)}, u32[]{:S(2)}, u32[]{:S(2)}) collective-permute-start(bf16[768,1152]{1,0:T(8,128)(2,1)S(1)} %bitcast.95), channel_id=1, source_target_pairs={{0,16},{16,0},{1,17},{17,1},{2,18},{18,2},{3,19},{19,3},{4,20},{20... | collective-permute-start | bytes 5308424 | tf_op jit(solution)/shard_map/ppermute | solution.py:1100
  46.2 14.2 %collective-permute-start.8 = (bf16[128,1152]{1,0:T(8,128)(2,1)S(1)}, bf16[128,1152]{1,0:T(8,128)(2,1)S(1)}, u32[]{:S(2)}, u32[]{:S(2)}) collective-permute-start(bf16[128,1152]{1,0:T(8,128)(2,1)S(1)} %get-tuple-element.204), channel_id=1, source_target_pairs={{0,8},{4,12},{8,0},{12,4},{1,9},{5,13},{9,1},{13,5},{2,10},{6,14},... | collective-permute-start | bytes 884744 | tf_op jit(solution)/shard_map/ppermute | solution.py:1100
  47.5 12.9 %collective-permute-start.9 = (bf16[128,1152]{1,0:T(8,128)(2,1)S(1)}, bf16[128,1152]{1,0:T(8,128)(2,1)S(1)}, u32[]{:S(2)}, u32[]{:S(2)}) collective-permute-start(bf16[128,1152]{1,0:T(8,128)(2,1)S(1)} %get-tuple-element.205), channel_id=1, source_target_pairs={{0,12},{4,8},{8,4},{12,0},{1,13},{5,9},{9,5},{13,1},{2,14},{6,10},... | collective-permute-start | bytes 884744 | tf_op jit(solution)/shard_map/ppermute | solution.py:1100
  78.6 12.8 %collective-permute-start.16 = (bf16[128,1152]{1,0:T(8,128)(2,1)S(1)}, bf16[128,1152]{1,0:T(8,128)(2,1)S(1)}, u32[]{:S(2)}, u32[]{:S(2)}) collective-permute-start(bf16[128,1152]{1,0:T(8,128)(2,1)S(1)} %get-tuple-element.220), channel_id=1, source_target_pairs={{0,8},{4,12},{8,0},{12,4},{1,9},{5,13},{9,1},{13,5},{2,10},{6,14},... | collective-permute-start | bytes 884744 | tf_op jit(solution)/shard_map/ppermute | solution.py:1100
  149.8 100.5 %reduce-scatter.7.cloned.1.call-start = ((), (), s32[]{:S(2)}) async-start(), calls=%async_computation.5 | async-start | bytes 2985984 | tf_op jit(solution)/shard_map/reduce_scatter | solution.py:1253
  192.5 13.6 %collective-permute-start.34 = (bf16[128,1152]{1,0:T(8,128)(2,1)S(1)}, bf16[128,1152]{1,0:T(8,128)(2,1)S(1)}, u32[]{:S(2)}, u32[]{:S(2)}) collective-permute-start(bf16[128,1152]{1,0:T(8,128)(2,1)S(1)} %get-tuple-element.266), channel_id=1, source_target_pairs={{0,8},{4,12},{8,0},{12,4},{1,9},{5,13},{9,1},{13,5},{2,10},{6,14},... | collective-permute-start | bytes 884744 | tf_op jit(solution)/shard_map/ppermute | solution.py:1100
  207.3 103.3 %reduce-scatter.9.cloned.1.call-start = ((), (), s32[]{:S(2)}) async-start(), calls=%async_computation.6 | async-start | bytes 5971968 | tf_op jit(solution)/shard_map/reduce_scatter | solution.py:1253
  212.5 13.3 %collective-permute-start.37 = (bf16[128,1152]{1,0:T(8,128)(2,1)S(1)}, bf16[128,1152]{1,0:T(8,128)(2,1)S(1)}, u32[]{:S(2)}, u32[]{:S(2)}) collective-permute-start(bf16[128,1152]{1,0:T(8,128)(2,1)S(1)} %get-tuple-element.278.refs_0_), channel_id=1, source_target_pairs={{0,8},{4,12},{8,0},{12,4},{1,9},{5,13},{9,1},{13,5},{2,10},{6,14},... | collective-permute-start | bytes 884744 | tf_op jit(solution)/shard_map/ppermute | solution.py:1100
  212.8 13.1 %collective-permute-start.36 = (bf16[128,1152]{1,0:T(8,128)(2,1)S(1)}, bf16[128,1152]{1,0:T(8,128)(2,1)S(1)}, u32[]{:S(2)}, u32[]{:S(2)}) collective-permute-start(bf16[128,1152]{1,0:T(8,128)(2,1)S(1)} %get-tuple-element.278.refs_0_), channel_id=1, source_target_pairs={{0,4},{4,0},{8,12},{12,8},{1,5},{5,1},{9,13},{13,9},{2,6},{6,2},{1... | collective-permute-start | bytes 884744 | tf_op jit(solution)/shard_map/ppermute | solution.py:1100
  237.2 13.0 %collective-permute-start.41 = (bf16[128,1152]{1,0:T(8,128)(2,1)S(1)}, bf16[128,1152]{1,0:T(8,128)(2,1)S(1)}, u32[]{:S(2)}, u32[]{:S(2)}) collective-permute-start(bf16[128,1152]{1,0:T(8,128)(2,1)S(1)} %get-tuple-element.285), channel_id=1, source_target_pairs={{0,12},{4,8},{8,4},{12,0},{1,13},{5,9},{9,5},{13,1},{2,14},{6,10},... | collective-permute-start | bytes 884744 | tf_op jit(solution)/shard_map/ppermute | solution.py:1100
  250.3 105.9 %reduce-scatter.11.cloned.1.call-start = ((), (), s32[]{:S(2)}) async-start(), calls=%async_computation.7 | async-start | bytes 2985984 | tf_op jit(solution)/shard_map/reduce_scatter | solution.py:1253
  256.1 15.1 %collective-permute-start.43 = (bf16[128,1152]{1,0:T(8,128)(2,1)S(1)}, bf16[128,1152]{1,0:T(8,128)(2,1)S(1)}, u32[]{:S(2)}, u32[]{:S(2)}) collective-permute-start(bf16[128,1152]{1,0:T(8,128)(2,1)S(1)} %get-tuple-element.299.b0), channel_id=1, source_target_pairs={{0,8},{4,12},{8,0},{12,4},{1,9},{5,13},{9,1},{13,5},{2,10},{6,14},... | collective-permute-start | bytes 884744 | tf_op jit(solution)/shard_map/ppermute | solution.py:1100
  256.1 15.1 %collective-permute-start.42 = (bf16[128,1152]{1,0:T(8,128)(2,1)S(1)}, bf16[128,1152]{1,0:T(8,128)(2,1)S(1)}, u32[]{:S(2)}, u32[]{:S(2)}) collective-permute-start(bf16[128,1152]{1,0:T(8,128)(2,1)S(1)} %get-tuple-element.299.b0), channel_id=1, source_target_pairs={{0,4},{4,0},{8,12},{12,8},{1,5},{5,1},{9,13},{13,9},{2,6},{6,2},{1... | collective-permute-start | bytes 884744 | tf_op jit(solution)/shard_map/ppermute | solution.py:1100
  285.2 12.8 %collective-permute-start.47 = (bf16[128,1152]{1,0:T(8,128)(2,1)S(1)}, bf16[128,1152]{1,0:T(8,128)(2,1)S(1)}, u32[]{:S(2)}, u32[]{:S(2)}) collective-permute-start(bf16[128,1152]{1,0:T(8,128)(2,1)S(1)} %get-tuple-element.309), channel_id=1, source_target_pairs={{0,12},{4,8},{8,4},{12,0},{1,13},{5,9},{9,5},{13,1},{2,14},{6,10},... | collective-permute-start | bytes 884744 | tf_op jit(solution)/shard_map/ppermute | solution.py:1100
  313.7 23.5 %collective-permute-start.60 = (bf16[128,1152]{1,0:T(8,128)(2,1)}, bf16[128,1152]{1,0:T(8,128)(2,1)S(1)}, u32[]{:S(2)}, u32[]{:S(2)}) collective-permute-start(bf16[128,1152]{1,0:T(8,128)(2,1)} %get-tuple-element.335.refs_1_), channel_id=1, source_target_pairs={{0,4},{4,0},{8,12},{12,8},{1,5},{5,1},{9,13},{13,9},{2,6},{6,2},{1... | collective-permute-start | bytes 884744 | tf_op jit(solution)/shard_map/ppermute | solution.py:1100
  319.4 13.6 %collective-permute-start.54 = (f32[8,3136]{1,0:T(8,128)S(1)}, f32[8,3136]{1,0:T(8,128)S(1)}, u32[]{:S(2)}, u32[]{:S(2)}) collective-permute-start(f32[8,3136]{1,0:T(8,128)S(1)} %concatenate.60), channel_id=1, source_target_pairs={{0,3},{1,2},{2,1},{3,0},{4,7},{5,6},{6,5},{7,4},{8,11},{9,10},{10,... | collective-permute-start | bytes 301064 | tf_op jit(solution)/shard_map/ppermute | solution.py:1100
  325.5 14.5 %collective-permute-start.61 = (bf16[128,1152]{1,0:T(8,128)(2,1)S(1)}, bf16[128,1152]{1,0:T(8,128)(2,1)S(1)}, u32[]{:S(2)}, u32[]{:S(2)}) collective-permute-start(bf16[128,1152]{1,0:T(8,128)(2,1)S(1)} %copy-done.15), channel_id=1, source_target_pairs={{0,8},{4,12},{8,0},{12,4},{1,9},{5,13},{9,1},{13,5},{2,10},{6,14},... | collective-permute-start | bytes 884744 | tf_op jit(solution)/shard_map/ppermute | solution.py:1100
  326.7 13.3 %collective-permute-start.62 = (bf16[128,1152]{1,0:T(8,128)(2,1)S(1)}, bf16[128,1152]{1,0:T(8,128)(2,1)S(1)}, u32[]{:S(2)}, u32[]{:S(2)}) collective-permute-start(bf16[128,1152]{1,0:T(8,128)(2,1)S(1)} %copy-done.14), channel_id=1, source_target_pairs={{0,12},{4,8},{8,4},{12,0},{1,13},{5,9},{9,5},{13,1},{2,14},{6,10},... | collective-permute-start | bytes 884744 | tf_op jit(solution)/shard_map/ppermute | solution.py:1100
  327.6 17.5 %collective-permute-start.56 = (bf16[144,2304]{1,0:T(8,128)(2,1)S(1)}, bf16[144,2304]{1,0:T(8,128)(2,1)S(1)}, u32[]{:S(2)}, u32[]{:S(2)}) collective-permute-start(bf16[144,2304]{1,0:T(8,128)(2,1)S(1)} %broadcast_select_fusion.2), channel_id=1, source_target_pairs={{0,16},{16,0},{1,17},{17,1},{2,18},{18,2},{3,19},{19,3},{4,20},{20... | collective-permute-start | bytes 1990664 | tf_op jit(solution)/shard_map/ppermute | solution.py:1100
  342.4 14.9 %collective-permute-start.63 = (f32[128,1152]{1,0:T(8,128)}, f32[128,1152]{1,0:T(8,128)}, u32[]{:S(2)}, u32[]{:S(2)}) collective-permute-start(f32[128,1152]{1,0:T(8,128)} %broadcast_select_fusion.8), channel_id=1, source_target_pairs={{0,16},{16,0},{1,17},{17,1},{2,18},{18,2},{3,19},{19,3},{4,20},{20... | collective-permute-start | bytes 1769480 | tf_op jit(solution)/shard_map/ppermute | solution.py:1100
  (63 other events, 490.3 us)
Sparse Core Ops, SparseCore 0:
  149.9 57.3 reduce-scatter.4
  209.6 35.6 reduce-scatter.6
  250.4 60.1 reduce-scatter.8
  315.0 41.1 reduce-scatter.10

commit v5 on v4

--- a/solution.py
+++ b/solution.py
@@ -366,13 +366,12 @@
         wq_ref, wo_ref, mask_ref = refs[:3]
         here = refs[3:10]
         sems, out_sems, carried_sems, a_x_ref, x_sems = refs[10:]
-        carried_copies = load(list(zip(carried_refs, carried_outs)), carried_sems)
         if raw_input:
             x_ref = a_x_ref
             x_copies = load(rows_of(in_refs[0], where_ref, x_ref), x_sems)
         qraw_ref, kraw_ref, qrot_ref, krot_ref, v_ref, mixed_ref, a_ref = here
-        weights_in = [(wq_in.at[layer, i], wq_ref.at[i]) for i in range(3)] + [(wo_in.at[layer], wo_ref)]
-        weights_in = load(weights_in, sems)
+        pairs = [(wq_in.at[layer, i], wq_ref.at[i]) for i in range(3)] + [(wo_in.at[layer], wo_ref)]
+        weights_in = load(pairs[:1], sems)
 
         def keep(i):
             pltpu.make_async_copy(here[i], kept[i], out_sems.at[i]).start()
@@ -388,12 +387,15 @@
         else:
             for k, ref in enumerate(in_refs):
                 a_ref[k * share : (k + 1) * share] = ref[...]
-        keep(6)
         mask_ref[...] = jnp.where(segc_ref[...] == segr_ref[...], 1.0, 0.0).astype(BF)
         cos = cos_ref[...]
         sin = sin_ref[...]
         for i, (raw_out, rot_out) in enumerate(((qraw_ref, qrot_ref), (kraw_ref, krot_ref))):
             weights_in[i].wait()
+            if i == 0:
+                weights_in += load(pairs[1:], sems.at[pl.ds(1, 3)])
+                carried_copies = load(list(zip(carried_refs, carried_outs)), carried_sems)
+                keep(6)
             gain = gain_ref[2 * layer + i : 2 * layer + i + 1]
             for h2 in range(0, heads, 2):
                 both = nn(a_ref[...], wq_ref[i, :, h2 * LANE : (h2 + 2) * LANE])
@@ -523,36 +525,79 @@
     )(*parts, after, mods, picks)[0]
 
 
-def last_gate_sums(where, parts, cotangent, picks):
-    share, width = parts[0].shape
-    rows = picks.shape[0]
-
-    def body(where_ref, *refs):
-        part_refs = refs[:4]
-        cot_in, picks_ref, sums_out, p_ref, g_ref, sums_ref, sems, cot_sems, out_sems = refs[4:]
-        copies = load([(ref, p_ref.at[pl.ds(k * share, share)]) for k, ref in enumerate(part_refs)], sems)
-        copies += load(rows_of(cot_in, where_ref, g_ref), cot_sems)
+def last_projection(layer, where, hidden, weights, cotangent, picks):
+    wd_own, wd_got = weights[2:]
+    rows, size = hidden.shape
+    width = wd_own.shape[1]
+    share = rows // 4
+    step = 3 * LANE
+
+    def body(where_ref, hid_in, wd_a, wd_b, cot_in, picks_ref, p0, p1, p2, p3, sums_out,
+             hid_ref, wd_ref, g_ref, q0, q1, q2, q3, sums_ref, sems, cot_sems, out_sems):
+        fetch(where_ref[0] == layer, wd_a, wd_b, wd_ref, sems.at[0])
+        copies = load([(hid_in, hid_ref)], sems.at[pl.ds(1, 1)]) + load(rows_of(cot_in, where_ref, g_ref), cot_sems)
+        arrived(wd_a, wd_ref, sems.at[0])
         finish(copies)
-        sums_ref[0] = image_sums(picks_ref[...], g_ref[...].astype(F32) * p_ref[...].astype(F32))
-        finish(load([(sums_ref, sums_out)], out_sems))
+        picked = picks_ref[...]
+        for j in range(width // step):
+            at = slice(j * step, (j + 1) * step)
+            part = nn(hid_ref[...], wd_ref[:, at])
+            split_store(part, at, (q0, q1, q2, q3))
+            sums_ref[0, :, at] = image_sums(picked, g_ref[:, at].astype(F32) * part)
+        finish(load([(q0, p0), (q1, p1), (q2, p2), (q3, p3), (sums_ref, sums_out)], out_sems))
 
     sums = (1, picks.shape[1], width)
+    result = call(
+        body,
+        [shape((share, width), BF)] * 4 + [shape(sums, F32)],
+        [SM] + [HB] * 4 + [VM],
+        [
+            pltpu.VMEM((rows, size), BF),
+            pltpu.VMEM((size, width), BF),
+            pltpu.VMEM((rows, width), BF),
+        ]
+        + [pltpu.VMEM((share, width), BF)] * 4
+        + [
+            pltpu.VMEM(sums, F32),
+            pltpu.SemaphoreType.DMA((2,)),
+            pltpu.SemaphoreType.DMA((4,)),
+            pltpu.SemaphoreType.DMA((5,)),
+        ],
+        name="last_projection",
+        limit=16,
+        kept=5,
+    )(where, hidden, wd_own, wd_got, cotangent, picks)
+    return list(result[:4]), result[4]
+
+
+def attention_results(where, mine, theirs):
+    half, columns = mine.shape
+    narrow = columns // 4
+    eye = jnp.eye(2 * half, dtype=BF)
+
+    def body(where_ref, mine_ref, theirs_ref, eye_ref, qkv_out, out_out, qkv_ref, out_ref, sems):
+        a, b = mine_ref[...].astype(F32), theirs_ref[...].astype(F32)
+        first = where_ref[0] == 0
+        full = jnp.concatenate([jnp.where(first, a, b), jnp.where(first, b, a)], axis=0)
+        for i in range(3):
+            qkv_ref[i] = full[:, i * narrow : (i + 1) * narrow]
+        copies = load([(qkv_ref, qkv_out)], sems)
+        out_ref[...] = tn(full[:, 3 * narrow :].astype(BF), eye_ref[...])
+        finish(copies + load([(out_ref, out_out)], sems.at[pl.ds(1, 1)]))
+
     return call(
         body,
-        [shape(sums, F32)],
-        [SM] + [HB] * 5 + [VM],
+        [shape((3, 2 * half, narrow), F32), shape((narrow, 2 * half), F32)],
+        [SM, VM, VM, FREE],
         [
-            pltpu.VMEM((rows, width), BF),
-            pltpu.VMEM((rows, width), BF),
-            pltpu.VMEM(sums, F32),
-            pltpu.SemaphoreType.DMA((4,)),
-            pltpu.SemaphoreType.DMA((4,)),
-            pltpu.SemaphoreType.DMA((1,)),
+            pltpu.VMEM((3, 2 * half, narrow), F32),
+            pltpu.VMEM((narrow, 2 * half), F32),
+            pltpu.SemaphoreType.DMA((2,)),
         ],
-        name="last_gate_sums",
-        limit=16,
-        kept=1,
-    )(where, *parts, cotangent, picks)[0]
+        name="attention_results",
+        limit=12,
+        kept=2,
+    )(where, mine, theirs, eye)
 
 
 def mlp_forward(layer, blocks, weights, section, carried, late):
@@ -711,23 +756,45 @@
     return list(result[:3]), list(result[3:6]), list(result[6:])
 
 
-def mlp_backward_last(layer, ahead, saved):
+def mlp_last(layer, blocks, weights, ahead, section, carried):
+    gu_own, gu_got = weights[:2]
     grad_projected, grad_hidden = ahead
-    hidden, c1, c2, mlp_in = saved
-    rows, width = grad_projected.shape
-    size = hidden.shape[1]
+    rows, size = grad_hidden.shape
+    width = gu_own.shape[1]
+    share = rows // 4
+    chunk = 2 * LANE
+    chunks = size // chunk
     step = 3 * LANE
 
-    def body(gp_in, gh_in, hid_in, c1_in, c2_in, a_in, gg_ref, gup_ref, out,
-             gh_ref, c1_ref, c2_ref, hid_ref, gp_ref, a_ref, full_ref, in_sems, out_sems):
-        ins = [(gh_in, gh_ref), (c1_in, c1_ref), (c2_in, c2_ref), (a_in, a_ref), (gp_in, gp_ref), (hid_in, hid_ref)]
-        ins = load(ins, in_sems)
-        finish(ins[:2])
-        gg_ref[...] = gh_ref[...] * c1_ref[...]
-        ins[2].wait()
-        gup_ref[...] = gh_ref[...] * c2_ref[...]
-        finish(ins[3:])
-        kept = []
+    def body(sec_ref, b0, b1, b2, b3, gu_a, gu_b, gp_in, gh_in, attended_ref, after_ref,
+             gg_ref, gup_ref, out, hid_out, attended_out, after_out,
+             a_ref, gu_ref, hid_ref, gh_ref, gp_ref, full_ref, sems, in_sems, out_sems, kept_sems):
+        own = sec_ref[0] == layer
+        for j in range(chunks):
+            at = pl.ds(j * chunk, chunk)
+            for i in range(2):
+                fetch(own, gu_a.at[i, :, at], gu_b.at[i, :, at], gu_ref.at[i, :, at], sems.at[2 * j + i])
+        ins = load([(gh_in, gh_ref), (gp_in, gp_ref)], in_sems)
+        kept = load([(attended_ref, attended_out), (after_ref, after_out)], kept_sems)
+        for k, ref in enumerate((b0, b1, b2, b3)):
+            a_ref[k * share : (k + 1) * share] = ref[...]
+        for j in range(chunks):
+            at = slice(j * chunk, (j + 1) * chunk)
+            for i in range(2):
+                here = pl.ds(j * chunk, chunk)
+                arrived(gu_a.at[i, :, here], gu_ref.at[i, :, here], sems.at[2 * j + i])
+            gate = nn(a_ref[...], gu_ref[0, :, at])
+            up = nn(a_ref[...], gu_ref[1, :, at])
+            if j == 0:
+                ins[0].wait()
+            sigma = jax.nn.sigmoid(gate)
+            silu = gate * sigma
+            grad = gh_ref[:, at].astype(F32)
+            hid_ref[:, at] = (silu * up).astype(BF)
+            gg_ref[:, at] = (grad * (up * (sigma + silu * (1.0 - sigma)))).astype(BF)
+            gup_ref[:, at] = (grad * silu).astype(BF)
+        kept += load([(hid_ref, hid_out)], kept_sems.at[pl.ds(2, 1)])
+        ins[1].wait()
         for j in range(width // step):
             at = slice(j * step, (j + 1) * step)
             left = a_ref[:, at]
@@ -735,26 +802,32 @@
             full_ref[at, size : 2 * size] = tn(left, gup_ref[...]).astype(BF)
             full_ref[at, 2 * size :] = tn(gp_ref[:, at], hid_ref[...]).astype(BF)
             here = pl.ds(j * step, step)
-            kept.append(pltpu.make_async_copy(full_ref.at[here], out.at[here], out_sems.at[j]))
-            kept[-1].start()
+            kept += load([(full_ref.at[here], out.at[here])], out_sems.at[pl.ds(j, 1)])
         finish(kept)
 
-    return call(
-        body,
-        [shape((rows, size), BF)] * 2 + [shape((width, 3 * size), BF)],
-        [HB] * 6,
-        [pltpu.VMEM((rows, size), BF)] * 4
-        + [
+    result = call(
+        body,
+        [shape((rows, size), BF)] * 2
+        + [shape((width, 3 * size), BF), shape((rows, size), BF)]
+        + [shape(c.shape, c.dtype) for c in carried],
+        [SM] + [VM] * 4 + [HB] * 4 + [VM] * 2,
+        [
             pltpu.VMEM((rows, width), BF),
+            pltpu.VMEM(gu_own.shape, BF),
+            pltpu.VMEM((rows, size), BF),
+            pltpu.VMEM((rows, size), BF),
             pltpu.VMEM((rows, width), BF),
             pltpu.VMEM((width, 3 * size), BF),
-            pltpu.SemaphoreType.DMA((6,)),
+            pltpu.SemaphoreType.DMA((2 * chunks,)),
+            pltpu.SemaphoreType.DMA((2,)),
             pltpu.SemaphoreType.DMA((width // step,)),
+            pltpu.SemaphoreType.DMA((3,)),
         ],
-        name=f"mlp_backward_{layer}",
-        kept=1,
-        limit=24,
-    )(grad_projected, grad_hidden, hidden, c1, c2, mlp_in)
+        name=f"mlp_last_{layer}",
+        kept=4,
+        limit=28,
+    )(section, *blocks, gu_own, gu_got, grad_projected, grad_hidden, *carried)
+    return list(result[:2]), result[2], result[3], list(result[4:])
 
 
 def mlp_input_grad(layer, section, grad_gate, grad_up, weights):
@@ -1235,7 +1308,13 @@
             state = carried[1]
             state_kept = kept[1]
         mlp_in, attended, after = after_attention(parts, state, mods[l], picks_own)
-        partial, mlp_saved, kept = mlp_forward(l, gather_blocks(mlp_in), mlp_weights, sec, (attended, after), l == 1)
+        if l == 1:
+            grads, mlp_grads, hidden, kept = mlp_last(
+                l, gather_blocks(mlp_in), mlp_weights, ahead, sec, (attended, after)
+            )
+            cache.append([saved] + kept)
+            break
+        partial, mlp_saved, kept = mlp_forward(l, gather_blocks(mlp_in), mlp_weights, sec, (attended, after), False)
         cache.append([saved, mlp_saved] + kept)
         if l == 0:
             where_late, partial[0] = lax.optimization_barrier((where, partial[0]))
@@ -1253,19 +1332,17 @@
         return lax.psum_scatter(value, ("dp", "section"), scatter_dimension=0, tiled=True)
 
     for l in (1, 0):
-        saved, (hidden, c1, c2, mlp_in), attended, after = cache[l][:4]
-        mixed, attention_in = saved[5:]
         if l == 1:
-            last_partial = partial
-            grad_gate, grad_up, mlp_grads = mlp_backward_last(l, ahead, cache[1][1])
+            saved, attended, after = cache[1]
             mlp_share = data_sum(mlp_grads)
-            partial = mlp_input_grad(l, sec, grad_gate, grad_up, mlp_weights)
+            partial = mlp_input_grad(l, sec, *grads, mlp_weights)
             where_late, partial[0] = lax.optimization_barrier((where, partial[0]))
-            last_sums = last_gate_sums(where_late, last_partial, cotangent, picks)
+            last_partial, last_sums = last_projection(l, where_late, hidden, mlp_weights, cotangent, picks)
             parts, last_sums = send_parts(partial, last_sums, True)
             grad_out = cotangent
             projected = None
         else:
+            saved, (hidden, c1, c2, mlp_in), attended, after = cache[0][:4]
             partial, grads, kept = mlp_backward(
                 l, where, grad_blocks, mlp_weights, (c1, c2), [grad_out]
             )
@@ -1275,6 +1352,7 @@
             parts, (mlp_grads, earlier) = send_parts([kept[0]] + partial, (mlp_grads, shares[1][1]), True)
             shares[1] = (shares[1][0], earlier)
             mlp_share = data_sum(mlp_grads)
+        mixed, attention_in = saved[5:]
         grad_attended, grad_after, sums2 = back_of_mlp(
             where, parts, grad_out, after, attended, projected, mods[l], picks_own
         )
@@ -1308,7 +1386,7 @@
     total, attention_grads, mlp_share = lax.optimization_barrier((total, attention_grads, mlp_share))
     shares[0] = (mlp_share, data_sum(attention_grads))
     last_partial[1:], total = lax.optimization_barrier((last_partial[1:], total))
-    output = last_output(send_parts(last_partial), cache[1][3], mods[1], picks_own)
+    output = last_output(send_parts(last_partial), cache[1][2], mods[1], picks_own)
     layers = total[:, :columns].reshape(2, items, columns).astype(BF).astype(F32)
     gain_rows = jnp.pad(total[:2, None, columns:], ((0, 0), (0, items - 1), (0, 0)))
     layers = jnp.concatenate([layers, gain_rows], axis=2)
@@ -1350,10 +1428,9 @@
     mlp_grads = joined(0)
     grad_pair = jnp.stack([mlp_grads[:, :size], mlp_grads[:, size : 2 * size]])
     grad_down = mlp_grads[:, 2 * size :].T
-    attention_grads = joined(1)
-    grad_qkv = jnp.stack([attention_grads[:, i * narrow : (i + 1) * narrow] for i in range(3)])
-    grad_out_w = attention_grads[:, 3 * narrow :].T
-
+    mine = jnp.where(is_first, shares[0][1], shares[1][1])
+    theirs = exchange(jnp.where(is_first, shares[1][1], shares[0][1]), "section", 1)
+    grad_qkv, grad_out_w = attention_results(where, mine, theirs)
     return (
         grad_ada[None],
         grad_qkv[None],

time: 375 us -> 370 us (0.987)
  transfers between devices with their start and end apart: 68 -> 68, of which waited for: 32 -> 33; matrix products, arithmetic and copies ran while one was open for 4% -> 4% of each run, Pallas kernels for 31% -> 31%
where the time goes in v5:
time: 370 us; the launch traced here: 364 us
  Pallas kernels  143 us (39%)
  waiting for transfers between devices  124 us (34%)
  starting transfers between devices  63.6 us (17%)
  between operations  14.9 us (4%)
  other arithmetic  8.06 us (2%)
  local copies, waits for them, and re-layouts  5.31 us (1%)
  matrix products  4.76 us (1%)
    pallas_call x64, Pallas kernels, run(): return kernel(*placed)  143 us
    ppermute x64, waiting for transfers between devices, exchange(): lax.ppermute(value, axis, [(i, i ^ k) for i in range(lax.axis_size(axis))])  113 us
    ppermute x64, starting transfers between devices, exchange(): lax.ppermute(value, axis, [(i, i ^ k) for i in range(lax.axis_size(axis))])  63.2 us
    reduce_scatter x4, waiting for transfers between devices, data_sum(): lax.psum_scatter(value, ('dp', 'section'), scatter_dimension=0, tiled=True)  10.7 us
  transfers between devices with their start and end apart: 68, of which 33 were waited for; matrix products, arithmetic and copies ran while one was open for 4% of the time, Pallas kernels for 31%

profile of v5, /device:TPU:1, one launch (start us, length us, event | category | flops | bytes accessed | tf_op | source)
XLA Modules:
  0.0 363.7 jit_solution(13054817647190217839)
XLA Ops:
  15.4 6.1 %prepare_weights.3 = (bf16[2,3,1152,512]{3,2,1,0:T(8,128)(2,1)}, bf16[2,512,1152]{2,1,0:T(8,128)(2,1)}) custom-call(s32[2]{0:T(128)S(1)} %pad_add_fusion.where_ref, bf16[3,288,1152]{2,1,0:T(8,128)(2,1)} %bitcast.88, bf16[288,1152]{1,0:T(8,128)(2,1)} %bitcast.92, bf16[288,512]{1,0:T(8,128)(2,1)S(1)} %copy-done), custom_call_target="tpu_custom_call" | custom-call | flops 1000 | bytes 1000 | tf_op jit(solution)/shard_map/prepare_weights/pallas_call | solution.py:56
  26.6 6.3 %prepare_weights.4 = (bf16[2,3,1152,512]{3,2,1,0:T(8,128)(2,1)}, bf16[2,512,1152]{2,1,0:T(8,128)(2,1)}) custom-call(s32[2]{0:T(128)S(1)} %pad_add_fusion.where_ref, bf16[3,288,1152]{2,1,0:T(8,128)(2,1)} %collective-permute-done.3.wq_in, bf16[288,1152]{1,0:T(8,128)(2,1)} %collective-permute-done.4.wo_in, ...), custom_call_target="tpu_custom_call", output_to_operand_aliasing={{0}: (4, {}), {1}: (5, {})} | custom-call | flops 1000 | bytes 1000 | tf_op jit(solution)/shard_map/prepare_weights/pallas_call | solution.py:56
  32.9 10.2 %attention_forward_0.1 = (bf16[128,1152]{1,0:T(8,128)(2,1)S(1)}, bf16[128,1152]{1,0:T(8,128)(2,1)S(1)}, bf16[128,1152]{1,0:T(8,128)(2,1)S(1)}, bf16[128,1152]{1,...) custom-call(s32[2]{0:T(128)S(1)} %pad_add_fusion.where_ref, ...), custom_call_target="tpu_custom_call" | custom-call | flops 1000 | bytes 1000 | tf_op jit(solution)/shard_map/attention_forward_0/pallas_call | solution.py:56
  50.6 8.4 %collective-permute-done.8.source = bf16[128,1152]{1,0:T(8,128)(2,1)S(1)} collective-permute-done((bf16[128,1152]{1,0:T(8,128)(2,1)S(1)}, bf16[128,1152]{1,0:T(8,128)(2,1)S(1)}, u32[]{:S(2)}, u32[]{:S(2)}) %collective-permute-start.8) | collective-permute-done | bytes 294944 | tf_op jit(solution)/shard_map/ppermute | solution.py:1173
  70.5 6.2 %mlp_forward_0.1 = (bf16[128,1152]{1,0:T(8,128)(2,1)S(1)}, bf16[128,1152]{1,0:T(8,128)(2,1)S(1)}, bf16[128,1152]{1,0:T(8,128)(2,1)S(1)}, bf16[128,1152]{1,0:T(8,...) custom-call(s32[1]{0:T(128)} %bitcast.sec_ref, ...), custom_call_target="tpu_custom_call" | custom-call | flops 1000 | bytes 1000 | tf_op jit(solution)/shard_map/mlp_forward_0/pallas_call | solution.py:56
  84.3 5.6 %collective-permute-done.16.source = bf16[128,1152]{1,0:T(8,128)(2,1)S(1)} collective-permute-done((bf16[128,1152]{1,0:T(8,128)(2,1)S(1)}, bf16[128,1152]{1,0:T(8,128)(2,1)S(1)}, u32[]{:S(2)}, u32[]{:S(2)}) %collective-permute-start.16) | collective-permute-done | bytes 294944 | tf_op jit(solution)/shard_map/ppermute | solution.py:1173
  100.2 9.2 %attention_forward_1.1 = (bf16[128,1152]{1,0:T(8,128)(2,1)S(1)}, bf16[128,1152]{1,0:T(8,128)(2,1)S(1)}, bf16[128,1152]{1,0:T(8,128)(2,1)S(1)}, bf16[128,1152]{1,...) custom-call(s32[2]{0:T(128)S(1)} %pad_add_fusion.where_ref, ...), custom_call_target="tpu_custom_call" | custom-call | flops 1000 | bytes 1000 | tf_op jit(solution)/shard_map/attention_forward_1/pallas_call | solution.py:56
  115.3 7.9 %collective-permute-done.22.source = bf16[128,1152]{1,0:T(8,128)(2,1)S(1)} collective-permute-done((bf16[128,1152]{1,0:T(8,128)(2,1)S(1)}, bf16[128,1152]{1,0:T(8,128)(2,1)S(1)}, u32[]{:S(2)}, u32[]{:S(2)}) %collective-permute-start.22) | collective-permute-done | bytes 294944 | tf_op jit(solution)/shard_map/ppermute | solution.py:1173
  134.0 9.2 %mlp_last_1.1 = (bf16[512,768]{1,0:T(8,128)(2,1)S(1)}, bf16[512,768]{1,0:T(8,128)(2,1)S(1)}, bf16[1152,2304]{1,0:T(8,128)(2,1)}, bf16[512,768]{1,0:T(8,128)(2,1)...) custom-call(s32[1]{0:T(128)} %bitcast.sec_ref, bf16[128,1152]{1,0:T(8,128)(2,1)S(1)} %get-tuple-element.231.b0, ...), custom_call_target="tpu_custom_call" | custom-call | flops 1000 | bytes 1000 | tf_op jit(solution)/shard_map/mlp_last_1/pallas_call | solution.py:56
  143.3 4.9 %mlp_input_grad.1 = (bf16[128,1152]{1,0:T(8,128)(2,1)S(1)}, bf16[128,1152]{1,0:T(8,128)(2,1)S(1)}, bf16[128,1152]{1,0:T(8,128)(2,1)S(1)}, bf16[128,1152]{1,0:T(8,128)(2,1)}) custom-call(s32[1]{0:T(128)} %bitcast.sec_ref, bf16[512,768]{1,0:T(8,128)(2,1)S(1)} %get-tuple-element.236.gg_ref, bf16[512,768]{1,0:T(8,128)(2,1)S(1)} %get-tuple-element.237.gup_ref, ...), custom_call_target="tpu_custom_call" | custom-call | flops 1000 | bytes 1000 | tf_op jit(solution)/shard_map/mlp_input_grad/pallas_call | solution.py:56
  151.0 5.9 %last_projection.1 = (bf16[128,1152]{1,0:T(8,128)(2,1)}, bf16[128,1152]{1,0:T(8,128)(2,1)}, bf16[128,1152]{1,0:T(8,128)(2,1)}, bf16[128,1152]{1,0:T(8,128)(2,1)}, f32[1,8,1152]{2,1,0:T(8,128)}) custom-call(s32[2]{0:T(128)S(1)} %pad_add_fusion.where_ref, bf16[512,768]{1,0:T(8,128)(2,1)} %get-tuple-element.240.hid_in, bf16[768,1152]{1,0:T(8,128)(2,1)} %bitcast.83, ...), custom_call_target="tpu_custom_call" | custom-call | flops 1000 | bytes 1000 | tf_op jit(solution)/shard_map/last_projection/pallas_call | solution.py:56
  164.5 5.1 %collective-permute-done.32.source = bf16[128,1152]{1,0:T(8,128)(2,1)S(1)} collective-permute-done((bf16[128,1152]{1,0:T(8,128)(2,1)S(1)}, bf16[128,1152]{1,0:T(8,128)(2,1)S(1)}, u32[]{:S(2)}, u32[]{:S(2)}) %collective-permute-start.32) | collective-permute-done | bytes 294944 | tf_op jit(solution)/shard_map/ppermute | solution.py:1173
  172.7 12.2 %attention_backward_1.1 = (bf16[128,1152]{1,0:T(8,128)(2,1)S(1)}, bf16[128,1152]{1,0:T(8,128)(2,1)S(1)}, bf16[128,1152]{1,0:T(8,128)(2,1)S(1)}, bf16[512,1536]{1...) custom-call(bf16[128,1152]{1,0:T(8,128)(2,1)S(1)} %get-tuple-element, ...), custom_call_target="tpu_custom_call" | custom-call | flops 1000 | bytes 1000 | tf_op jit(solution)/shard_map/attention_backward_1/pallas_call | solution.py:56
  187.7 6.5 %attention_weight_grads.2 = bf16[1152,1152]{1,0:T(8,128)(2,1)} custom-call(bf16[512,1152]{1,0:T(8,128)(2,1)} %get-tuple-element.265.a_in, bf16[512,1536]{1,0:T(8,128)(2,1)} %get-tuple-element.266.g_in, bf16[512,512]{1,0:T(8,128)(2,1)} %get-tuple-element.267.mixed_in, bf16[512,1152]{1,0:T(8,128)(2,1)} %get-tuple-element.268.ga_in, bf16[512,288]{1,0:T(8,128)(2,1)S(1)} %copy-done.1), custom_call_target="tpu_custom_call" | custom-call | flops 1000 | bytes 1000 | tf_op jit(solution)/shard_map/attention_weight_grads/pallas_call | solution.py:56
  194.2 5.4 %collective-permute-done.34.p2 = bf16[128,1152]{1,0:T(8,128)(2,1)S(1)} collective-permute-done((bf16[128,1152]{1,0:T(8,128)(2,1)S(1)}, bf16[128,1152]{1,0:T(8,128)(2,1)S(1)}, u32[]{:S(2)}, u32[]{:S(2)}) %collective-permute-start.34) | collective-permute-done | bytes 294944 | tf_op jit(solution)/shard_map/ppermute | solution.py:1173
  210.4 8.8 %collective-permute-done.37.source = bf16[128,1152]{1,0:T(8,128)(2,1)S(1)} collective-permute-done((bf16[128,1152]{1,0:T(8,128)(2,1)S(1)}, bf16[128,1152]{1,0:T(8,128)(2,1)S(1)}, u32[]{:S(2)}, u32[]{:S(2)}) %collective-permute-start.37) | collective-permute-done | bytes 294944 | tf_op jit(solution)/shard_map/ppermute | solution.py:1173
  219.2 9.4 %mlp_backward_0.1 = (bf16[128,1152]{1,0:T(8,128)(2,1)S(1)}, bf16[128,1152]{1,0:T(8,128)(2,1)S(1)}, bf16[128,1152]{1,0:T(8,128)(2,1)S(1)}, bf16[512,1152]{1,0:T(8...) custom-call(s32[2]{0:T(128)S(1)} %pad_add_fusion.where_ref, ...), custom_call_target="tpu_custom_call" | custom-call | flops 1000 | bytes 1000 | tf_op jit(solution)/shard_map/mlp_backward_0/pallas_call | solution.py:56
  231.6 6.4 %mlp_weight_grads.1 = bf16[1152,2304]{1,0:T(8,128)(2,1)} custom-call(bf16[512,1152]{1,0:T(8,128)(2,1)} %get-tuple-element.283.a_in, bf16[512,768]{1,0:T(8,128)(2,1)} %get-tuple-element.284.gg_in, bf16[512,768]{1,0:T(8,128)(2,1)} %get-tuple-element.285.gu_in, bf16[512,1152]{1,0:T(8,128)(2,1)} %get-tuple-element.286.gp_in, ...), custom_call_target="tpu_custom_call" | custom-call | flops 1000 | bytes 1000 | tf_op jit(solution)/shard_map/mlp_weight_grads/pallas_call | solution.py:56
  237.9 5.6 %collective-permute-done.41.p3 = bf16[128,1152]{1,0:T(8,128)(2,1)S(1)} collective-permute-done((bf16[128,1152]{1,0:T(8,128)(2,1)S(1)}, bf16[128,1152]{1,0:T(8,128)(2,1)S(1)}, u32[]{:S(2)}, u32[]{:S(2)}) %collective-permute-start.41) | collective-permute-done | bytes 294944 | tf_op jit(solution)/shard_map/ppermute | solution.py:1173
  255.4 9.1 %collective-permute-done.43.source = bf16[128,1152]{1,0:T(8,128)(2,1)S(1)} collective-permute-done((bf16[128,1152]{1,0:T(8,128)(2,1)S(1)}, bf16[128,1152]{1,0:T(8,128)(2,1)S(1)}, u32[]{:S(2)}, u32[]{:S(2)}) %collective-permute-start.43) | collective-permute-done | bytes 294944 | tf_op jit(solution)/shard_map/ppermute | solution.py:1173
  264.6 12.4 %attention_backward_0.1 = (bf16[128,1152]{1,0:T(8,128)(2,1)}, bf16[128,1152]{1,0:T(8,128)(2,1)S(1)}, bf16[128,1152]{1,0:T(8,128)(2,1)S(1)}, bf16[512,1536]{1,0:T...) custom-call(bf16[128,1152]{1,0:T(8,128)(2,1)S(1)} %get-tuple-element, ...), custom_call_target="tpu_custom_call" | custom-call | flops 1000 | bytes 1000 | tf_op jit(solution)/shard_map/attention_backward_0/pallas_call | solution.py:56
  279.8 6.7 %attention_weight_grads.3 = bf16[1152,1152]{1,0:T(8,128)(2,1)} custom-call(bf16[512,1152]{1,0:T(8,128)(2,1)} %get-tuple-element.307.a_in, bf16[512,1536]{1,0:T(8,128)(2,1)} %get-tuple-element.308.g_in, bf16[512,512]{1,0:T(8,128)(2,1)} %get-tuple-element.309.mixed_in, bf16[512,1152]{1,0:T(8,128)(2,1)} %get-tuple-element.310.ga_in, bf16[512,288]{1,0:T(8,128)(2,1)S(1)} %copy-done.1), custom_call_target="tpu_custom_call" | custom-call | flops 1000 | bytes 1000 | tf_op jit(solution)/shard_map/attention_weight_grads/pallas_call | solution.py:56
  321.2 4.9 %collective-permute-done.53 = f32[8,3136]{1,0:T(8,128)S(1)} collective-permute-done((f32[8,3136]{1,0:T(8,128)S(1)}, f32[8,3136]{1,0:T(8,128)S(1)}, u32[]{:S(2)}, u32[]{:S(2)}) %collective-permute-start.53) | collective-permute-done | bytes 100384 | tf_op jit(solution)/shard_map/ppermute | solution.py:1173
  341.4 7.1 %reduce-scatter.11.cloned.1.call-done = bf16[144,1152]{1,0:T(8,128)(2,1)} async-done(((bf16[1152,1152]{1,0:T(8,128)(2,1)}), bf16[144,1152]{1,0:T(8,128)(2,1)}) %reduce-scatter.11.cloned.1.call-update) | async-done | bytes 331792 | tf_op jit(solution)/shard_map/reduce_scatter | solution.py:1332
  (267 shorter events, 168.9 us)
Async XLA Ops:
  7.2 193.5 %reduce-scatter.5.cloned.1.call-start = ((), (), s32[]{:S(2)}) async-start(), calls=%async_computation.4 | async-start | bytes 5971968 | tf_op jit(solution)/shard_map/reduce_scatter | solution.py:1332
  7.2 16.8 %collective-permute-start.3 = (bf16[3,288,1152]{2,1,0:T(8,128)(2,1)}, bf16[3,288,1152]{2,1,0:T(8,128)(2,1)}, u32[]{:S(2)}, u32[]{:S(2)}) collective-permute-start(bf16[3,288,1152]{2,1,0:T(8,128)(2,1)} %bitcast.87), channel_id=1, source_target_pairs={{0,16},{16,0},{1,17},{17,1},{2,18},{18,2},{3,19},{19,3},{4,20},{20... | collective-permute-start | bytes 5971976 | tf_op jit(solution)/shard_map/ppermute | solution.py:1173
  7.3 16.6 %collective-permute-start.4 = (bf16[288,1152]{1,0:T(8,128)(2,1)}, bf16[288,1152]{1,0:T(8,128)(2,1)}, u32[]{:S(2)}, u32[]{:S(2)}) collective-permute-start(bf16[288,1152]{1,0:T(8,128)(2,1)} %bitcast.91), channel_id=1, source_target_pairs={{0,16},{16,0},{1,17},{17,1},{2,18},{18,2},{3,19},{19,3},{4,20},{20... | collective-permute-start | bytes 1990664 | tf_op jit(solution)/shard_map/ppermute | solution.py:1173
  26.1 43.2 %collective-permute-start.13 = (bf16[2,1152,768]{2,1,0:T(8,128)(2,1)}, bf16[2,1152,768]{2,1,0:T(8,128)(2,1)}, u32[]{:S(2)}, u32[]{:S(2)}) collective-permute-start(bf16[2,1152,768]{2,1,0:T(8,128)(2,1)} %bitcast.76), channel_id=1, source_target_pairs={{0,16},{16,0},{1,17},{17,1},{2,18},{18,2},{3,19},{19,3},{4,20},{20... | collective-permute-start | bytes 10616840 | tf_op jit(solution)/shard_map/ppermute | solution.py:1173
  26.3 43.1 %collective-permute-start.14 = (bf16[768,1152]{1,0:T(8,128)(2,1)S(1)}, bf16[768,1152]{1,0:T(8,128)(2,1)S(1)}, u32[]{:S(2)}, u32[]{:S(2)}) collective-permute-start(bf16[768,1152]{1,0:T(8,128)(2,1)S(1)} %bitcast.85), channel_id=1, source_target_pairs={{0,16},{16,0},{1,17},{17,1},{2,18},{18,2},{3,19},{19,3},{4,20},{20... | collective-permute-start | bytes 5308424 | tf_op jit(solution)/shard_map/ppermute | solution.py:1173
  44.9 14.2 %collective-permute-start.8 = (bf16[128,1152]{1,0:T(8,128)(2,1)S(1)}, bf16[128,1152]{1,0:T(8,128)(2,1)S(1)}, u32[]{:S(2)}, u32[]{:S(2)}) collective-permute-start(bf16[128,1152]{1,0:T(8,128)(2,1)S(1)} %get-tuple-element.204), channel_id=1, source_target_pairs={{0,8},{4,12},{8,0},{12,4},{1,9},{5,13},{9,1},{13,5},{2,10},{6,14},... | collective-permute-start | bytes 884744 | tf_op jit(solution)/shard_map/ppermute | solution.py:1173
  46.1 13.0 %collective-permute-start.9 = (bf16[128,1152]{1,0:T(8,128)(2,1)S(1)}, bf16[128,1152]{1,0:T(8,128)(2,1)S(1)}, u32[]{:S(2)}, u32[]{:S(2)}) collective-permute-start(bf16[128,1152]{1,0:T(8,128)(2,1)S(1)} %get-tuple-element.205), channel_id=1, source_target_pairs={{0,12},{4,8},{8,4},{12,0},{1,13},{5,9},{9,5},{13,1},{2,14},{6,10},... | collective-permute-start | bytes 884744 | tf_op jit(solution)/shard_map/ppermute | solution.py:1173
  77.2 12.8 %collective-permute-start.16 = (bf16[128,1152]{1,0:T(8,128)(2,1)S(1)}, bf16[128,1152]{1,0:T(8,128)(2,1)S(1)}, u32[]{:S(2)}, u32[]{:S(2)}) collective-permute-start(bf16[128,1152]{1,0:T(8,128)(2,1)S(1)} %get-tuple-element.220), channel_id=1, source_target_pairs={{0,8},{4,12},{8,0},{12,4},{1,9},{5,13},{9,1},{13,5},{2,10},{6,14},... | collective-permute-start | bytes 884744 | tf_op jit(solution)/shard_map/ppermute | solution.py:1173
  143.3 100.3 %reduce-scatter.7.cloned.1.call-start = ((), (), s32[]{:S(2)}) async-start(), calls=%async_computation.5 | async-start | bytes 2985984 | tf_op jit(solution)/shard_map/reduce_scatter | solution.py:1332
  185.9 13.8 %collective-permute-start.34 = (bf16[128,1152]{1,0:T(8,128)(2,1)S(1)}, bf16[128,1152]{1,0:T(8,128)(2,1)S(1)}, u32[]{:S(2)}, u32[]{:S(2)}) collective-permute-start(bf16[128,1152]{1,0:T(8,128)(2,1)S(1)} %get-tuple-element.263), channel_id=1, source_target_pairs={{0,8},{4,12},{8,0},{12,4},{1,9},{5,13},{9,1},{13,5},{2,10},{6,14},... | collective-permute-start | bytes 884744 | tf_op jit(solution)/shard_map/ppermute | solution.py:1173
  200.7 103.5 %reduce-scatter.9.cloned.1.call-start = ((), (), s32[]{:S(2)}) async-start(), calls=%async_computation.6 | async-start | bytes 5971968 | tf_op jit(solution)/shard_map/reduce_scatter | solution.py:1332
  205.9 13.3 %collective-permute-start.37 = (bf16[128,1152]{1,0:T(8,128)(2,1)S(1)}, bf16[128,1152]{1,0:T(8,128)(2,1)S(1)}, u32[]{:S(2)}, u32[]{:S(2)}) collective-permute-start(bf16[128,1152]{1,0:T(8,128)(2,1)S(1)} %get-tuple-element.275.refs_0_), channel_id=1, source_target_pairs={{0,8},{4,12},{8,0},{12,4},{1,9},{5,13},{9,1},{13,5},{2,10},{6,14},... | collective-permute-start | bytes 884744 | tf_op jit(solution)/shard_map/ppermute | solution.py:1173
  206.2 13.0 %collective-permute-start.36 = (bf16[128,1152]{1,0:T(8,128)(2,1)S(1)}, bf16[128,1152]{1,0:T(8,128)(2,1)S(1)}, u32[]{:S(2)}, u32[]{:S(2)}) collective-permute-start(bf16[128,1152]{1,0:T(8,128)(2,1)S(1)} %get-tuple-element.275.refs_0_), channel_id=1, source_target_pairs={{0,4},{4,0},{8,12},{12,8},{1,5},{5,1},{9,13},{13,9},{2,6},{6,2},{1... | collective-permute-start | bytes 884744 | tf_op jit(solution)/shard_map/ppermute | solution.py:1173
  230.5 13.0 %collective-permute-start.41 = (bf16[128,1152]{1,0:T(8,128)(2,1)S(1)}, bf16[128,1152]{1,0:T(8,128)(2,1)S(1)}, u32[]{:S(2)}, u32[]{:S(2)}) collective-permute-start(bf16[128,1152]{1,0:T(8,128)(2,1)S(1)} %get-tuple-element.282), channel_id=1, source_target_pairs={{0,12},{4,8},{8,4},{12,0},{1,13},{5,9},{9,5},{13,1},{2,14},{6,10},... | collective-permute-start | bytes 884744 | tf_op jit(solution)/shard_map/ppermute | solution.py:1173
  243.6 104.8 %reduce-scatter.11.cloned.1.call-start = ((), (), s32[]{:S(2)}) async-start(), calls=%async_computation.7 | async-start | bytes 2985984 | tf_op jit(solution)/shard_map/reduce_scatter | solution.py:1332
  249.5 15.0 %collective-permute-start.43 = (bf16[128,1152]{1,0:T(8,128)(2,1)S(1)}, bf16[128,1152]{1,0:T(8,128)(2,1)S(1)}, u32[]{:S(2)}, u32[]{:S(2)}) collective-permute-start(bf16[128,1152]{1,0:T(8,128)(2,1)S(1)} %get-tuple-element.296.b0), channel_id=1, source_target_pairs={{0,8},{4,12},{8,0},{12,4},{1,9},{5,13},{9,1},{13,5},{2,10},{6,14},... | collective-permute-start | bytes 884744 | tf_op jit(solution)/shard_map/ppermute | solution.py:1173
  249.5 15.1 %collective-permute-start.42 = (bf16[128,1152]{1,0:T(8,128)(2,1)S(1)}, bf16[128,1152]{1,0:T(8,128)(2,1)S(1)}, u32[]{:S(2)}, u32[]{:S(2)}) collective-permute-start(bf16[128,1152]{1,0:T(8,128)(2,1)S(1)} %get-tuple-element.296.b0), channel_id=1, source_target_pairs={{0,4},{4,0},{8,12},{12,8},{1,5},{5,1},{9,13},{13,9},{2,6},{6,2},{1... | collective-permute-start | bytes 884744 | tf_op jit(solution)/shard_map/ppermute | solution.py:1173
  278.6 12.8 %collective-permute-start.47 = (bf16[128,1152]{1,0:T(8,128)(2,1)S(1)}, bf16[128,1152]{1,0:T(8,128)(2,1)S(1)}, u32[]{:S(2)}, u32[]{:S(2)}) collective-permute-start(bf16[128,1152]{1,0:T(8,128)(2,1)S(1)} %get-tuple-element.306), channel_id=1, source_target_pairs={{0,12},{4,8},{8,4},{12,0},{1,13},{5,9},{9,5},{13,1},{2,14},{6,10},... | collective-permute-start | bytes 884744 | tf_op jit(solution)/shard_map/ppermute | solution.py:1173
  307.3 23.9 %collective-permute-start.60 = (bf16[128,1152]{1,0:T(8,128)(2,1)}, bf16[128,1152]{1,0:T(8,128)(2,1)S(1)}, u32[]{:S(2)}, u32[]{:S(2)}) collective-permute-start(bf16[128,1152]{1,0:T(8,128)(2,1)} %get-tuple-element.335), channel_id=1, source_target_pairs={{0,4},{4,0},{8,12},{12,8},{1,5},{5,1},{9,13},{13,9},{2,6},{6,2},{1... | collective-permute-start | bytes 884744 | tf_op jit(solution)/shard_map/ppermute | solution.py:1173
  312.7 13.4 %collective-permute-start.53 = (f32[8,3136]{1,0:T(8,128)S(1)}, f32[8,3136]{1,0:T(8,128)S(1)}, u32[]{:S(2)}, u32[]{:S(2)}) collective-permute-start(f32[8,3136]{1,0:T(8,128)S(1)} %concatenate.57), channel_id=1, source_target_pairs={{0,2},{1,3},{2,0},{3,1},{4,6},{5,7},{6,4},{7,5},{8,10},{9,11},{10,... | collective-permute-start | bytes 301064 | tf_op jit(solution)/shard_map/ppermute | solution.py:1173
  312.9 14.0 %collective-permute-start.52 = (f32[8,3136]{1,0:T(8,128)S(1)}, f32[8,3136]{1,0:T(8,128)S(1)}, u32[]{:S(2)}, u32[]{:S(2)}) collective-permute-start(f32[8,3136]{1,0:T(8,128)S(1)} %concatenate.57), channel_id=1, source_target_pairs={{0,1},{1,0},{2,3},{3,2},{4,5},{5,4},{6,7},{7,6},{8,9},{9,8},{10,11... | collective-permute-start | bytes 301064 | tf_op jit(solution)/shard_map/ppermute | solution.py:1173
  319.1 14.6 %collective-permute-start.61 = (bf16[128,1152]{1,0:T(8,128)(2,1)S(1)}, bf16[128,1152]{1,0:T(8,128)(2,1)S(1)}, u32[]{:S(2)}, u32[]{:S(2)}) collective-permute-start(bf16[128,1152]{1,0:T(8,128)(2,1)S(1)} %copy-done.17), channel_id=1, source_target_pairs={{0,8},{4,12},{8,0},{12,4},{1,9},{5,13},{9,1},{13,5},{2,10},{6,14},... | collective-permute-start | bytes 884744 | tf_op jit(solution)/shard_map/ppermute | solution.py:1173
  320.6 13.1 %collective-permute-start.62 = (bf16[128,1152]{1,0:T(8,128)(2,1)S(1)}, bf16[128,1152]{1,0:T(8,128)(2,1)S(1)}, u32[]{:S(2)}, u32[]{:S(2)}) collective-permute-start(bf16[128,1152]{1,0:T(8,128)(2,1)S(1)} %copy-done.16), channel_id=1, source_target_pairs={{0,12},{4,8},{8,4},{12,0},{1,13},{5,9},{9,5},{13,1},{2,14},{6,10},... | collective-permute-start | bytes 884744 | tf_op jit(solution)/shard_map/ppermute | solution.py:1173
  335.9 16.4 %collective-permute-start.63 = (f32[128,1152]{1,0:T(8,128)}, f32[128,1152]{1,0:T(8,128)}, u32[]{:S(2)}, u32[]{:S(2)}) collective-permute-start(f32[128,1152]{1,0:T(8,128)} %broadcast_select_fusion.6), channel_id=1, source_target_pairs={{0,16},{16,0},{1,17},{17,1},{2,18},{18,2},{3,19},{19,3},{4,20},{20... | collective-permute-start | bytes 1769480 | tf_op jit(solution)/shard_map/ppermute | solution.py:1173
  (62 other events, 498.1 us)
Sparse Core Ops, SparseCore 0:
  143.4 57.2 reduce-scatter.4
  202.9 35.8 reduce-scatter.6
  243.7 60.3 reduce-scatter.8
  307.4 40.9 reduce-scatter.10

commit v6 on v5

--- a/solution.py
+++ b/solution.py
@@ -397,14 +397,13 @@
                 carried_copies = load(list(zip(carried_refs, carried_outs)), carried_sems)
                 keep(6)
             gain = gain_ref[2 * layer + i : 2 * layer + i + 1]
-            for h2 in range(0, heads, 2):
-                both = nn(a_ref[...], wq_ref[i, :, h2 * LANE : (h2 + 2) * LANE])
-                for h in (h2, h2 + 1):
-                    at = slice(h * LANE, (h + 1) * LANE)
-                    raw = both[:, (h - h2) * LANE : (h - h2 + 1) * LANE]
-                    raw_out[:, at] = raw.astype(BF)
-                    turned = rotate(raw * head_inverse(raw) * gain, cos, sin)
-                    rot_out[:, at] = turned.astype(BF)
+            all_raw = nn(a_ref[...], wq_ref[i])
+            for h in range(heads):
+                at = slice(h * LANE, (h + 1) * LANE)
+                raw = all_raw[:, at]
+                raw_out[:, at] = raw.astype(BF)
+                turned = rotate(raw * head_inverse(raw) * gain, cos, sin)
+                rot_out[:, at] = turned.astype(BF)
             keep(i)
             keep(2 + i)
         weights_in[2].wait()
@@ -682,7 +681,7 @@
     hidden_size, width = wd_own.shape
     rows = c1.shape[0]
     share = rows // 4
-    chunk = 2 * LANE
+    chunk = 3 * LANE
     chunks = hidden_size // chunk
 
     def body(where_ref, *refs):

time: 370 us -> 367 us (level)
  no operation moved by 1% of the time
where the time goes in v6:
time: 367 us; the launch traced here: 361 us
  Pallas kernels  140 us (38%)
  waiting for transfers between devices  125 us (34%)
  starting transfers between devices  63 us (17%)
  between operations  14.9 us (4%)
  other arithmetic  8.06 us (2%)
  local copies, waits for them, and re-layouts  5.31 us (1%)
  matrix products  4.76 us (1%)
    pallas_call x64, Pallas kernels, run(): return kernel(*placed)  140 us
    ppermute x64, waiting for transfers between devices, exchange(): lax.ppermute(value, axis, [(i, i ^ k) for i in range(lax.axis_size(axis))])  114 us
    ppermute x64, starting transfers between devices, exchange(): lax.ppermute(value, axis, [(i, i ^ k) for i in range(lax.axis_size(axis))])  62.6 us
    reduce_scatter x4, waiting for transfers between devices, data_sum(): lax.psum_scatter(value, ('dp', 'section'), scatter_dimension=0, tiled=True)  10.9 us
  transfers between devices with their start and end apart: 68, of which 33 were waited for; matrix products, arithmetic and copies ran while one was open for 4% of the time, Pallas kernels for 31%

profile of v6, /device:TPU:1, one launch (start us, length us, event | category | flops | bytes accessed | tf_op | source)
XLA Modules:
  0.0 360.5 jit_solution(4101540990144962144)
XLA Ops:
  15.4 6.1 %prepare_weights.3 = (bf16[2,3,1152,512]{3,2,1,0:T(8,128)(2,1)}, bf16[2,512,1152]{2,1,0:T(8,128)(2,1)}) custom-call(s32[2]{0:T(128)S(1)} %pad_add_fusion.where_ref, bf16[3,288,1152]{2,1,0:T(8,128)(2,1)} %bitcast.88, bf16[288,1152]{1,0:T(8,128)(2,1)} %bitcast.92, bf16[288,512]{1,0:T(8,128)(2,1)S(1)} %copy-done), custom_call_target="tpu_custom_call" | custom-call | flops 1000 | bytes 1000 | tf_op jit(solution)/shard_map/prepare_weights/pallas_call | solution.py:56
  26.6 6.3 %prepare_weights.4 = (bf16[2,3,1152,512]{3,2,1,0:T(8,128)(2,1)}, bf16[2,512,1152]{2,1,0:T(8,128)(2,1)}) custom-call(s32[2]{0:T(128)S(1)} %pad_add_fusion.where_ref, bf16[3,288,1152]{2,1,0:T(8,128)(2,1)} %collective-permute-done.3.wq_in, bf16[288,1152]{1,0:T(8,128)(2,1)} %collective-permute-done.4.wo_in, ...), custom_call_target="tpu_custom_call", output_to_operand_aliasing={{0}: (4, {}), {1}: (5, {})} | custom-call | flops 1000 | bytes 1000 | tf_op jit(solution)/shard_map/prepare_weights/pallas_call | solution.py:56
  32.9 9.3 %attention_forward_0.1 = (bf16[128,1152]{1,0:T(8,128)(2,1)S(1)}, bf16[128,1152]{1,0:T(8,128)(2,1)S(1)}, bf16[128,1152]{1,0:T(8,128)(2,1)S(1)}, bf16[128,1152]{1,...) custom-call(s32[2]{0:T(128)S(1)} %pad_add_fusion.where_ref, ...), custom_call_target="tpu_custom_call" | custom-call | flops 1000 | bytes 1000 | tf_op jit(solution)/shard_map/attention_forward_0/pallas_call | solution.py:56
  49.7 8.4 %collective-permute-done.8.source = bf16[128,1152]{1,0:T(8,128)(2,1)S(1)} collective-permute-done((bf16[128,1152]{1,0:T(8,128)(2,1)S(1)}, bf16[128,1152]{1,0:T(8,128)(2,1)S(1)}, u32[]{:S(2)}, u32[]{:S(2)}) %collective-permute-start.8) | collective-permute-done | bytes 294944 | tf_op jit(solution)/shard_map/ppermute | solution.py:1172
  69.6 6.2 %mlp_forward_0.1 = (bf16[128,1152]{1,0:T(8,128)(2,1)S(1)}, bf16[128,1152]{1,0:T(8,128)(2,1)S(1)}, bf16[128,1152]{1,0:T(8,128)(2,1)S(1)}, bf16[128,1152]{1,0:T(8,...) custom-call(s32[1]{0:T(128)} %bitcast.sec_ref, ...), custom_call_target="tpu_custom_call" | custom-call | flops 1000 | bytes 1000 | tf_op jit(solution)/shard_map/mlp_forward_0/pallas_call | solution.py:56
  83.4 5.6 %collective-permute-done.16.source = bf16[128,1152]{1,0:T(8,128)(2,1)S(1)} collective-permute-done((bf16[128,1152]{1,0:T(8,128)(2,1)S(1)}, bf16[128,1152]{1,0:T(8,128)(2,1)S(1)}, u32[]{:S(2)}, u32[]{:S(2)}) %collective-permute-start.16) | collective-permute-done | bytes 294944 | tf_op jit(solution)/shard_map/ppermute | solution.py:1172
  99.3 8.4 %attention_forward_1.1 = (bf16[128,1152]{1,0:T(8,128)(2,1)S(1)}, bf16[128,1152]{1,0:T(8,128)(2,1)S(1)}, bf16[128,1152]{1,0:T(8,128)(2,1)S(1)}, bf16[128,1152]{1,...) custom-call(s32[2]{0:T(128)S(1)} %pad_add_fusion.where_ref, ...), custom_call_target="tpu_custom_call" | custom-call | flops 1000 | bytes 1000 | tf_op jit(solution)/shard_map/attention_forward_1/pallas_call | solution.py:56
  113.5 7.8 %collective-permute-done.22.source = bf16[128,1152]{1,0:T(8,128)(2,1)S(1)} collective-permute-done((bf16[128,1152]{1,0:T(8,128)(2,1)S(1)}, bf16[128,1152]{1,0:T(8,128)(2,1)S(1)}, u32[]{:S(2)}, u32[]{:S(2)}) %collective-permute-start.22) | collective-permute-done | bytes 294944 | tf_op jit(solution)/shard_map/ppermute | solution.py:1172
  132.0 9.3 %mlp_last_1.1 = (bf16[512,768]{1,0:T(8,128)(2,1)S(1)}, bf16[512,768]{1,0:T(8,128)(2,1)S(1)}, bf16[1152,2304]{1,0:T(8,128)(2,1)}, bf16[512,768]{1,0:T(8,128)(2,1)...) custom-call(s32[1]{0:T(128)} %bitcast.sec_ref, bf16[128,1152]{1,0:T(8,128)(2,1)S(1)} %get-tuple-element.231.b0, ...), custom_call_target="tpu_custom_call" | custom-call | flops 1000 | bytes 1000 | tf_op jit(solution)/shard_map/mlp_last_1/pallas_call | solution.py:56
  141.5 4.9 %mlp_input_grad.1 = (bf16[128,1152]{1,0:T(8,128)(2,1)S(1)}, bf16[128,1152]{1,0:T(8,128)(2,1)S(1)}, bf16[128,1152]{1,0:T(8,128)(2,1)S(1)}, bf16[128,1152]{1,0:T(8,128)(2,1)}) custom-call(s32[1]{0:T(128)} %bitcast.sec_ref, bf16[512,768]{1,0:T(8,128)(2,1)S(1)} %get-tuple-element.236.gg_ref, bf16[512,768]{1,0:T(8,128)(2,1)S(1)} %get-tuple-element.237.gup_ref, ...), custom_call_target="tpu_custom_call" | custom-call | flops 1000 | bytes 1000 | tf_op jit(solution)/shard_map/mlp_input_grad/pallas_call | solution.py:56
  149.1 5.9 %last_projection.1 = (bf16[128,1152]{1,0:T(8,128)(2,1)}, bf16[128,1152]{1,0:T(8,128)(2,1)}, bf16[128,1152]{1,0:T(8,128)(2,1)}, bf16[128,1152]{1,0:T(8,128)(2,1)}, f32[1,8,1152]{2,1,0:T(8,128)}) custom-call(s32[2]{0:T(128)S(1)} %pad_add_fusion.where_ref, bf16[512,768]{1,0:T(8,128)(2,1)} %get-tuple-element.240.hid_in, bf16[768,1152]{1,0:T(8,128)(2,1)} %bitcast.83, ...), custom_call_target="tpu_custom_call" | custom-call | flops 1000 | bytes 1000 | tf_op jit(solution)/shard_map/last_projection/pallas_call | solution.py:56
  162.9 5.1 %collective-permute-done.32.source = bf16[128,1152]{1,0:T(8,128)(2,1)S(1)} collective-permute-done((bf16[128,1152]{1,0:T(8,128)(2,1)S(1)}, bf16[128,1152]{1,0:T(8,128)(2,1)S(1)}, u32[]{:S(2)}, u32[]{:S(2)}) %collective-permute-start.32) | collective-permute-done | bytes 294944 | tf_op jit(solution)/shard_map/ppermute | solution.py:1172
  171.1 12.3 %attention_backward_1.1 = (bf16[128,1152]{1,0:T(8,128)(2,1)S(1)}, bf16[128,1152]{1,0:T(8,128)(2,1)S(1)}, bf16[128,1152]{1,0:T(8,128)(2,1)S(1)}, bf16[512,1536]{1...) custom-call(bf16[128,1152]{1,0:T(8,128)(2,1)S(1)} %get-tuple-element, ...), custom_call_target="tpu_custom_call" | custom-call | flops 1000 | bytes 1000 | tf_op jit(solution)/shard_map/attention_backward_1/pallas_call | solution.py:56
  186.1 6.5 %attention_weight_grads.2 = bf16[1152,1152]{1,0:T(8,128)(2,1)} custom-call(bf16[512,1152]{1,0:T(8,128)(2,1)} %get-tuple-element.265.a_in, bf16[512,1536]{1,0:T(8,128)(2,1)} %get-tuple-element.266.g_in, bf16[512,512]{1,0:T(8,128)(2,1)} %get-tuple-element.267.mixed_in, bf16[512,1152]{1,0:T(8,128)(2,1)} %get-tuple-element.268.ga_in, bf16[512,288]{1,0:T(8,128)(2,1)S(1)} %copy-done.1), custom_call_target="tpu_custom_call" | custom-call | flops 1000 | bytes 1000 | tf_op jit(solution)/shard_map/attention_weight_grads/pallas_call | solution.py:56
  192.7 5.4 %collective-permute-done.34.p2 = bf16[128,1152]{1,0:T(8,128)(2,1)S(1)} collective-permute-done((bf16[128,1152]{1,0:T(8,128)(2,1)S(1)}, bf16[128,1152]{1,0:T(8,128)(2,1)S(1)}, u32[]{:S(2)}, u32[]{:S(2)}) %collective-permute-start.34) | collective-permute-done | bytes 294944 | tf_op jit(solution)/shard_map/ppermute | solution.py:1172
  208.7 8.8 %collective-permute-done.37.source = bf16[128,1152]{1,0:T(8,128)(2,1)S(1)} collective-permute-done((bf16[128,1152]{1,0:T(8,128)(2,1)S(1)}, bf16[128,1152]{1,0:T(8,128)(2,1)S(1)}, u32[]{:S(2)}, u32[]{:S(2)}) %collective-permute-start.37) | collective-permute-done | bytes 294944 | tf_op jit(solution)/shard_map/ppermute | solution.py:1172
  217.4 7.9 %mlp_backward_0.1 = (bf16[128,1152]{1,0:T(8,128)(2,1)S(1)}, bf16[128,1152]{1,0:T(8,128)(2,1)S(1)}, bf16[128,1152]{1,0:T(8,128)(2,1)S(1)}, bf16[512,1152]{1,0:T(8...) custom-call(s32[2]{0:T(128)S(1)} %pad_add_fusion.where_ref, ...), custom_call_target="tpu_custom_call" | custom-call | flops 1000 | bytes 1000 | tf_op jit(solution)/shard_map/mlp_backward_0/pallas_call | solution.py:56
  228.4 6.4 %mlp_weight_grads.1 = bf16[1152,2304]{1,0:T(8,128)(2,1)} custom-call(bf16[512,1152]{1,0:T(8,128)(2,1)} %get-tuple-element.283.a_in, bf16[512,768]{1,0:T(8,128)(2,1)} %get-tuple-element.284.gg_in, bf16[512,768]{1,0:T(8,128)(2,1)} %get-tuple-element.285.gu_in, bf16[512,1152]{1,0:T(8,128)(2,1)} %get-tuple-element.286.gp_in, ...), custom_call_target="tpu_custom_call" | custom-call | flops 1000 | bytes 1000 | tf_op jit(solution)/shard_map/mlp_weight_grads/pallas_call | solution.py:56
  234.7 5.7 %collective-permute-done.41.p3 = bf16[128,1152]{1,0:T(8,128)(2,1)S(1)} collective-permute-done((bf16[128,1152]{1,0:T(8,128)(2,1)S(1)}, bf16[128,1152]{1,0:T(8,128)(2,1)S(1)}, u32[]{:S(2)}, u32[]{:S(2)}) %collective-permute-start.41) | collective-permute-done | bytes 294944 | tf_op jit(solution)/shard_map/ppermute | solution.py:1172
  252.4 9.1 %collective-permute-done.43.source = bf16[128,1152]{1,0:T(8,128)(2,1)S(1)} collective-permute-done((bf16[128,1152]{1,0:T(8,128)(2,1)S(1)}, bf16[128,1152]{1,0:T(8,128)(2,1)S(1)}, u32[]{:S(2)}, u32[]{:S(2)}) %collective-permute-start.43) | collective-permute-done | bytes 294944 | tf_op jit(solution)/shard_map/ppermute | solution.py:1172
  261.5 12.4 %attention_backward_0.1 = (bf16[128,1152]{1,0:T(8,128)(2,1)}, bf16[128,1152]{1,0:T(8,128)(2,1)S(1)}, bf16[128,1152]{1,0:T(8,128)(2,1)S(1)}, bf16[512,1536]{1,0:T...) custom-call(bf16[128,1152]{1,0:T(8,128)(2,1)S(1)} %get-tuple-element, ...), custom_call_target="tpu_custom_call" | custom-call | flops 1000 | bytes 1000 | tf_op jit(solution)/shard_map/attention_backward_0/pallas_call | solution.py:56
  276.6 6.7 %attention_weight_grads.3 = bf16[1152,1152]{1,0:T(8,128)(2,1)} custom-call(bf16[512,1152]{1,0:T(8,128)(2,1)} %get-tuple-element.307.a_in, bf16[512,1536]{1,0:T(8,128)(2,1)} %get-tuple-element.308.g_in, bf16[512,512]{1,0:T(8,128)(2,1)} %get-tuple-element.309.mixed_in, bf16[512,1152]{1,0:T(8,128)(2,1)} %get-tuple-element.310.ga_in, bf16[512,288]{1,0:T(8,128)(2,1)S(1)} %copy-done.1), custom_call_target="tpu_custom_call" | custom-call | flops 1000 | bytes 1000 | tf_op jit(solution)/shard_map/attention_weight_grads/pallas_call | solution.py:56
  317.9 5.2 %collective-permute-done.53 = f32[8,3136]{1,0:T(8,128)S(1)} collective-permute-done((f32[8,3136]{1,0:T(8,128)S(1)}, f32[8,3136]{1,0:T(8,128)S(1)}, u32[]{:S(2)}, u32[]{:S(2)}) %collective-permute-start.53) | collective-permute-done | bytes 100384 | tf_op jit(solution)/shard_map/ppermute | solution.py:1172
  338.1 7.6 %reduce-scatter.11.cloned.1.call-done = bf16[144,1152]{1,0:T(8,128)(2,1)} async-done(((bf16[1152,1152]{1,0:T(8,128)(2,1)}), bf16[144,1152]{1,0:T(8,128)(2,1)}) %reduce-scatter.11.cloned.1.call-update) | async-done | bytes 331792 | tf_op jit(solution)/shard_map/reduce_scatter | solution.py:1331
  (267 shorter events, 168.2 us)
Async XLA Ops:
  7.2 191.7 %reduce-scatter.5.cloned.1.call-start = ((), (), s32[]{:S(2)}) async-start(), calls=%async_computation.4 | async-start | bytes 5971968 | tf_op jit(solution)/shard_map/reduce_scatter | solution.py:1331
  7.2 16.8 %collective-permute-start.3 = (bf16[3,288,1152]{2,1,0:T(8,128)(2,1)}, bf16[3,288,1152]{2,1,0:T(8,128)(2,1)}, u32[]{:S(2)}, u32[]{:S(2)}) collective-permute-start(bf16[3,288,1152]{2,1,0:T(8,128)(2,1)} %bitcast.87), channel_id=1, source_target_pairs={{0,16},{16,0},{1,17},{17,1},{2,18},{18,2},{3,19},{19,3},{4,20},{20... | collective-permute-start | bytes 5971976 | tf_op jit(solution)/shard_map/ppermute | solution.py:1172
  7.3 16.6 %collective-permute-start.4 = (bf16[288,1152]{1,0:T(8,128)(2,1)}, bf16[288,1152]{1,0:T(8,128)(2,1)}, u32[]{:S(2)}, u32[]{:S(2)}) collective-permute-start(bf16[288,1152]{1,0:T(8,128)(2,1)} %bitcast.91), channel_id=1, source_target_pairs={{0,16},{16,0},{1,17},{17,1},{2,18},{18,2},{3,19},{19,3},{4,20},{20... | collective-permute-start | bytes 1990664 | tf_op jit(solution)/shard_map/ppermute | solution.py:1172
  26.1 42.3 %collective-permute-start.13 = (bf16[2,1152,768]{2,1,0:T(8,128)(2,1)}, bf16[2,1152,768]{2,1,0:T(8,128)(2,1)}, u32[]{:S(2)}, u32[]{:S(2)}) collective-permute-start(bf16[2,1152,768]{2,1,0:T(8,128)(2,1)} %bitcast.76), channel_id=1, source_target_pairs={{0,16},{16,0},{1,17},{17,1},{2,18},{18,2},{3,19},{19,3},{4,20},{20... | collective-permute-start | bytes 10616840 | tf_op jit(solution)/shard_map/ppermute | solution.py:1172
  26.3 42.1 %collective-permute-start.14 = (bf16[768,1152]{1,0:T(8,128)(2,1)S(1)}, bf16[768,1152]{1,0:T(8,128)(2,1)S(1)}, u32[]{:S(2)}, u32[]{:S(2)}) collective-permute-start(bf16[768,1152]{1,0:T(8,128)(2,1)S(1)} %bitcast.85), channel_id=1, source_target_pairs={{0,16},{16,0},{1,17},{17,1},{2,18},{18,2},{3,19},{19,3},{4,20},{20... | collective-permute-start | bytes 5308424 | tf_op jit(solution)/shard_map/ppermute | solution.py:1172
  43.9 14.2 %collective-permute-start.8 = (bf16[128,1152]{1,0:T(8,128)(2,1)S(1)}, bf16[128,1152]{1,0:T(8,128)(2,1)S(1)}, u32[]{:S(2)}, u32[]{:S(2)}) collective-permute-start(bf16[128,1152]{1,0:T(8,128)(2,1)S(1)} %get-tuple-element.204), channel_id=1, source_target_pairs={{0,8},{4,12},{8,0},{12,4},{1,9},{5,13},{9,1},{13,5},{2,10},{6,14},... | collective-permute-start | bytes 884744 | tf_op jit(solution)/shard_map/ppermute | solution.py:1172
  45.2 12.9 %collective-permute-start.9 = (bf16[128,1152]{1,0:T(8,128)(2,1)S(1)}, bf16[128,1152]{1,0:T(8,128)(2,1)S(1)}, u32[]{:S(2)}, u32[]{:S(2)}) collective-permute-start(bf16[128,1152]{1,0:T(8,128)(2,1)S(1)} %get-tuple-element.205), channel_id=1, source_target_pairs={{0,12},{4,8},{8,4},{12,0},{1,13},{5,9},{9,5},{13,1},{2,14},{6,10},... | collective-permute-start | bytes 884744 | tf_op jit(solution)/shard_map/ppermute | solution.py:1172
  76.2 12.8 %collective-permute-start.16 = (bf16[128,1152]{1,0:T(8,128)(2,1)S(1)}, bf16[128,1152]{1,0:T(8,128)(2,1)S(1)}, u32[]{:S(2)}, u32[]{:S(2)}) collective-permute-start(bf16[128,1152]{1,0:T(8,128)(2,1)S(1)} %get-tuple-element.220), channel_id=1, source_target_pairs={{0,8},{4,12},{8,0},{12,4},{1,9},{5,13},{9,1},{13,5},{2,10},{6,14},... | collective-permute-start | bytes 884744 | tf_op jit(solution)/shard_map/ppermute | solution.py:1172
  141.4 99.0 %reduce-scatter.7.cloned.1.call-start = ((), (), s32[]{:S(2)}) async-start(), calls=%async_computation.5 | async-start | bytes 2985984 | tf_op jit(solution)/shard_map/reduce_scatter | solution.py:1331
  184.5 13.6 %collective-permute-start.34 = (bf16[128,1152]{1,0:T(8,128)(2,1)S(1)}, bf16[128,1152]{1,0:T(8,128)(2,1)S(1)}, u32[]{:S(2)}, u32[]{:S(2)}) collective-permute-start(bf16[128,1152]{1,0:T(8,128)(2,1)S(1)} %get-tuple-element.263), channel_id=1, source_target_pairs={{0,8},{4,12},{8,0},{12,4},{1,9},{5,13},{9,1},{13,5},{2,10},{6,14},... | collective-permute-start | bytes 884744 | tf_op jit(solution)/shard_map/ppermute | solution.py:1172
  198.9 101.9 %reduce-scatter.9.cloned.1.call-start = ((), (), s32[]{:S(2)}) async-start(), calls=%async_computation.6 | async-start | bytes 5971968 | tf_op jit(solution)/shard_map/reduce_scatter | solution.py:1331
  204.1 13.3 %collective-permute-start.37 = (bf16[128,1152]{1,0:T(8,128)(2,1)S(1)}, bf16[128,1152]{1,0:T(8,128)(2,1)S(1)}, u32[]{:S(2)}, u32[]{:S(2)}) collective-permute-start(bf16[128,1152]{1,0:T(8,128)(2,1)S(1)} %get-tuple-element.275.refs_0_), channel_id=1, source_target_pairs={{0,8},{4,12},{8,0},{12,4},{1,9},{5,13},{9,1},{13,5},{2,10},{6,14},... | collective-permute-start | bytes 884744 | tf_op jit(solution)/shard_map/ppermute | solution.py:1172
  204.4 13.0 %collective-permute-start.36 = (bf16[128,1152]{1,0:T(8,128)(2,1)S(1)}, bf16[128,1152]{1,0:T(8,128)(2,1)S(1)}, u32[]{:S(2)}, u32[]{:S(2)}) collective-permute-start(bf16[128,1152]{1,0:T(8,128)(2,1)S(1)} %get-tuple-element.275.refs_0_), channel_id=1, source_target_pairs={{0,4},{4,0},{8,12},{12,8},{1,5},{5,1},{9,13},{13,9},{2,6},{6,2},{1... | collective-permute-start | bytes 884744 | tf_op jit(solution)/shard_map/ppermute | solution.py:1172
  227.4 13.1 %collective-permute-start.41 = (bf16[128,1152]{1,0:T(8,128)(2,1)S(1)}, bf16[128,1152]{1,0:T(8,128)(2,1)S(1)}, u32[]{:S(2)}, u32[]{:S(2)}) collective-permute-start(bf16[128,1152]{1,0:T(8,128)(2,1)S(1)} %get-tuple-element.282), channel_id=1, source_target_pairs={{0,12},{4,8},{8,4},{12,0},{1,13},{5,9},{9,5},{13,1},{2,14},{6,10},... | collective-permute-start | bytes 884744 | tf_op jit(solution)/shard_map/ppermute | solution.py:1172
  240.5 105.2 %reduce-scatter.11.cloned.1.call-start = ((), (), s32[]{:S(2)}) async-start(), calls=%async_computation.7 | async-start | bytes 2985984 | tf_op jit(solution)/shard_map/reduce_scatter | solution.py:1331
  246.3 15.2 %collective-permute-start.43 = (bf16[128,1152]{1,0:T(8,128)(2,1)S(1)}, bf16[128,1152]{1,0:T(8,128)(2,1)S(1)}, u32[]{:S(2)}, u32[]{:S(2)}) collective-permute-start(bf16[128,1152]{1,0:T(8,128)(2,1)S(1)} %get-tuple-element.296.b0), channel_id=1, source_target_pairs={{0,8},{4,12},{8,0},{12,4},{1,9},{5,13},{9,1},{13,5},{2,10},{6,14},... | collective-permute-start | bytes 884744 | tf_op jit(solution)/shard_map/ppermute | solution.py:1172
  246.3 15.2 %collective-permute-start.42 = (bf16[128,1152]{1,0:T(8,128)(2,1)S(1)}, bf16[128,1152]{1,0:T(8,128)(2,1)S(1)}, u32[]{:S(2)}, u32[]{:S(2)}) collective-permute-start(bf16[128,1152]{1,0:T(8,128)(2,1)S(1)} %get-tuple-element.296.b0), channel_id=1, source_target_pairs={{0,4},{4,0},{8,12},{12,8},{1,5},{5,1},{9,13},{13,9},{2,6},{6,2},{1... | collective-permute-start | bytes 884744 | tf_op jit(solution)/shard_map/ppermute | solution.py:1172
  275.3 12.7 %collective-permute-start.47 = (bf16[128,1152]{1,0:T(8,128)(2,1)S(1)}, bf16[128,1152]{1,0:T(8,128)(2,1)S(1)}, u32[]{:S(2)}, u32[]{:S(2)}) collective-permute-start(bf16[128,1152]{1,0:T(8,128)(2,1)S(1)} %get-tuple-element.306), channel_id=1, source_target_pairs={{0,12},{4,8},{8,4},{12,0},{1,13},{5,9},{9,5},{13,1},{2,14},{6,10},... | collective-permute-start | bytes 884744 | tf_op jit(solution)/shard_map/ppermute | solution.py:1172
  304.0 23.7 %collective-permute-start.60 = (bf16[128,1152]{1,0:T(8,128)(2,1)}, bf16[128,1152]{1,0:T(8,128)(2,1)S(1)}, u32[]{:S(2)}, u32[]{:S(2)}) collective-permute-start(bf16[128,1152]{1,0:T(8,128)(2,1)} %get-tuple-element.335), channel_id=1, source_target_pairs={{0,4},{4,0},{8,12},{12,8},{1,5},{5,1},{9,13},{13,9},{2,6},{6,2},{1... | collective-permute-start | bytes 884744 | tf_op jit(solution)/shard_map/ppermute | solution.py:1172
  309.4 13.7 %collective-permute-start.53 = (f32[8,3136]{1,0:T(8,128)S(1)}, f32[8,3136]{1,0:T(8,128)S(1)}, u32[]{:S(2)}, u32[]{:S(2)}) collective-permute-start(f32[8,3136]{1,0:T(8,128)S(1)} %concatenate.57), channel_id=1, source_target_pairs={{0,2},{1,3},{2,0},{3,1},{4,6},{5,7},{6,4},{7,5},{8,10},{9,11},{10,... | collective-permute-start | bytes 301064 | tf_op jit(solution)/shard_map/ppermute | solution.py:1172
  309.7 14.0 %collective-permute-start.52 = (f32[8,3136]{1,0:T(8,128)S(1)}, f32[8,3136]{1,0:T(8,128)S(1)}, u32[]{:S(2)}, u32[]{:S(2)}) collective-permute-start(f32[8,3136]{1,0:T(8,128)S(1)} %concatenate.57), channel_id=1, source_target_pairs={{0,1},{1,0},{2,3},{3,2},{4,5},{5,4},{6,7},{7,6},{8,9},{9,8},{10,11... | collective-permute-start | bytes 301064 | tf_op jit(solution)/shard_map/ppermute | solution.py:1172
  315.8 14.6 %collective-permute-start.61 = (bf16[128,1152]{1,0:T(8,128)(2,1)S(1)}, bf16[128,1152]{1,0:T(8,128)(2,1)S(1)}, u32[]{:S(2)}, u32[]{:S(2)}) collective-permute-start(bf16[128,1152]{1,0:T(8,128)(2,1)S(1)} %copy-done.17), channel_id=1, source_target_pairs={{0,8},{4,12},{8,0},{12,4},{1,9},{5,13},{9,1},{13,5},{2,10},{6,14},... | collective-permute-start | bytes 884744 | tf_op jit(solution)/shard_map/ppermute | solution.py:1172
  317.2 13.2 %collective-permute-start.62 = (bf16[128,1152]{1,0:T(8,128)(2,1)S(1)}, bf16[128,1152]{1,0:T(8,128)(2,1)S(1)}, u32[]{:S(2)}, u32[]{:S(2)}) collective-permute-start(bf16[128,1152]{1,0:T(8,128)(2,1)S(1)} %copy-done.16), channel_id=1, source_target_pairs={{0,12},{4,8},{8,4},{12,0},{1,13},{5,9},{9,5},{13,1},{2,14},{6,10},... | collective-permute-start | bytes 884744 | tf_op jit(solution)/shard_map/ppermute | solution.py:1172
  332.7 16.5 %collective-permute-start.63 = (f32[128,1152]{1,0:T(8,128)}, f32[128,1152]{1,0:T(8,128)}, u32[]{:S(2)}, u32[]{:S(2)}) collective-permute-start(f32[128,1152]{1,0:T(8,128)} %broadcast_select_fusion.6), channel_id=1, source_target_pairs={{0,16},{16,0},{1,17},{17,1},{2,18},{18,2},{3,19},{19,3},{4,20},{20... | collective-permute-start | bytes 1769480 | tf_op jit(solution)/shard_map/ppermute | solution.py:1172
  (62 other events, 499.7 us)
Sparse Core Ops, SparseCore 0:
  141.5 57.3 reduce-scatter.4
  201.2 35.9 reduce-scatter.6
  240.6 60.2 reduce-scatter.8
  304.1 41.4 reduce-scatter.10

commit v7 on v6

--- a/solution.py
+++ b/solution.py
@@ -763,7 +763,7 @@
     share = rows // 4
     chunk = 2 * LANE
     chunks = size // chunk
-    step = 3 * LANE
+    step = LANE
 
     def body(sec_ref, b0, b1, b2, b3, gu_a, gu_b, gp_in, gh_in, attended_ref, after_ref,
              gg_ref, gup_ref, out, hid_out, attended_out, after_out,

time: 367 us -> 366 us (level)
  no operation moved by 1% of the time
where the time goes in v7:
time: 366 us; the launch traced here: 360 us
  Pallas kernels  139 us (38%)
  waiting for transfers between devices  125 us (34%)
  starting transfers between devices  63 us (17%)
  between operations  14.9 us (4%)
  other arithmetic  8.06 us (2%)
  local copies, waits for them, and re-layouts  5.31 us (1%)
  matrix products  4.76 us (1%)
    pallas_call x64, Pallas kernels, run(): return kernel(*placed)  139 us
    ppermute x64, waiting for transfers between devices, exchange(): lax.ppermute(value, axis, [(i, i ^ k) for i in range(lax.axis_size(axis))])  114 us
    ppermute x64, starting transfers between devices, exchange(): lax.ppermute(value, axis, [(i, i ^ k) for i in range(lax.axis_size(axis))])  62.7 us
    reduce_scatter x4, waiting for transfers between devices, data_sum(): lax.psum_scatter(value, ('dp', 'section'), scatter_dimension=0, tiled=True)  10.7 us
  transfers between devices with their start and end apart: 68, of which 33 were waited for; matrix products, arithmetic and copies ran while one was open for 4% of the time, Pallas kernels for 31%

profile of v7, /device:TPU:1, one launch (start us, length us, event | category | flops | bytes accessed | tf_op | source)
XLA Modules:
  0.0 360.0 jit_solution(2718039857382710883)
XLA Ops:
  15.4 6.1 %prepare_weights.3 = (bf16[2,3,1152,512]{3,2,1,0:T(8,128)(2,1)}, bf16[2,512,1152]{2,1,0:T(8,128)(2,1)}) custom-call(s32[2]{0:T(128)S(1)} %pad_add_fusion.where_ref, bf16[3,288,1152]{2,1,0:T(8,128)(2,1)} %bitcast.88, bf16[288,1152]{1,0:T(8,128)(2,1)} %bitcast.92, bf16[288,512]{1,0:T(8,128)(2,1)S(1)} %copy-done), custom_call_target="tpu_custom_call" | custom-call | flops 1000 | bytes 1000 | tf_op jit(solution)/shard_map/prepare_weights/pallas_call | solution.py:56
  26.6 6.3 %prepare_weights.4 = (bf16[2,3,1152,512]{3,2,1,0:T(8,128)(2,1)}, bf16[2,512,1152]{2,1,0:T(8,128)(2,1)}) custom-call(s32[2]{0:T(128)S(1)} %pad_add_fusion.where_ref, bf16[3,288,1152]{2,1,0:T(8,128)(2,1)} %collective-permute-done.3.wq_in, bf16[288,1152]{1,0:T(8,128)(2,1)} %collective-permute-done.4.wo_in, ...), custom_call_target="tpu_custom_call", output_to_operand_aliasing={{0}: (4, {}), {1}: (5, {})} | custom-call | flops 1000 | bytes 1000 | tf_op jit(solution)/shard_map/prepare_weights/pallas_call | solution.py:56
  32.9 9.3 %attention_forward_0.1 = (bf16[128,1152]{1,0:T(8,128)(2,1)S(1)}, bf16[128,1152]{1,0:T(8,128)(2,1)S(1)}, bf16[128,1152]{1,0:T(8,128)(2,1)S(1)}, bf16[128,1152]{1,...) custom-call(s32[2]{0:T(128)S(1)} %pad_add_fusion.where_ref, ...), custom_call_target="tpu_custom_call" | custom-call | flops 1000 | bytes 1000 | tf_op jit(solution)/shard_map/attention_forward_0/pallas_call | solution.py:56
  49.7 8.4 %collective-permute-done.8.source = bf16[128,1152]{1,0:T(8,128)(2,1)S(1)} collective-permute-done((bf16[128,1152]{1,0:T(8,128)(2,1)S(1)}, bf16[128,1152]{1,0:T(8,128)(2,1)S(1)}, u32[]{:S(2)}, u32[]{:S(2)}) %collective-permute-start.8) | collective-permute-done | bytes 294944 | tf_op jit(solution)/shard_map/ppermute | solution.py:1172
  69.6 6.2 %mlp_forward_0.1 = (bf16[128,1152]{1,0:T(8,128)(2,1)S(1)}, bf16[128,1152]{1,0:T(8,128)(2,1)S(1)}, bf16[128,1152]{1,0:T(8,128)(2,1)S(1)}, bf16[128,1152]{1,0:T(8,...) custom-call(s32[1]{0:T(128)} %bitcast.sec_ref, ...), custom_call_target="tpu_custom_call" | custom-call | flops 1000 | bytes 1000 | tf_op jit(solution)/shard_map/mlp_forward_0/pallas_call | solution.py:56
  83.4 5.6 %collective-permute-done.16.source = bf16[128,1152]{1,0:T(8,128)(2,1)S(1)} collective-permute-done((bf16[128,1152]{1,0:T(8,128)(2,1)S(1)}, bf16[128,1152]{1,0:T(8,128)(2,1)S(1)}, u32[]{:S(2)}, u32[]{:S(2)}) %collective-permute-start.16) | collective-permute-done | bytes 294944 | tf_op jit(solution)/shard_map/ppermute | solution.py:1172
  99.3 8.4 %attention_forward_1.1 = (bf16[128,1152]{1,0:T(8,128)(2,1)S(1)}, bf16[128,1152]{1,0:T(8,128)(2,1)S(1)}, bf16[128,1152]{1,0:T(8,128)(2,1)S(1)}, bf16[128,1152]{1,...) custom-call(s32[2]{0:T(128)S(1)} %pad_add_fusion.where_ref, ...), custom_call_target="tpu_custom_call" | custom-call | flops 1000 | bytes 1000 | tf_op jit(solution)/shard_map/attention_forward_1/pallas_call | solution.py:56
  113.5 7.8 %collective-permute-done.22.source = bf16[128,1152]{1,0:T(8,128)(2,1)S(1)} collective-permute-done((bf16[128,1152]{1,0:T(8,128)(2,1)S(1)}, bf16[128,1152]{1,0:T(8,128)(2,1)S(1)}, u32[]{:S(2)}, u32[]{:S(2)}) %collective-permute-start.22) | collective-permute-done | bytes 294944 | tf_op jit(solution)/shard_map/ppermute | solution.py:1172
  132.0 8.9 %mlp_last_1.1 = (bf16[512,768]{1,0:T(8,128)(2,1)S(1)}, bf16[512,768]{1,0:T(8,128)(2,1)S(1)}, bf16[1152,2304]{1,0:T(8,128)(2,1)}, bf16[512,768]{1,0:T(8,128)(2,1)...) custom-call(s32[1]{0:T(128)} %bitcast.sec_ref, bf16[128,1152]{1,0:T(8,128)(2,1)S(1)} %get-tuple-element.231.b0, ...), custom_call_target="tpu_custom_call" | custom-call | flops 1000 | bytes 1000 | tf_op jit(solution)/shard_map/mlp_last_1/pallas_call | solution.py:56
  141.0 4.9 %mlp_input_grad.1 = (bf16[128,1152]{1,0:T(8,128)(2,1)S(1)}, bf16[128,1152]{1,0:T(8,128)(2,1)S(1)}, bf16[128,1152]{1,0:T(8,128)(2,1)S(1)}, bf16[128,1152]{1,0:T(8,128)(2,1)}) custom-call(s32[1]{0:T(128)} %bitcast.sec_ref, bf16[512,768]{1,0:T(8,128)(2,1)S(1)} %get-tuple-element.236.gg_ref, bf16[512,768]{1,0:T(8,128)(2,1)S(1)} %get-tuple-element.237.gup_ref, ...), custom_call_target="tpu_custom_call" | custom-call | flops 1000 | bytes 1000 | tf_op jit(solution)/shard_map/mlp_input_grad/pallas_call | solution.py:56
  148.7 5.9 %last_projection.1 = (bf16[128,1152]{1,0:T(8,128)(2,1)}, bf16[128,1152]{1,0:T(8,128)(2,1)}, bf16[128,1152]{1,0:T(8,128)(2,1)}, bf16[128,1152]{1,0:T(8,128)(2,1)}, f32[1,8,1152]{2,1,0:T(8,128)}) custom-call(s32[2]{0:T(128)S(1)} %pad_add_fusion.where_ref, bf16[512,768]{1,0:T(8,128)(2,1)} %get-tuple-element.240.hid_in, bf16[768,1152]{1,0:T(8,128)(2,1)} %bitcast.83, ...), custom_call_target="tpu_custom_call" | custom-call | flops 1000 | bytes 1000 | tf_op jit(solution)/shard_map/last_projection/pallas_call | solution.py:56
  162.4 5.1 %collective-permute-done.32.source = bf16[128,1152]{1,0:T(8,128)(2,1)S(1)} collective-permute-done((bf16[128,1152]{1,0:T(8,128)(2,1)S(1)}, bf16[128,1152]{1,0:T(8,128)(2,1)S(1)}, u32[]{:S(2)}, u32[]{:S(2)}) %collective-permute-start.32) | collective-permute-done | bytes 294944 | tf_op jit(solution)/shard_map/ppermute | solution.py:1172
  170.7 12.2 %attention_backward_1.1 = (bf16[128,1152]{1,0:T(8,128)(2,1)S(1)}, bf16[128,1152]{1,0:T(8,128)(2,1)S(1)}, bf16[128,1152]{1,0:T(8,128)(2,1)S(1)}, bf16[512,1536]{1...) custom-call(bf16[128,1152]{1,0:T(8,128)(2,1)S(1)} %get-tuple-element, ...), custom_call_target="tpu_custom_call" | custom-call | flops 1000 | bytes 1000 | tf_op jit(solution)/shard_map/attention_backward_1/pallas_call | solution.py:56
  185.6 6.5 %attention_weight_grads.2 = bf16[1152,1152]{1,0:T(8,128)(2,1)} custom-call(bf16[512,1152]{1,0:T(8,128)(2,1)} %get-tuple-element.265.a_in, bf16[512,1536]{1,0:T(8,128)(2,1)} %get-tuple-element.266.g_in, bf16[512,512]{1,0:T(8,128)(2,1)} %get-tuple-element.267.mixed_in, bf16[512,1152]{1,0:T(8,128)(2,1)} %get-tuple-element.268.ga_in, bf16[512,288]{1,0:T(8,128)(2,1)S(1)} %copy-done.1), custom_call_target="tpu_custom_call" | custom-call | flops 1000 | bytes 1000 | tf_op jit(solution)/shard_map/attention_weight_grads/pallas_call | solution.py:56
  192.2 5.4 %collective-permute-done.34.p2 = bf16[128,1152]{1,0:T(8,128)(2,1)S(1)} collective-permute-done((bf16[128,1152]{1,0:T(8,128)(2,1)S(1)}, bf16[128,1152]{1,0:T(8,128)(2,1)S(1)}, u32[]{:S(2)}, u32[]{:S(2)}) %collective-permute-start.34) | collective-permute-done | bytes 294944 | tf_op jit(solution)/shard_map/ppermute | solution.py:1172
  208.2 8.8 %collective-permute-done.37.source = bf16[128,1152]{1,0:T(8,128)(2,1)S(1)} collective-permute-done((bf16[128,1152]{1,0:T(8,128)(2,1)S(1)}, bf16[128,1152]{1,0:T(8,128)(2,1)S(1)}, u32[]{:S(2)}, u32[]{:S(2)}) %collective-permute-start.37) | collective-permute-done | bytes 294944 | tf_op jit(solution)/shard_map/ppermute | solution.py:1172
  217.0 7.9 %mlp_backward_0.1 = (bf16[128,1152]{1,0:T(8,128)(2,1)S(1)}, bf16[128,1152]{1,0:T(8,128)(2,1)S(1)}, bf16[128,1152]{1,0:T(8,128)(2,1)S(1)}, bf16[512,1152]{1,0:T(8...) custom-call(s32[2]{0:T(128)S(1)} %pad_add_fusion.where_ref, ...), custom_call_target="tpu_custom_call" | custom-call | flops 1000 | bytes 1000 | tf_op jit(solution)/shard_map/mlp_backward_0/pallas_call | solution.py:56
  227.9 6.4 %mlp_weight_grads.1 = bf16[1152,2304]{1,0:T(8,128)(2,1)} custom-call(bf16[512,1152]{1,0:T(8,128)(2,1)} %get-tuple-element.283.a_in, bf16[512,768]{1,0:T(8,128)(2,1)} %get-tuple-element.284.gg_in, bf16[512,768]{1,0:T(8,128)(2,1)} %get-tuple-element.285.gu_in, bf16[512,1152]{1,0:T(8,128)(2,1)} %get-tuple-element.286.gp_in, ...), custom_call_target="tpu_custom_call" | custom-call | flops 1000 | bytes 1000 | tf_op jit(solution)/shard_map/mlp_weight_grads/pallas_call | solution.py:56
  234.3 5.7 %collective-permute-done.41.p3 = bf16[128,1152]{1,0:T(8,128)(2,1)S(1)} collective-permute-done((bf16[128,1152]{1,0:T(8,128)(2,1)S(1)}, bf16[128,1152]{1,0:T(8,128)(2,1)S(1)}, u32[]{:S(2)}, u32[]{:S(2)}) %collective-permute-start.41) | collective-permute-done | bytes 294944 | tf_op jit(solution)/shard_map/ppermute | solution.py:1172
  251.9 9.1 %collective-permute-done.43.source = bf16[128,1152]{1,0:T(8,128)(2,1)S(1)} collective-permute-done((bf16[128,1152]{1,0:T(8,128)(2,1)S(1)}, bf16[128,1152]{1,0:T(8,128)(2,1)S(1)}, u32[]{:S(2)}, u32[]{:S(2)}) %collective-permute-start.43) | collective-permute-done | bytes 294944 | tf_op jit(solution)/shard_map/ppermute | solution.py:1172
  261.0 12.5 %attention_backward_0.1 = (bf16[128,1152]{1,0:T(8,128)(2,1)}, bf16[128,1152]{1,0:T(8,128)(2,1)S(1)}, bf16[128,1152]{1,0:T(8,128)(2,1)S(1)}, bf16[512,1536]{1,0:T...) custom-call(bf16[128,1152]{1,0:T(8,128)(2,1)S(1)} %get-tuple-element, ...), custom_call_target="tpu_custom_call" | custom-call | flops 1000 | bytes 1000 | tf_op jit(solution)/shard_map/attention_backward_0/pallas_call | solution.py:56
  276.2 6.7 %attention_weight_grads.3 = bf16[1152,1152]{1,0:T(8,128)(2,1)} custom-call(bf16[512,1152]{1,0:T(8,128)(2,1)} %get-tuple-element.307.a_in, bf16[512,1536]{1,0:T(8,128)(2,1)} %get-tuple-element.308.g_in, bf16[512,512]{1,0:T(8,128)(2,1)} %get-tuple-element.309.mixed_in, bf16[512,1152]{1,0:T(8,128)(2,1)} %get-tuple-element.310.ga_in, bf16[512,288]{1,0:T(8,128)(2,1)S(1)} %copy-done.1), custom_call_target="tpu_custom_call" | custom-call | flops 1000 | bytes 1000 | tf_op jit(solution)/shard_map/attention_weight_grads/pallas_call | solution.py:56
  317.4 5.2 %collective-permute-done.53 = f32[8,3136]{1,0:T(8,128)S(1)} collective-permute-done((f32[8,3136]{1,0:T(8,128)S(1)}, f32[8,3136]{1,0:T(8,128)S(1)}, u32[]{:S(2)}, u32[]{:S(2)}) %collective-permute-start.53) | collective-permute-done | bytes 100384 | tf_op jit(solution)/shard_map/ppermute | solution.py:1172
  337.6 7.4 %reduce-scatter.11.cloned.1.call-done = bf16[144,1152]{1,0:T(8,128)(2,1)} async-done(((bf16[1152,1152]{1,0:T(8,128)(2,1)}), bf16[144,1152]{1,0:T(8,128)(2,1)}) %reduce-scatter.11.cloned.1.call-update) | async-done | bytes 331792 | tf_op jit(solution)/shard_map/reduce_scatter | solution.py:1331
  (267 shorter events, 168.3 us)
Async XLA Ops:
  7.2 191.3 %reduce-scatter.5.cloned.1.call-start = ((), (), s32[]{:S(2)}) async-start(), calls=%async_computation.4 | async-start | bytes 5971968 | tf_op jit(solution)/shard_map/reduce_scatter | solution.py:1331
  7.2 16.8 %collective-permute-start.3 = (bf16[3,288,1152]{2,1,0:T(8,128)(2,1)}, bf16[3,288,1152]{2,1,0:T(8,128)(2,1)}, u32[]{:S(2)}, u32[]{:S(2)}) collective-permute-start(bf16[3,288,1152]{2,1,0:T(8,128)(2,1)} %bitcast.87), channel_id=1, source_target_pairs={{0,16},{16,0},{1,17},{17,1},{2,18},{18,2},{3,19},{19,3},{4,20},{20... | collective-permute-start | bytes 5971976 | tf_op jit(solution)/shard_map/ppermute | solution.py:1172
  7.3 16.6 %collective-permute-start.4 = (bf16[288,1152]{1,0:T(8,128)(2,1)}, bf16[288,1152]{1,0:T(8,128)(2,1)}, u32[]{:S(2)}, u32[]{:S(2)}) collective-permute-start(bf16[288,1152]{1,0:T(8,128)(2,1)} %bitcast.91), channel_id=1, source_target_pairs={{0,16},{16,0},{1,17},{17,1},{2,18},{18,2},{3,19},{19,3},{4,20},{20... | collective-permute-start | bytes 1990664 | tf_op jit(solution)/shard_map/ppermute | solution.py:1172
  26.1 42.3 %collective-permute-start.13 = (bf16[2,1152,768]{2,1,0:T(8,128)(2,1)}, bf16[2,1152,768]{2,1,0:T(8,128)(2,1)}, u32[]{:S(2)}, u32[]{:S(2)}) collective-permute-start(bf16[2,1152,768]{2,1,0:T(8,128)(2,1)} %bitcast.76), channel_id=1, source_target_pairs={{0,16},{16,0},{1,17},{17,1},{2,18},{18,2},{3,19},{19,3},{4,20},{20... | collective-permute-start | bytes 10616840 | tf_op jit(solution)/shard_map/ppermute | solution.py:1172
  26.3 42.1 %collective-permute-start.14 = (bf16[768,1152]{1,0:T(8,128)(2,1)S(1)}, bf16[768,1152]{1,0:T(8,128)(2,1)S(1)}, u32[]{:S(2)}, u32[]{:S(2)}) collective-permute-start(bf16[768,1152]{1,0:T(8,128)(2,1)S(1)} %bitcast.85), channel_id=1, source_target_pairs={{0,16},{16,0},{1,17},{17,1},{2,18},{18,2},{3,19},{19,3},{4,20},{20... | collective-permute-start | bytes 5308424 | tf_op jit(solution)/shard_map/ppermute | solution.py:1172
  43.9 14.2 %collective-permute-start.8 = (bf16[128,1152]{1,0:T(8,128)(2,1)S(1)}, bf16[128,1152]{1,0:T(8,128)(2,1)S(1)}, u32[]{:S(2)}, u32[]{:S(2)}) collective-permute-start(bf16[128,1152]{1,0:T(8,128)(2,1)S(1)} %get-tuple-element.204), channel_id=1, source_target_pairs={{0,8},{4,12},{8,0},{12,4},{1,9},{5,13},{9,1},{13,5},{2,10},{6,14},... | collective-permute-start | bytes 884744 | tf_op jit(solution)/shard_map/ppermute | solution.py:1172
  45.2 12.9 %collective-permute-start.9 = (bf16[128,1152]{1,0:T(8,128)(2,1)S(1)}, bf16[128,1152]{1,0:T(8,128)(2,1)S(1)}, u32[]{:S(2)}, u32[]{:S(2)}) collective-permute-start(bf16[128,1152]{1,0:T(8,128)(2,1)S(1)} %get-tuple-element.205), channel_id=1, source_target_pairs={{0,12},{4,8},{8,4},{12,0},{1,13},{5,9},{9,5},{13,1},{2,14},{6,10},... | collective-permute-start | bytes 884744 | tf_op jit(solution)/shard_map/ppermute | solution.py:1172
  76.2 12.8 %collective-permute-start.16 = (bf16[128,1152]{1,0:T(8,128)(2,1)S(1)}, bf16[128,1152]{1,0:T(8,128)(2,1)S(1)}, u32[]{:S(2)}, u32[]{:S(2)}) collective-permute-start(bf16[128,1152]{1,0:T(8,128)(2,1)S(1)} %get-tuple-element.220), channel_id=1, source_target_pairs={{0,8},{4,12},{8,0},{12,4},{1,9},{5,13},{9,1},{13,5},{2,10},{6,14},... | collective-permute-start | bytes 884744 | tf_op jit(solution)/shard_map/ppermute | solution.py:1172
  141.0 99.0 %reduce-scatter.7.cloned.1.call-start = ((), (), s32[]{:S(2)}) async-start(), calls=%async_computation.5 | async-start | bytes 2985984 | tf_op jit(solution)/shard_map/reduce_scatter | solution.py:1331
  184.0 13.6 %collective-permute-start.34 = (bf16[128,1152]{1,0:T(8,128)(2,1)S(1)}, bf16[128,1152]{1,0:T(8,128)(2,1)S(1)}, u32[]{:S(2)}, u32[]{:S(2)}) collective-permute-start(bf16[128,1152]{1,0:T(8,128)(2,1)S(1)} %get-tuple-element.263), channel_id=1, source_target_pairs={{0,8},{4,12},{8,0},{12,4},{1,9},{5,13},{9,1},{13,5},{2,10},{6,14},... | collective-permute-start | bytes 884744 | tf_op jit(solution)/shard_map/ppermute | solution.py:1172
  198.5 101.9 %reduce-scatter.9.cloned.1.call-start = ((), (), s32[]{:S(2)}) async-start(), calls=%async_computation.6 | async-start | bytes 5971968 | tf_op jit(solution)/shard_map/reduce_scatter | solution.py:1331
  203.7 13.3 %collective-permute-start.37 = (bf16[128,1152]{1,0:T(8,128)(2,1)S(1)}, bf16[128,1152]{1,0:T(8,128)(2,1)S(1)}, u32[]{:S(2)}, u32[]{:S(2)}) collective-permute-start(bf16[128,1152]{1,0:T(8,128)(2,1)S(1)} %get-tuple-element.275.refs_0_), channel_id=1, source_target_pairs={{0,8},{4,12},{8,0},{12,4},{1,9},{5,13},{9,1},{13,5},{2,10},{6,14},... | collective-permute-start | bytes 884744 | tf_op jit(solution)/shard_map/ppermute | solution.py:1172
  203.9 13.1 %collective-permute-start.36 = (bf16[128,1152]{1,0:T(8,128)(2,1)S(1)}, bf16[128,1152]{1,0:T(8,128)(2,1)S(1)}, u32[]{:S(2)}, u32[]{:S(2)}) collective-permute-start(bf16[128,1152]{1,0:T(8,128)(2,1)S(1)} %get-tuple-element.275.refs_0_), channel_id=1, source_target_pairs={{0,4},{4,0},{8,12},{12,8},{1,5},{5,1},{9,13},{13,9},{2,6},{6,2},{1... | collective-permute-start | bytes 884744 | tf_op jit(solution)/shard_map/ppermute | solution.py:1172
  226.9 13.0 %collective-permute-start.41 = (bf16[128,1152]{1,0:T(8,128)(2,1)S(1)}, bf16[128,1152]{1,0:T(8,128)(2,1)S(1)}, u32[]{:S(2)}, u32[]{:S(2)}) collective-permute-start(bf16[128,1152]{1,0:T(8,128)(2,1)S(1)} %get-tuple-element.282), channel_id=1, source_target_pairs={{0,12},{4,8},{8,4},{12,0},{1,13},{5,9},{9,5},{13,1},{2,14},{6,10},... | collective-permute-start | bytes 884744 | tf_op jit(solution)/shard_map/ppermute | solution.py:1172
  240.0 105.0 %reduce-scatter.11.cloned.1.call-start = ((), (), s32[]{:S(2)}) async-start(), calls=%async_computation.7 | async-start | bytes 2985984 | tf_op jit(solution)/shard_map/reduce_scatter | solution.py:1331
  245.8 15.1 %collective-permute-start.43 = (bf16[128,1152]{1,0:T(8,128)(2,1)S(1)}, bf16[128,1152]{1,0:T(8,128)(2,1)S(1)}, u32[]{:S(2)}, u32[]{:S(2)}) collective-permute-start(bf16[128,1152]{1,0:T(8,128)(2,1)S(1)} %get-tuple-element.296.b0), channel_id=1, source_target_pairs={{0,8},{4,12},{8,0},{12,4},{1,9},{5,13},{9,1},{13,5},{2,10},{6,14},... | collective-permute-start | bytes 884744 | tf_op jit(solution)/shard_map/ppermute | solution.py:1172
  245.8 15.2 %collective-permute-start.42 = (bf16[128,1152]{1,0:T(8,128)(2,1)S(1)}, bf16[128,1152]{1,0:T(8,128)(2,1)S(1)}, u32[]{:S(2)}, u32[]{:S(2)}) collective-permute-start(bf16[128,1152]{1,0:T(8,128)(2,1)S(1)} %get-tuple-element.296.b0), channel_id=1, source_target_pairs={{0,4},{4,0},{8,12},{12,8},{1,5},{5,1},{9,13},{13,9},{2,6},{6,2},{1... | collective-permute-start | bytes 884744 | tf_op jit(solution)/shard_map/ppermute | solution.py:1172
  274.9 12.7 %collective-permute-start.47 = (bf16[128,1152]{1,0:T(8,128)(2,1)S(1)}, bf16[128,1152]{1,0:T(8,128)(2,1)S(1)}, u32[]{:S(2)}, u32[]{:S(2)}) collective-permute-start(bf16[128,1152]{1,0:T(8,128)(2,1)S(1)} %get-tuple-element.306), channel_id=1, source_target_pairs={{0,12},{4,8},{8,4},{12,0},{1,13},{5,9},{9,5},{13,1},{2,14},{6,10},... | collective-permute-start | bytes 884744 | tf_op jit(solution)/shard_map/ppermute | solution.py:1172
  303.5 23.7 %collective-permute-start.60 = (bf16[128,1152]{1,0:T(8,128)(2,1)}, bf16[128,1152]{1,0:T(8,128)(2,1)S(1)}, u32[]{:S(2)}, u32[]{:S(2)}) collective-permute-start(bf16[128,1152]{1,0:T(8,128)(2,1)} %get-tuple-element.335), channel_id=1, source_target_pairs={{0,4},{4,0},{8,12},{12,8},{1,5},{5,1},{9,13},{13,9},{2,6},{6,2},{1... | collective-permute-start | bytes 884744 | tf_op jit(solution)/shard_map/ppermute | solution.py:1172
  308.9 13.7 %collective-permute-start.53 = (f32[8,3136]{1,0:T(8,128)S(1)}, f32[8,3136]{1,0:T(8,128)S(1)}, u32[]{:S(2)}, u32[]{:S(2)}) collective-permute-start(f32[8,3136]{1,0:T(8,128)S(1)} %concatenate.57), channel_id=1, source_target_pairs={{0,2},{1,3},{2,0},{3,1},{4,6},{5,7},{6,4},{7,5},{8,10},{9,11},{10,... | collective-permute-start | bytes 301064 | tf_op jit(solution)/shard_map/ppermute | solution.py:1172
  309.2 14.0 %collective-permute-start.52 = (f32[8,3136]{1,0:T(8,128)S(1)}, f32[8,3136]{1,0:T(8,128)S(1)}, u32[]{:S(2)}, u32[]{:S(2)}) collective-permute-start(f32[8,3136]{1,0:T(8,128)S(1)} %concatenate.57), channel_id=1, source_target_pairs={{0,1},{1,0},{2,3},{3,2},{4,5},{5,4},{6,7},{7,6},{8,9},{9,8},{10,11... | collective-permute-start | bytes 301064 | tf_op jit(solution)/shard_map/ppermute | solution.py:1172
  315.3 14.6 %collective-permute-start.61 = (bf16[128,1152]{1,0:T(8,128)(2,1)S(1)}, bf16[128,1152]{1,0:T(8,128)(2,1)S(1)}, u32[]{:S(2)}, u32[]{:S(2)}) collective-permute-start(bf16[128,1152]{1,0:T(8,128)(2,1)S(1)} %copy-done.17), channel_id=1, source_target_pairs={{0,8},{4,12},{8,0},{12,4},{1,9},{5,13},{9,1},{13,5},{2,10},{6,14},... | collective-permute-start | bytes 884744 | tf_op jit(solution)/shard_map/ppermute | solution.py:1172
  316.8 13.2 %collective-permute-start.62 = (bf16[128,1152]{1,0:T(8,128)(2,1)S(1)}, bf16[128,1152]{1,0:T(8,128)(2,1)S(1)}, u32[]{:S(2)}, u32[]{:S(2)}) collective-permute-start(bf16[128,1152]{1,0:T(8,128)(2,1)S(1)} %copy-done.16), channel_id=1, source_target_pairs={{0,12},{4,8},{8,4},{12,0},{1,13},{5,9},{9,5},{13,1},{2,14},{6,10},... | collective-permute-start | bytes 884744 | tf_op jit(solution)/shard_map/ppermute | solution.py:1172
  332.2 16.4 %collective-permute-start.63 = (f32[128,1152]{1,0:T(8,128)}, f32[128,1152]{1,0:T(8,128)}, u32[]{:S(2)}, u32[]{:S(2)}) collective-permute-start(f32[128,1152]{1,0:T(8,128)} %broadcast_select_fusion.6), channel_id=1, source_target_pairs={{0,16},{16,0},{1,17},{17,1},{2,18},{18,2},{3,19},{19,3},{4,20},{20... | collective-permute-start | bytes 1769480 | tf_op jit(solution)/shard_map/ppermute | solution.py:1172
  (62 other events, 499.5 us)
Sparse Core Ops, SparseCore 0:
  141.1 57.3 reduce-scatter.4
  200.8 35.9 reduce-scatter.6
  240.1 60.2 reduce-scatter.8
  303.7 41.2 reduce-scatter.10
